TPU v7x, 512 devices: a whole 4x8x8 slice. The times are simulated.
512 devices in a mesh: ctx: 16 (over z_lo, y), head: 8 (over x, core), batch: 4 (over z_hi).
Axes of the slice: x: 4, y: 8, z: 8 (z_hi: 4, z_lo: 2; z = z_hi * 2 + z_lo), core: 2. Of those that a mesh axis runs over, the one named last changes fastest.
Arguments:
- ingest: bfloat16 [16, 4, 12, 128, 4, 1024], P('ctx', 'batch', None, None, None, 'head'), may hold values from -6 to 6
- src_shard: int32 [16, 4, 6], P('ctx'), may hold values from 0 to 3, as said below
- src_slot: int32 [16, 4, 6], P('ctx'), may hold values from 0 to 11
- hist_len: int32 [4, 4], P('batch'), may hold values from 1 to 6144, 12288 in all within a row
- w_out: bfloat16 [1024, 1024], P('head'), may hold values from -0.1875 to 0.1875
Outputs:
- mixed: bfloat16 [4, 12288, 1024], P('batch', 'ctx', 'head')
Inputs may be any that keep to these rules, and one draw needn't show every extreme that they name: `src_shard`: for each owner index, every owner's 6 blocks come from exactly two different ingestion shards, 3 from each; no (shard, slot) pair of one owner index feeds two blocks. `hist_len`: the 4 histories of a group fill its 12288 positions in order.
All inputs are finite; a program needn't handle non-finite values.
Results may differ from a plain program's by a relative error of at most 0.0058.
Values may be sent and summed in bfloat16 or wider, within the bound.
No kernel may reach another device: no remote copies, remote signals or barrier semaphores. Data moves between devices by JAX's collectives and lax.ppermute only.
A program may use at most 64 MiB of HBM per device.

v0:
```python
import math

import jax
import jax.numpy as jnp
from jax import lax
from jax.sharding import PartitionSpec as P

HD = 128


key_block = 512


def side_by_side(arrays, axis, dim, along):
    both = jnp.concatenate(arrays, axis=along)
    out, at, done = (lax.all_gather(both, axis, axis=dim, tiled=True), 0, [])
    for a in arrays:
        done.append(lax.slice_in_dim(out, at, at + a.shape[along], axis=along))
        at += a.shape[along]
    return tuple(done)


def laid_out(blocks, dim):
    blocks = jnp.moveaxis(blocks, 0, dim)
    lengths = blocks.shape
    return blocks.reshape(*lengths[:dim], lengths[dim] * lengths[dim + 1], *lengths[dim + 2 :])


def copy_for_each(x, axis):
    size = lax.axis_size(axis)
    return lax.all_to_all(jnp.broadcast_to(x[None], (size, *x.shape)), axis, 0, 0, tiled=True)


def gather_directly(x, axis, dim):
    return laid_out(copy_for_each(x, axis), dim)


def body(ingest, src_shard, src_slot, hist_len, w_out):
    groups = lax.axis_size("batch")
    me_batch = lax.axis_index("batch")
    ingested = ingest[0, 0]
    slot_total, block_rows, kinds, local_width = ingested.shape
    shards = src_shard[0]
    slot_ids = src_slot[0]
    per_owner = shards.shape[1]
    capacity = per_owner // 2
    matching = shards == me_batch
    sender_rank = jnp.cumsum(matching.astype(jnp.int32), axis=1) - 1
    slot_order = jnp.arange(capacity, dtype=jnp.int32)
    picked = matching[:, :, None] & (sender_rank[:, :, None] == slot_order[None, None, :])
    send_slot = jnp.sum(jnp.where(picked, slot_ids[:, :, None], 0), axis=1)
    send_live = jnp.any(picked, axis=1)
    outgoing = jnp.take(ingested, send_slot.reshape(-1), axis=0)
    outgoing = outgoing.reshape(groups, capacity, block_rows, kinds, local_width)
    outgoing = jnp.where(send_live[:, :, None, None, None], outgoing, jnp.zeros_like(outgoing))
    incoming = lax.all_to_all(outgoing, "batch", split_axis=0, concat_axis=0, tiled=True)
    owner_flags = jnp.arange(groups, dtype=jnp.int32) == me_batch
    own_sources = jnp.sum(jnp.where(owner_flags[:, None], shards, 0), axis=0)
    block_pos = jnp.arange(per_owner)
    earlier = (own_sources[None, :] == own_sources[:, None]) & (
        block_pos[None, :] < block_pos[:, None]
    )
    arrival = jnp.sum(earlier.astype(jnp.int32), axis=1)
    flat_index = own_sources * capacity + arrival
    owned = jnp.take(
        incoming.reshape(groups * capacity, block_rows, kinds, local_width), flat_index, axis=0
    )
    row_count = per_owner * block_rows
    owned = owned.reshape(row_count, kinds, local_width)
    heads_local = local_width // HD
    queries = owned[:, 0].reshape(row_count, heads_local, HD)
    key_part = owned[:, 1]
    value_part = owned[:, 2]
    update_rows = owned[:, 3].reshape(row_count, heads_local, HD)
    query_pos = lax.axis_index("ctx") * row_count + jnp.arange(row_count, dtype=jnp.int32)
    seg_ends = jnp.cumsum(hist_len[0])

    def segment_of(positions):
        return jnp.sum((positions[:, None] >= seg_ends[None, :]).astype(jnp.int32), axis=1)

    query_seg = segment_of(query_pos)
    score_scale = 1.0 / math.sqrt(HD)

    def tile_update(running, key_rows, value_rows, offset):
        key_count = key_rows.shape[0]
        key_pos = offset + jnp.arange(key_count, dtype=jnp.int32)
        visible = (query_seg[:, None] == segment_of(key_pos)[None, :]) & (
            key_pos[None, :] <= query_pos[:, None]
        )
        key_heads = key_rows.reshape(key_count, heads_local, HD)
        value_heads = value_rows.reshape(key_count, heads_local, HD)
        scores = (
            jnp.einsum("qhd,khd->hqk", queries, key_heads, preferred_element_type=jnp.float32)
            * score_scale
        )
        weights = jnp.where(visible[None], jax.nn.silu(scores), 0.0).astype(jnp.bfloat16)
        return running + jnp.einsum(
            "hqk,khd->qhd", weights, value_heads, preferred_element_type=jnp.float32
        )

    empty = jnp.zeros((row_count, heads_local, HD), jnp.float32)
    key_rows, value_rows = side_by_side((key_part, value_part), "ctx", 0, 1)
    key_count = key_rows.shape[0]
    blocks = key_count // key_block
    key_blocks = key_rows.reshape(blocks, key_block, key_rows.shape[1])
    value_blocks = value_rows.reshape(blocks, key_block, value_rows.shape[1])
    block_offsets = key_block * jnp.arange(blocks, dtype=jnp.int32)

    def step_block(carry, block_args):
        key_tile, value_tile, tile_offset = block_args
        return (tile_update(carry, key_tile, value_tile, tile_offset), None)

    attended = lax.scan(step_block, empty, (key_blocks, value_blocks, block_offsets))[0]
    mean_square = jnp.mean(attended * attended, axis=-1, keepdims=True)
    normed = attended * lax.rsqrt(mean_square + 1e-06)
    gated_out = (
        (normed * update_rows.astype(jnp.float32))
        .astype(jnp.bfloat16)
        .reshape(row_count, local_width)
    )
    column_block = lax.all_to_all(w_out, "head", split_axis=1, concat_axis=0, tiled=True)
    mixed_rows = jnp.dot(
        gather_directly(gated_out, "head", 1), column_block, preferred_element_type=jnp.float32
    )
    return mixed_rows.astype(jnp.bfloat16)[None]


def solution(mesh):
    in_specs = (
        P("ctx", "batch", None, None, None, "head"),
        P("ctx", None, None),
        P("ctx", None, None),
        P("batch", None),
        P("head", None),
    )
    out_specs = P("batch", "ctx", "head")
    return jax.shard_map(body, mesh=mesh, in_specs=in_specs, out_specs=out_specs, check_vma=False)
```

profile of v0, /device:TPU:1, one launch (start us, length us, event | category | flops | bytes accessed | tf_op | source)
XLA Modules:
  0.0 269.4 jit_solution(10393651953535403583)
XLA Ops:
  12.3 11.0 %all-to-all-start = ((bf16[4,3,128,4,128]{4,2,3,1,0:T(8,128)(2,1)}), bf16[4,3,128,4,128]{4,2,3,1,0:T(8,128)(2,1)S(1)}, u32[]{:S(2)}, u32[]{:S(2)}) async-start(bf16[4,3,128,4,128]{4,2,3,1,0:T(8,128)(2,1)} %fusion.32), calls=%async_computation | async-start | bytes 3145728 | tf_op jit(solution)/shard_map/all_to_all | solution.py:56
  23.7 25.0 %all-to-all-done = bf16[4,3,128,4,128]{4,2,3,1,0:T(8,128)(2,1)S(1)} async-done(((bf16[4,3,128,4,128]{4,2,3,1,0:T(8,128)(2,1)}), bf16[4,3,128,4,128]{4,2,3,1,0:T(8,128)(2,1)S(1)}, u32[]{:S(2)}, u32[]{:S(2)}) %all-to-all-start) | async-done | bytes 1572896 | tf_op jit(solution)/shard_map/all_to_all | solution.py:56
  53.6 7.2 %all-to-all-start.2 = ((bf16[128,8,128]{2,0,1:T(8,128)(2,1)}), bf16[128,8,128]{2,0,1:T(8,128)(2,1)S(1)}, u32[]{:S(2)}, u32[]{:S(2)}) async-start(bf16[128,8,128]{2,0,1:T(8,128)(2,1)} %copy.22), calls=%async_computation.2 | async-start | bytes 524288 | tf_op jit(solution)/shard_map/all_to_all | solution.py:121
  61.1 83.8 %all-gather.2.cloned.1.call-done = bf16[12288,256]{1,0:T(8,128)(2,1)} async-done(((bf16[768,256]{1,0:T(8,128)(2,1)}), bf16[12288,256]{1,0:T(8,128)(2,1)}) %all-gather.2.cloned.1.call-update) | async-done | bytes 6291472 | tf_op jit(solution)/shard_map/all_gather | solution.py:16
  144.9 4.7 %fusion.51 = (bf16[12288,128]{1,0:T(8,128)(2,1)}, bf16[12288,128]{1,0:T(8,128)(2,1)}) fusion(bf16[12288,256]{1,0:T(8,128)(2,1)} %all-gather.2.cloned.1.call-done), kind=kLoop, calls=%fused_computation.76 | loop fusion | bytes 12582912 | tf_op jit(solution)/shard_map/slice | solution.py:18
  149.6 81.8 %while.11 = (s32[]{:T(128)}, f32[768,1,128]{0,2,1:T(8,128)S(1)}, bf16[24,512,128]{2,1,0:T(8,128)(2,1)}, s32[768]{0:T(1024)S(1)}, s32[24]{0:T(128)S(1)}, /*index=...) while((s32[]{:T(128)}, f32[768,1,128]{0,2,1:T(8,128)S(1)}, ...), condition=%wide.region_9.10_spmd.clone, body=%wide.region_7.9_spmd.clone.sunk | while | flops 205462272 | bytes 1265819 | solution.py:113
  151.1 1.9 fusion.60
  154.5 1.9 fusion.60
  157.9 1.9 fusion.60
  164.7 1.9 fusion.60
  171.5 1.9 fusion.60
  174.9 1.9 fusion.60
  178.3 1.9 fusion.60
  185.1 1.9 fusion.60
  191.9 1.9 fusion.60
  195.4 1.9 fusion.60
  198.8 1.9 fusion.60
  205.6 1.9 fusion.60
  209.0 1.9 fusion.60
  212.4 1.9 fusion.60
  215.8 1.9 fusion.60
  219.2 1.9 fusion.60
  226.0 1.9 fusion.60
  232.0 29.3 %all_to_all.26 = bf16[8,768,128]{2,1,0:T(8,128)(2,1)S(1)} all-to-all(bf16[8,768,128]{2,1,0:T(8,128)(2,1)S(1)} %broadcast_in_dim.112), channel_id=1, replica_groups=mesh['ctx'=16,'head'=8,'batch'=4] {'head'}, dimensions={0} | all-to-all | bytes 3145728 | tf_op jit(solution)/shard_map/all_to_all | solution.py:31
  (153 shorter events, 61.3 us)
Async XLA Ops:
  6.5 2.4 copy-start
  12.3 11.0 %copy-start.2 = (s32[1,4,6]{2,1,0:T(4,128)S(1)}, s32[1,4,6]{2,1,0:T(4,128)}, u32[]{:S(2)}) copy-start(s32[1,4,6]{2,1,0:T(4,128)} %param.8) | copy-start | bytes 292
  12.3 36.4 %all-to-all-start = ((bf16[4,3,128,4,128]{4,2,3,1,0:T(8,128)(2,1)}), bf16[4,3,128,4,128]{4,2,3,1,0:T(8,128)(2,1)S(1)}, u32[]{:S(2)}, u32[]{:S(2)}) async-start(bf16[4,3,128,4,128]{4,2,3,1,0:T(8,128)(2,1)} %fusion.32), calls=%async_computation | async-start | bytes 3145728 | tf_op jit(solution)/shard_map/all_to_all | solution.py:56
  23.3 121.6 %all-gather.2.cloned.1.call-start = ((), (), s32[]{:S(2)}) async-start(), calls=%async_computation.3 | async-start | bytes 6684672 | tf_op jit(solution)/shard_map/all_gather | solution.py:16
  51.6 1.0 copy-start.1
  51.7 9.1 %copy-start.3 = (s32[1,4]{1,0:T(1,128)S(1)}, s32[1,4]{1,0:T(1,128)}, u32[]{:S(2)}) copy-start(s32[1,4]{1,0:T(1,128)} %param.10) | copy-start | bytes 52
  53.6 178.2 %all-to-all-start.2 = ((bf16[128,8,128]{2,0,1:T(8,128)(2,1)}), bf16[128,8,128]{2,0,1:T(8,128)(2,1)S(1)}, u32[]{:S(2)}, u32[]{:S(2)}) async-start(bf16[128,8,128]{2,0,1:T(8,128)(2,1)} %copy.22), calls=%async_computation.2 | async-start | bytes 524288 | tf_op jit(solution)/shard_map/all_to_all | solution.py:121
Sparse Core Ops, SparseCore 0:
  52.6 92.1 all-gather.1
where the time goes:
time: 271 us; the launch traced here: 269 us
  waiting for transfers between devices  109 us (40%)
  matrix products  47.6 us (18%)
  blocking collectives  29.3 us (11%)
  local copies, waits for them, and re-layouts  27.3 us (10%)
  other arithmetic  23.9 us (9%)
  starting transfers between devices  18.2 us (7%)
  between operations  13.5 us (5%)
    all_gather x1, waiting for transfers between devices, side_by_side(): out, at, done = (lax.all_gather(both, axis, axis=dim, tiled=True), 0, [])  83.8 us
    dot_general x24, matrix products, tile_update(): jnp.einsum('hqk,khd->qhd', weights, value_heads, preferred_element_type=j...  46.3 us
    all_to_all x1, blocking collectives, copy_for_each(): lax.all_to_all(jnp.broadcast_to(x[None], (size, *x.shape)), axis, 0, 0, t...  29.3 us
    all_to_all x1, waiting for transfers between devices, body(): lax.all_to_all(outgoing, 'batch', split_axis=0, concat_axis=0, tiled=True)  25 us
    add x24, other arithmetic, tile_update(): key_pos = offset + jnp.arange(key_count, dtype=jnp.int32)  16.6 us
    dynamic_slice x24, local copies, waits for them, and re-layouts, body(): lax.scan(step_block, empty, (key_blocks, value_blocks, block_offsets))[0]  16 us
    all_to_all x1, starting transfers between devices, body(): lax.all_to_all(outgoing, 'batch', split_axis=0, concat_axis=0, tiled=True)  11 us
    all_to_all x1, starting transfers between devices, body(): lax.all_to_all(w_out, 'head', split_axis=1, concat_axis=0, tiled=True)  7.19 us
  transfers between devices with their start and end apart: 3, of which 2 were waited for; matrix products, arithmetic and copies ran while one was open for 33% of the time, Pallas kernels for 0%

commit v1 on v0

v1 whole, which is shorter than its diff:
```python
import functools
import math

import jax
import jax.numpy as jnp
from jax import lax
from jax.experimental import pallas as pl
from jax.experimental.pallas import tpu as pltpu
from jax.sharding import PartitionSpec as P

HD = 128
BLOCK = 128
PER_OWNER = 6
CAPACITY = 3
GROUPS = 4
CTXS = 16
PLANE = 8
HEADS = 8
ROWS = BLOCK * PER_OWNER
CHUNK = ROWS // HEADS
TILE = 256
HALF_SCALE = 0.5 / math.sqrt(HD)
VMEM = pl.BlockSpec(memory_space=pltpu.VMEM)
SMEM = pl.BlockSpec(memory_space=pltpu.SMEM)
ANY = pl.BlockSpec(memory_space=pl.ANY)


def params():
    return pltpu.CompilerParams(vmem_limit_bytes=48 * 1024 * 1024)


def pick_kernel(kinds, shard_ref, slot_ref, ingest_ref, out_ref, buf, sems):
    me = lax.axis_index("batch")
    copies = []
    for g in range(GROUPS):
        seen = jnp.int32(0)
        slots = [jnp.int32(0)] * CAPACITY
        for k in range(PER_OWNER):
            hit = shard_ref[g, k] == me
            slot = slot_ref[g, k]
            for r in range(CAPACITY):
                slots[r] = jnp.where(hit & (seen == r), slot, slots[r])
            seen = seen + hit.astype(jnp.int32)
        for r in range(CAPACITY):
            at = g * CAPACITY + r
            copy = pltpu.make_async_copy(ingest_ref.at[slots[r]], buf.at[at], sems.at[at])
            copy.start()
            copies.append(copy)
    for at, copy in enumerate(copies):
        copy.wait()
        for place, kind in enumerate(kinds):
            out_ref[at, :, place * HD : (place + 1) * HD] = buf[at, :, kind, :]


def pick(shards, slots, ingested, kinds):
    count = GROUPS * CAPACITY
    return pl.pallas_call(
        functools.partial(pick_kernel, kinds),
        out_shape=jax.ShapeDtypeStruct((count, BLOCK, 2 * HD), jnp.bfloat16),
        in_specs=[SMEM, SMEM, ANY],
        out_specs=VMEM,
        scratch_shapes=[
            pltpu.VMEM((count, BLOCK, 4, HD), jnp.bfloat16),
            pltpu.SemaphoreType.DMA((count,)),
        ],
        compiler_params=params(),
    )(shards, slots, ingested)


def order_kernel(split, shard_ref, in_ref, *out_refs):
    me = lax.axis_index("batch")
    shards = [shard_ref[me, k] for k in range(PER_OWNER)]
    for k in range(PER_OWNER):
        rank = jnp.int32(0)
        for earlier in range(k):
            rank = rank + (shards[earlier] == shards[k]).astype(jnp.int32)
        block = in_ref[shards[k] * CAPACITY + rank]
        rows = slice(k * BLOCK, (k + 1) * BLOCK)
        if split:
            out_refs[0][rows, :] = block[:, :HD]
            out_refs[1][rows, :] = block[:, HD:]
        else:
            out_refs[0][rows, :] = block


def in_order(shards, blocks, split):
    width = HD if split else 2 * HD
    shape = jax.ShapeDtypeStruct((ROWS, width), jnp.bfloat16)
    return pl.pallas_call(
        functools.partial(order_kernel, split),
        out_shape=[shape] * (2 if split else 1),
        in_specs=[SMEM, VMEM],
        out_specs=[VMEM] * (2 if split else 1),
        compiler_params=params(),
    )(shards, blocks)


def unit_owner(me, kind, step):
    if kind == "up":
        return me - step
    plane, row = me // PLANE, me % PLANE
    return plane * PLANE + (row + step) % PLANE


def history_ends(hist_ref):
    ends, total = [], jnp.int32(0)
    for u in range(4):
        total = total + hist_ref[0, u]
        ends.append(total)
    return ends


def start_of(ends, pos):
    start = jnp.zeros_like(pos)
    for e in ends:
        start = jnp.where(pos >= e, jnp.maximum(start, e), start)
    return start


def silu_of_dot(q, k):
    s = lax.dot_general(q, k, (((1,), (1,)), ((), ())), preferred_element_type=jnp.float32)
    h = s * HALF_SCALE
    return h + h * jnp.tanh(h)


def add_units(ends, q_base, q_ref, units, acc_ref):
    def row_tile(t, _):
        rows = pl.ds(pl.multiple_of(t * TILE, TILE), TILE)
        first = q_base + t * TILE
        last = first + TILE - 1
        low, high = start_of(ends, first), start_of(ends, last)
        for owner, unit in units:
            base = owner * ROWS
            some = (base <= last) & (base + ROWS - 1 >= low)
            whole = (base + ROWS - 1 <= first) & (base >= high)

            @pl.when(whole)
            def _():
                w = silu_of_dot(q_ref[rows, :], unit[:, :HD]).astype(jnp.bfloat16)
                acc_ref[rows, :] += jnp.dot(w, unit[:, HD:], preferred_element_type=jnp.float32)

            @pl.when(some & jnp.logical_not(whole))
            def _():
                for part in range(ROWS // TILE):
                    k_first = base + part * TILE
                    keys = slice(part * TILE, (part + 1) * TILE)

                    @pl.when((k_first <= last) & (k_first + TILE - 1 >= low))
                    def _():
                        pos = first + lax.broadcasted_iota(jnp.int32, (TILE, TILE), 0)
                        key = k_first + lax.broadcasted_iota(jnp.int32, (TILE, TILE), 1)
                        seen = (key <= pos) & (key >= start_of(ends, pos))
                        w = silu_of_dot(q_ref[rows, :], unit[keys, :HD])
                        w = jnp.where(seen, w, 0.0).astype(jnp.bfloat16)
                        acc_ref[rows, :] += jnp.dot(
                            w, unit[keys, HD:], preferred_element_type=jnp.float32
                        )

        return 0

    lax.fori_loop(0, ROWS // TILE, row_tile, 0)


def attend_kernel(names, first, hist_ref, q_ref, *refs):
    units, refs = refs[: len(names)], refs[len(names) :]
    acc_ref = refs[-1]
    if first:
        acc_ref[...] = jnp.zeros_like(acc_ref)
    else:
        acc_ref[...] = refs[0][...]
    me = lax.axis_index("ctx")
    ends = history_ends(hist_ref)
    owners = [unit_owner(me, *name) for name in names]
    add_units(ends, me * ROWS, q_ref, list(zip(owners, units)), acc_ref)


def estimate(units):
    return pl.CostEstimate(
        flops=4 * ROWS * ROWS * HD * units, bytes_accessed=1 << 20, transcendentals=ROWS * ROWS * units
    )


def attend(hist, q, units, names, acc=None):
    first = acc is None
    return pl.pallas_call(
        functools.partial(attend_kernel, names, first),
        out_shape=jax.ShapeDtypeStruct((ROWS, HD), jnp.float32),
        in_specs=[SMEM] + [VMEM] * (1 + len(units) + (0 if first else 1)),
        out_specs=VMEM,
        cost_estimate=estimate(len(units)),
        compiler_params=params(),
    )(hist, q, *units, *(() if first else (acc,)))


def lent_kernel(names, hist_ref, q_ref, *refs):
    units, out_ref, acc_ref = refs[: len(names)], refs[-2], refs[-1]
    acc_ref[...] = jnp.zeros_like(acc_ref)
    me = lax.axis_index("ctx")

    @pl.when(me < PLANE)
    def _():
        ends = history_ends(hist_ref)
        owners = [unit_owner(me, *name) for name in names]
        add_units(ends, (me + PLANE) * ROWS, q_ref, list(zip(owners, units)), acc_ref)

    out_ref[...] = acc_ref[...].astype(jnp.bfloat16)


def attend_lent(hist, q, units, names):
    return pl.pallas_call(
        functools.partial(lent_kernel, names),
        out_shape=jax.ShapeDtypeStruct((ROWS, HD), jnp.bfloat16),
        in_specs=[SMEM] + [VMEM] * (1 + len(units)),
        out_specs=VMEM,
        scratch_shapes=[pltpu.VMEM((ROWS, HD), jnp.float32)],
        cost_estimate=estimate(len(units)),
        compiler_params=params(),
    )(hist, q, *units)


def last_kernel(names, hist_ref, q_ref, *refs):
    units = refs[: len(names)]
    acc_in, lent_ref, update_ref, out_ref, acc_ref = refs[len(names) :]
    me = lax.axis_index("ctx")
    acc_ref[...] = acc_in[...]

    @pl.when(me >= PLANE)
    def _():
        acc_ref[...] += lent_ref[...].astype(jnp.float32)

    ends = history_ends(hist_ref)
    owners = [unit_owner(me, *name) for name in names]
    add_units(ends, me * ROWS, q_ref, list(zip(owners, units)), acc_ref)
    a = acc_ref[...]
    mean = jnp.mean(a * a, axis=-1, keepdims=True)
    normed = a * lax.rsqrt(mean + 1e-6)
    out_ref[...] = (normed * update_ref[...].astype(jnp.float32)).astype(jnp.bfloat16)


def attend_last(hist, q, units, names, acc, lent, update):
    return pl.pallas_call(
        functools.partial(last_kernel, names),
        out_shape=jax.ShapeDtypeStruct((ROWS, HD), jnp.bfloat16),
        in_specs=[SMEM] + [VMEM] * (4 + len(units)),
        out_specs=VMEM,
        scratch_shapes=[pltpu.VMEM((ROWS, HD), jnp.float32)],
        cost_estimate=estimate(len(units)),
        compiler_params=params(),
    )(hist, q, *units, acc, lent, update)


def project_kernel(rows_ref, w_ref, out_ref):
    rows = jnp.concatenate([rows_ref[h] for h in range(HEADS)], axis=1)
    mixed = jnp.dot(rows, w_ref[...], preferred_element_type=jnp.float32).astype(jnp.bfloat16)
    for h in range(HEADS):
        out_ref[h] = mixed[:, h * HD : (h + 1) * HD]


def project(rows, w):
    return pl.pallas_call(
        project_kernel,
        out_shape=jax.ShapeDtypeStruct((HEADS, CHUNK, HD), jnp.bfloat16),
        in_specs=[VMEM, VMEM],
        out_specs=VMEM,
        compiler_params=params(),
    )(rows, w)


UP = [(i, i + 1) for i in range(CTXS - 1)]
DOWN = [(i, i // PLANE * PLANE + (i - 1) % PLANE) for i in range(CTXS)]
LEND = [(i + PLANE, i) for i in range(PLANE)]
RETURN = [(i, i + PLANE) for i in range(PLANE)]


def body(ingest, src_shard, src_slot, hist_len, w_out):
    ingested, shards, slots = ingest[0, 0], src_shard[0], src_slot[0]
    move = functools.partial(lax.ppermute, axis_name="ctx")

    def to_owners(kinds):
        blocks = pick(shards, slots, ingested, kinds)
        return lax.all_to_all(blocks, "batch", split_axis=0, concat_axis=0, tiled=True)

    whole_w = lax.all_gather(w_out, "head", axis=0, tiled=True)
    (own,) = in_order(shards, to_owners((1, 2)), False)
    q, update = in_order(shards, to_owners((0, 3)), True)
    up, down = [own], [own]
    for step in range(4):
        up.append(move(up[-1], perm=UP))
        if step < 3:
            down.append(move(down[-1], perm=DOWN))
    lent_q = move(q, perm=LEND)
    acc = attend(hist_len, q, (own, up[1], down[1]), (("up", 0), ("up", 1), ("down", 1)))
    acc = attend(hist_len, q, (up[2], down[2]), (("up", 2), ("down", 2)), acc)
    lent = attend_lent(hist_len, lent_q, tuple(down), tuple(("down", k) for k in range(4)))
    lent = move(lent, perm=RETURN)
    acc = attend(hist_len, q, (up[3], down[3]), (("up", 3), ("down", 3)), acc)
    gated = attend_last(hist_len, q, (up[4],), (("up", 4),), acc, lent, update)
    rows = lax.all_to_all(gated.reshape(HEADS, CHUNK, HD), "head", 0, 0, tiled=True)
    mixed = project(rows, whole_w)
    mixed = lax.all_to_all(mixed, "head", 0, 0, tiled=True)
    return mixed.reshape(1, ROWS, HD)


def solution(mesh):
    in_specs = (
        P("ctx", "batch", None, None, None, "head"),
        P("ctx", None, None),
        P("ctx", None, None),
        P("batch", None),
        P("head", None),
    )
    out_specs = P("batch", "ctx", "head")
    return jax.shard_map(body, mesh=mesh, in_specs=in_specs, out_specs=out_specs, check_vma=False)
```

time: 271 us -> 143 us (0.53)
  waiting for transfers between devices: 109 us -> 28 us
  matrix products: 47.6 us -> 0 us
  starting transfers between devices: 18.2 us -> 55.1 us
  other arithmetic: 23.9 us -> 0 us
  local copies, waits for them, and re-layouts: 27.3 us -> 5.05 us
  Pallas kernels: 0 us -> 19.9 us
  blocking collectives: 29.3 us -> 20.4 us
    all_gather x1, waiting for transfers between devices: 83.8 us -> 0.01 us  [body(): whole_w = lax.all_gather(w_out, 'head', axis=0, tiled=True)]
    dot_general x25 -> x0, matrix products: 47.6 us -> none  [the longest x24 46.3 us: tile_update(): jnp.einsum('hqk,khd->qhd', weights, value_heads, preferred_element_type=j...]
    ppermute x0 -> x9, starting transfers between devices: none -> 36.7 us  [the longest x3 25.4 us: body(): down.append(move(down[-1], perm=DOWN))]
    pallas_call x0 -> x10, Pallas kernels: none -> 19.9 us  [the longest x2 11.2 us: pick(): pl.pallas_call(functools.partial(pick_kernel, kinds), out_shape=jax.Shape...]
    ppermute x0 -> x9, waiting for transfers between devices: none -> 17.7 us  [the longest x3 7.53 us: body(): down.append(move(down[-1], perm=DOWN))]
    add x49 -> x0, other arithmetic: 16.7 us -> none  [the longest x24 16.6 us: tile_update(): key_pos = offset + jnp.arange(key_count, dtype=jnp.int32)]
    dynamic_slice x24 -> x0, local copies, waits for them, and re-layouts: 16 us -> none  [body(): lax.scan(step_block, empty, (key_blocks, value_blocks, block_offsets))[0]]
    all_to_all x2, waiting for transfers between devices: 25 us -> 9.53 us  [to_owners(): lax.all_to_all(blocks, 'batch', split_axis=0, concat_axis=0, tiled=True)]
  transfers between devices with their start and end apart: 3 -> 12, of which waited for: 2 -> 5; matrix products, arithmetic and copies ran while one was open for 33% -> 0% of each run, Pallas kernels for 0% -> 14%
where the time goes in v1:
time: 143 us; the launch traced here: 142 us
  starting transfers between devices  55.1 us (39%)
  waiting for transfers between devices  28 us (20%)
  blocking collectives  20.4 us (14%)
  Pallas kernels  19.9 us (14%)
  between operations  13.6 us (10%)
  local copies, waits for them, and re-layouts  5.05 us (4%)
    ppermute x3, starting transfers between devices, body(): down.append(move(down[-1], perm=DOWN))  25.4 us
    all_to_all x2, starting transfers between devices, to_owners(): lax.all_to_all(blocks, 'batch', split_axis=0, concat_axis=0, tiled=True)  18.4 us
    pallas_call x2, Pallas kernels, pick(): pl.pallas_call(functools.partial(pick_kernel, kinds), out_shape=jax.Shape...  11.2 us
    all_to_all x1, blocking collectives, body(): lax.all_to_all(gated.reshape(HEADS, CHUNK, HD), 'head', 0, 0, tiled=True)  11.2 us
    all_to_all x2, waiting for transfers between devices, to_owners(): lax.all_to_all(blocks, 'batch', split_axis=0, concat_axis=0, tiled=True)  9.53 us
    all_to_all x1, blocking collectives, body(): mixed = lax.all_to_all(mixed, 'head', 0, 0, tiled=True)  9.23 us
    ppermute x4, starting transfers between devices, body(): up.append(move(up[-1], perm=UP))  8.39 us
    ppermute x3, waiting for transfers between devices, body(): down.append(move(down[-1], perm=DOWN))  7.53 us
  transfers between devices with their start and end apart: 12, of which 5 were waited for; matrix products, arithmetic and copies ran while one was open for 0% of the time, Pallas kernels for 14%

profile of v1, /device:TPU:1, one launch (start us, length us, event | category | flops | bytes accessed | tf_op | source)
XLA Modules:
  0.0 142.0 jit_solution(16641252935064788189)
XLA Ops:
  7.3 1.4 copy-done
  10.0 5.6 %shard_map.57 = bf16[12,128,256]{2,1,0:T(8,128)(2,1)} custom-call(s32[4,6]{1,0:T(4,128)S(1)} %bitcast.8, s32[4,6]{1,0:T(4,128)S(1)} %bitcast.12, bf16[12,128,4,128]{3,2,1,0:T(4,128)(2,1)S(1)} %bitcast.5), custom_call_target="tpu_custom_call" | custom-call | tf_op jit(solution)/shard_map/pallas_call | solution.py:57
  15.7 10.9 %all-to-all-start.1 = ((bf16[12,128,256]{2,1,0:T(8,128)(2,1)}), bf16[12,128,256]{2,1,0:T(8,128)(2,1)S(1)}, u32[]{:S(2)}, u32[]{:S(2)}) async-start(bf16[12,128,256]{2,1,0:T(8,128)(2,1)} %shard_map.57), calls=%async_computation.1 | async-start | bytes 1572864 | tf_op jit(solution)/shard_map/all_to_all | solution.py:281
  26.5 5.6 %shard_map.55 = bf16[12,128,256]{2,1,0:T(8,128)(2,1)} custom-call(s32[4,6]{1,0:T(4,128)S(1)} %bitcast.9, s32[4,6]{1,0:T(4,128)S(1)} %bitcast.13, bf16[12,128,4,128]{3,2,1,0:T(4,128)(2,1)S(1)} %bitcast.6), custom_call_target="tpu_custom_call" | custom-call | tf_op jit(solution)/shard_map/pallas_call | solution.py:57
  32.2 9.5 %all-to-all-done.1.in_ref = bf16[12,128,256]{2,1,0:T(8,128)(2,1)S(1)} async-done(((bf16[12,128,256]{2,1,0:T(8,128)(2,1)}), bf16[12,128,256]{2,1,0:T(8,128)(2,1)S(1)}, u32[]{:S(2)}, u32[]{:S(2)}) %all-to-all-start.1) | async-done | bytes 786464 | tf_op jit(solution)/shard_map/all_to_all | solution.py:281
  41.7 7.5 %all-to-all-start = ((bf16[12,128,256]{2,1,0:T(8,128)(2,1)}), bf16[12,128,256]{2,1,0:T(8,128)(2,1)S(1)}, u32[]{:S(2)}, u32[]{:S(2)}) async-start(bf16[12,128,256]{2,1,0:T(8,128)(2,1)} %shard_map.55), calls=%async_computation | async-start | bytes 1572864 | tf_op jit(solution)/shard_map/all_to_all | solution.py:281
  49.8 3.2 %collective-permute-start = (bf16[768,256]{1,0:T(8,128)(2,1)S(1)}, bf16[768,256]{1,0:T(8,128)(2,1)S(1)}, u32[]{:S(2)}, u32[]{:S(2)}) collective-permute-start(bf16[768,256]{1,0:T(8,128)(2,1)S(1)} %shard_map.58.refs_0_), channel_id=1, source_target_pairs={{0,32},{32,64},{64,96},{96,128},{128,160},{160,192},{192,224},{224... | collective-permute-start | bytes 1179656 | tf_op jit(solution)/shard_map/ppermute | solution.py:288
  53.1 6.7 %collective-permute-start.4 = (bf16[768,256]{1,0:T(8,128)(2,1)S(1)}, bf16[768,256]{1,0:T(8,128)(2,1)S(1)}, u32[]{:S(2)}, u32[]{:S(2)}) collective-permute-start(bf16[768,256]{1,0:T(8,128)(2,1)S(1)} %shard_map.58.refs_0_), channel_id=1, source_target_pairs={{0,224},{32,0},{64,32},{96,64},{128,96},{160,128},{192,160},{224,1... | collective-permute-start | bytes 1179656 | tf_op jit(solution)/shard_map/ppermute | solution.py:290
  59.8 2.5 %collective-permute-start.1 = (bf16[768,256]{1,0:T(8,128)(2,1)S(1)}, bf16[768,256]{1,0:T(8,128)(2,1)S(1)}, u32[]{:S(2)}, u32[]{:S(2)}) collective-permute-start(bf16[768,256]{1,0:T(8,128)(2,1)S(1)} %collective-permute-done.refs_1_), channel_id=1, source_target_pairs={{0,32},{32,64},{64,96},{96,128},{128,160},{160,192},{192,224},{224... | collective-permute-start | bytes 1179656 | tf_op jit(solution)/shard_map/ppermute | solution.py:288
  62.4 4.2 %collective-permute-done.4.refs_2_.refs_1_ = bf16[768,256]{1,0:T(8,128)(2,1)S(1)} collective-permute-done((bf16[768,256]{1,0:T(8,128)(2,1)S(1)}, bf16[768,256]{1,0:T(8,128)(2,1)S(1)}, u32[]{:S(2)}, u32[]{:S(2)}) %collective-permute-start.4) | collective-permute-done | bytes 393248 | tf_op jit(solution)/shard_map/ppermute | solution.py:290
  66.5 10.0 %collective-permute-start.5 = (bf16[768,256]{1,0:T(8,128)(2,1)S(1)}, bf16[768,256]{1,0:T(8,128)(2,1)S(1)}, u32[]{:S(2)}, u32[]{:S(2)}) collective-permute-start(bf16[768,256]{1,0:T(8,128)(2,1)S(1)} %collective-permute-done.4.refs_2_.refs_1_), channel_id=1, source_target_pairs={{0,224},{32,0},{64,32},{96,64},{128,96},{160,128},{192,160},{224,1... | collective-permute-start | bytes 1179656 | tf_op jit(solution)/shard_map/ppermute | solution.py:290
  76.6 1.3 collective-permute-start.2
  77.9 3.4 %collective-permute-done.5.refs_1_.refs_2_ = bf16[768,256]{1,0:T(8,128)(2,1)S(1)} collective-permute-done((bf16[768,256]{1,0:T(8,128)(2,1)S(1)}, bf16[768,256]{1,0:T(8,128)(2,1)S(1)}, u32[]{:S(2)}, u32[]{:S(2)}) %collective-permute-start.5) | collective-permute-done | bytes 393248 | tf_op jit(solution)/shard_map/ppermute | solution.py:290
  81.3 8.7 %collective-permute-start.6 = (bf16[768,256]{1,0:T(8,128)(2,1)S(1)}, bf16[768,256]{1,0:T(8,128)(2,1)}, u32[]{:S(2)}, u32[]{:S(2)}) collective-permute-start(bf16[768,256]{1,0:T(8,128)(2,1)S(1)} %collective-permute-done.5.refs_1_.refs_2_), channel_id=1, source_target_pairs={{0,224},{32,0},{64,32},{96,64},{128,96},{160,128},{192,160},{224,1... | collective-permute-start | bytes 1179656 | tf_op jit(solution)/shard_map/ppermute | solution.py:290
  90.6 1.3 collective-permute-start.7
  91.9 1.3 collective-permute-start.3
  93.2 3.8 %collective-permute-done.7.q_ref = bf16[768,128]{1,0:T(8,128)(2,1)S(1)} collective-permute-done((bf16[768,128]{1,0:T(8,128)(2,1)S(1)}, bf16[768,128]{1,0:T(8,128)(2,1)S(1)}, u32[]{:S(2)}, u32[]{:S(2)}) %collective-permute-start.7) | collective-permute-done | bytes 196640 | tf_op jit(solution)/shard_map/ppermute | solution.py:291
  97.0 1.3 shard_map.62
  98.3 1.6 %collective-permute-start.8 = (bf16[768,128]{1,0:T(8,128)(2,1)S(1)}, bf16[768,128]{1,0:T(8,128)(2,1)S(1)}, u32[]{:S(2)}, u32[]{:S(2)}) collective-permute-start(bf16[768,128]{1,0:T(8,128)(2,1)S(1)} %shard_map.62), channel_id=1, source_target_pairs={{0,256},{32,288},{64,320},{96,352},{128,384},{160,416},{192,448},{... | collective-permute-start | bytes 589832 | tf_op jit(solution)/shard_map/ppermute | solution.py:295
  99.9 2.9 %shard_map.59.refs_2_ = f32[768,128]{1,0:T(8,128)S(1)} custom-call(s32[1,4]{1,0:T(1,128)S(1)} %copy-done.7, bf16[768,128]{1,0:T(8,128)(2,1)S(1)} %get-tuple-element.7.q_ref, bf16[768,256]{1,0:T(8,128)(2,1)S(1)} %shard_map.58.refs_0_, bf16[768,256]{1,0:T(8,128)(2,1)S(1)} %collective-permute-done.refs_1_, ...), custom_call_target="tpu_custom_call" | custom-call | flops 905969664 | bytes 1048576 | tf_op jit(solution)/shard_map/pallas_call | solution.py:185
  104.8 6.4 %collective-permute-done.8.refs_2_ = bf16[768,128]{1,0:T(8,128)(2,1)S(1)} collective-permute-done((bf16[768,128]{1,0:T(8,128)(2,1)S(1)}, bf16[768,128]{1,0:T(8,128)(2,1)S(1)}, u32[]{:S(2)}, u32[]{:S(2)}) %collective-permute-start.8) | collective-permute-done | bytes 196640 | tf_op jit(solution)/shard_map/ppermute | solution.py:295
  112.0 11.2 %all_to_all.20.rows_ref = bf16[8,96,128]{2,1,0:T(8,128)(2,1)S(1)} all-to-all(bf16[8,96,128]{2,1,0:T(8,128)(2,1)S(1)} %bitcast.7), channel_id=1, replica_groups=mesh['ctx'=16,'head'=8,'batch'=4] {'head'}, dimensions={0} | all-to-all | bytes 393216 | tf_op jit(solution)/shard_map/all_to_all | solution.py:298
  123.2 1.6 %copy-done.2 = bf16[1024,1024]{1,0:T(8,128)(2,1)S(1)} copy-done((bf16[1024,1024]{1,0:T(8,128)(2,1)S(1)}, bf16[1024,1024]{1,0:T(8,128)(2,1)}, u32[]{:S(2)}) %copy-start.2) | copy-done | bytes 2097176
  125.3 9.2 %all_to_all.21 = bf16[8,96,128]{2,1,0:T(8,128)(2,1)S(1)} all-to-all(bf16[8,96,128]{2,1,0:T(8,128)(2,1)S(1)} %shard_map.64), channel_id=1, replica_groups=mesh['ctx'=16,'head'=8,'batch'=4] {'head'}, dimensions={0} | all-to-all | bytes 393216 | tf_op jit(solution)/shard_map/all_to_all | solution.py:300
  (30 shorter events, 7.2 us)
Async XLA Ops:
  6.5 20.0 %copy-start.4 = (s32[1,4,6]{2,1,0:T(4,128)S(1)}, s32[1,4,6]{2,1,0:T(4,128)}, u32[]{:S(2)}) copy-start(s32[1,4,6]{2,1,0:T(4,128)} %param.6) | copy-start | bytes 292
  6.5 20.0 %copy-start.6 = (s32[1,4,6]{2,1,0:T(4,128)S(1)}, s32[1,4,6]{2,1,0:T(4,128)}, u32[]{:S(2)}) copy-start(s32[1,4,6]{2,1,0:T(4,128)} %param.7) | copy-start | bytes 292
  6.5 116.7 %all-gather.2.cloned.1.call-start = ((), (), s32[]{:S(2)}) async-start(), calls=%async_computation.4 | async-start | bytes 2359296 | tf_op jit(solution)/shard_map/all_gather | solution.py:283
  7.3 1.4 copy-start
  8.7 0.7 copy-start.3
  9.4 0.7 copy-start.5
  10.0 16.5 %copy-start.1 = (bf16[1,1,12,128,4,128]{5,4,3,2,1,0:T(4,128)(2,1)S(1)}, bf16[1,1,12,128,4,128]{5,4,3,2,1,0:T(4,128)(2,1)}, u32[]{:S(2)}) copy-start(bf16[1,1,12,128,4,128]{5,4,3,2,1,0:T(4,128)(2,1)} %param.5) | copy-start | bytes 4718596
  15.7 26.0 %all-to-all-start.1 = ((bf16[12,128,256]{2,1,0:T(8,128)(2,1)}), bf16[12,128,256]{2,1,0:T(8,128)(2,1)S(1)}, u32[]{:S(2)}, u32[]{:S(2)}) async-start(bf16[12,128,256]{2,1,0:T(8,128)(2,1)} %shard_map.57), calls=%async_computation.1 | async-start | bytes 1572864 | tf_op jit(solution)/shard_map/all_to_all | solution.py:281
  32.2 64.9 %copy-start.7 = (s32[1,4]{1,0:T(1,128)S(1)}, s32[1,4]{1,0:T(1,128)}, u32[]{:S(2)}) copy-start(s32[1,4]{1,0:T(1,128)} %hist_ref.9) | copy-start | bytes 52
  41.7 48.2 %all-to-all-start = ((bf16[12,128,256]{2,1,0:T(8,128)(2,1)}), bf16[12,128,256]{2,1,0:T(8,128)(2,1)S(1)}, u32[]{:S(2)}, u32[]{:S(2)}) async-start(bf16[12,128,256]{2,1,0:T(8,128)(2,1)} %shard_map.55), calls=%async_computation | async-start | bytes 1572864 | tf_op jit(solution)/shard_map/all_to_all | solution.py:281
  49.8 10.0 %collective-permute-start = (bf16[768,256]{1,0:T(8,128)(2,1)S(1)}, bf16[768,256]{1,0:T(8,128)(2,1)S(1)}, u32[]{:S(2)}, u32[]{:S(2)}) collective-permute-start(bf16[768,256]{1,0:T(8,128)(2,1)S(1)} %shard_map.58.refs_0_), channel_id=1, source_target_pairs={{0,32},{32,64},{64,96},{96,128},{128,160},{160,192},{192,224},{224... | collective-permute-start | bytes 1179656 | tf_op jit(solution)/shard_map/ppermute | solution.py:288
  53.1 13.5 %collective-permute-start.4 = (bf16[768,256]{1,0:T(8,128)(2,1)S(1)}, bf16[768,256]{1,0:T(8,128)(2,1)S(1)}, u32[]{:S(2)}, u32[]{:S(2)}) collective-permute-start(bf16[768,256]{1,0:T(8,128)(2,1)S(1)} %shard_map.58.refs_0_), channel_id=1, source_target_pairs={{0,224},{32,0},{64,32},{96,64},{128,96},{160,128},{192,160},{224,1... | collective-permute-start | bytes 1179656 | tf_op jit(solution)/shard_map/ppermute | solution.py:290
  59.8 16.7 %collective-permute-start.1 = (bf16[768,256]{1,0:T(8,128)(2,1)S(1)}, bf16[768,256]{1,0:T(8,128)(2,1)S(1)}, u32[]{:S(2)}, u32[]{:S(2)}) collective-permute-start(bf16[768,256]{1,0:T(8,128)(2,1)S(1)} %collective-permute-done.refs_1_), channel_id=1, source_target_pairs={{0,32},{32,64},{64,96},{96,128},{128,160},{160,192},{192,224},{224... | collective-permute-start | bytes 1179656 | tf_op jit(solution)/shard_map/ppermute | solution.py:288
  66.5 14.7 %collective-permute-start.5 = (bf16[768,256]{1,0:T(8,128)(2,1)S(1)}, bf16[768,256]{1,0:T(8,128)(2,1)S(1)}, u32[]{:S(2)}, u32[]{:S(2)}) collective-permute-start(bf16[768,256]{1,0:T(8,128)(2,1)S(1)} %collective-permute-done.4.refs_2_.refs_1_), channel_id=1, source_target_pairs={{0,224},{32,0},{64,32},{96,64},{128,96},{160,128},{192,160},{224,1... | collective-permute-start | bytes 1179656 | tf_op jit(solution)/shard_map/ppermute | solution.py:290
  76.6 15.3 %collective-permute-start.2 = (bf16[768,256]{1,0:T(8,128)(2,1)S(1)}, bf16[768,256]{1,0:T(8,128)(2,1)S(1)}, u32[]{:S(2)}, u32[]{:S(2)}) collective-permute-start(bf16[768,256]{1,0:T(8,128)(2,1)S(1)} %collective-permute-done.1.refs_0_), channel_id=1, source_target_pairs={{0,32},{32,64},{64,96},{96,128},{128,160},{160,192},{192,224},{224... | collective-permute-start | bytes 1179656 | tf_op jit(solution)/shard_map/ppermute | solution.py:288
  81.3 15.8 %collective-permute-start.6 = (bf16[768,256]{1,0:T(8,128)(2,1)S(1)}, bf16[768,256]{1,0:T(8,128)(2,1)}, u32[]{:S(2)}, u32[]{:S(2)}) collective-permute-start(bf16[768,256]{1,0:T(8,128)(2,1)S(1)} %collective-permute-done.5.refs_1_.refs_2_), channel_id=1, source_target_pairs={{0,224},{32,0},{64,32},{96,64},{128,96},{160,128},{192,160},{224,1... | collective-permute-start | bytes 1179656 | tf_op jit(solution)/shard_map/ppermute | solution.py:290
  90.6 6.4 %collective-permute-start.7 = (bf16[768,128]{1,0:T(8,128)(2,1)S(1)}, bf16[768,128]{1,0:T(8,128)(2,1)S(1)}, u32[]{:S(2)}, u32[]{:S(2)}) collective-permute-start(bf16[768,128]{1,0:T(8,128)(2,1)S(1)} %get-tuple-element.7.q_ref), channel_id=1, source_target_pairs={{256,0},{288,32},{320,64},{352,96},{384,128},{416,160},{448,192},{... | collective-permute-start | bytes 589832 | tf_op jit(solution)/shard_map/ppermute | solution.py:291
  91.9 19.3 %collective-permute-start.3 = (bf16[768,256]{1,0:T(8,128)(2,1)S(1)}, bf16[768,256]{1,0:T(8,128)(2,1)S(1)}, u32[]{:S(2)}, u32[]{:S(2)}) collective-permute-start(bf16[768,256]{1,0:T(8,128)(2,1)S(1)} %collective-permute-done.2.refs_0_), channel_id=1, source_target_pairs={{0,32},{32,64},{64,96},{96,128},{128,160},{160,192},{192,224},{224... | collective-permute-start | bytes 1179656 | tf_op jit(solution)/shard_map/ppermute | solution.py:288
  98.3 12.8 %collective-permute-start.8 = (bf16[768,128]{1,0:T(8,128)(2,1)S(1)}, bf16[768,128]{1,0:T(8,128)(2,1)S(1)}, u32[]{:S(2)}, u32[]{:S(2)}) collective-permute-start(bf16[768,128]{1,0:T(8,128)(2,1)S(1)} %shard_map.62), channel_id=1, source_target_pairs={{0,256},{32,288},{64,320},{96,352},{128,384},{160,416},{192,448},{... | collective-permute-start | bytes 589832 | tf_op jit(solution)/shard_map/ppermute | solution.py:295
  123.2 1.6 %copy-start.2 = (bf16[1024,1024]{1,0:T(8,128)(2,1)S(1)}, bf16[1024,1024]{1,0:T(8,128)(2,1)}, u32[]{:S(2)}) copy-start(bf16[1024,1024]{1,0:T(8,128)(2,1)} %all-gather.2.cloned.1.call-done.w_ref) | copy-start | bytes 6291460
Sparse Core Ops, SparseCore 0:
  9.5 36.3 all-gather.1

commit v2 on v1

--- a/solution.py
+++ b/solution.py
@@ -25,11 +25,11 @@
 ANY = pl.BlockSpec(memory_space=pl.ANY)
 
 
-def params():
-    return pltpu.CompilerParams(vmem_limit_bytes=48 * 1024 * 1024)
-
-
-def pick_kernel(kinds, shard_ref, slot_ref, ingest_ref, out_ref, buf, sems):
+def params(mib=16):
+    return pltpu.CompilerParams(vmem_limit_bytes=mib * 1024 * 1024)
+
+
+def pick_kernel(shard_ref, slot_ref, ingest_ref, out_ref, buf, sems):
     me = lax.axis_index("batch")
     copies = []
     for g in range(GROUPS):
@@ -48,49 +48,45 @@
             copies.append(copy)
     for at, copy in enumerate(copies):
         copy.wait()
-        for place, kind in enumerate(kinds):
-            out_ref[at, :, place * HD : (place + 1) * HD] = buf[at, :, kind, :]
-
-
-def pick(shards, slots, ingested, kinds):
+        out_ref[at] = buf[at].reshape(BLOCK, 4 * HD)
+
+
+def pick(shards, slots, ingested):
     count = GROUPS * CAPACITY
     return pl.pallas_call(
-        functools.partial(pick_kernel, kinds),
-        out_shape=jax.ShapeDtypeStruct((count, BLOCK, 2 * HD), jnp.bfloat16),
+        pick_kernel,
+        out_shape=jax.ShapeDtypeStruct((count, BLOCK, 4 * HD), jnp.bfloat16),
         in_specs=[SMEM, SMEM, ANY],
         out_specs=VMEM,
         scratch_shapes=[
             pltpu.VMEM((count, BLOCK, 4, HD), jnp.bfloat16),
             pltpu.SemaphoreType.DMA((count,)),
         ],
-        compiler_params=params(),
+        compiler_params=params(56),
     )(shards, slots, ingested)
 
 
-def order_kernel(split, shard_ref, in_ref, *out_refs):
+def order_kernel(shard_ref, in_ref, unit_ref, query_ref, update_ref):
     me = lax.axis_index("batch")
     shards = [shard_ref[me, k] for k in range(PER_OWNER)]
     for k in range(PER_OWNER):
         rank = jnp.int32(0)
         for earlier in range(k):
             rank = rank + (shards[earlier] == shards[k]).astype(jnp.int32)
-        block = in_ref[shards[k] * CAPACITY + rank]
+        at = shards[k] * CAPACITY + rank
         rows = slice(k * BLOCK, (k + 1) * BLOCK)
-        if split:
-            out_refs[0][rows, :] = block[:, :HD]
-            out_refs[1][rows, :] = block[:, HD:]
-        else:
-            out_refs[0][rows, :] = block
-
-
-def in_order(shards, blocks, split):
-    width = HD if split else 2 * HD
-    shape = jax.ShapeDtypeStruct((ROWS, width), jnp.bfloat16)
-    return pl.pallas_call(
-        functools.partial(order_kernel, split),
-        out_shape=[shape] * (2 if split else 1),
+        query_ref[rows, :] = in_ref[at, :, :HD]
+        unit_ref[rows, :] = in_ref[at, :, HD : 3 * HD]
+        update_ref[rows, :] = in_ref[at, :, 3 * HD :]
+
+
+def in_order(shards, blocks):
+    shape = jax.ShapeDtypeStruct((ROWS, HD), jnp.bfloat16)
+    return pl.pallas_call(
+        order_kernel,
+        out_shape=[jax.ShapeDtypeStruct((ROWS, 2 * HD), jnp.bfloat16), shape, shape],
         in_specs=[SMEM, VMEM],
-        out_specs=[VMEM] * (2 if split else 1),
+        out_specs=[VMEM] * 3,
         compiler_params=params(),
     )(shards, blocks)
 
@@ -192,9 +188,13 @@
     )(hist, q, *units, *(() if first else (acc,)))
 
 
-def lent_kernel(names, hist_ref, q_ref, *refs):
-    units, out_ref, acc_ref = refs[: len(names)], refs[-2], refs[-1]
-    acc_ref[...] = jnp.zeros_like(acc_ref)
+def lent_kernel(names, first, final, hist_ref, q_ref, *refs):
+    units, refs = refs[: len(names)], refs[len(names) :]
+    acc_ref = refs[-1]
+    if first:
+        acc_ref[...] = jnp.zeros_like(acc_ref)
+    else:
+        acc_ref[...] = refs[0][...]
     me = lax.axis_index("ctx")
 
     @pl.when(me < PLANE)
@@ -203,19 +203,21 @@
         owners = [unit_owner(me, *name) for name in names]
         add_units(ends, (me + PLANE) * ROWS, q_ref, list(zip(owners, units)), acc_ref)
 
-    out_ref[...] = acc_ref[...].astype(jnp.bfloat16)
-
-
-def attend_lent(hist, q, units, names):
-    return pl.pallas_call(
-        functools.partial(lent_kernel, names),
-        out_shape=jax.ShapeDtypeStruct((ROWS, HD), jnp.bfloat16),
-        in_specs=[SMEM] + [VMEM] * (1 + len(units)),
-        out_specs=VMEM,
-        scratch_shapes=[pltpu.VMEM((ROWS, HD), jnp.float32)],
+    if final:
+        refs[-2][...] = acc_ref[...].astype(jnp.bfloat16)
+
+
+def attend_lent(hist, q, units, names, acc=None, final=False):
+    first = acc is None
+    return pl.pallas_call(
+        functools.partial(lent_kernel, names, first, final),
+        out_shape=jax.ShapeDtypeStruct((ROWS, HD), jnp.bfloat16 if final else jnp.float32),
+        in_specs=[SMEM] + [VMEM] * (1 + len(units) + (0 if first else 1)),
+        out_specs=VMEM,
+        scratch_shapes=[pltpu.VMEM((ROWS, HD), jnp.float32)] if final else [],
         cost_estimate=estimate(len(units)),
         compiler_params=params(),
-    )(hist, q, *units)
+    )(hist, q, *units, *(() if first else (acc,)))
 
 
 def last_kernel(names, hist_ref, q_ref, *refs):
@@ -249,23 +251,31 @@
     )(hist, q, *units, acc, lent, update)
 
 
-def project_kernel(rows_ref, w_ref, out_ref):
-    rows = jnp.concatenate([rows_ref[h] for h in range(HEADS)], axis=1)
-    mixed = jnp.dot(rows, w_ref[...], preferred_element_type=jnp.float32).astype(jnp.bfloat16)
+def project_kernel(rows_ref, same_ref, other_ref, out_ref):
+    me = lax.axis_index("head")
+    total = 0.0
+    for first, w_ref in ((me, same_ref), (me + 1 - 2 * (me % 2), other_ref)):
+        heads = [rows_ref[(first + ahead) % HEADS] for ahead in (0, HEADS - 2, 2, 4)]
+        rows = jnp.concatenate(heads, axis=1)
+        total = total + jnp.dot(rows, w_ref[...], preferred_element_type=jnp.float32)
+    mixed = total.astype(jnp.bfloat16)
     for h in range(HEADS):
         out_ref[h] = mixed[:, h * HD : (h + 1) * HD]
 
 
-def project(rows, w):
+def project(rows, same, other):
     return pl.pallas_call(
         project_kernel,
         out_shape=jax.ShapeDtypeStruct((HEADS, CHUNK, HD), jnp.bfloat16),
-        in_specs=[VMEM, VMEM],
-        out_specs=VMEM,
-        compiler_params=params(),
-    )(rows, w)
-
-
+        in_specs=[VMEM] * 3,
+        out_specs=VMEM,
+        compiler_params=params(),
+    )(rows, same, other)
+
+
+X_UP = [(h, (h + 2) % HEADS) for h in range(HEADS)]
+X_DOWN = [(h, (h - 2) % HEADS) for h in range(HEADS)]
+CORE = [(h, h ^ 1) for h in range(HEADS)]
 UP = [(i, i + 1) for i in range(CTXS - 1)]
 DOWN = [(i, i // PLANE * PLANE + (i - 1) % PLANE) for i in range(CTXS)]
 LEND = [(i + PLANE, i) for i in range(PLANE)]
@@ -276,28 +286,38 @@
     ingested, shards, slots = ingest[0, 0], src_shard[0], src_slot[0]
     move = functools.partial(lax.ppermute, axis_name="ctx")
 
-    def to_owners(kinds):
-        blocks = pick(shards, slots, ingested, kinds)
-        return lax.all_to_all(blocks, "batch", split_axis=0, concat_axis=0, tiled=True)
-
-    whole_w = lax.all_gather(w_out, "head", axis=0, tiled=True)
-    (own,) = in_order(shards, to_owners((1, 2)), False)
-    q, update = in_order(shards, to_owners((0, 3)), True)
+    def to_all(x):
+        return lax.all_to_all(x, "head", 0, 0, tiled=True)
+
+    blocks = pick(shards, slots, ingested)
+    w_late, blocks = lax.optimization_barrier((w_out, blocks))
+    arrived = lax.all_to_all(blocks, "batch", split_axis=0, concat_axis=0, tiled=True)
+    cross = functools.partial(lax.ppermute, axis_name="head")
+    half = HD // 2
+    w_up, w_down = cross(w_late, perm=X_UP), cross(w_late, perm=X_DOWN)
+    w_far = [cross(w_up[:half], perm=X_UP), cross(w_down[half:], perm=X_DOWN)]
+    w_same = jnp.concatenate([w_late, w_up, w_down, *w_far])
+    w_other = cross(w_same, perm=CORE)
+    w_same, w_other, arrived = lax.optimization_barrier((w_same, w_other, arrived))
+    own, q, update = in_order(shards, arrived)
     up, down = [own], [own]
     for step in range(4):
         up.append(move(up[-1], perm=UP))
         if step < 3:
             down.append(move(down[-1], perm=DOWN))
     lent_q = move(q, perm=LEND)
-    acc = attend(hist_len, q, (own, up[1], down[1]), (("up", 0), ("up", 1), ("down", 1)))
+    acc = attend(hist_len, q, (own,), (("up", 0),))
+    acc = attend(hist_len, q, (up[1], down[1]), (("up", 1), ("down", 1)), acc)
+    lent = attend_lent(hist_len, lent_q, tuple(down[:2]), (("down", 0), ("down", 1)))
     acc = attend(hist_len, q, (up[2], down[2]), (("up", 2), ("down", 2)), acc)
-    lent = attend_lent(hist_len, lent_q, tuple(down), tuple(("down", k) for k in range(4)))
+    lent = attend_lent(
+        hist_len, lent_q, tuple(down[2:]), (("down", 2), ("down", 3)), lent, final=True
+    )
     lent = move(lent, perm=RETURN)
     acc = attend(hist_len, q, (up[3], down[3]), (("up", 3), ("down", 3)), acc)
     gated = attend_last(hist_len, q, (up[4],), (("up", 4),), acc, lent, update)
-    rows = lax.all_to_all(gated.reshape(HEADS, CHUNK, HD), "head", 0, 0, tiled=True)
-    mixed = project(rows, whole_w)
-    mixed = lax.all_to_all(mixed, "head", 0, 0, tiled=True)
+    rows = to_all(gated.reshape(HEADS, CHUNK, HD))
+    mixed = to_all(project(rows, w_same, w_other))
     return mixed.reshape(1, ROWS, HD)
 
 

time: 143 us -> 133 us (0.930)
  between operations: 13.6 us -> 0.32 us
  starting transfers between devices: 55.1 us -> 66.1 us
  Pallas kernels: 19.9 us -> 12.5 us
  local copies, waits for them, and re-layouts: 5.05 us -> 1.77 us
  waiting for transfers between devices: 28 us -> 30.3 us
    ppermute x0 -> x5, starting transfers between devices: none -> 18.6 us  [the longest x2 7.24 us: body(): w_far = [cross(w_up[:half], perm=X_UP), cross(w_down[half:], perm=X_DOWN)]]
    ppermute x0 -> x5, waiting for transfers between devices: none -> 10.2 us  [the longest x2 5.24 us: body(): w_far = [cross(w_up[:half], perm=X_UP), cross(w_down[half:], perm=X_DOWN)]]
    all_to_all x2 -> x1, waiting for transfers between devices: 9.53 us -> 0.01 us  [body(): lax.all_to_all(blocks, 'batch', split_axis=0, concat_axis=0, tiled=True)]
    all_to_all x2 -> x1, starting transfers between devices: 18.4 us -> 10.8 us  [body(): lax.all_to_all(blocks, 'batch', split_axis=0, concat_axis=0, tiled=True)]
    pallas_call x5 -> x4, Pallas kernels: 13.8 us -> 6.29 us  [the longest x1 4.17 us: pick(): pl.pallas_call(pick_kernel, out_shape=jax.ShapeDtypeStruct((count, BLOCK,...]
    unnamed x17 -> x15, local copies, waits for them, and re-layouts: 5.05 us -> 1.74 us
    ppermute x3, waiting for transfers between devices: 7.53 us -> 9.83 us  [body(): down.append(move(down[-1], perm=DOWN))]
    pallas_call x3 -> x4, Pallas kernels: 4.79 us -> 4.92 us  [attend(): pl.pallas_call(functools.partial(attend_kernel, names, first), out_shape=...]
  transfers between devices with their start and end apart: 12 -> 15, of which waited for: 5 -> 7; matrix products, arithmetic and copies ran while one was open for 0% -> 0% of each run, Pallas kernels for 14% -> 5%
where the time goes in v2:
time: 133 us; the launch traced here: 131 us
  starting transfers between devices  66.1 us (50%)
  waiting for transfers between devices  30.3 us (23%)
  blocking collectives  20.1 us (15%)
  Pallas kernels  12.5 us (9%)
  local copies, waits for them, and re-layouts  1.77 us (1%)
    ppermute x3, starting transfers between devices, body(): down.append(move(down[-1], perm=DOWN))  25.7 us
    all_to_all x2, blocking collectives, to_all(): return lax.all_to_all(x, 'head', 0, 0, tiled=True)  20.1 us
    all_to_all x1, starting transfers between devices, body(): lax.all_to_all(blocks, 'batch', split_axis=0, concat_axis=0, tiled=True)  10.8 us
    ppermute x3, waiting for transfers between devices, body(): down.append(move(down[-1], perm=DOWN))  9.83 us
    ppermute x4, starting transfers between devices, body(): up.append(move(up[-1], perm=UP))  7.39 us
    ppermute x2, starting transfers between devices, body(): w_far = [cross(w_up[:half], perm=X_UP), cross(w_down[half:], perm=X_DOWN)]  7.24 us
    ppermute x2, starting transfers between devices, body(): w_up, w_down = (cross(w_late, perm=X_UP), cross(w_late, perm=X_DOWN))  6.43 us
    ppermute x1, waiting for transfers between devices, body(): lent = move(lent, perm=RETURN)  6.42 us
  transfers between devices with their start and end apart: 15, of which 7 were waited for; matrix products, arithmetic and copies ran while one was open for 0% of the time, Pallas kernels for 5%

profile of v2, /device:TPU:1, one launch (start us, length us, event | category | flops | bytes accessed | tf_op | source)
XLA Modules:
  0.0 131.2 jit_solution(960549413554542404)
XLA Ops:
  0.0 4.2 %shard_map.55 = bf16[12,128,512]{2,1,0:T(8,128)(2,1)} custom-call(s32[4,6]{1,0:T(4,128)} %bitcast.6, s32[4,6]{1,0:T(4,128)} %bitcast.10, bf16[12,128,4,128]{3,2,1,0:T(4,128)(2,1)} %bitcast.8), custom_call_target="tpu_custom_call" | custom-call | tf_op jit(solution)/shard_map/pallas_call | solution.py:56
  4.2 10.8 %all-to-all-start = ((bf16[12,128,512]{2,1,0:T(8,128)(2,1)}), bf16[12,128,512]{2,1,0:T(8,128)(2,1)S(1)}, u32[]{:S(2)}, u32[]{:S(2)}) async-start(bf16[12,128,512]{2,1,0:T(8,128)(2,1)} %shard_map.55), calls=%async_computation | async-start | bytes 3145728 | tf_op jit(solution)/shard_map/all_to_all | solution.py:294
  15.0 4.5 %collective-permute-start.1 = (bf16[128,1024]{1,0:T(8,128)(2,1)S(1)}, bf16[128,1024]{1,0:T(8,128)(2,1)S(1)}, u32[]{:S(2)}, u32[]{:S(2)}) collective-permute-start(bf16[128,1024]{1,0:T(8,128)(2,1)S(1)} %copy-done.4), channel_id=1, source_target_pairs={{0,24},{4,28},{8,0},{12,4},{16,8},{20,12},{24,16},{28,20},{1,25},{... | collective-permute-start | bytes 786440 | tf_op jit(solution)/shard_map/ppermute | solution.py:297
  19.5 1.9 %collective-permute-start = (bf16[128,1024]{1,0:T(8,128)(2,1)S(1)}, bf16[128,1024]{1,0:T(8,128)(2,1)S(1)}, u32[]{:S(2)}, u32[]{:S(2)}) collective-permute-start(bf16[128,1024]{1,0:T(8,128)(2,1)S(1)} %copy-done.4), channel_id=1, source_target_pairs={{0,8},{4,12},{8,16},{12,20},{16,24},{20,28},{24,0},{28,4},{1,9},{5... | collective-permute-start | bytes 786440 | tf_op jit(solution)/shard_map/ppermute | solution.py:297
  21.4 2.7 %collective-permute-done.1 = bf16[128,1024]{1,0:T(8,128)(2,1)S(1)} collective-permute-done((bf16[128,1024]{1,0:T(8,128)(2,1)S(1)}, bf16[128,1024]{1,0:T(8,128)(2,1)S(1)}, u32[]{:S(2)}, u32[]{:S(2)}) %collective-permute-start.1) | collective-permute-done | bytes 262176 | tf_op jit(solution)/shard_map/ppermute | solution.py:297
  24.1 5.3 %collective-permute-start.3 = (bf16[64,1024]{1,0:T(8,128)(2,1)S(1)}, bf16[64,1024]{1,0:T(8,128)(2,1)S(1)}, u32[]{:S(2)}, u32[]{:S(2)}) collective-permute-start(bf16[64,1024]{1,0:T(8,128)(2,1)S(1)} %slice.9), channel_id=1, source_target_pairs={{0,24},{4,28},{8,0},{12,4},{16,8},{20,12},{24,16},{28,20},{1,25},{... | collective-permute-start | bytes 393224 | tf_op jit(solution)/shard_map/ppermute | solution.py:298
  29.5 1.9 %collective-permute-start.2 = (bf16[64,1024]{1,0:T(8,128)(2,1)S(1)}, bf16[64,1024]{1,0:T(8,128)(2,1)S(1)}, u32[]{:S(2)}, u32[]{:S(2)}) collective-permute-start(bf16[64,1024]{1,0:T(8,128)(2,1)S(1)} %slice.8), channel_id=1, source_target_pairs={{0,8},{4,12},{8,16},{12,20},{16,24},{20,28},{24,0},{28,4},{1,9},{5... | collective-permute-start | bytes 393224 | tf_op jit(solution)/shard_map/ppermute | solution.py:298
  31.5 5.2 %collective-permute-done.2 = bf16[64,1024]{1,0:T(8,128)(2,1)S(1)} collective-permute-done((bf16[64,1024]{1,0:T(8,128)(2,1)S(1)}, bf16[64,1024]{1,0:T(8,128)(2,1)S(1)}, u32[]{:S(2)}, u32[]{:S(2)}) %collective-permute-start.2) | collective-permute-done | bytes 131104 | tf_op jit(solution)/shard_map/ppermute | solution.py:298
  36.8 4.9 %collective-permute-start.4 = (bf16[512,1024]{1,0:T(8,128)(2,1)S(1)}, bf16[512,1024]{1,0:T(8,128)(2,1)S(1)}, u32[]{:S(2)}, u32[]{:S(2)}) collective-permute-start(bf16[512,1024]{1,0:T(8,128)(2,1)S(1)} %constant_dynamic-update-slice_fusion.same_ref), channel_id=1, source_target_pairs={{0,4},{4,0},{8,12},{12,8},{16,20},{20,16},{24,28},{28,24},{1,5},{5... | collective-permute-start | bytes 3145736 | tf_op jit(solution)/shard_map/ppermute | solution.py:300
  41.7 2.3 %collective-permute-done.4.other_ref = bf16[512,1024]{1,0:T(8,128)(2,1)S(1)} collective-permute-done((bf16[512,1024]{1,0:T(8,128)(2,1)S(1)}, bf16[512,1024]{1,0:T(8,128)(2,1)S(1)}, u32[]{:S(2)}, u32[]{:S(2)}) %collective-permute-start.4) | collective-permute-done | bytes 1048608 | tf_op jit(solution)/shard_map/ppermute | solution.py:300
  45.6 3.4 %collective-permute-start.5 = (bf16[768,256]{1,0:T(8,128)(2,1)S(1)}, bf16[768,256]{1,0:T(8,128)(2,1)S(1)}, u32[]{:S(2)}, u32[]{:S(2)}) collective-permute-start(bf16[768,256]{1,0:T(8,128)(2,1)S(1)} %get-tuple-element.17.refs_0_), channel_id=1, source_target_pairs={{0,32},{32,64},{64,96},{96,128},{128,160},{160,192},{192,224},{224... | collective-permute-start | bytes 1179656 | tf_op jit(solution)/shard_map/ppermute | solution.py:305
  49.1 12.7 %collective-permute-start.9 = (bf16[768,256]{1,0:T(8,128)(2,1)S(1)}, bf16[768,256]{1,0:T(8,128)(2,1)S(1)}, u32[]{:S(2)}, u32[]{:S(2)}) collective-permute-start(bf16[768,256]{1,0:T(8,128)(2,1)S(1)} %get-tuple-element.17.refs_0_), channel_id=1, source_target_pairs={{0,224},{32,0},{64,32},{96,64},{128,96},{160,128},{192,160},{224,1... | collective-permute-start | bytes 1179656 | tf_op jit(solution)/shard_map/ppermute | solution.py:307
  63.1 5.4 %collective-permute-done.9.refs_1_ = bf16[768,256]{1,0:T(8,128)(2,1)S(1)} collective-permute-done((bf16[768,256]{1,0:T(8,128)(2,1)S(1)}, bf16[768,256]{1,0:T(8,128)(2,1)S(1)}, u32[]{:S(2)}, u32[]{:S(2)}) %collective-permute-start.9) | collective-permute-done | bytes 393248 | tf_op jit(solution)/shard_map/ppermute | solution.py:307
  68.5 6.5 %collective-permute-start.10 = (bf16[768,256]{1,0:T(8,128)(2,1)S(1)}, bf16[768,256]{1,0:T(8,128)(2,1)S(1)}, u32[]{:S(2)}, u32[]{:S(2)}) collective-permute-start(bf16[768,256]{1,0:T(8,128)(2,1)S(1)} %collective-permute-done.9.refs_1_), channel_id=1, source_target_pairs={{0,224},{32,0},{64,32},{96,64},{128,96},{160,128},{192,160},{224,1... | collective-permute-start | bytes 1179656 | tf_op jit(solution)/shard_map/ppermute | solution.py:307
  75.0 1.3 %collective-permute-start.7 = (bf16[768,256]{1,0:T(8,128)(2,1)S(1)}, bf16[768,256]{1,0:T(8,128)(2,1)S(1)}, u32[]{:S(2)}, u32[]{:S(2)}) collective-permute-start(bf16[768,256]{1,0:T(8,128)(2,1)S(1)} %collective-permute-done.6.refs_0_), channel_id=1, source_target_pairs={{0,32},{32,64},{64,96},{96,128},{128,160},{160,192},{192,224},{224... | collective-permute-start | bytes 1179656 | tf_op jit(solution)/shard_map/ppermute | solution.py:305
  76.3 4.5 %collective-permute-done.10.refs_1_.refs_0_ = bf16[768,256]{1,0:T(8,128)(2,1)S(1)} collective-permute-done((bf16[768,256]{1,0:T(8,128)(2,1)S(1)}, bf16[768,256]{1,0:T(8,128)(2,1)S(1)}, u32[]{:S(2)}, u32[]{:S(2)}) %collective-permute-start.10) | collective-permute-done | bytes 393248 | tf_op jit(solution)/shard_map/ppermute | solution.py:307
  80.8 6.5 %collective-permute-start.11 = (bf16[768,256]{1,0:T(8,128)(2,1)S(1)}, bf16[768,256]{1,0:T(8,128)(2,1)S(1)}, u32[]{:S(2)}, u32[]{:S(2)}) collective-permute-start(bf16[768,256]{1,0:T(8,128)(2,1)S(1)} %collective-permute-done.10.refs_1_.refs_0_), channel_id=1, source_target_pairs={{0,224},{32,0},{64,32},{96,64},{128,96},{160,128},{192,160},{224,1... | collective-permute-start | bytes 1179656 | tf_op jit(solution)/shard_map/ppermute | solution.py:307
  88.6 1.3 %collective-permute-start.8 = (bf16[768,256]{1,0:T(8,128)(2,1)S(1)}, bf16[768,256]{1,0:T(8,128)(2,1)S(1)}, u32[]{:S(2)}, u32[]{:S(2)}) collective-permute-start(bf16[768,256]{1,0:T(8,128)(2,1)S(1)} %collective-permute-done.7.refs_0_), channel_id=1, source_target_pairs={{0,32},{32,64},{64,96},{96,128},{128,160},{160,192},{192,224},{224... | collective-permute-start | bytes 1179656 | tf_op jit(solution)/shard_map/ppermute | solution.py:305
  89.9 3.9 %collective-permute-done.12.q_ref = bf16[768,128]{1,0:T(8,128)(2,1)S(1)} collective-permute-done((bf16[768,128]{1,0:T(8,128)(2,1)S(1)}, bf16[768,128]{1,0:T(8,128)(2,1)S(1)}, u32[]{:S(2)}, u32[]{:S(2)}) %collective-permute-start.12) | collective-permute-done | bytes 196640 | tf_op jit(solution)/shard_map/ppermute | solution.py:308
  95.3 2.3 %collective-permute-start.13 = (bf16[768,128]{1,0:T(8,128)(2,1)S(1)}, bf16[768,128]{1,0:T(8,128)(2,1)S(1)}, u32[]{:S(2)}, u32[]{:S(2)}) collective-permute-start(bf16[768,128]{1,0:T(8,128)(2,1)S(1)} %shard_map.62), channel_id=1, source_target_pairs={{0,256},{32,288},{64,320},{96,352},{128,384},{160,416},{192,448},{... | collective-permute-start | bytes 589832 | tf_op jit(solution)/shard_map/ppermute | solution.py:316
  97.6 2.8 %shard_map.57.refs_2_ = f32[768,128]{1,0:T(8,128)S(1)} custom-call(s32[1,4]{1,0:T(1,128)S(1)} %copy-done.3, bf16[768,128]{1,0:T(8,128)(2,1)S(1)} %get-tuple-element.16.q_ref, bf16[768,256]{1,0:T(8,128)(2,1)S(1)} %get-tuple-element.17.refs_0_), custom_call_target="tpu_custom_call" | custom-call | flops 301989888 | bytes 1048576 | tf_op jit(solution)/shard_map/pallas_call | solution.py:181
  102.6 6.4 %collective-permute-done.13.refs_2_ = bf16[768,128]{1,0:T(8,128)(2,1)S(1)} collective-permute-done((bf16[768,128]{1,0:T(8,128)(2,1)S(1)}, bf16[768,128]{1,0:T(8,128)(2,1)S(1)}, u32[]{:S(2)}, u32[]{:S(2)}) %collective-permute-start.13) | collective-permute-done | bytes 196640 | tf_op jit(solution)/shard_map/ppermute | solution.py:316
  109.9 10.9 %all_to_all.15.rows_ref = bf16[8,96,128]{2,1,0:T(8,128)(2,1)S(1)} all-to-all(bf16[8,96,128]{2,1,0:T(8,128)(2,1)S(1)} %bitcast.5), channel_id=1, replica_groups=mesh['ctx'=16,'head'=8,'batch'=4] {'head'}, dimensions={0} | all-to-all | bytes 393216 | tf_op jit(solution)/shard_map/all_to_all | solution.py:290
  121.3 9.2 %all_to_all.16 = bf16[8,96,128]{2,1,0:T(8,128)(2,1)S(1)} all-to-all(bf16[8,96,128]{2,1,0:T(8,128)(2,1)S(1)} %shard_map.64), channel_id=1, replica_groups=mesh['ctx'=16,'head'=8,'batch'=4] {'head'}, dimensions={0} | all-to-all | bytes 393216 | tf_op jit(solution)/shard_map/all_to_all | solution.py:290
  (36 shorter events, 10.0 us)
Async XLA Ops:
  4.2 10.8 %copy-start.4 = (bf16[128,1024]{1,0:T(8,128)(2,1)S(1)}, bf16[128,1024]{1,0:T(8,128)(2,1)}, u32[]{:S(2)}) copy-start(bf16[128,1024]{1,0:T(8,128)(2,1)} %param.9) | copy-start | bytes 786436
  4.2 40.7 %all-to-all-start = ((bf16[12,128,512]{2,1,0:T(8,128)(2,1)}), bf16[12,128,512]{2,1,0:T(8,128)(2,1)S(1)}, u32[]{:S(2)}, u32[]{:S(2)}) async-start(bf16[12,128,512]{2,1,0:T(8,128)(2,1)} %shard_map.55), calls=%async_computation | async-start | bytes 3145728 | tf_op jit(solution)/shard_map/all_to_all | solution.py:294
  15.0 30.0 %copy-start.2 = (s32[1,4,6]{2,1,0:T(4,128)S(1)}, s32[1,4,6]{2,1,0:T(4,128)}, u32[]{:S(2)}) copy-start(s32[1,4,6]{2,1,0:T(4,128)} %param.6) | copy-start | bytes 292
  15.0 9.1 %collective-permute-start.1 = (bf16[128,1024]{1,0:T(8,128)(2,1)S(1)}, bf16[128,1024]{1,0:T(8,128)(2,1)S(1)}, u32[]{:S(2)}, u32[]{:S(2)}) collective-permute-start(bf16[128,1024]{1,0:T(8,128)(2,1)S(1)} %copy-done.4), channel_id=1, source_target_pairs={{0,24},{4,28},{8,0},{12,4},{16,8},{20,12},{24,16},{28,20},{1,25},{... | collective-permute-start | bytes 786440 | tf_op jit(solution)/shard_map/ppermute | solution.py:297
  19.5 10.0 %collective-permute-start = (bf16[128,1024]{1,0:T(8,128)(2,1)S(1)}, bf16[128,1024]{1,0:T(8,128)(2,1)S(1)}, u32[]{:S(2)}, u32[]{:S(2)}) collective-permute-start(bf16[128,1024]{1,0:T(8,128)(2,1)S(1)} %copy-done.4), channel_id=1, source_target_pairs={{0,8},{4,12},{8,16},{12,20},{16,24},{20,28},{24,0},{28,4},{1,9},{5... | collective-permute-start | bytes 786440 | tf_op jit(solution)/shard_map/ppermute | solution.py:297
  24.1 12.6 %collective-permute-start.3 = (bf16[64,1024]{1,0:T(8,128)(2,1)S(1)}, bf16[64,1024]{1,0:T(8,128)(2,1)S(1)}, u32[]{:S(2)}, u32[]{:S(2)}) collective-permute-start(bf16[64,1024]{1,0:T(8,128)(2,1)S(1)} %slice.9), channel_id=1, source_target_pairs={{0,24},{4,28},{8,0},{12,4},{16,8},{20,12},{24,16},{28,20},{1,25},{... | collective-permute-start | bytes 393224 | tf_op jit(solution)/shard_map/ppermute | solution.py:298
  29.5 64.3 %copy-start.3 = (s32[1,4]{1,0:T(1,128)S(1)}, s32[1,4]{1,0:T(1,128)}, u32[]{:S(2)}) copy-start(s32[1,4]{1,0:T(1,128)} %hist_ref.13) | copy-start | bytes 52
  29.5 7.2 %collective-permute-start.2 = (bf16[64,1024]{1,0:T(8,128)(2,1)S(1)}, bf16[64,1024]{1,0:T(8,128)(2,1)S(1)}, u32[]{:S(2)}, u32[]{:S(2)}) collective-permute-start(bf16[64,1024]{1,0:T(8,128)(2,1)S(1)} %slice.8), channel_id=1, source_target_pairs={{0,8},{4,12},{8,16},{12,20},{16,24},{20,28},{24,0},{28,4},{1,9},{5... | collective-permute-start | bytes 393224 | tf_op jit(solution)/shard_map/ppermute | solution.py:298
  36.8 7.2 %collective-permute-start.4 = (bf16[512,1024]{1,0:T(8,128)(2,1)S(1)}, bf16[512,1024]{1,0:T(8,128)(2,1)S(1)}, u32[]{:S(2)}, u32[]{:S(2)}) collective-permute-start(bf16[512,1024]{1,0:T(8,128)(2,1)S(1)} %constant_dynamic-update-slice_fusion.same_ref), channel_id=1, source_target_pairs={{0,4},{4,0},{8,12},{12,8},{16,20},{20,16},{24,28},{28,24},{1,5},{5... | collective-permute-start | bytes 3145736 | tf_op jit(solution)/shard_map/ppermute | solution.py:300
  43.9 1.0 copy-start
  45.6 16.2 %collective-permute-start.5 = (bf16[768,256]{1,0:T(8,128)(2,1)S(1)}, bf16[768,256]{1,0:T(8,128)(2,1)S(1)}, u32[]{:S(2)}, u32[]{:S(2)}) collective-permute-start(bf16[768,256]{1,0:T(8,128)(2,1)S(1)} %get-tuple-element.17.refs_0_), channel_id=1, source_target_pairs={{0,32},{32,64},{64,96},{96,128},{128,160},{160,192},{192,224},{224... | collective-permute-start | bytes 1179656 | tf_op jit(solution)/shard_map/ppermute | solution.py:305
  49.1 19.4 %collective-permute-start.9 = (bf16[768,256]{1,0:T(8,128)(2,1)S(1)}, bf16[768,256]{1,0:T(8,128)(2,1)S(1)}, u32[]{:S(2)}, u32[]{:S(2)}) collective-permute-start(bf16[768,256]{1,0:T(8,128)(2,1)S(1)} %get-tuple-element.17.refs_0_), channel_id=1, source_target_pairs={{0,224},{32,0},{64,32},{96,64},{128,96},{160,128},{192,160},{224,1... | collective-permute-start | bytes 1179656 | tf_op jit(solution)/shard_map/ppermute | solution.py:307
  61.8 13.2 %collective-permute-start.6 = (bf16[768,256]{1,0:T(8,128)(2,1)S(1)}, bf16[768,256]{1,0:T(8,128)(2,1)S(1)}, u32[]{:S(2)}, u32[]{:S(2)}) collective-permute-start(bf16[768,256]{1,0:T(8,128)(2,1)S(1)} %collective-permute-done.5.refs_0_), channel_id=1, source_target_pairs={{0,32},{32,64},{64,96},{96,128},{128,160},{160,192},{192,224},{224... | collective-permute-start | bytes 1179656 | tf_op jit(solution)/shard_map/ppermute | solution.py:305
  68.5 12.3 %collective-permute-start.10 = (bf16[768,256]{1,0:T(8,128)(2,1)S(1)}, bf16[768,256]{1,0:T(8,128)(2,1)S(1)}, u32[]{:S(2)}, u32[]{:S(2)}) collective-permute-start(bf16[768,256]{1,0:T(8,128)(2,1)S(1)} %collective-permute-done.9.refs_1_), channel_id=1, source_target_pairs={{0,224},{32,0},{64,32},{96,64},{128,96},{160,128},{192,160},{224,1... | collective-permute-start | bytes 1179656 | tf_op jit(solution)/shard_map/ppermute | solution.py:307
  75.0 13.6 %collective-permute-start.7 = (bf16[768,256]{1,0:T(8,128)(2,1)S(1)}, bf16[768,256]{1,0:T(8,128)(2,1)S(1)}, u32[]{:S(2)}, u32[]{:S(2)}) collective-permute-start(bf16[768,256]{1,0:T(8,128)(2,1)S(1)} %collective-permute-done.6.refs_0_), channel_id=1, source_target_pairs={{0,32},{32,64},{64,96},{96,128},{128,160},{160,192},{192,224},{224... | collective-permute-start | bytes 1179656 | tf_op jit(solution)/shard_map/ppermute | solution.py:305
  80.8 13.7 %collective-permute-start.11 = (bf16[768,256]{1,0:T(8,128)(2,1)S(1)}, bf16[768,256]{1,0:T(8,128)(2,1)S(1)}, u32[]{:S(2)}, u32[]{:S(2)}) collective-permute-start(bf16[768,256]{1,0:T(8,128)(2,1)S(1)} %collective-permute-done.10.refs_1_.refs_0_), channel_id=1, source_target_pairs={{0,224},{32,0},{64,32},{96,64},{128,96},{160,128},{192,160},{224,1... | collective-permute-start | bytes 1179656 | tf_op jit(solution)/shard_map/ppermute | solution.py:307
  87.3 6.5 %collective-permute-start.12 = (bf16[768,128]{1,0:T(8,128)(2,1)S(1)}, bf16[768,128]{1,0:T(8,128)(2,1)S(1)}, u32[]{:S(2)}, u32[]{:S(2)}) collective-permute-start(bf16[768,128]{1,0:T(8,128)(2,1)S(1)} %get-tuple-element.16.q_ref), channel_id=1, source_target_pairs={{256,0},{288,32},{320,64},{352,96},{384,128},{416,160},{448,192},{... | collective-permute-start | bytes 589832 | tf_op jit(solution)/shard_map/ppermute | solution.py:308
  88.6 20.4 %collective-permute-start.8 = (bf16[768,256]{1,0:T(8,128)(2,1)S(1)}, bf16[768,256]{1,0:T(8,128)(2,1)S(1)}, u32[]{:S(2)}, u32[]{:S(2)}) collective-permute-start(bf16[768,256]{1,0:T(8,128)(2,1)S(1)} %collective-permute-done.7.refs_0_), channel_id=1, source_target_pairs={{0,32},{32,64},{64,96},{96,128},{128,160},{160,192},{192,224},{224... | collective-permute-start | bytes 1179656 | tf_op jit(solution)/shard_map/ppermute | solution.py:305
  95.3 13.7 %collective-permute-start.13 = (bf16[768,128]{1,0:T(8,128)(2,1)S(1)}, bf16[768,128]{1,0:T(8,128)(2,1)S(1)}, u32[]{:S(2)}, u32[]{:S(2)}) collective-permute-start(bf16[768,128]{1,0:T(8,128)(2,1)S(1)} %shard_map.62), channel_id=1, source_target_pairs={{0,256},{32,288},{64,320},{96,352},{128,384},{160,416},{192,448},{... | collective-permute-start | bytes 589832 | tf_op jit(solution)/shard_map/ppermute | solution.py:316
  101.9 18.9 %copy-start.1 = (bf16[512,1024]{1,0:T(8,128)(2,1)S(1)}, bf16[512,1024]{1,0:T(8,128)(2,1)}, u32[]{:S(2)}) copy-start(bf16[512,1024]{1,0:T(8,128)(2,1)} %copy-done) | copy-start | bytes 3145732

commit v3 on v2

--- a/solution.py
+++ b/solution.py
@@ -91,11 +91,11 @@
     )(shards, blocks)
 
 
-def unit_owner(me, kind, step):
-    if kind == "up":
-        return me - step
+def unit_owner(stream, step):
+    me = lax.axis_index("ctx")
     plane, row = me // PLANE, me % PLANE
-    return plane * PLANE + (row + step) % PLANE
+    wrapped = plane * PLANE + (row + step) % PLANE if step < 4 else -1
+    return jnp.where(lax.axis_index("head") % 2 == stream, me - step, wrapped)
 
 
 def history_ends(hist_ref):
@@ -166,7 +166,7 @@
         acc_ref[...] = refs[0][...]
     me = lax.axis_index("ctx")
     ends = history_ends(hist_ref)
-    owners = [unit_owner(me, *name) for name in names]
+    owners = [unit_owner(*name) for name in names]
     add_units(ends, me * ROWS, q_ref, list(zip(owners, units)), acc_ref)
 
 
@@ -200,7 +200,7 @@
     @pl.when(me < PLANE)
     def _():
         ends = history_ends(hist_ref)
-        owners = [unit_owner(me, *name) for name in names]
+        owners = [unit_owner(*name) for name in names]
         add_units(ends, (me + PLANE) * ROWS, q_ref, list(zip(owners, units)), acc_ref)
 
     if final:
@@ -231,7 +231,7 @@
         acc_ref[...] += lent_ref[...].astype(jnp.float32)
 
     ends = history_ends(hist_ref)
-    owners = [unit_owner(me, *name) for name in names]
+    owners = [unit_owner(*name) for name in names]
     add_units(ends, me * ROWS, q_ref, list(zip(owners, units)), acc_ref)
     a = acc_ref[...]
     mean = jnp.mean(a * a, axis=-1, keepdims=True)
@@ -251,37 +251,55 @@
     )(hist, q, *units, acc, lent, update)
 
 
-def project_kernel(rows_ref, same_ref, other_ref, out_ref):
+def project_kernel(rows_ref, own_ref, partner_ref, mine_ref, theirs_ref, out_ref):
     me = lax.axis_index("head")
-    total = 0.0
-    for first, w_ref in ((me, same_ref), (me + 1 - 2 * (me % 2), other_ref)):
-        heads = [rows_ref[(first + ahead) % HEADS] for ahead in (0, HEADS - 2, 2, 4)]
-        rows = jnp.concatenate(heads, axis=1)
-        total = total + jnp.dot(rows, w_ref[...], preferred_element_type=jnp.float32)
+    partner = me + 1 - 2 * (me % 2)
+    total = jnp.dot(rows_ref[me], own_ref[...], preferred_element_type=jnp.float32)
+    total += jnp.dot(rows_ref[partner], partner_ref[...], preferred_element_type=jnp.float32)
+    for first, other, w_ref in ((me, partner, mine_ref), (partner, me, theirs_ref)):
+        ahead = HEADS - 2 + 4 * (first % 2)
+        heads = ((first + ahead) % HEADS, (other + ahead) % HEADS, (first + 4) % HEADS)
+        rows = jnp.concatenate([rows_ref[h] for h in heads], axis=1)
+        total += jnp.dot(rows, w_ref[...], preferred_element_type=jnp.float32)
     mixed = total.astype(jnp.bfloat16)
     for h in range(HEADS):
         out_ref[h] = mixed[:, h * HD : (h + 1) * HD]
 
 
-def project(rows, same, other):
+def project(rows, *w):
     return pl.pallas_call(
         project_kernel,
         out_shape=jax.ShapeDtypeStruct((HEADS, CHUNK, HD), jnp.bfloat16),
-        in_specs=[VMEM] * 3,
-        out_specs=VMEM,
-        compiler_params=params(),
-    )(rows, same, other)
-
-
-X_UP = [(h, (h + 2) % HEADS) for h in range(HEADS)]
-X_DOWN = [(h, (h - 2) % HEADS) for h in range(HEADS)]
+        in_specs=[VMEM] * (1 + len(w)),
+        out_specs=VMEM,
+        compiler_params=params(),
+    )(rows, *w)
+
+
 CORE = [(h, h ^ 1) for h in range(HEADS)]
+X_TURN = [(h, (h + 2 - 4 * (h % 2)) % HEADS) for h in range(HEADS)]
 UP = [(i, i + 1) for i in range(CTXS - 1)]
 DOWN = [(i, i // PLANE * PLANE + (i - 1) % PLANE) for i in range(CTXS)]
 LEND = [(i + PLANE, i) for i in range(PLANE)]
 RETURN = [(i, i + PLANE) for i in range(PLANE)]
 
 
+def stream_pairs(stream, step):
+    pairs = []
+    for h in range(HEADS):
+        moves = UP if h % 2 == stream else DOWN if step < 4 else []
+        pairs += [(i * HEADS + h, j * HEADS + h) for i, j in moves]
+    return pairs
+
+
+def gather_w(w):
+    cross = functools.partial(lax.ppermute, axis_name="head")
+    partner = cross(w, perm=CORE)
+    near = cross(jnp.concatenate([w, partner]), perm=X_TURN)
+    mine = jnp.concatenate([near, cross(near[:HD], perm=X_TURN)])
+    return w, partner, mine, cross(mine, perm=CORE)
+
+
 def body(ingest, src_shard, src_slot, hist_len, w_out):
     ingested, shards, slots = ingest[0, 0], src_shard[0], src_slot[0]
     move = functools.partial(lax.ppermute, axis_name="ctx")
@@ -292,32 +310,30 @@
     blocks = pick(shards, slots, ingested)
     w_late, blocks = lax.optimization_barrier((w_out, blocks))
     arrived = lax.all_to_all(blocks, "batch", split_axis=0, concat_axis=0, tiled=True)
-    cross = functools.partial(lax.ppermute, axis_name="head")
-    half = HD // 2
-    w_up, w_down = cross(w_late, perm=X_UP), cross(w_late, perm=X_DOWN)
-    w_far = [cross(w_up[:half], perm=X_UP), cross(w_down[half:], perm=X_DOWN)]
-    w_same = jnp.concatenate([w_late, w_up, w_down, *w_far])
-    w_other = cross(w_same, perm=CORE)
-    w_same, w_other, arrived = lax.optimization_barrier((w_same, w_other, arrived))
+    whole_w, arrived = lax.optimization_barrier((gather_w(w_late), arrived))
     own, q, update = in_order(shards, arrived)
-    up, down = [own], [own]
-    for step in range(4):
-        up.append(move(up[-1], perm=UP))
-        if step < 3:
-            down.append(move(down[-1], perm=DOWN))
+    units = [(own,)]
+    last = [own, own]
+    for step in range(1, 5):
+        last = [
+            lax.ppermute(last[stream], ("ctx", "head"), stream_pairs(stream, step))
+            for stream in range(2)
+        ]
+        units.append(tuple(last))
+    names = [((0, 0),)] + [((0, step), (1, step)) for step in range(1, 5)]
     lent_q = move(q, perm=LEND)
-    acc = attend(hist_len, q, (own,), (("up", 0),))
-    acc = attend(hist_len, q, (up[1], down[1]), (("up", 1), ("down", 1)), acc)
-    lent = attend_lent(hist_len, lent_q, tuple(down[:2]), (("down", 0), ("down", 1)))
-    acc = attend(hist_len, q, (up[2], down[2]), (("up", 2), ("down", 2)), acc)
+    acc = attend(hist_len, q, units[0], names[0])
+    acc = attend(hist_len, q, units[1], names[1], acc)
+    lent = attend_lent(hist_len, lent_q, units[0] + units[1], names[0] + names[1])
+    acc = attend(hist_len, q, units[2], names[2], acc)
     lent = attend_lent(
-        hist_len, lent_q, tuple(down[2:]), (("down", 2), ("down", 3)), lent, final=True
+        hist_len, lent_q, units[2] + units[3], names[2] + names[3], lent, final=True
     )
     lent = move(lent, perm=RETURN)
-    acc = attend(hist_len, q, (up[3], down[3]), (("up", 3), ("down", 3)), acc)
-    gated = attend_last(hist_len, q, (up[4],), (("up", 4),), acc, lent, update)
+    acc = attend(hist_len, q, units[3], names[3], acc)
+    gated = attend_last(hist_len, q, units[4], names[4], acc, lent, update)
     rows = to_all(gated.reshape(HEADS, CHUNK, HD))
-    mixed = to_all(project(rows, w_same, w_other))
+    mixed = to_all(project(rows, *whole_w))
     return mixed.reshape(1, ROWS, HD)
 
 

time: 133 us -> 148 us (1.11)
  the two profiles are of different devices: /device:TPU:1 before, /device:TPU:56 now
where the time goes in v3:
time: 148 us; the launch traced here: 147 us
  starting transfers between devices  70.5 us (48%)
  waiting for transfers between devices  33 us (22%)
  Pallas kernels  21.5 us (15%)
  blocking collectives  20.2 us (14%)
  local copies, waits for them, and re-layouts  1.64 us (1%)
    ppermute x8, starting transfers between devices, body(): lax.ppermute(last[stream], ('ctx', 'head'), stream_pairs(stream, step))  47.5 us
    all_to_all x2, blocking collectives, to_all(): return lax.all_to_all(x, 'head', 0, 0, tiled=True)  20.2 us
    ppermute x8, waiting for transfers between devices, body(): lax.ppermute(last[stream], ('ctx', 'head'), stream_pairs(stream, step))  13.2 us
    pallas_call x4, Pallas kernels, attend(): pl.pallas_call(functools.partial(attend_kernel, names, first), out_shape=...  12.5 us
    all_to_all x1, starting transfers between devices, body(): lax.all_to_all(blocks, 'batch', split_axis=0, concat_axis=0, tiled=True)  10.7 us
    ppermute x1, waiting for transfers between devices, gather_w(): near = cross(jnp.concatenate([w, partner]), perm=X_TURN)  8.88 us
    ppermute x1, waiting for transfers between devices, gather_w(): mine = jnp.concatenate([near, cross(near[:HD], perm=X_TURN)])  7.24 us
    pallas_call x1, Pallas kernels, pick(): pl.pallas_call(pick_kernel, out_shape=jax.ShapeDtypeStruct((count, BLOCK,...  3.91 us
  transfers between devices with their start and end apart: 15, of which 8 were waited for; matrix products, arithmetic and copies ran while one was open for 0% of the time, Pallas kernels for 10%

profile of v3, /device:TPU:56, one launch (start us, length us, event | category | flops | bytes accessed | tf_op | source)
XLA Modules:
  0.0 147.1 jit_solution(3354541089355899986)
XLA Ops:
  0.0 3.9 %shard_map.55 = bf16[12,128,512]{2,1,0:T(8,128)(2,1)} custom-call(s32[4,6]{1,0:T(4,128)} %bitcast.6, s32[4,6]{1,0:T(4,128)} %bitcast.10, bf16[12,128,4,128]{3,2,1,0:T(4,128)(2,1)} %bitcast.8), custom_call_target="tpu_custom_call" | custom-call | tf_op jit(solution)/shard_map/pallas_call | solution.py:56
  3.9 10.7 %all-to-all-start = ((bf16[12,128,512]{2,1,0:T(8,128)(2,1)}), bf16[12,128,512]{2,1,0:T(8,128)(2,1)S(1)}, u32[]{:S(2)}, u32[]{:S(2)}) async-start(bf16[12,128,512]{2,1,0:T(8,128)(2,1)} %shard_map.55), calls=%async_computation | async-start | bytes 3145728 | tf_op jit(solution)/shard_map/all_to_all | solution.py:312
  14.6 2.0 %collective-permute-start = (bf16[128,1024]{1,0:T(8,128)(2,1)S(1)}, bf16[128,1024]{1,0:T(8,128)(2,1)S(1)}, u32[]{:S(2)}, u32[]{:S(2)}) collective-permute-start(bf16[128,1024]{1,0:T(8,128)(2,1)S(1)} %copy-done), channel_id=1, source_target_pairs={{0,4},{4,0},{8,12},{12,8},{16,20},{20,16},{24,28},{28,24},{1,5},{5... | collective-permute-start | bytes 786440 | tf_op jit(solution)/shard_map/ppermute | solution.py:297
  18.2 3.4 %collective-permute-start.1 = (bf16[256,1024]{1,0:T(8,128)(2,1)S(1)}, bf16[256,1024]{1,0:T(8,128)(2,1)S(1)}, u32[]{:S(2)}, u32[]{:S(2)}) collective-permute-start(bf16[256,1024]{1,0:T(8,128)(2,1)S(1)} %pad_maximum_fusion), channel_id=1, source_target_pairs={{0,8},{4,28},{8,16},{12,4},{16,24},{20,12},{24,0},{28,20},{1,9},{5... | collective-permute-start | bytes 1572872 | tf_op jit(solution)/shard_map/ppermute | solution.py:298
  21.6 8.9 %collective-permute-done.1 = bf16[256,1024]{1,0:T(8,128)(2,1)S(1)} collective-permute-done((bf16[256,1024]{1,0:T(8,128)(2,1)S(1)}, bf16[256,1024]{1,0:T(8,128)(2,1)S(1)}, u32[]{:S(2)}, u32[]{:S(2)}) %collective-permute-start.1) | collective-permute-done | bytes 524320 | tf_op jit(solution)/shard_map/ppermute | solution.py:298
  30.5 2.2 %collective-permute-start.2 = (bf16[128,1024]{1,0:T(8,128)(2,1)S(1)}, bf16[128,1024]{1,0:T(8,128)(2,1)S(1)}, u32[]{:S(2)}, u32[]{:S(2)}) collective-permute-start(bf16[128,1024]{1,0:T(8,128)(2,1)S(1)} %slice.4), channel_id=1, source_target_pairs={{0,8},{4,28},{8,16},{12,4},{16,24},{20,12},{24,0},{28,20},{1,9},{5... | collective-permute-start | bytes 786440 | tf_op jit(solution)/shard_map/ppermute | solution.py:299
  32.8 7.2 %collective-permute-done.2 = bf16[128,1024]{1,0:T(8,128)(2,1)S(1)} collective-permute-done((bf16[128,1024]{1,0:T(8,128)(2,1)S(1)}, bf16[128,1024]{1,0:T(8,128)(2,1)S(1)}, u32[]{:S(2)}, u32[]{:S(2)}) %collective-permute-start.2) | collective-permute-done | bytes 262176 | tf_op jit(solution)/shard_map/ppermute | solution.py:299
  41.9 2.3 %collective-permute-done.3.theirs_ref = bf16[384,1024]{1,0:T(8,128)(2,1)S(1)} collective-permute-done((bf16[384,1024]{1,0:T(8,128)(2,1)S(1)}, bf16[384,1024]{1,0:T(8,128)(2,1)S(1)}, u32[]{:S(2)}, u32[]{:S(2)}) %collective-permute-start.3) | collective-permute-done | bytes 786464 | tf_op jit(solution)/shard_map/ppermute | solution.py:300
  45.8 3.3 %collective-permute-start.8 = (bf16[768,256]{1,0:T(8,128)(2,1)S(1)}, bf16[768,256]{1,0:T(8,128)(2,1)S(1)}, u32[]{:S(2)}, u32[]{:S(2)}) collective-permute-start(bf16[768,256]{1,0:T(8,128)(2,1)S(1)} %get-tuple-element.19.refs_0_), channel_id=1, source_target_pairs={{0,224},{32,0},{64,32},{96,64},{128,96},{160,128},{192,160},{224,1... | collective-permute-start | bytes 1179656 | tf_op jit(solution)/shard_map/ppermute | solution.py:319
  49.1 13.3 %collective-permute-start.4 = (bf16[768,256]{1,0:T(8,128)(2,1)S(1)}, bf16[768,256]{1,0:T(8,128)(2,1)S(1)}, u32[]{:S(2)}, u32[]{:S(2)}) collective-permute-start(bf16[768,256]{1,0:T(8,128)(2,1)S(1)} %get-tuple-element.19.refs_0_), channel_id=1, source_target_pairs={{0,32},{32,64},{64,96},{96,128},{128,160},{160,192},{192,224},{224... | collective-permute-start | bytes 1179656 | tf_op jit(solution)/shard_map/ppermute | solution.py:319
  62.4 5.8 %collective-permute-start.9 = (bf16[768,256]{1,0:T(8,128)(2,1)S(1)}, bf16[768,256]{1,0:T(8,128)(2,1)S(1)}, u32[]{:S(2)}, u32[]{:S(2)}) collective-permute-start(bf16[768,256]{1,0:T(8,128)(2,1)S(1)} %collective-permute-done.8.refs_1_.refs_2_), channel_id=1, source_target_pairs={{0,224},{32,0},{64,32},{96,64},{128,96},{160,128},{192,160},{224,1... | collective-permute-start | bytes 1179656 | tf_op jit(solution)/shard_map/ppermute | solution.py:319
  69.9 7.0 %collective-permute-start.5 = (bf16[768,256]{1,0:T(8,128)(2,1)S(1)}, bf16[768,256]{1,0:T(8,128)(2,1)S(1)}, u32[]{:S(2)}, u32[]{:S(2)}) collective-permute-start(bf16[768,256]{1,0:T(8,128)(2,1)S(1)} %collective-permute-done.4.refs_0_.refs_1_), channel_id=1, source_target_pairs={{0,32},{32,64},{64,96},{96,128},{128,160},{160,192},{192,224},{224... | collective-permute-start | bytes 1179656 | tf_op jit(solution)/shard_map/ppermute | solution.py:319
  77.0 4.4 %collective-permute-start.10 = (bf16[768,256]{1,0:T(8,128)(2,1)S(1)}, bf16[768,256]{1,0:T(8,128)(2,1)S(1)}, u32[]{:S(2)}, u32[]{:S(2)}) collective-permute-start(bf16[768,256]{1,0:T(8,128)(2,1)S(1)} %collective-permute-done.9.refs_1_), channel_id=1, source_target_pairs={{0,224},{32,0},{64,32},{96,64},{128,96},{160,128},{192,160},{224,1... | collective-permute-start | bytes 1179656 | tf_op jit(solution)/shard_map/ppermute | solution.py:319
  81.4 4.7 %collective-permute-done.5.refs_0_ = bf16[768,256]{1,0:T(8,128)(2,1)S(1)} collective-permute-done((bf16[768,256]{1,0:T(8,128)(2,1)S(1)}, bf16[768,256]{1,0:T(8,128)(2,1)S(1)}, u32[]{:S(2)}, u32[]{:S(2)}) %collective-permute-start.5) | collective-permute-done | bytes 393248 | tf_op jit(solution)/shard_map/ppermute | solution.py:319
  86.1 6.5 %collective-permute-start.6 = (bf16[768,256]{1,0:T(8,128)(2,1)S(1)}, bf16[768,256]{1,0:T(8,128)(2,1)S(1)}, u32[]{:S(2)}, u32[]{:S(2)}) collective-permute-start(bf16[768,256]{1,0:T(8,128)(2,1)S(1)} %collective-permute-done.5.refs_0_), channel_id=1, source_target_pairs={{0,32},{32,64},{64,96},{96,128},{128,160},{160,192},{192,224},{224... | collective-permute-start | bytes 1179656 | tf_op jit(solution)/shard_map/ppermute | solution.py:319
  94.6 6.7 %collective-permute-done.6.refs_0_.refs_2_ = bf16[768,256]{1,0:T(8,128)(2,1)S(1)} collective-permute-done((bf16[768,256]{1,0:T(8,128)(2,1)S(1)}, bf16[768,256]{1,0:T(8,128)(2,1)S(1)}, u32[]{:S(2)}, u32[]{:S(2)}) %collective-permute-start.6) | collective-permute-done | bytes 393248 | tf_op jit(solution)/shard_map/ppermute | solution.py:319
  101.2 6.6 %collective-permute-start.7 = (bf16[768,256]{1,0:T(8,128)(2,1)S(1)}, bf16[768,256]{1,0:T(8,128)(2,1)S(1)}, u32[]{:S(2)}, u32[]{:S(2)}) collective-permute-start(bf16[768,256]{1,0:T(8,128)(2,1)S(1)} %collective-permute-done.6.refs_0_.refs_2_), channel_id=1, source_target_pairs={{0,32},{32,64},{64,96},{96,128},{128,160},{160,192},{192,224},{224... | collective-permute-start | bytes 1179656 | tf_op jit(solution)/shard_map/ppermute | solution.py:319
  110.9 2.8 %shard_map.57.refs_2_ = f32[768,128]{1,0:T(8,128)S(1)} custom-call(s32[1,4]{1,0:T(1,128)S(1)} %copy-done.4, bf16[768,128]{1,0:T(8,128)(2,1)S(1)} %get-tuple-element.18.q_ref, bf16[768,256]{1,0:T(8,128)(2,1)S(1)} %get-tuple-element.19.refs_0_), custom_call_target="tpu_custom_call" | custom-call | flops 301989888 | bytes 1048576 | tf_op jit(solution)/shard_map/pallas_call | solution.py:181
  113.7 3.2 %shard_map.58.refs_2_ = f32[768,128]{1,0:T(8,128)S(1)} custom-call(s32[1,4]{1,0:T(1,128)S(1)} %copy-done.4, bf16[768,128]{1,0:T(8,128)(2,1)S(1)} %get-tuple-element.18.q_ref, bf16[768,256]{1,0:T(8,128)(2,1)S(1)} %collective-permute-done.4.refs_0_.refs_1_, bf16[768,256]{1,0:T(8,128)(2,1)S(1)} %collective-permute-done.8.refs_1_.refs_2_, ...), custom_call_target="tpu_custom_call" | custom-call | flops 603979776 | bytes 1048576 | tf_op jit(solution)/shard_map/pallas_call | solution.py:181
  117.0 3.3 %shard_map.59.refs_2_ = f32[768,128]{1,0:T(8,128)S(1)} custom-call(s32[1,4]{1,0:T(1,128)S(1)} %copy-done.4, bf16[768,128]{1,0:T(8,128)(2,1)S(1)} %get-tuple-element.18.q_ref, bf16[768,256]{1,0:T(8,128)(2,1)S(1)} %collective-permute-done.5.refs_0_, bf16[768,256]{1,0:T(8,128)(2,1)S(1)} %collective-permute-done.9.refs_1_, f32[768,128]{1,0:T(8,128)S(1)} %shard_map.58.refs_2_), custom_call_target="tpu_custom_call" | custom-call | flops 603979776 | bytes 1048576 | tf_op jit(solution)/shard_map/pallas_call | solution.py:181
  120.2 3.3 %shard_map.60.refs_2_ = f32[768,128]{1,0:T(8,128)S(1)} custom-call(s32[1,4]{1,0:T(1,128)S(1)} %copy-done.4, bf16[768,128]{1,0:T(8,128)(2,1)S(1)} %get-tuple-element.18.q_ref, bf16[768,256]{1,0:T(8,128)(2,1)S(1)} %collective-permute-done.6.refs_0_.refs_2_, bf16[768,256]{1,0:T(8,128)(2,1)S(1)} %collective-permute-done.10.refs_1_.refs_3_, ...), custom_call_target="tpu_custom_call" | custom-call | flops 603979776 | bytes 1048576 | tf_op jit(solution)/shard_map/pallas_call | solution.py:181
  123.6 2.2 %shard_map.63 = bf16[768,128]{1,0:T(8,128)(2,1)S(1)} custom-call(s32[1,4]{1,0:T(1,128)S(1)} %copy-done.4, bf16[768,128]{1,0:T(8,128)(2,1)S(1)} %get-tuple-element.18.q_ref, bf16[768,256]{1,0:T(8,128)(2,1)S(1)} %collective-permute-done.7.refs_0_, bf16[768,256]{1,0:T(8,128)(2,1)S(1)} %collective-permute-done.11.refs_1_, f32[768,128]{1,0:T(8,128)S(1)} %shard_map.60.refs_2_, ...), custom_call_target="tpu_custom_call" | custom-call | flops 603979776 | bytes 1048576 | tf_op jit(solution)/shard_map/pallas_call | solution.py:243
  125.7 10.9 %all_to_all.15.rows_ref = bf16[8,96,128]{2,1,0:T(8,128)(2,1)S(1)} all-to-all(bf16[8,96,128]{2,1,0:T(8,128)(2,1)S(1)} %bitcast.5), channel_id=1, replica_groups=mesh['ctx'=16,'head'=8,'batch'=4] {'head'}, dimensions={0} | all-to-all | bytes 393216 | tf_op jit(solution)/shard_map/all_to_all | solution.py:308
  137.2 9.2 %all_to_all.16 = bf16[8,96,128]{2,1,0:T(8,128)(2,1)S(1)} all-to-all(bf16[8,96,128]{2,1,0:T(8,128)(2,1)S(1)} %shard_map.64), channel_id=1, replica_groups=mesh['ctx'=16,'head'=8,'batch'=4] {'head'}, dimensions={0} | all-to-all | bytes 393216 | tf_op jit(solution)/shard_map/all_to_all | solution.py:308
  (33 shorter events, 13.2 us)
Async XLA Ops:
  3.9 10.7 %copy-start = (bf16[128,1024]{1,0:T(8,128)(2,1)S(1)}, bf16[128,1024]{1,0:T(8,128)(2,1)}, u32[]{:S(2)}) copy-start(bf16[128,1024]{1,0:T(8,128)(2,1)} %own_ref) | copy-start | bytes 786436
  3.9 41.1 %all-to-all-start = ((bf16[12,128,512]{2,1,0:T(8,128)(2,1)}), bf16[12,128,512]{2,1,0:T(8,128)(2,1)S(1)}, u32[]{:S(2)}, u32[]{:S(2)}) async-start(bf16[12,128,512]{2,1,0:T(8,128)(2,1)} %shard_map.55), calls=%async_computation | async-start | bytes 3145728 | tf_op jit(solution)/shard_map/all_to_all | solution.py:312
  14.6 30.5 %copy-start.3 = (s32[1,4,6]{2,1,0:T(4,128)S(1)}, s32[1,4,6]{2,1,0:T(4,128)}, u32[]{:S(2)}) copy-start(s32[1,4,6]{2,1,0:T(4,128)} %param.6) | copy-start | bytes 292
  14.6 3.5 %collective-permute-start = (bf16[128,1024]{1,0:T(8,128)(2,1)S(1)}, bf16[128,1024]{1,0:T(8,128)(2,1)S(1)}, u32[]{:S(2)}, u32[]{:S(2)}) collective-permute-start(bf16[128,1024]{1,0:T(8,128)(2,1)S(1)} %copy-done), channel_id=1, source_target_pairs={{0,4},{4,0},{8,12},{12,8},{16,20},{20,16},{24,28},{28,24},{1,5},{5... | collective-permute-start | bytes 786440 | tf_op jit(solution)/shard_map/ppermute | solution.py:297
  18.2 12.3 %collective-permute-start.1 = (bf16[256,1024]{1,0:T(8,128)(2,1)S(1)}, bf16[256,1024]{1,0:T(8,128)(2,1)S(1)}, u32[]{:S(2)}, u32[]{:S(2)}) collective-permute-start(bf16[256,1024]{1,0:T(8,128)(2,1)S(1)} %pad_maximum_fusion), channel_id=1, source_target_pairs={{0,8},{4,28},{8,16},{12,4},{16,24},{20,12},{24,0},{28,20},{1,9},{5... | collective-permute-start | bytes 1572872 | tf_op jit(solution)/shard_map/ppermute | solution.py:298
  30.5 77.3 %copy-start.4 = (s32[1,4]{1,0:T(1,128)S(1)}, s32[1,4]{1,0:T(1,128)}, u32[]{:S(2)}) copy-start(s32[1,4]{1,0:T(1,128)} %hist_ref.13) | copy-start | bytes 52
  30.5 9.5 %collective-permute-start.2 = (bf16[128,1024]{1,0:T(8,128)(2,1)S(1)}, bf16[128,1024]{1,0:T(8,128)(2,1)S(1)}, u32[]{:S(2)}, u32[]{:S(2)}) collective-permute-start(bf16[128,1024]{1,0:T(8,128)(2,1)S(1)} %slice.4), channel_id=1, source_target_pairs={{0,8},{4,28},{8,16},{12,4},{16,24},{20,12},{24,0},{28,20},{1,9},{5... | collective-permute-start | bytes 786440 | tf_op jit(solution)/shard_map/ppermute | solution.py:299
  40.0 4.2 %collective-permute-start.3 = (bf16[384,1024]{1,0:T(8,128)(2,1)S(1)}, bf16[384,1024]{1,0:T(8,128)(2,1)S(1)}, u32[]{:S(2)}, u32[]{:S(2)}) collective-permute-start(bf16[384,1024]{1,0:T(8,128)(2,1)S(1)} %constant_dynamic-update-slice_fusion.mine_ref), channel_id=1, source_target_pairs={{0,4},{4,0},{8,12},{12,8},{16,20},{20,16},{24,28},{28,24},{1,5},{5... | collective-permute-start | bytes 2359304 | tf_op jit(solution)/shard_map/ppermute | solution.py:300
  44.2 0.9 copy-start.1
  45.8 16.7 %collective-permute-start.8 = (bf16[768,256]{1,0:T(8,128)(2,1)S(1)}, bf16[768,256]{1,0:T(8,128)(2,1)S(1)}, u32[]{:S(2)}, u32[]{:S(2)}) collective-permute-start(bf16[768,256]{1,0:T(8,128)(2,1)S(1)} %get-tuple-element.19.refs_0_), channel_id=1, source_target_pairs={{0,224},{32,0},{64,32},{96,64},{128,96},{160,128},{192,160},{224,1... | collective-permute-start | bytes 1179656 | tf_op jit(solution)/shard_map/ppermute | solution.py:319
  49.1 20.8 %collective-permute-start.4 = (bf16[768,256]{1,0:T(8,128)(2,1)S(1)}, bf16[768,256]{1,0:T(8,128)(2,1)S(1)}, u32[]{:S(2)}, u32[]{:S(2)}) collective-permute-start(bf16[768,256]{1,0:T(8,128)(2,1)S(1)} %get-tuple-element.19.refs_0_), channel_id=1, source_target_pairs={{0,32},{32,64},{64,96},{96,128},{128,160},{160,192},{192,224},{224... | collective-permute-start | bytes 1179656 | tf_op jit(solution)/shard_map/ppermute | solution.py:319
  62.4 14.6 %collective-permute-start.9 = (bf16[768,256]{1,0:T(8,128)(2,1)S(1)}, bf16[768,256]{1,0:T(8,128)(2,1)S(1)}, u32[]{:S(2)}, u32[]{:S(2)}) collective-permute-start(bf16[768,256]{1,0:T(8,128)(2,1)S(1)} %collective-permute-done.8.refs_1_.refs_2_), channel_id=1, source_target_pairs={{0,224},{32,0},{64,32},{96,64},{128,96},{160,128},{192,160},{224,1... | collective-permute-start | bytes 1179656 | tf_op jit(solution)/shard_map/ppermute | solution.py:319
  69.9 16.2 %collective-permute-start.5 = (bf16[768,256]{1,0:T(8,128)(2,1)S(1)}, bf16[768,256]{1,0:T(8,128)(2,1)S(1)}, u32[]{:S(2)}, u32[]{:S(2)}) collective-permute-start(bf16[768,256]{1,0:T(8,128)(2,1)S(1)} %collective-permute-done.4.refs_0_.refs_1_), channel_id=1, source_target_pairs={{0,32},{32,64},{64,96},{96,128},{128,160},{160,192},{192,224},{224... | collective-permute-start | bytes 1179656 | tf_op jit(solution)/shard_map/ppermute | solution.py:319
  77.0 16.9 %collective-permute-start.10 = (bf16[768,256]{1,0:T(8,128)(2,1)S(1)}, bf16[768,256]{1,0:T(8,128)(2,1)S(1)}, u32[]{:S(2)}, u32[]{:S(2)}) collective-permute-start(bf16[768,256]{1,0:T(8,128)(2,1)S(1)} %collective-permute-done.9.refs_1_), channel_id=1, source_target_pairs={{0,224},{32,0},{64,32},{96,64},{128,96},{160,128},{192,160},{224,1... | collective-permute-start | bytes 1179656 | tf_op jit(solution)/shard_map/ppermute | solution.py:319
  86.1 15.2 %collective-permute-start.6 = (bf16[768,256]{1,0:T(8,128)(2,1)S(1)}, bf16[768,256]{1,0:T(8,128)(2,1)S(1)}, u32[]{:S(2)}, u32[]{:S(2)}) collective-permute-start(bf16[768,256]{1,0:T(8,128)(2,1)S(1)} %collective-permute-done.5.refs_0_), channel_id=1, source_target_pairs={{0,32},{32,64},{64,96},{96,128},{128,160},{160,192},{192,224},{224... | collective-permute-start | bytes 1179656 | tf_op jit(solution)/shard_map/ppermute | solution.py:319
  92.6 15.2 %collective-permute-start.12 = (bf16[768,128]{1,0:T(8,128)(2,1)S(1)}, bf16[768,128]{1,0:T(8,128)(2,1)S(1)}, u32[]{:S(2)}, u32[]{:S(2)}) collective-permute-start(bf16[768,128]{1,0:T(8,128)(2,1)S(1)} %get-tuple-element.18.q_ref), channel_id=1, source_target_pairs={{256,0},{288,32},{320,64},{352,96},{384,128},{416,160},{448,192},{... | collective-permute-start | bytes 589832 | tf_op jit(solution)/shard_map/ppermute | solution.py:324
  93.9 29.7 %collective-permute-start.11 = (bf16[768,256]{1,0:T(8,128)(2,1)S(1)}, bf16[768,256]{1,0:T(8,128)(2,1)S(1)}, u32[]{:S(2)}, u32[]{:S(2)}) collective-permute-start(bf16[768,256]{1,0:T(8,128)(2,1)S(1)} %collective-permute-done.10.refs_1_.refs_3_), channel_id=1, source_target_pairs={{4,36},{36,68},{68,100},{100,132},{132,164},{164,196},{196,228},{2... | collective-permute-start | bytes 1179656 | tf_op jit(solution)/shard_map/ppermute | solution.py:319
  101.2 22.3 %collective-permute-start.7 = (bf16[768,256]{1,0:T(8,128)(2,1)S(1)}, bf16[768,256]{1,0:T(8,128)(2,1)S(1)}, u32[]{:S(2)}, u32[]{:S(2)}) collective-permute-start(bf16[768,256]{1,0:T(8,128)(2,1)S(1)} %collective-permute-done.6.refs_0_.refs_2_), channel_id=1, source_target_pairs={{0,32},{32,64},{64,96},{96,128},{128,160},{160,192},{192,224},{224... | collective-permute-start | bytes 1179656 | tf_op jit(solution)/shard_map/ppermute | solution.py:319
  109.5 14.1 %collective-permute-start.13 = (bf16[768,128]{1,0:T(8,128)(2,1)S(1)}, bf16[768,128]{1,0:T(8,128)(2,1)S(1)}, u32[]{:S(2)}, u32[]{:S(2)}) collective-permute-start(bf16[768,128]{1,0:T(8,128)(2,1)S(1)} %shard_map.62), channel_id=1, source_target_pairs={{0,256},{32,288},{64,320},{96,352},{128,384},{160,416},{192,448},{... | collective-permute-start | bytes 589832 | tf_op jit(solution)/shard_map/ppermute | solution.py:332
  123.5 13.2 %copy-start.2 = (bf16[384,1024]{1,0:T(8,128)(2,1)S(1)}, bf16[384,1024]{1,0:T(8,128)(2,1)}, u32[]{:S(2)}) copy-start(bf16[384,1024]{1,0:T(8,128)(2,1)} %copy-done.1) | copy-start | bytes 2359300

commit v4 on v3

--- a/solution.py
+++ b/solution.py
@@ -95,7 +95,7 @@
     me = lax.axis_index("ctx")
     plane, row = me // PLANE, me % PLANE
     wrapped = plane * PLANE + (row + step) % PLANE if step < 4 else -1
-    return jnp.where(lax.axis_index("head") % 2 == stream, me - step, wrapped)
+    return jnp.where((row + stream) % 2 == 1, me - step, wrapped)
 
 
 def history_ends(hist_ref):
@@ -251,33 +251,37 @@
     )(hist, q, *units, acc, lent, update)
 
 
-def project_kernel(rows_ref, own_ref, partner_ref, mine_ref, theirs_ref, out_ref):
+def near_heads(head):
+    chip, core = head // 2, head % 2
+    even = chip + 1 - 2 * (chip % 2)
+    odd = (chip + 3 + 2 * (chip % 2)) % 4
+    return head, even * 2 + core, odd * 2 + core, (head + 4) % HEADS
+
+
+def project_kernel(rows_ref, mine_ref, theirs_ref, out_ref):
     me = lax.axis_index("head")
-    partner = me + 1 - 2 * (me % 2)
-    total = jnp.dot(rows_ref[me], own_ref[...], preferred_element_type=jnp.float32)
-    total += jnp.dot(rows_ref[partner], partner_ref[...], preferred_element_type=jnp.float32)
-    for first, other, w_ref in ((me, partner, mine_ref), (partner, me, theirs_ref)):
-        ahead = HEADS - 2 + 4 * (first % 2)
-        heads = ((first + ahead) % HEADS, (other + ahead) % HEADS, (first + 4) % HEADS)
-        rows = jnp.concatenate([rows_ref[h] for h in heads], axis=1)
-        total += jnp.dot(rows, w_ref[...], preferred_element_type=jnp.float32)
+    total = 0.0
+    for head, w_ref in ((me, mine_ref), (me + 1 - 2 * (me % 2), theirs_ref)):
+        rows = jnp.concatenate([rows_ref[h] for h in near_heads(head)], axis=1)
+        total = total + jnp.dot(rows, w_ref[...], preferred_element_type=jnp.float32)
     mixed = total.astype(jnp.bfloat16)
     for h in range(HEADS):
         out_ref[h] = mixed[:, h * HD : (h + 1) * HD]
 
 
-def project(rows, *w):
+def project(rows, mine, theirs):
     return pl.pallas_call(
         project_kernel,
         out_shape=jax.ShapeDtypeStruct((HEADS, CHUNK, HD), jnp.bfloat16),
-        in_specs=[VMEM] * (1 + len(w)),
-        out_specs=VMEM,
-        compiler_params=params(),
-    )(rows, *w)
+        in_specs=[VMEM] * 3,
+        out_specs=VMEM,
+        compiler_params=params(),
+    )(rows, mine, theirs)
 
 
 CORE = [(h, h ^ 1) for h in range(HEADS)]
-X_TURN = [(h, (h + 2 - 4 * (h % 2)) % HEADS) for h in range(HEADS)]
+X_EVEN = [(h, near_heads(h)[1]) for h in range(HEADS)]
+X_ODD = [(h, near_heads(h)[2]) for h in range(HEADS)]
 UP = [(i, i + 1) for i in range(CTXS - 1)]
 DOWN = [(i, i // PLANE * PLANE + (i - 1) % PLANE) for i in range(CTXS)]
 LEND = [(i + PLANE, i) for i in range(PLANE)]
@@ -285,19 +289,18 @@
 
 
 def stream_pairs(stream, step):
-    pairs = []
-    for h in range(HEADS):
-        moves = UP if h % 2 == stream else DOWN if step < 4 else []
-        pairs += [(i * HEADS + h, j * HEADS + h) for i, j in moves]
-    return pairs
+    ups = [(i, j) for i, j in UP if i % 2 == stream]
+    downs = [(i, j) for i, j in DOWN if i % 2 != stream]
+    return ups + (downs if step < 4 else [])
 
 
 def gather_w(w):
     cross = functools.partial(lax.ppermute, axis_name="head")
-    partner = cross(w, perm=CORE)
-    near = cross(jnp.concatenate([w, partner]), perm=X_TURN)
-    mine = jnp.concatenate([near, cross(near[:HD], perm=X_TURN)])
-    return w, partner, mine, cross(mine, perm=CORE)
+    half = HD // 2
+    even, odd = cross(w, perm=X_EVEN), cross(w, perm=X_ODD)
+    far = [cross(odd[:half], perm=X_EVEN), cross(even[half:], perm=X_ODD)]
+    mine = jnp.concatenate([w, even, odd, *far])
+    return mine, cross(mine, perm=CORE)
 
 
 def body(ingest, src_shard, src_slot, hist_len, w_out):
@@ -315,10 +318,7 @@
     units = [(own,)]
     last = [own, own]
     for step in range(1, 5):
-        last = [
-            lax.ppermute(last[stream], ("ctx", "head"), stream_pairs(stream, step))
-            for stream in range(2)
-        ]
+        last = [move(last[1 - stream], perm=stream_pairs(stream, step)) for stream in range(2)]
         units.append(tuple(last))
     names = [((0, 0),)] + [((0, step), (1, step)) for step in range(1, 5)]
     lent_q = move(q, perm=LEND)

time: 148 us -> 135 us (0.912)
  the two profiles are of different devices: /device:TPU:56 before, /device:TPU:32 now
where the time goes in v4:
time: 135 us; the launch traced here: 134 us
  starting transfers between devices  53.7 us (40%)
  waiting for transfers between devices  34.6 us (26%)
  Pallas kernels  23.7 us (18%)
  blocking collectives  20.2 us (15%)
  local copies, waits for them, and re-layouts  1.77 us (1%)
    ppermute x8, starting transfers between devices, body(): move(last[1 - stream], perm=stream_pairs(stream, step))  26.3 us
    ppermute x8, waiting for transfers between devices, body(): move(last[1 - stream], perm=stream_pairs(stream, step))  22.4 us
    all_to_all x2, blocking collectives, to_all(): return lax.all_to_all(x, 'head', 0, 0, tiled=True)  20.2 us
    all_to_all x1, starting transfers between devices, body(): lax.all_to_all(blocks, 'batch', split_axis=0, concat_axis=0, tiled=True)  10.2 us
    pallas_call x4, Pallas kernels, attend(): pl.pallas_call(functools.partial(attend_kernel, names, first), out_shape=...  8.73 us
    pallas_call x2, Pallas kernels, attend_lent(): pl.pallas_call(functools.partial(lent_kernel, names, first, final), out_s...  7.35 us
    ppermute x2, starting transfers between devices, gather_w(): even, odd = (cross(w, perm=X_EVEN), cross(w, perm=X_ODD))  6.92 us
    ppermute x2, starting transfers between devices, gather_w(): far = [cross(odd[:half], perm=X_EVEN), cross(even[half:], perm=X_ODD)]  5.63 us
  transfers between devices with their start and end apart: 16, of which 10 were waited for; matrix products, arithmetic and copies ran while one was open for 0% of the time, Pallas kernels for 12%

profile of v4, /device:TPU:32, one launch (start us, length us, event | category | flops | bytes accessed | tf_op | source)
XLA Modules:
  0.0 134.2 jit_solution(9687141746732418091)
XLA Ops:
  0.0 4.3 %shard_map.55 = bf16[12,128,512]{2,1,0:T(8,128)(2,1)} custom-call(s32[4,6]{1,0:T(4,128)} %bitcast.6, s32[4,6]{1,0:T(4,128)} %bitcast.10, bf16[12,128,4,128]{3,2,1,0:T(4,128)(2,1)} %bitcast.8), custom_call_target="tpu_custom_call" | custom-call | tf_op jit(solution)/shard_map/pallas_call | solution.py:56
  4.3 10.2 %all-to-all-start = ((bf16[12,128,512]{2,1,0:T(8,128)(2,1)}), bf16[12,128,512]{2,1,0:T(8,128)(2,1)S(1)}, u32[]{:S(2)}, u32[]{:S(2)}) async-start(bf16[12,128,512]{2,1,0:T(8,128)(2,1)} %shard_map.55), calls=%async_computation | async-start | bytes 3145728 | tf_op jit(solution)/shard_map/all_to_all | solution.py:315
  14.5 4.8 %collective-permute-start.1 = (bf16[128,1024]{1,0:T(8,128)(2,1)S(1)}, bf16[128,1024]{1,0:T(8,128)(2,1)S(1)}, u32[]{:S(2)}, u32[]{:S(2)}) collective-permute-start(bf16[128,1024]{1,0:T(8,128)(2,1)S(1)} %copy-done.4), channel_id=1, source_target_pairs={{0,24},{4,28},{8,16},{12,20},{16,8},{20,12},{24,0},{28,4},{1,25},{... | collective-permute-start | bytes 786440 | tf_op jit(solution)/shard_map/ppermute | solution.py:300
  19.3 2.1 %collective-permute-start = (bf16[128,1024]{1,0:T(8,128)(2,1)S(1)}, bf16[128,1024]{1,0:T(8,128)(2,1)S(1)}, u32[]{:S(2)}, u32[]{:S(2)}) collective-permute-start(bf16[128,1024]{1,0:T(8,128)(2,1)S(1)} %copy-done.4), channel_id=1, source_target_pairs={{0,8},{4,12},{8,0},{12,4},{16,24},{20,28},{24,16},{28,20},{1,9},{5... | collective-permute-start | bytes 786440 | tf_op jit(solution)/shard_map/ppermute | solution.py:300
  21.5 4.0 %collective-permute-done.1 = bf16[128,1024]{1,0:T(8,128)(2,1)S(1)} collective-permute-done((bf16[128,1024]{1,0:T(8,128)(2,1)S(1)}, bf16[128,1024]{1,0:T(8,128)(2,1)S(1)}, u32[]{:S(2)}, u32[]{:S(2)}) %collective-permute-start.1) | collective-permute-done | bytes 262176 | tf_op jit(solution)/shard_map/ppermute | solution.py:300
  25.5 2.2 %collective-permute-start.2 = (bf16[64,1024]{1,0:T(8,128)(2,1)S(1)}, bf16[64,1024]{1,0:T(8,128)(2,1)S(1)}, u32[]{:S(2)}, u32[]{:S(2)}) collective-permute-start(bf16[64,1024]{1,0:T(8,128)(2,1)S(1)} %slice.8), channel_id=1, source_target_pairs={{0,8},{4,12},{8,0},{12,4},{16,24},{20,28},{24,16},{28,20},{1,9},{5... | collective-permute-start | bytes 393224 | tf_op jit(solution)/shard_map/ppermute | solution.py:301
  28.7 3.4 %collective-permute-start.3 = (bf16[64,1024]{1,0:T(8,128)(2,1)S(1)}, bf16[64,1024]{1,0:T(8,128)(2,1)S(1)}, u32[]{:S(2)}, u32[]{:S(2)}) collective-permute-start(bf16[64,1024]{1,0:T(8,128)(2,1)S(1)} %slice.9), channel_id=1, source_target_pairs={{0,24},{4,28},{8,16},{12,20},{16,8},{20,12},{24,0},{28,4},{1,25},{... | collective-permute-start | bytes 393224 | tf_op jit(solution)/shard_map/ppermute | solution.py:301
  32.4 4.4 %collective-permute-done.3 = bf16[64,1024]{1,0:T(8,128)(2,1)S(1)} collective-permute-done((bf16[64,1024]{1,0:T(8,128)(2,1)S(1)}, bf16[64,1024]{1,0:T(8,128)(2,1)S(1)}, u32[]{:S(2)}, u32[]{:S(2)}) %collective-permute-start.3) | collective-permute-done | bytes 131104 | tf_op jit(solution)/shard_map/ppermute | solution.py:301
  38.7 2.6 %collective-permute-done.4.theirs_ref = bf16[512,1024]{1,0:T(8,128)(2,1)S(1)} collective-permute-done((bf16[512,1024]{1,0:T(8,128)(2,1)S(1)}, bf16[512,1024]{1,0:T(8,128)(2,1)S(1)}, u32[]{:S(2)}, u32[]{:S(2)}) %collective-permute-start.4) | collective-permute-done | bytes 1048608 | tf_op jit(solution)/shard_map/ppermute | solution.py:303
  43.0 2.5 %collective-permute-start.9 = (bf16[768,256]{1,0:T(8,128)(2,1)S(1)}, bf16[768,256]{1,0:T(8,128)(2,1)S(1)}, u32[]{:S(2)}, u32[]{:S(2)}) collective-permute-start(bf16[768,256]{1,0:T(8,128)(2,1)S(1)} %get-tuple-element.17.refs_0_), channel_id=1, source_target_pairs={{0,32},{64,96},{128,160},{192,224},{256,288},{320,352},{384,416},{... | collective-permute-start | bytes 1179656 | tf_op jit(solution)/shard_map/ppermute | solution.py:321
  45.5 2.4 %collective-permute-start.5 = (bf16[768,256]{1,0:T(8,128)(2,1)S(1)}, bf16[768,256]{1,0:T(8,128)(2,1)S(1)}, u32[]{:S(2)}, u32[]{:S(2)}) collective-permute-start(bf16[768,256]{1,0:T(8,128)(2,1)S(1)} %get-tuple-element.17.refs_0_), channel_id=1, source_target_pairs={{32,64},{96,128},{160,192},{224,256},{288,320},{352,384},{416,448}... | collective-permute-start | bytes 1179656 | tf_op jit(solution)/shard_map/ppermute | solution.py:321
  47.9 8.2 %collective-permute-done.9.refs_0_.refs_1_ = bf16[768,256]{1,0:T(8,128)(2,1)S(1)} collective-permute-done((bf16[768,256]{1,0:T(8,128)(2,1)S(1)}, bf16[768,256]{1,0:T(8,128)(2,1)S(1)}, u32[]{:S(2)}, u32[]{:S(2)}) %collective-permute-start.9) | collective-permute-done | bytes 393248 | tf_op jit(solution)/shard_map/ppermute | solution.py:321
  56.0 2.6 %collective-permute-start.10 = (bf16[768,256]{1,0:T(8,128)(2,1)S(1)}, bf16[768,256]{1,0:T(8,128)(2,1)S(1)}, u32[]{:S(2)}, u32[]{:S(2)}) collective-permute-start(bf16[768,256]{1,0:T(8,128)(2,1)S(1)} %collective-permute-done.9.refs_0_.refs_1_), channel_id=1, source_target_pairs={{32,64},{96,128},{160,192},{224,256},{288,320},{352,384},{416,448}... | collective-permute-start | bytes 1179656 | tf_op jit(solution)/shard_map/ppermute | solution.py:321
  59.5 2.2 %collective-permute-start.6 = (bf16[768,256]{1,0:T(8,128)(2,1)S(1)}, bf16[768,256]{1,0:T(8,128)(2,1)S(1)}, u32[]{:S(2)}, u32[]{:S(2)}) collective-permute-start(bf16[768,256]{1,0:T(8,128)(2,1)S(1)} %collective-permute-done.5.refs_1_.refs_2_), channel_id=1, source_target_pairs={{0,32},{64,96},{128,160},{192,224},{256,288},{320,352},{384,416},{... | collective-permute-start | bytes 1179656 | tf_op jit(solution)/shard_map/ppermute | solution.py:321
  61.6 7.9 %collective-permute-done.10.refs_1_ = bf16[768,256]{1,0:T(8,128)(2,1)S(1)} collective-permute-done((bf16[768,256]{1,0:T(8,128)(2,1)S(1)}, bf16[768,256]{1,0:T(8,128)(2,1)S(1)}, u32[]{:S(2)}, u32[]{:S(2)}) %collective-permute-start.10) | collective-permute-done | bytes 393248 | tf_op jit(solution)/shard_map/ppermute | solution.py:321
  71.4 4.4 %collective-permute-start.7 = (bf16[768,256]{1,0:T(8,128)(2,1)S(1)}, bf16[768,256]{1,0:T(8,128)(2,1)S(1)}, u32[]{:S(2)}, u32[]{:S(2)}) collective-permute-start(bf16[768,256]{1,0:T(8,128)(2,1)S(1)} %collective-permute-done.6.refs_0_), channel_id=1, source_target_pairs={{32,64},{96,128},{160,192},{224,256},{288,320},{352,384},{416,448}... | collective-permute-start | bytes 1179656 | tf_op jit(solution)/shard_map/ppermute | solution.py:321
  77.1 3.6 %collective-permute-done.11.refs_0_.refs_2_ = bf16[768,256]{1,0:T(8,128)(2,1)S(1)} collective-permute-done((bf16[768,256]{1,0:T(8,128)(2,1)S(1)}, bf16[768,256]{1,0:T(8,128)(2,1)S(1)}, u32[]{:S(2)}, u32[]{:S(2)}) %collective-permute-start.11) | collective-permute-done | bytes 393248 | tf_op jit(solution)/shard_map/ppermute | solution.py:321
  83.9 9.1 %collective-permute-start.8 = (bf16[768,256]{1,0:T(8,128)(2,1)S(1)}, bf16[768,256]{1,0:T(8,128)(2,1)S(1)}, u32[]{:S(2)}, u32[]{:S(2)}) collective-permute-start(bf16[768,256]{1,0:T(8,128)(2,1)S(1)} %collective-permute-done.7.refs_1_.refs_3_), channel_id=1, source_target_pairs={{0,32},{64,96},{128,160},{192,224},{256,288},{320,352},{384,416},{... | collective-permute-start | bytes 1179656 | tf_op jit(solution)/shard_map/ppermute | solution.py:321
  93.0 4.0 %shard_map.61.refs_4_ = f32[768,128]{1,0:T(8,128)S(1)} custom-call(s32[1,4]{1,0:T(1,128)S(1)} %copy-done.3, bf16[768,128]{1,0:T(8,128)(2,1)S(1)} %collective-permute-done.13.q_ref, bf16[768,256]{1,0:T(8,128)(2,1)S(1)} %get-tuple-element.17.refs_0_, bf16[768,256]{1,0:T(8,128)(2,1)S(1)} %collective-permute-done.9.refs_0_.refs_1_, ...), custom_call_target="tpu_custom_call" | custom-call | flops 905969664 | bytes 1048576 | tf_op jit(solution)/shard_map/pallas_call | solution.py:212
  97.0 3.4 %shard_map.62 = bf16[768,128]{1,0:T(8,128)(2,1)S(1)} custom-call(s32[1,4]{1,0:T(1,128)S(1)} %copy-done.3, bf16[768,128]{1,0:T(8,128)(2,1)S(1)} %collective-permute-done.13.q_ref, bf16[768,256]{1,0:T(8,128)(2,1)S(1)} %collective-permute-done.6.refs_0_, bf16[768,256]{1,0:T(8,128)(2,1)S(1)} %collective-permute-done.10.refs_1_, ...), custom_call_target="tpu_custom_call" | custom-call | flops 1207959552 | bytes 1048576 | tf_op jit(solution)/shard_map/pallas_call | solution.py:212
  101.9 2.8 %shard_map.57.refs_2_ = f32[768,128]{1,0:T(8,128)S(1)} custom-call(s32[1,4]{1,0:T(1,128)S(1)} %copy-done.3, bf16[768,128]{1,0:T(8,128)(2,1)S(1)} %get-tuple-element.16.q_ref, bf16[768,256]{1,0:T(8,128)(2,1)S(1)} %get-tuple-element.17.refs_0_), custom_call_target="tpu_custom_call" | custom-call | flops 301989888 | bytes 1048576 | tf_op jit(solution)/shard_map/pallas_call | solution.py:181
  110.7 2.2 %shard_map.63 = bf16[768,128]{1,0:T(8,128)(2,1)S(1)} custom-call(s32[1,4]{1,0:T(1,128)S(1)} %copy-done.3, bf16[768,128]{1,0:T(8,128)(2,1)S(1)} %get-tuple-element.16.q_ref, bf16[768,256]{1,0:T(8,128)(2,1)S(1)} %collective-permute-done.8.refs_0_, bf16[768,256]{1,0:T(8,128)(2,1)S(1)} %collective-permute-done.12.refs_1_, f32[768,128]{1,0:T(8,128)S(1)} %shard_map.60.refs_2_, ...), custom_call_target="tpu_custom_call" | custom-call | flops 603979776 | bytes 1048576 | tf_op jit(solution)/shard_map/pallas_call | solution.py:243
  112.9 11.0 %all_to_all.15.rows_ref = bf16[8,96,128]{2,1,0:T(8,128)(2,1)S(1)} all-to-all(bf16[8,96,128]{2,1,0:T(8,128)(2,1)S(1)} %bitcast.5), channel_id=1, replica_groups=mesh['ctx'=16,'head'=8,'batch'=4] {'head'}, dimensions={0} | all-to-all | bytes 393216 | tf_op jit(solution)/shard_map/all_to_all | solution.py:311
  124.3 9.2 %all_to_all.16 = bf16[8,96,128]{2,1,0:T(8,128)(2,1)S(1)} all-to-all(bf16[8,96,128]{2,1,0:T(8,128)(2,1)S(1)} %shard_map.64), channel_id=1, replica_groups=mesh['ctx'=16,'head'=8,'batch'=4] {'head'}, dimensions={0} | all-to-all | bytes 393216 | tf_op jit(solution)/shard_map/all_to_all | solution.py:311
  (38 shorter events, 20.6 us)
Async XLA Ops:
  4.3 10.2 %copy-start.4 = (bf16[128,1024]{1,0:T(8,128)(2,1)S(1)}, bf16[128,1024]{1,0:T(8,128)(2,1)}, u32[]{:S(2)}) copy-start(bf16[128,1024]{1,0:T(8,128)(2,1)} %param.9) | copy-start | bytes 786436
  4.3 38.0 %all-to-all-start = ((bf16[12,128,512]{2,1,0:T(8,128)(2,1)}), bf16[12,128,512]{2,1,0:T(8,128)(2,1)S(1)}, u32[]{:S(2)}, u32[]{:S(2)}) async-start(bf16[12,128,512]{2,1,0:T(8,128)(2,1)} %shard_map.55), calls=%async_computation | async-start | bytes 3145728 | tf_op jit(solution)/shard_map/all_to_all | solution.py:315
  14.5 27.8 %copy-start.2 = (s32[1,4,6]{2,1,0:T(4,128)S(1)}, s32[1,4,6]{2,1,0:T(4,128)}, u32[]{:S(2)}) copy-start(s32[1,4,6]{2,1,0:T(4,128)} %param.6) | copy-start | bytes 292
  14.5 11.0 %collective-permute-start.1 = (bf16[128,1024]{1,0:T(8,128)(2,1)S(1)}, bf16[128,1024]{1,0:T(8,128)(2,1)S(1)}, u32[]{:S(2)}, u32[]{:S(2)}) collective-permute-start(bf16[128,1024]{1,0:T(8,128)(2,1)S(1)} %copy-done.4), channel_id=1, source_target_pairs={{0,24},{4,28},{8,16},{12,20},{16,8},{20,12},{24,0},{28,4},{1,25},{... | collective-permute-start | bytes 786440 | tf_op jit(solution)/shard_map/ppermute | solution.py:300
  19.3 9.4 %collective-permute-start = (bf16[128,1024]{1,0:T(8,128)(2,1)S(1)}, bf16[128,1024]{1,0:T(8,128)(2,1)S(1)}, u32[]{:S(2)}, u32[]{:S(2)}) collective-permute-start(bf16[128,1024]{1,0:T(8,128)(2,1)S(1)} %copy-done.4), channel_id=1, source_target_pairs={{0,8},{4,12},{8,0},{12,4},{16,24},{20,28},{24,16},{28,20},{1,9},{5... | collective-permute-start | bytes 786440 | tf_op jit(solution)/shard_map/ppermute | solution.py:300
  25.5 6.9 %collective-permute-start.2 = (bf16[64,1024]{1,0:T(8,128)(2,1)S(1)}, bf16[64,1024]{1,0:T(8,128)(2,1)S(1)}, u32[]{:S(2)}, u32[]{:S(2)}) collective-permute-start(bf16[64,1024]{1,0:T(8,128)(2,1)S(1)} %slice.8), channel_id=1, source_target_pairs={{0,8},{4,12},{8,0},{12,4},{16,24},{20,28},{24,16},{28,20},{1,9},{5... | collective-permute-start | bytes 393224 | tf_op jit(solution)/shard_map/ppermute | solution.py:301
  28.7 64.3 %copy-start.3 = (s32[1,4]{1,0:T(1,128)S(1)}, s32[1,4]{1,0:T(1,128)}, u32[]{:S(2)}) copy-start(s32[1,4]{1,0:T(1,128)} %hist_ref.13) | copy-start | bytes 52
  28.7 8.1 %collective-permute-start.3 = (bf16[64,1024]{1,0:T(8,128)(2,1)S(1)}, bf16[64,1024]{1,0:T(8,128)(2,1)S(1)}, u32[]{:S(2)}, u32[]{:S(2)}) collective-permute-start(bf16[64,1024]{1,0:T(8,128)(2,1)S(1)} %slice.9), channel_id=1, source_target_pairs={{0,24},{4,28},{8,16},{12,20},{16,8},{20,12},{24,0},{28,4},{1,25},{... | collective-permute-start | bytes 393224 | tf_op jit(solution)/shard_map/ppermute | solution.py:301
  36.8 4.6 %collective-permute-start.4 = (bf16[512,1024]{1,0:T(8,128)(2,1)S(1)}, bf16[512,1024]{1,0:T(8,128)(2,1)S(1)}, u32[]{:S(2)}, u32[]{:S(2)}) collective-permute-start(bf16[512,1024]{1,0:T(8,128)(2,1)S(1)} %constant_dynamic-update-slice_fusion.mine_ref), channel_id=1, source_target_pairs={{0,4},{4,0},{8,12},{12,8},{16,20},{20,16},{24,28},{28,24},{1,5},{5... | collective-permute-start | bytes 3145736 | tf_op jit(solution)/shard_map/ppermute | solution.py:303
  41.3 1.0 copy-start
  43.0 13.1 %collective-permute-start.9 = (bf16[768,256]{1,0:T(8,128)(2,1)S(1)}, bf16[768,256]{1,0:T(8,128)(2,1)S(1)}, u32[]{:S(2)}, u32[]{:S(2)}) collective-permute-start(bf16[768,256]{1,0:T(8,128)(2,1)S(1)} %get-tuple-element.17.refs_0_), channel_id=1, source_target_pairs={{0,32},{64,96},{128,160},{192,224},{256,288},{320,352},{384,416},{... | collective-permute-start | bytes 1179656 | tf_op jit(solution)/shard_map/ppermute | solution.py:321
  45.5 14.0 %collective-permute-start.5 = (bf16[768,256]{1,0:T(8,128)(2,1)S(1)}, bf16[768,256]{1,0:T(8,128)(2,1)S(1)}, u32[]{:S(2)}, u32[]{:S(2)}) collective-permute-start(bf16[768,256]{1,0:T(8,128)(2,1)S(1)} %get-tuple-element.17.refs_0_), channel_id=1, source_target_pairs={{32,64},{96,128},{160,192},{224,256},{288,320},{352,384},{416,448}... | collective-permute-start | bytes 1179656 | tf_op jit(solution)/shard_map/ppermute | solution.py:321
  56.0 13.4 %collective-permute-start.10 = (bf16[768,256]{1,0:T(8,128)(2,1)S(1)}, bf16[768,256]{1,0:T(8,128)(2,1)S(1)}, u32[]{:S(2)}, u32[]{:S(2)}) collective-permute-start(bf16[768,256]{1,0:T(8,128)(2,1)S(1)} %collective-permute-done.9.refs_0_.refs_1_), channel_id=1, source_target_pairs={{32,64},{96,128},{160,192},{224,256},{288,320},{352,384},{416,448}... | collective-permute-start | bytes 1179656 | tf_op jit(solution)/shard_map/ppermute | solution.py:321
  59.5 11.9 %collective-permute-start.6 = (bf16[768,256]{1,0:T(8,128)(2,1)S(1)}, bf16[768,256]{1,0:T(8,128)(2,1)S(1)}, u32[]{:S(2)}, u32[]{:S(2)}) collective-permute-start(bf16[768,256]{1,0:T(8,128)(2,1)S(1)} %collective-permute-done.5.refs_1_.refs_2_), channel_id=1, source_target_pairs={{0,32},{64,96},{128,160},{192,224},{256,288},{320,352},{384,416},{... | collective-permute-start | bytes 1179656 | tf_op jit(solution)/shard_map/ppermute | solution.py:321
  69.5 11.3 %collective-permute-start.11 = (bf16[768,256]{1,0:T(8,128)(2,1)S(1)}, bf16[768,256]{1,0:T(8,128)(2,1)S(1)}, u32[]{:S(2)}, u32[]{:S(2)}) collective-permute-start(bf16[768,256]{1,0:T(8,128)(2,1)S(1)} %collective-permute-done.10.refs_1_), channel_id=1, source_target_pairs={{0,32},{64,96},{128,160},{192,224},{256,288},{320,352},{384,416},{... | collective-permute-start | bytes 1179656 | tf_op jit(solution)/shard_map/ppermute | solution.py:321
  71.4 12.5 %collective-permute-start.7 = (bf16[768,256]{1,0:T(8,128)(2,1)S(1)}, bf16[768,256]{1,0:T(8,128)(2,1)S(1)}, u32[]{:S(2)}, u32[]{:S(2)}) collective-permute-start(bf16[768,256]{1,0:T(8,128)(2,1)S(1)} %collective-permute-done.6.refs_0_), channel_id=1, source_target_pairs={{32,64},{96,128},{160,192},{224,256},{288,320},{352,384},{416,448}... | collective-permute-start | bytes 1179656 | tf_op jit(solution)/shard_map/ppermute | solution.py:321
  75.8 17.2 %collective-permute-start.13 = (bf16[768,128]{1,0:T(8,128)(2,1)S(1)}, bf16[768,128]{1,0:T(8,128)(2,1)S(1)}, u32[]{:S(2)}, u32[]{:S(2)}) collective-permute-start(bf16[768,128]{1,0:T(8,128)(2,1)S(1)} %get-tuple-element.16.q_ref), channel_id=1, source_target_pairs={{256,0},{288,32},{320,64},{352,96},{384,128},{416,160},{448,192},{... | collective-permute-start | bytes 589832 | tf_op jit(solution)/shard_map/ppermute | solution.py:324
  80.8 29.9 %collective-permute-start.12 = (bf16[768,256]{1,0:T(8,128)(2,1)S(1)}, bf16[768,256]{1,0:T(8,128)(2,1)S(1)}, u32[]{:S(2)}, u32[]{:S(2)}) collective-permute-start(bf16[768,256]{1,0:T(8,128)(2,1)S(1)} %collective-permute-done.11.refs_0_.refs_2_), channel_id=1, source_target_pairs={{32,64},{96,128},{160,192},{224,256},{288,320},{352,384},{416,448}... | collective-permute-start | bytes 1179656 | tf_op jit(solution)/shard_map/ppermute | solution.py:321
  83.9 26.8 %collective-permute-start.8 = (bf16[768,256]{1,0:T(8,128)(2,1)S(1)}, bf16[768,256]{1,0:T(8,128)(2,1)S(1)}, u32[]{:S(2)}, u32[]{:S(2)}) collective-permute-start(bf16[768,256]{1,0:T(8,128)(2,1)S(1)} %collective-permute-done.7.refs_1_.refs_3_), channel_id=1, source_target_pairs={{0,32},{64,96},{128,160},{192,224},{256,288},{320,352},{384,416},{... | collective-permute-start | bytes 1179656 | tf_op jit(solution)/shard_map/ppermute | solution.py:321
  100.4 10.3 %collective-permute-start.14 = (bf16[768,128]{1,0:T(8,128)(2,1)S(1)}, bf16[768,128]{1,0:T(8,128)(2,1)S(1)}, u32[]{:S(2)}, u32[]{:S(2)}) collective-permute-start(bf16[768,128]{1,0:T(8,128)(2,1)S(1)} %shard_map.62), channel_id=1, source_target_pairs={{0,256},{32,288},{64,320},{96,352},{128,384},{160,416},{192,448},{... | collective-permute-start | bytes 589832 | tf_op jit(solution)/shard_map/ppermute | solution.py:332
  110.6 13.2 %copy-start.1 = (bf16[512,1024]{1,0:T(8,128)(2,1)S(1)}, bf16[512,1024]{1,0:T(8,128)(2,1)}, u32[]{:S(2)}) copy-start(bf16[512,1024]{1,0:T(8,128)(2,1)} %copy-done) | copy-start | bytes 3145732

commit v5 on v4

--- a/solution.py
+++ b/solution.py
@@ -19,6 +19,7 @@
 ROWS = BLOCK * PER_OWNER
 CHUNK = ROWS // HEADS
 TILE = 256
+WEIGHT = 8
 HALF_SCALE = 0.5 / math.sqrt(HD)
 VMEM = pl.BlockSpec(memory_space=pltpu.VMEM)
 SMEM = pl.BlockSpec(memory_space=pltpu.SMEM)
@@ -29,7 +30,7 @@
     return pltpu.CompilerParams(vmem_limit_bytes=mib * 1024 * 1024)
 
 
-def pick_kernel(shard_ref, slot_ref, ingest_ref, out_ref, buf, sems):
+def pick_kernel(shard_ref, slot_ref, ingest_ref, first_ref, update_ref, buf, sems):
     me = lax.axis_index("batch")
     copies = []
     for g in range(GROUPS):
@@ -48,16 +49,21 @@
             copies.append(copy)
     for at, copy in enumerate(copies):
         copy.wait()
-        out_ref[at] = buf[at].reshape(BLOCK, 4 * HD)
+        flat = buf[at].reshape(BLOCK, 4 * HD)
+        first_ref[at] = flat[:, : 3 * HD]
+        update_ref[at] = flat[:, 3 * HD :]
 
 
 def pick(shards, slots, ingested):
     count = GROUPS * CAPACITY
     return pl.pallas_call(
         pick_kernel,
-        out_shape=jax.ShapeDtypeStruct((count, BLOCK, 4 * HD), jnp.bfloat16),
+        out_shape=[
+            jax.ShapeDtypeStruct((count, BLOCK, 3 * HD), jnp.bfloat16),
+            jax.ShapeDtypeStruct((count, BLOCK, HD), jnp.bfloat16),
+        ],
         in_specs=[SMEM, SMEM, ANY],
-        out_specs=VMEM,
+        out_specs=[VMEM] * 2,
         scratch_shapes=[
             pltpu.VMEM((count, BLOCK, 4, HD), jnp.bfloat16),
             pltpu.SemaphoreType.DMA((count,)),
@@ -66,27 +72,31 @@
     )(shards, slots, ingested)
 
 
-def order_kernel(shard_ref, in_ref, unit_ref, query_ref, update_ref):
+def block_places(shard_ref):
     me = lax.axis_index("batch")
     shards = [shard_ref[me, k] for k in range(PER_OWNER)]
     for k in range(PER_OWNER):
         rank = jnp.int32(0)
         for earlier in range(k):
             rank = rank + (shards[earlier] == shards[k]).astype(jnp.int32)
-        at = shards[k] * CAPACITY + rank
-        rows = slice(k * BLOCK, (k + 1) * BLOCK)
+        yield slice(k * BLOCK, (k + 1) * BLOCK), shards[k] * CAPACITY + rank
+
+
+def order_kernel(shard_ref, in_ref, unit_ref, query_ref):
+    for rows, at in block_places(shard_ref):
         query_ref[rows, :] = in_ref[at, :, :HD]
-        unit_ref[rows, :] = in_ref[at, :, HD : 3 * HD]
-        update_ref[rows, :] = in_ref[at, :, 3 * HD :]
+        unit_ref[rows, :] = in_ref[at, :, HD:]
 
 
 def in_order(shards, blocks):
-    shape = jax.ShapeDtypeStruct((ROWS, HD), jnp.bfloat16)
     return pl.pallas_call(
         order_kernel,
-        out_shape=[jax.ShapeDtypeStruct((ROWS, 2 * HD), jnp.bfloat16), shape, shape],
+        out_shape=[
+            jax.ShapeDtypeStruct((ROWS, 2 * HD), jnp.bfloat16),
+            jax.ShapeDtypeStruct((ROWS, HD), jnp.bfloat16),
+        ],
         in_specs=[SMEM, VMEM],
-        out_specs=[VMEM] * 3,
+        out_specs=[VMEM] * 2,
         compiler_params=params(),
     )(shards, blocks)
 
@@ -157,35 +167,41 @@
     lax.fori_loop(0, ROWS // TILE, row_tile, 0)
 
 
-def attend_kernel(names, first, hist_ref, q_ref, *refs):
+def attend_kernel(names, first, hand_on, hist_ref, q_ref, *refs):
     units, refs = refs[: len(names)], refs[len(names) :]
-    acc_ref = refs[-1]
+    acc_ref = refs[-2] if hand_on else refs[-1]
     if first:
         acc_ref[...] = jnp.zeros_like(acc_ref)
     else:
         acc_ref[...] = refs[0][...]
-    me = lax.axis_index("ctx")
     ends = history_ends(hist_ref)
     owners = [unit_owner(*name) for name in names]
-    add_units(ends, me * ROWS, q_ref, list(zip(owners, units)), acc_ref)
+    add_units(ends, lax.axis_index("ctx") * ROWS, q_ref, list(zip(owners, units)), acc_ref)
 
 
 def estimate(units):
     return pl.CostEstimate(
-        flops=4 * ROWS * ROWS * HD * units, bytes_accessed=1 << 20, transcendentals=ROWS * ROWS * units
+        flops=WEIGHT * 4 * ROWS * ROWS * HD * units,
+        bytes_accessed=1 << 20,
+        transcendentals=ROWS * ROWS * units,
     )
 
 
-def attend(hist, q, units, names, acc=None):
-    first = acc is None
-    return pl.pallas_call(
-        functools.partial(attend_kernel, names, first),
-        out_shape=jax.ShapeDtypeStruct((ROWS, HD), jnp.float32),
-        in_specs=[SMEM] + [VMEM] * (1 + len(units) + (0 if first else 1)),
-        out_specs=VMEM,
+def attend(hist, q, units, names, acc=None, later=None):
+    first, hand_on = acc is None, later is not None
+    args = [hist, q, *units] + ([] if first else [acc])
+    own = jax.ShapeDtypeStruct((ROWS, HD), jnp.float32)
+    passed = [jax.ShapeDtypeStruct(later.shape, later.dtype)] if hand_on else []
+    out = pl.pallas_call(
+        functools.partial(attend_kernel, names, first, hand_on),
+        out_shape=[own, *passed],
+        in_specs=[SMEM] + [VMEM] * (len(args) - 1) + [ANY] * hand_on,
+        out_specs=[VMEM] + [ANY] * hand_on,
+        input_output_aliases={len(args): 1} if hand_on else {},
         cost_estimate=estimate(len(units)),
         compiler_params=params(),
-    )(hist, q, *units, *(() if first else (acc,)))
+    )(*args, *([later] if hand_on else []))
+    return out if hand_on else out[0]
 
 
 def lent_kernel(names, first, final, hist_ref, q_ref, *refs):
@@ -220,7 +236,7 @@
     )(hist, q, *units, *(() if first else (acc,)))
 
 
-def last_kernel(names, hist_ref, q_ref, *refs):
+def last_kernel(names, hist_ref, shard_ref, q_ref, *refs):
     units = refs[: len(names)]
     acc_in, lent_ref, update_ref, out_ref, acc_ref = refs[len(names) :]
     me = lax.axis_index("ctx")
@@ -233,22 +249,23 @@
     ends = history_ends(hist_ref)
     owners = [unit_owner(*name) for name in names]
     add_units(ends, me * ROWS, q_ref, list(zip(owners, units)), acc_ref)
-    a = acc_ref[...]
-    mean = jnp.mean(a * a, axis=-1, keepdims=True)
-    normed = a * lax.rsqrt(mean + 1e-6)
-    out_ref[...] = (normed * update_ref[...].astype(jnp.float32)).astype(jnp.bfloat16)
-
-
-def attend_last(hist, q, units, names, acc, lent, update):
+    for rows, at in block_places(shard_ref):
+        a = acc_ref[rows, :]
+        mean = jnp.mean(a * a, axis=-1, keepdims=True)
+        normed = a * lax.rsqrt(mean + 1e-6)
+        out_ref[rows, :] = (normed * update_ref[at].astype(jnp.float32)).astype(jnp.bfloat16)
+
+
+def attend_last(hist, shards, q, units, names, acc, lent, update):
     return pl.pallas_call(
         functools.partial(last_kernel, names),
         out_shape=jax.ShapeDtypeStruct((ROWS, HD), jnp.bfloat16),
-        in_specs=[SMEM] + [VMEM] * (4 + len(units)),
+        in_specs=[SMEM, SMEM] + [VMEM] * (4 + len(units)),
         out_specs=VMEM,
         scratch_shapes=[pltpu.VMEM((ROWS, HD), jnp.float32)],
         cost_estimate=estimate(len(units)),
         compiler_params=params(),
-    )(hist, q, *units, acc, lent, update)
+    )(hist, shards, q, *units, acc, lent, update)
 
 
 def near_heads(head):
@@ -310,30 +327,37 @@
     def to_all(x):
         return lax.all_to_all(x, "head", 0, 0, tiled=True)
 
-    blocks = pick(shards, slots, ingested)
-    w_late, blocks = lax.optimization_barrier((w_out, blocks))
-    arrived = lax.all_to_all(blocks, "batch", split_axis=0, concat_axis=0, tiled=True)
-    whole_w, arrived = lax.optimization_barrier((gather_w(w_late), arrived))
-    own, q, update = in_order(shards, arrived)
-    units = [(own,)]
-    last = [own, own]
-    for step in range(1, 5):
-        last = [move(last[1 - stream], perm=stream_pairs(stream, step)) for stream in range(2)]
-        units.append(tuple(last))
+    def to_owners(x):
+        return lax.all_to_all(x, "batch", split_axis=0, concat_axis=0, tiled=True)
+
+    def step_on(last, step):
+        return [move(last[1 - stream], perm=stream_pairs(stream, step)) for stream in range(2)]
+
+    tie = lax.optimization_barrier
     names = [((0, 0),)] + [((0, step), (1, step)) for step in range(1, 5)]
+    blocks, updates = pick(shards, slots, ingested)
+    w_late, blocks = tie((w_out, blocks))
+    arrived = to_owners(blocks)
+    mine, theirs = gather_w(w_late)
+    mine, arrived = tie((mine, arrived))
+    own, q = in_order(shards, arrived)
+    first = step_on([own, own], 1)
+    second = step_on(first, 2)
+    third = step_on(second, 3)
+    fourth = step_on(third, 4)
     lent_q = move(q, perm=LEND)
-    acc = attend(hist_len, q, units[0], names[0])
-    acc = attend(hist_len, q, units[1], names[1], acc)
-    lent = attend_lent(hist_len, lent_q, units[0] + units[1], names[0] + names[1])
-    acc = attend(hist_len, q, units[2], names[2], acc)
-    lent = attend_lent(
-        hist_len, lent_q, units[2] + units[3], names[2] + names[3], lent, final=True
-    )
+    acc, updates = attend(hist_len, q, (own,), names[0], None, updates)
+    acc, updates = attend(hist_len, q, first, names[1], acc, updates)
+    update = to_owners(updates)
+    lent = attend_lent(hist_len, lent_q, (own, *first), names[0] + names[1])
+    acc = attend(hist_len, q, second, names[2], acc)
+    lent = attend_lent(hist_len, lent_q, second, names[2], lent)
+    lent = attend_lent(hist_len, lent_q, third, names[3], lent, final=True)
     lent = move(lent, perm=RETURN)
-    acc = attend(hist_len, q, units[3], names[3], acc)
-    gated = attend_last(hist_len, q, units[4], names[4], acc, lent, update)
+    acc = attend(hist_len, q, third, names[3], acc)
+    gated = attend_last(hist_len, shards, q, fourth, names[4], acc, lent, update)
     rows = to_all(gated.reshape(HEADS, CHUNK, HD))
-    mixed = to_all(project(rows, *whole_w))
+    mixed = to_all(project(rows, mine, theirs))
     return mixed.reshape(1, ROWS, HD)
 
 

time: 135 us -> 144 us (1.067)
  the two profiles are of different devices: /device:TPU:32 before, /device:TPU:1 now
where the time goes in v5:
time: 144 us
  starting transfers between devices  81.6 us (57%)
  waiting for transfers between devices  31.4 us (22%)
  Pallas kernels  16.7 us (12%)
  blocking collectives  9.23 us (6%)
  local copies, waits for them, and re-layouts  4.3 us (3%)
    ppermute x8, starting transfers between devices, step_on(): move(last[1 - stream], perm=stream_pairs(stream, step))  27.8 us
    all_to_all x2, starting transfers between devices, to_owners(): return lax.all_to_all(x, 'batch', split_axis=0, concat_axis=0, tiled=True)  16.6 us
    ppermute x8, waiting for transfers between devices, step_on(): move(last[1 - stream], perm=stream_pairs(stream, step))  14.9 us
    all_to_all x1, blocking collectives, to_all(): return lax.all_to_all(x, 'head', 0, 0, tiled=True)  9.23 us
    all_to_all x1, starting transfers between devices, to_all(): return lax.all_to_all(x, 'head', 0, 0, tiled=True)  8.9 us
    ppermute x1, starting transfers between devices, gather_w(): return (mine, cross(mine, perm=CORE))  7.93 us
    ppermute x1, starting transfers between devices, body(): lent = move(lent, perm=RETURN)  7.38 us
    ppermute x2, starting transfers between devices, gather_w(): even, odd = (cross(w, perm=X_EVEN), cross(w, perm=X_ODD))  6.3 us
  transfers between devices with their start and end apart: 18, of which 10 were waited for; matrix products, arithmetic and copies ran while one was open for 0% of the time, Pallas kernels for 8%

profile of v5, /device:TPU:1, one launch (start us, length us, event | category | flops | bytes accessed | tf_op | source)
XLA Modules:
  0.0 143.5 jit_solution(16549863644076791047)
XLA Ops:
  0.0 4.2 %shard_map.55 = (bf16[12,128,384]{2,1,0:T(8,128)(2,1)}, bf16[12,128,128]{2,1,0:T(8,128)(2,1)}) custom-call(s32[4,6]{1,0:T(4,128)} %bitcast.5, s32[4,6]{1,0:T(4,128)} %bitcast.10, bf16[12,128,4,128]{3,2,1,0:T(4,128)(2,1)} %bitcast.8), custom_call_target="tpu_custom_call" | custom-call | tf_op jit(solution)/shard_map/pallas_call | solution.py:59
  4.2 11.2 %all-to-all-start = ((bf16[12,128,384]{2,1,0:T(8,128)(2,1)}), bf16[12,128,384]{2,1,0:T(8,128)(2,1)S(1)}, u32[]{:S(2)}, u32[]{:S(2)}) async-start(bf16[12,128,384]{2,1,0:T(8,128)(2,1)} %get-tuple-element.19), calls=%async_computation | async-start | bytes 2359296 | tf_op jit(solution)/shard_map/all_to_all | solution.py:331
  15.4 4.4 %collective-permute-start.1 = (bf16[128,1024]{1,0:T(8,128)(2,1)S(1)}, bf16[128,1024]{1,0:T(8,128)(2,1)S(1)}, u32[]{:S(2)}, u32[]{:S(2)}) collective-permute-start(bf16[128,1024]{1,0:T(8,128)(2,1)S(1)} %copy-done.8), channel_id=1, source_target_pairs={{0,24},{4,28},{8,16},{12,20},{16,8},{20,12},{24,0},{28,4},{1,25},{... | collective-permute-start | bytes 786440 | tf_op jit(solution)/shard_map/ppermute | solution.py:317
  21.7 3.6 %collective-permute-done.1 = bf16[128,1024]{1,0:T(8,128)(2,1)S(1)} collective-permute-done((bf16[128,1024]{1,0:T(8,128)(2,1)S(1)}, bf16[128,1024]{1,0:T(8,128)(2,1)S(1)}, u32[]{:S(2)}, u32[]{:S(2)}) %collective-permute-start.1) | collective-permute-done | bytes 262176 | tf_op jit(solution)/shard_map/ppermute | solution.py:317
  25.3 1.9 %collective-permute-start.2 = (bf16[64,1024]{1,0:T(8,128)(2,1)S(1)}, bf16[64,1024]{1,0:T(8,128)(2,1)S(1)}, u32[]{:S(2)}, u32[]{:S(2)}) collective-permute-start(bf16[64,1024]{1,0:T(8,128)(2,1)S(1)} %slice.8), channel_id=1, source_target_pairs={{0,8},{4,12},{8,0},{12,4},{16,24},{20,28},{24,16},{28,20},{1,9},{5... | collective-permute-start | bytes 393224 | tf_op jit(solution)/shard_map/ppermute | solution.py:318
  28.2 3.5 %collective-permute-start.3 = (bf16[64,1024]{1,0:T(8,128)(2,1)S(1)}, bf16[64,1024]{1,0:T(8,128)(2,1)S(1)}, u32[]{:S(2)}, u32[]{:S(2)}) collective-permute-start(bf16[64,1024]{1,0:T(8,128)(2,1)S(1)} %slice.9), channel_id=1, source_target_pairs={{0,24},{4,28},{8,16},{12,20},{16,8},{20,12},{24,0},{28,4},{1,25},{... | collective-permute-start | bytes 393224 | tf_op jit(solution)/shard_map/ppermute | solution.py:318
  31.8 3.7 %collective-permute-done.3 = bf16[64,1024]{1,0:T(8,128)(2,1)S(1)} collective-permute-done((bf16[64,1024]{1,0:T(8,128)(2,1)S(1)}, bf16[64,1024]{1,0:T(8,128)(2,1)S(1)}, u32[]{:S(2)}, u32[]{:S(2)}) %collective-permute-start.3) | collective-permute-done | bytes 131104 | tf_op jit(solution)/shard_map/ppermute | solution.py:318
  35.5 2.4 %all-to-all-done.in_ref = bf16[12,128,384]{2,1,0:T(8,128)(2,1)S(1)} async-done(((bf16[12,128,384]{2,1,0:T(8,128)(2,1)}), bf16[12,128,384]{2,1,0:T(8,128)(2,1)S(1)}, u32[]{:S(2)}, u32[]{:S(2)}) %all-to-all-start) | async-done | bytes 1179680 | tf_op jit(solution)/shard_map/all_to_all | solution.py:331
  38.5 7.2 %collective-permute-start.8 = (bf16[768,256]{1,0:T(8,128)(2,1)S(1)}, bf16[768,256]{1,0:T(8,128)(2,1)S(1)}, u32[]{:S(2)}, u32[]{:S(2)}) collective-permute-start(bf16[768,256]{1,0:T(8,128)(2,1)S(1)} %get-tuple-element.22.refs_0_), channel_id=1, source_target_pairs={{0,32},{64,96},{128,160},{192,224},{256,288},{320,352},{384,416},{... | collective-permute-start | bytes 1179656 | tf_op jit(solution)/shard_map/ppermute | solution.py:334
  47.0 7.9 %collective-permute-start.14 = (bf16[512,1024]{1,0:T(8,128)(2,1)S(1)}, bf16[512,1024]{1,0:T(8,128)(2,1)S(1)}, u32[]{:S(2)}, u32[]{:S(2)}) collective-permute-start(bf16[512,1024]{1,0:T(8,128)(2,1)S(1)} %constant_dynamic-update-slice_fusion.mine_ref), channel_id=1, source_target_pairs={{0,4},{4,0},{8,12},{12,8},{16,20},{20,16},{24,28},{28,24},{1,5},{5... | collective-permute-start | bytes 3145736 | tf_op jit(solution)/shard_map/ppermute | solution.py:320
  56.3 2.8 %shard_map.57 = (f32[768,128]{1,0:T(8,128)S(1)}, bf16[12,128,128]{2,1,0:T(8,128)(2,1)}) custom-call(s32[1,4]{1,0:T(1,128)S(1)} %copy-done.3, bf16[768,128]{1,0:T(8,128)(2,1)S(1)} %get-tuple-element.21.q_ref, bf16[768,256]{1,0:T(8,128)(2,1)S(1)} %get-tuple-element.22.refs_0_, ...), custom_call_target="tpu_custom_call", output_to_operand_aliasing={{1}: (3, {})} | custom-call | flops 2415919104 | bytes 1048576 | tf_op jit(solution)/shard_map/pallas_call | solution.py:195
  60.6 5.5 %all-to-all-start.1 = ((bf16[12,128,128]{2,1,0:T(8,128)(2,1)}), bf16[12,128,128]{2,1,0:T(8,128)(2,1)S(1)}, u32[]{:S(2)}, u32[]{:S(2)}) async-start(bf16[12,128,128]{2,1,0:T(8,128)(2,1)} %get-tuple-element.27), calls=%async_computation.1 | async-start | bytes 786432 | tf_op jit(solution)/shard_map/all_to_all | solution.py:331
  66.1 7.1 %collective-permute-start.9 = (bf16[768,256]{1,0:T(8,128)(2,1)}, bf16[768,256]{1,0:T(8,128)(2,1)S(1)}, u32[]{:S(2)}, u32[]{:S(2)}) collective-permute-start(bf16[768,256]{1,0:T(8,128)(2,1)} %copy-done.1), channel_id=1, source_target_pairs={{32,64},{96,128},{160,192},{224,256},{288,320},{352,384},{416,448}... | collective-permute-start | bytes 1179656 | tf_op jit(solution)/shard_map/ppermute | solution.py:334
  77.3 4.7 %collective-permute-done.9.refs_1_ = bf16[768,256]{1,0:T(8,128)(2,1)S(1)} collective-permute-done((bf16[768,256]{1,0:T(8,128)(2,1)}, bf16[768,256]{1,0:T(8,128)(2,1)S(1)}, u32[]{:S(2)}, u32[]{:S(2)}) %collective-permute-start.9) | collective-permute-done | bytes 393248 | tf_op jit(solution)/shard_map/ppermute | solution.py:334
  85.5 3.7 %collective-permute-start.6 = (bf16[768,256]{1,0:T(8,128)(2,1)S(1)}, bf16[768,256]{1,0:T(8,128)(2,1)S(1)}, u32[]{:S(2)}, u32[]{:S(2)}) collective-permute-start(bf16[768,256]{1,0:T(8,128)(2,1)S(1)} %collective-permute-done.5.refs_0_), channel_id=1, source_target_pairs={{32,64},{96,128},{160,192},{224,256},{288,320},{352,384},{416,448}... | collective-permute-start | bytes 1179656 | tf_op jit(solution)/shard_map/ppermute | solution.py:334
  91.2 2.5 %collective-permute-done.10.refs_0_ = bf16[768,256]{1,0:T(8,128)(2,1)S(1)} collective-permute-done((bf16[768,256]{1,0:T(8,128)(2,1)S(1)}, bf16[768,256]{1,0:T(8,128)(2,1)S(1)}, u32[]{:S(2)}, u32[]{:S(2)}) %collective-permute-start.10) | collective-permute-done | bytes 393248 | tf_op jit(solution)/shard_map/ppermute | solution.py:334
  93.7 2.9 %collective-permute-done.6.refs_1_ = bf16[768,256]{1,0:T(8,128)(2,1)S(1)} collective-permute-done((bf16[768,256]{1,0:T(8,128)(2,1)S(1)}, bf16[768,256]{1,0:T(8,128)(2,1)S(1)}, u32[]{:S(2)}, u32[]{:S(2)}) %collective-permute-start.6) | collective-permute-done | bytes 393248 | tf_op jit(solution)/shard_map/ppermute | solution.py:334
  98.4 7.4 %collective-permute-start.13 = (bf16[768,128]{1,0:T(8,128)(2,1)}, bf16[768,128]{1,0:T(8,128)(2,1)}, u32[]{:S(2)}, u32[]{:S(2)}) collective-permute-start(bf16[768,128]{1,0:T(8,128)(2,1)} %shard_map.63), channel_id=1, source_target_pairs={{0,256},{32,288},{64,320},{96,352},{128,384},{160,416},{192,448},{... | collective-permute-start | bytes 589832 | tf_op jit(solution)/shard_map/ppermute | solution.py:356
  107.2 3.2 %collective-permute-start.7 = (bf16[768,256]{1,0:T(8,128)(2,1)S(1)}, bf16[768,256]{1,0:T(8,128)(2,1)}, u32[]{:S(2)}, u32[]{:S(2)}) collective-permute-start(bf16[768,256]{1,0:T(8,128)(2,1)S(1)} %collective-permute-done.6.refs_1_), channel_id=1, source_target_pairs={{0,32},{64,96},{128,160},{192,224},{256,288},{320,352},{384,416},{... | collective-permute-start | bytes 1179656 | tf_op jit(solution)/shard_map/ppermute | solution.py:334
  112.0 3.2 %collective-permute-done.7.refs_0_ = bf16[768,256]{1,0:T(8,128)(2,1)} collective-permute-done((bf16[768,256]{1,0:T(8,128)(2,1)S(1)}, bf16[768,256]{1,0:T(8,128)(2,1)}, u32[]{:S(2)}, u32[]{:S(2)}) %collective-permute-start.7) | collective-permute-done | bytes 393248 | tf_op jit(solution)/shard_map/ppermute | solution.py:334
  116.1 2.2 %shard_map.64 = bf16[768,128]{1,0:T(8,128)(2,1)} custom-call(s32[1,4]{1,0:T(1,128)S(1)} %copy-done.3, s32[4,6]{1,0:T(4,128)S(1)} %bitcast.7, bf16[768,128]{1,0:T(8,128)(2,1)S(1)} %get-tuple-element.21.q_ref, bf16[768,256]{1,0:T(8,128)(2,1)} %collective-permute-done.7.refs_0_, bf16[768,256]{1,0:T(8,128)(2,1)} %collective-permute-done.11.refs_1_, ...), custom_call_target="tpu_custom_call" | custom-call | flops 4831838208 | bytes 1048576 | tf_op jit(solution)/shard_map/pallas_call | solution.py:260
  118.3 8.9 %all-to-all-start.2 = ((bf16[8,96,128]{2,1,0:T(8,128)(2,1)}), bf16[8,96,128]{2,1,0:T(8,128)(2,1)S(1)}, u32[]{:S(2)}, u32[]{:S(2)}) async-start(bf16[8,96,128]{2,1,0:T(8,128)(2,1)} %bitcast.3), calls=%async_computation.2 | async-start | bytes 393216 | tf_op jit(solution)/shard_map/all_to_all | solution.py:328
  127.3 5.9 %all-to-all-done.2.rows_ref = bf16[8,96,128]{2,1,0:T(8,128)(2,1)S(1)} async-done(((bf16[8,96,128]{2,1,0:T(8,128)(2,1)}), bf16[8,96,128]{2,1,0:T(8,128)(2,1)S(1)}, u32[]{:S(2)}, u32[]{:S(2)}) %all-to-all-start.2) | async-done | bytes 196640 | tf_op jit(solution)/shard_map/all_to_all | solution.py:328
  133.6 9.2 %all_to_all.20 = bf16[8,96,128]{2,1,0:T(8,128)(2,1)S(1)} all-to-all(bf16[8,96,128]{2,1,0:T(8,128)(2,1)S(1)} %shard_map.65), channel_id=1, replica_groups=mesh['ctx'=16,'head'=8,'batch'=4] {'head'}, dimensions={0} | all-to-all | bytes 393216 | tf_op jit(solution)/shard_map/all_to_all | solution.py:328
  (50 shorter events, 24.1 us)
Async XLA Ops:
  4.2 11.2 %copy-start.8 = (bf16[128,1024]{1,0:T(8,128)(2,1)S(1)}, bf16[128,1024]{1,0:T(8,128)(2,1)}, u32[]{:S(2)}) copy-start(bf16[128,1024]{1,0:T(8,128)(2,1)} %param.9) | copy-start | bytes 786436
  4.2 33.6 %all-to-all-start = ((bf16[12,128,384]{2,1,0:T(8,128)(2,1)}), bf16[12,128,384]{2,1,0:T(8,128)(2,1)S(1)}, u32[]{:S(2)}, u32[]{:S(2)}) async-start(bf16[12,128,384]{2,1,0:T(8,128)(2,1)} %get-tuple-element.19), calls=%async_computation | async-start | bytes 2359296 | tf_op jit(solution)/shard_map/all_to_all | solution.py:331
  15.4 9.9 %collective-permute-start.1 = (bf16[128,1024]{1,0:T(8,128)(2,1)S(1)}, bf16[128,1024]{1,0:T(8,128)(2,1)S(1)}, u32[]{:S(2)}, u32[]{:S(2)}) collective-permute-start(bf16[128,1024]{1,0:T(8,128)(2,1)S(1)} %copy-done.8), channel_id=1, source_target_pairs={{0,24},{4,28},{8,16},{12,20},{16,8},{20,12},{24,0},{28,4},{1,25},{... | collective-permute-start | bytes 786440 | tf_op jit(solution)/shard_map/ppermute | solution.py:317
  19.8 8.5 %collective-permute-start = (bf16[128,1024]{1,0:T(8,128)(2,1)S(1)}, bf16[128,1024]{1,0:T(8,128)(2,1)S(1)}, u32[]{:S(2)}, u32[]{:S(2)}) collective-permute-start(bf16[128,1024]{1,0:T(8,128)(2,1)S(1)} %copy-done.8), channel_id=1, source_target_pairs={{0,8},{4,12},{8,0},{12,4},{16,24},{20,28},{24,16},{28,20},{1,9},{5... | collective-permute-start | bytes 786440 | tf_op jit(solution)/shard_map/ppermute | solution.py:317
  21.7 16.1 %copy-start = (s32[1,4,6]{2,1,0:T(4,128)S(1)}, s32[1,4,6]{2,1,0:T(4,128)}, u32[]{:S(2)}) copy-start(s32[1,4,6]{2,1,0:T(4,128)} %param.6) | copy-start | bytes 292
  25.3 6.4 %collective-permute-start.2 = (bf16[64,1024]{1,0:T(8,128)(2,1)S(1)}, bf16[64,1024]{1,0:T(8,128)(2,1)S(1)}, u32[]{:S(2)}, u32[]{:S(2)}) collective-permute-start(bf16[64,1024]{1,0:T(8,128)(2,1)S(1)} %slice.8), channel_id=1, source_target_pairs={{0,8},{4,12},{8,0},{12,4},{16,24},{20,28},{24,16},{28,20},{1,9},{5... | collective-permute-start | bytes 393224 | tf_op jit(solution)/shard_map/ppermute | solution.py:318
  28.2 7.2 %collective-permute-start.3 = (bf16[64,1024]{1,0:T(8,128)(2,1)S(1)}, bf16[64,1024]{1,0:T(8,128)(2,1)S(1)}, u32[]{:S(2)}, u32[]{:S(2)}) collective-permute-start(bf16[64,1024]{1,0:T(8,128)(2,1)S(1)} %slice.9), channel_id=1, source_target_pairs={{0,24},{4,28},{8,16},{12,20},{16,8},{20,12},{24,0},{28,4},{1,25},{... | collective-permute-start | bytes 393224 | tf_op jit(solution)/shard_map/ppermute | solution.py:318
  31.7 24.5 %copy-start.3 = (s32[1,4]{1,0:T(1,128)S(1)}, s32[1,4]{1,0:T(1,128)}, u32[]{:S(2)}) copy-start(s32[1,4]{1,0:T(1,128)} %hist_ref.15) | copy-start | bytes 52
  38.5 20.6 %collective-permute-start.8 = (bf16[768,256]{1,0:T(8,128)(2,1)S(1)}, bf16[768,256]{1,0:T(8,128)(2,1)S(1)}, u32[]{:S(2)}, u32[]{:S(2)}) collective-permute-start(bf16[768,256]{1,0:T(8,128)(2,1)S(1)} %get-tuple-element.22.refs_0_), channel_id=1, source_target_pairs={{0,32},{64,96},{128,160},{192,224},{256,288},{320,352},{384,416},{... | collective-permute-start | bytes 1179656 | tf_op jit(solution)/shard_map/ppermute | solution.py:334
  45.7 13.4 %collective-permute-start.4 = (bf16[768,256]{1,0:T(8,128)(2,1)S(1)}, bf16[768,256]{1,0:T(8,128)(2,1)S(1)}, u32[]{:S(2)}, u32[]{:S(2)}) collective-permute-start(bf16[768,256]{1,0:T(8,128)(2,1)S(1)} %get-tuple-element.22.refs_0_), channel_id=1, source_target_pairs={{32,64},{96,128},{160,192},{224,256},{288,320},{352,384},{416,448}... | collective-permute-start | bytes 1179656 | tf_op jit(solution)/shard_map/ppermute | solution.py:334
  47.0 80.2 %collective-permute-start.14 = (bf16[512,1024]{1,0:T(8,128)(2,1)S(1)}, bf16[512,1024]{1,0:T(8,128)(2,1)S(1)}, u32[]{:S(2)}, u32[]{:S(2)}) collective-permute-start(bf16[512,1024]{1,0:T(8,128)(2,1)S(1)} %constant_dynamic-update-slice_fusion.mine_ref), channel_id=1, source_target_pairs={{0,4},{4,0},{8,12},{12,8},{16,20},{20,16},{24,28},{28,24},{1,5},{5... | collective-permute-start | bytes 3145736 | tf_op jit(solution)/shard_map/ppermute | solution.py:320
  55.0 20.1 %collective-permute-start.12 = (bf16[768,128]{1,0:T(8,128)(2,1)S(1)}, bf16[768,128]{1,0:T(8,128)(2,1)}, u32[]{:S(2)}, u32[]{:S(2)}) collective-permute-start(bf16[768,128]{1,0:T(8,128)(2,1)S(1)} %get-tuple-element.21.q_ref), channel_id=1, source_target_pairs={{256,0},{288,32},{320,64},{352,96},{384,128},{416,160},{448,192},{... | collective-permute-start | bytes 589832 | tf_op jit(solution)/shard_map/ppermute | solution.py:348
  60.6 51.4 %all-to-all-start.1 = ((bf16[12,128,128]{2,1,0:T(8,128)(2,1)}), bf16[12,128,128]{2,1,0:T(8,128)(2,1)S(1)}, u32[]{:S(2)}, u32[]{:S(2)}) async-start(bf16[12,128,128]{2,1,0:T(8,128)(2,1)} %get-tuple-element.27), calls=%async_computation.1 | async-start | bytes 786432 | tf_op jit(solution)/shard_map/all_to_all | solution.py:331
  66.1 15.9 %collective-permute-start.9 = (bf16[768,256]{1,0:T(8,128)(2,1)}, bf16[768,256]{1,0:T(8,128)(2,1)S(1)}, u32[]{:S(2)}, u32[]{:S(2)}) collective-permute-start(bf16[768,256]{1,0:T(8,128)(2,1)} %copy-done.1), channel_id=1, source_target_pairs={{32,64},{96,128},{160,192},{224,256},{288,320},{352,384},{416,448}... | collective-permute-start | bytes 1179656 | tf_op jit(solution)/shard_map/ppermute | solution.py:334
  73.1 12.3 %collective-permute-start.5 = (bf16[768,256]{1,0:T(8,128)(2,1)S(1)}, bf16[768,256]{1,0:T(8,128)(2,1)S(1)}, u32[]{:S(2)}, u32[]{:S(2)}) collective-permute-start(bf16[768,256]{1,0:T(8,128)(2,1)S(1)} %collective-permute-done.4.refs_1_.refs_2_), channel_id=1, source_target_pairs={{0,32},{64,96},{128,160},{192,224},{256,288},{320,352},{384,416},{... | collective-permute-start | bytes 1179656 | tf_op jit(solution)/shard_map/ppermute | solution.py:334
  75.1 1.0 copy-start.2
  77.2 13.2 %copy-start.7 = (f32[768,128]{1,0:T(8,128)S(1)}, f32[768,128]{1,0:T(8,128)}, u32[]{:S(2)}) copy-start(f32[768,128]{1,0:T(8,128)} %copy-done.6) | copy-start | bytes 1179652
  82.0 11.7 %collective-permute-start.10 = (bf16[768,256]{1,0:T(8,128)(2,1)S(1)}, bf16[768,256]{1,0:T(8,128)(2,1)S(1)}, u32[]{:S(2)}, u32[]{:S(2)}) collective-permute-start(bf16[768,256]{1,0:T(8,128)(2,1)S(1)} %collective-permute-done.9.refs_1_), channel_id=1, source_target_pairs={{0,32},{64,96},{128,160},{192,224},{256,288},{320,352},{384,416},{... | collective-permute-start | bytes 1179656 | tf_op jit(solution)/shard_map/ppermute | solution.py:334
  85.5 11.2 %collective-permute-start.6 = (bf16[768,256]{1,0:T(8,128)(2,1)S(1)}, bf16[768,256]{1,0:T(8,128)(2,1)S(1)}, u32[]{:S(2)}, u32[]{:S(2)}) collective-permute-start(bf16[768,256]{1,0:T(8,128)(2,1)S(1)} %collective-permute-done.5.refs_0_), channel_id=1, source_target_pairs={{32,64},{96,128},{160,192},{224,256},{288,320},{352,384},{416,448}... | collective-permute-start | bytes 1179656 | tf_op jit(solution)/shard_map/ppermute | solution.py:334
  98.4 13.5 %collective-permute-start.13 = (bf16[768,128]{1,0:T(8,128)(2,1)}, bf16[768,128]{1,0:T(8,128)(2,1)}, u32[]{:S(2)}, u32[]{:S(2)}) collective-permute-start(bf16[768,128]{1,0:T(8,128)(2,1)} %shard_map.63), channel_id=1, source_target_pairs={{0,256},{32,288},{64,320},{96,352},{128,384},{160,416},{192,448},{... | collective-permute-start | bytes 589832 | tf_op jit(solution)/shard_map/ppermute | solution.py:356
  105.8 6.2 %collective-permute-start.11 = (bf16[768,256]{1,0:T(8,128)(2,1)S(1)}, bf16[768,256]{1,0:T(8,128)(2,1)}, u32[]{:S(2)}, u32[]{:S(2)}) collective-permute-start(bf16[768,256]{1,0:T(8,128)(2,1)S(1)} %collective-permute-done.10.refs_0_), channel_id=1, source_target_pairs={{32,64},{96,128},{160,192},{224,256},{288,320},{352,384},{416,448}... | collective-permute-start | bytes 1179656 | tf_op jit(solution)/shard_map/ppermute | solution.py:334
  107.2 7.9 %collective-permute-start.7 = (bf16[768,256]{1,0:T(8,128)(2,1)S(1)}, bf16[768,256]{1,0:T(8,128)(2,1)}, u32[]{:S(2)}, u32[]{:S(2)}) collective-permute-start(bf16[768,256]{1,0:T(8,128)(2,1)S(1)} %collective-permute-done.6.refs_1_), channel_id=1, source_target_pairs={{0,32},{64,96},{128,160},{192,224},{256,288},{320,352},{384,416},{... | collective-permute-start | bytes 1179656 | tf_op jit(solution)/shard_map/ppermute | solution.py:334
  115.1 1.0 copy-start.5
  118.3 14.8 %all-to-all-start.2 = ((bf16[8,96,128]{2,1,0:T(8,128)(2,1)}), bf16[8,96,128]{2,1,0:T(8,128)(2,1)S(1)}, u32[]{:S(2)}, u32[]{:S(2)}) async-start(bf16[8,96,128]{2,1,0:T(8,128)(2,1)} %bitcast.3), calls=%async_computation.2 | async-start | bytes 393216 | tf_op jit(solution)/shard_map/all_to_all | solution.py:328
  (3 other events, 2.3 us)

commit v6 on v4

--- a/solution.py
+++ b/solution.py
@@ -19,6 +19,7 @@
 ROWS = BLOCK * PER_OWNER
 CHUNK = ROWS // HEADS
 TILE = 256
+WEIGHT = 8
 HALF_SCALE = 0.5 / math.sqrt(HD)
 VMEM = pl.BlockSpec(memory_space=pltpu.VMEM)
 SMEM = pl.BlockSpec(memory_space=pltpu.SMEM)
@@ -66,15 +67,18 @@
     )(shards, slots, ingested)
 
 
-def order_kernel(shard_ref, in_ref, unit_ref, query_ref, update_ref):
+def block_places(shard_ref):
     me = lax.axis_index("batch")
     shards = [shard_ref[me, k] for k in range(PER_OWNER)]
     for k in range(PER_OWNER):
         rank = jnp.int32(0)
         for earlier in range(k):
             rank = rank + (shards[earlier] == shards[k]).astype(jnp.int32)
-        at = shards[k] * CAPACITY + rank
-        rows = slice(k * BLOCK, (k + 1) * BLOCK)
+        yield slice(k * BLOCK, (k + 1) * BLOCK), shards[k] * CAPACITY + rank
+
+
+def order_kernel(shard_ref, in_ref, unit_ref, query_ref, update_ref):
+    for rows, at in block_places(shard_ref):
         query_ref[rows, :] = in_ref[at, :, :HD]
         unit_ref[rows, :] = in_ref[at, :, HD : 3 * HD]
         update_ref[rows, :] = in_ref[at, :, 3 * HD :]
@@ -125,6 +129,8 @@
         first = q_base + t * TILE
         last = first + TILE - 1
         low, high = start_of(ends, first), start_of(ends, last)
+        pos = first + lax.broadcasted_iota(jnp.int32, (TILE, 1), 0)
+        start = start_of(ends, pos)
         for owner, unit in units:
             base = owner * ROWS
             some = (base <= last) & (base + ROWS - 1 >= low)
@@ -143,9 +149,8 @@
 
                     @pl.when((k_first <= last) & (k_first + TILE - 1 >= low))
                     def _():
-                        pos = first + lax.broadcasted_iota(jnp.int32, (TILE, TILE), 0)
                         key = k_first + lax.broadcasted_iota(jnp.int32, (TILE, TILE), 1)
-                        seen = (key <= pos) & (key >= start_of(ends, pos))
+                        seen = (key <= pos) & (key >= start)
                         w = silu_of_dot(q_ref[rows, :], unit[keys, :HD])
                         w = jnp.where(seen, w, 0.0).astype(jnp.bfloat16)
                         acc_ref[rows, :] += jnp.dot(
@@ -172,7 +177,9 @@
 
 def estimate(units):
     return pl.CostEstimate(
-        flops=4 * ROWS * ROWS * HD * units, bytes_accessed=1 << 20, transcendentals=ROWS * ROWS * units
+        flops=WEIGHT * 4 * ROWS * ROWS * HD * units,
+        bytes_accessed=1 << 20,
+        transcendentals=ROWS * ROWS * units,
     )
 
 
@@ -310,30 +317,32 @@
     def to_all(x):
         return lax.all_to_all(x, "head", 0, 0, tiled=True)
 
+    def step_on(last, step):
+        return [move(last[1 - stream], perm=stream_pairs(stream, step)) for stream in range(2)]
+
+    names = [((0, 0),)] + [((0, step), (1, step)) for step in range(1, 5)]
     blocks = pick(shards, slots, ingested)
     w_late, blocks = lax.optimization_barrier((w_out, blocks))
     arrived = lax.all_to_all(blocks, "batch", split_axis=0, concat_axis=0, tiled=True)
-    whole_w, arrived = lax.optimization_barrier((gather_w(w_late), arrived))
+    mine, theirs = gather_w(w_late)
+    mine, theirs, arrived = lax.optimization_barrier((mine, theirs, arrived))
     own, q, update = in_order(shards, arrived)
-    units = [(own,)]
-    last = [own, own]
-    for step in range(1, 5):
-        last = [move(last[1 - stream], perm=stream_pairs(stream, step)) for stream in range(2)]
-        units.append(tuple(last))
-    names = [((0, 0),)] + [((0, step), (1, step)) for step in range(1, 5)]
+    first = step_on([own, own], 1)
+    second = step_on(first, 2)
+    third = step_on(second, 3)
+    fourth = step_on(third, 4)
     lent_q = move(q, perm=LEND)
-    acc = attend(hist_len, q, units[0], names[0])
-    acc = attend(hist_len, q, units[1], names[1], acc)
-    lent = attend_lent(hist_len, lent_q, units[0] + units[1], names[0] + names[1])
-    acc = attend(hist_len, q, units[2], names[2], acc)
-    lent = attend_lent(
-        hist_len, lent_q, units[2] + units[3], names[2] + names[3], lent, final=True
-    )
+    acc = attend(hist_len, q, (own,), names[0])
+    acc = attend(hist_len, q, first, names[1], acc)
+    lent = attend_lent(hist_len, lent_q, (own, *first), names[0] + names[1])
+    acc = attend(hist_len, q, second, names[2], acc)
+    lent = attend_lent(hist_len, lent_q, second, names[2], lent)
+    lent = attend_lent(hist_len, lent_q, third, names[3], lent, final=True)
     lent = move(lent, perm=RETURN)
-    acc = attend(hist_len, q, units[3], names[3], acc)
-    gated = attend_last(hist_len, q, units[4], names[4], acc, lent, update)
+    acc = attend(hist_len, q, third, names[3], acc)
+    gated = attend_last(hist_len, q, fourth, names[4], acc, lent, update)
     rows = to_all(gated.reshape(HEADS, CHUNK, HD))
-    mixed = to_all(project(rows, *whole_w))
+    mixed = to_all(project(rows, mine, theirs))
     return mixed.reshape(1, ROWS, HD)
 
 

time: 135 us -> 134 us (level)
  the two profiles are of different devices: /device:TPU:32 before, /device:TPU:1 now
where the time goes in v6:
time: 134 us; the launch traced here: 133 us
  starting transfers between devices  67 us (50%)
  blocking collectives  26.7 us (20%)
  waiting for transfers between devices  22.4 us (17%)
  Pallas kernels  14.4 us (11%)
  local copies, waits for them, and re-layouts  1.77 us (1%)
    ppermute x8, starting transfers between devices, step_on(): move(last[1 - stream], perm=stream_pairs(stream, step))  31.6 us
    all_to_all x2, blocking collectives, to_all(): return lax.all_to_all(x, 'head', 0, 0, tiled=True)  26.7 us
    ppermute x8, waiting for transfers between devices, step_on(): move(last[1 - stream], perm=stream_pairs(stream, step))  11.9 us
    all_to_all x1, starting transfers between devices, body(): lax.all_to_all(blocks, 'batch', split_axis=0, concat_axis=0, tiled=True)  11.3 us
    ppermute x2, starting transfers between devices, gather_w(): even, odd = (cross(w, perm=X_EVEN), cross(w, perm=X_ODD))  6.43 us
    ppermute x1, starting transfers between devices, body(): lent = move(lent, perm=RETURN)  6.14 us
    pallas_call x4, Pallas kernels, attend(): pl.pallas_call(functools.partial(attend_kernel, names, first), out_shape=...  5.54 us
    ppermute x2, starting transfers between devices, gather_w(): far = [cross(odd[:half], perm=X_EVEN), cross(even[half:], perm=X_ODD)]  5.38 us
  transfers between devices with their start and end apart: 16, of which 8 were waited for; matrix products, arithmetic and copies ran while one was open for 0% of the time, Pallas kernels for 6%

profile of v6, /device:TPU:1, one launch (start us, length us, event | category | flops | bytes accessed | tf_op | source)
XLA Modules:
  0.0 132.6 jit_solution(17079435195289311073)
XLA Ops:
  0.0 3.7 %shard_map.55 = bf16[12,128,512]{2,1,0:T(8,128)(2,1)} custom-call(s32[4,6]{1,0:T(4,128)} %bitcast.6, s32[4,6]{1,0:T(4,128)} %bitcast.10, bf16[12,128,4,128]{3,2,1,0:T(4,128)(2,1)} %bitcast.8), custom_call_target="tpu_custom_call" | custom-call | tf_op jit(solution)/shard_map/pallas_call | solution.py:57
  3.8 11.3 %all-to-all-start = ((bf16[12,128,512]{2,1,0:T(8,128)(2,1)}), bf16[12,128,512]{2,1,0:T(8,128)(2,1)S(1)}, u32[]{:S(2)}, u32[]{:S(2)}) async-start(bf16[12,128,512]{2,1,0:T(8,128)(2,1)} %shard_map.55), calls=%async_computation | async-start | bytes 3145728 | tf_op jit(solution)/shard_map/all_to_all | solution.py:326
  15.0 4.5 %collective-permute-start.1 = (bf16[128,1024]{1,0:T(8,128)(2,1)S(1)}, bf16[128,1024]{1,0:T(8,128)(2,1)S(1)}, u32[]{:S(2)}, u32[]{:S(2)}) collective-permute-start(bf16[128,1024]{1,0:T(8,128)(2,1)S(1)} %copy-done.4), channel_id=1, source_target_pairs={{0,24},{4,28},{8,16},{12,20},{16,8},{20,12},{24,0},{28,4},{1,25},{... | collective-permute-start | bytes 786440 | tf_op jit(solution)/shard_map/ppermute | solution.py:307
  19.5 1.9 %collective-permute-start = (bf16[128,1024]{1,0:T(8,128)(2,1)S(1)}, bf16[128,1024]{1,0:T(8,128)(2,1)S(1)}, u32[]{:S(2)}, u32[]{:S(2)}) collective-permute-start(bf16[128,1024]{1,0:T(8,128)(2,1)S(1)} %copy-done.4), channel_id=1, source_target_pairs={{0,8},{4,12},{8,0},{12,4},{16,24},{20,28},{24,16},{28,20},{1,9},{5... | collective-permute-start | bytes 786440 | tf_op jit(solution)/shard_map/ppermute | solution.py:307
  21.5 3.6 %collective-permute-done.1 = bf16[128,1024]{1,0:T(8,128)(2,1)S(1)} collective-permute-done((bf16[128,1024]{1,0:T(8,128)(2,1)S(1)}, bf16[128,1024]{1,0:T(8,128)(2,1)S(1)}, u32[]{:S(2)}, u32[]{:S(2)}) %collective-permute-start.1) | collective-permute-done | bytes 262176 | tf_op jit(solution)/shard_map/ppermute | solution.py:307
  25.1 1.9 %collective-permute-start.2 = (bf16[64,1024]{1,0:T(8,128)(2,1)S(1)}, bf16[64,1024]{1,0:T(8,128)(2,1)S(1)}, u32[]{:S(2)}, u32[]{:S(2)}) collective-permute-start(bf16[64,1024]{1,0:T(8,128)(2,1)S(1)} %slice.8), channel_id=1, source_target_pairs={{0,8},{4,12},{8,0},{12,4},{16,24},{20,28},{24,16},{28,20},{1,9},{5... | collective-permute-start | bytes 393224 | tf_op jit(solution)/shard_map/ppermute | solution.py:308
  28.0 3.5 %collective-permute-start.3 = (bf16[64,1024]{1,0:T(8,128)(2,1)S(1)}, bf16[64,1024]{1,0:T(8,128)(2,1)S(1)}, u32[]{:S(2)}, u32[]{:S(2)}) collective-permute-start(bf16[64,1024]{1,0:T(8,128)(2,1)S(1)} %slice.9), channel_id=1, source_target_pairs={{0,24},{4,28},{8,16},{12,20},{16,8},{20,12},{24,0},{28,4},{1,25},{... | collective-permute-start | bytes 393224 | tf_op jit(solution)/shard_map/ppermute | solution.py:308
  31.6 3.7 %collective-permute-done.3 = bf16[64,1024]{1,0:T(8,128)(2,1)S(1)} collective-permute-done((bf16[64,1024]{1,0:T(8,128)(2,1)S(1)}, bf16[64,1024]{1,0:T(8,128)(2,1)S(1)}, u32[]{:S(2)}, u32[]{:S(2)}) %collective-permute-start.3) | collective-permute-done | bytes 131104 | tf_op jit(solution)/shard_map/ppermute | solution.py:308
  35.3 4.9 %collective-permute-start.4 = (bf16[512,1024]{1,0:T(8,128)(2,1)S(1)}, bf16[512,1024]{1,0:T(8,128)(2,1)S(1)}, u32[]{:S(2)}, u32[]{:S(2)}) collective-permute-start(bf16[512,1024]{1,0:T(8,128)(2,1)S(1)} %constant_dynamic-update-slice_fusion.mine_ref), channel_id=1, source_target_pairs={{0,4},{4,0},{8,12},{12,8},{16,20},{20,16},{24,28},{28,24},{1,5},{5... | collective-permute-start | bytes 3145736 | tf_op jit(solution)/shard_map/ppermute | solution.py:310
  40.2 2.3 %collective-permute-done.4.theirs_ref = bf16[512,1024]{1,0:T(8,128)(2,1)S(1)} collective-permute-done((bf16[512,1024]{1,0:T(8,128)(2,1)S(1)}, bf16[512,1024]{1,0:T(8,128)(2,1)S(1)}, u32[]{:S(2)}, u32[]{:S(2)}) %collective-permute-start.4) | collective-permute-done | bytes 1048608 | tf_op jit(solution)/shard_map/ppermute | solution.py:310
  44.1 2.9 %collective-permute-start.9 = (bf16[768,256]{1,0:T(8,128)(2,1)S(1)}, bf16[768,256]{1,0:T(8,128)(2,1)S(1)}, u32[]{:S(2)}, u32[]{:S(2)}) collective-permute-start(bf16[768,256]{1,0:T(8,128)(2,1)S(1)} %get-tuple-element.17.refs_0_), channel_id=1, source_target_pairs={{0,32},{64,96},{128,160},{192,224},{256,288},{320,352},{384,416},{... | collective-permute-start | bytes 1179656 | tf_op jit(solution)/shard_map/ppermute | solution.py:321
  47.1 5.4 %collective-permute-start.5 = (bf16[768,256]{1,0:T(8,128)(2,1)S(1)}, bf16[768,256]{1,0:T(8,128)(2,1)S(1)}, u32[]{:S(2)}, u32[]{:S(2)}) collective-permute-start(bf16[768,256]{1,0:T(8,128)(2,1)S(1)} %get-tuple-element.17.refs_0_), channel_id=1, source_target_pairs={{32,64},{96,128},{160,192},{224,256},{288,320},{352,384},{416,448}... | collective-permute-start | bytes 1179656 | tf_op jit(solution)/shard_map/ppermute | solution.py:321
  53.8 2.9 %shard_map.57.refs_2_ = f32[768,128]{1,0:T(8,128)S(1)} custom-call(s32[1,4]{1,0:T(1,128)S(1)} %copy-done.3, bf16[768,128]{1,0:T(8,128)(2,1)S(1)} %get-tuple-element.16.q_ref, bf16[768,256]{1,0:T(8,128)(2,1)S(1)} %get-tuple-element.17.refs_0_), custom_call_target="tpu_custom_call" | custom-call | flops 2415919104 | bytes 1048576 | tf_op jit(solution)/shard_map/pallas_call | solution.py:188
  56.7 12.6 %collective-permute-start.10 = (bf16[768,256]{1,0:T(8,128)(2,1)S(1)}, bf16[768,256]{1,0:T(8,128)(2,1)S(1)}, u32[]{:S(2)}, u32[]{:S(2)}) collective-permute-start(bf16[768,256]{1,0:T(8,128)(2,1)S(1)} %collective-permute-done.9.refs_0_.refs_1_), channel_id=1, source_target_pairs={{32,64},{96,128},{160,192},{224,256},{288,320},{352,384},{416,448}... | collective-permute-start | bytes 1179656 | tf_op jit(solution)/shard_map/ppermute | solution.py:321
  69.4 1.9 %collective-permute-start.6 = (bf16[768,256]{1,0:T(8,128)(2,1)S(1)}, bf16[768,256]{1,0:T(8,128)(2,1)S(1)}, u32[]{:S(2)}, u32[]{:S(2)}) collective-permute-start(bf16[768,256]{1,0:T(8,128)(2,1)S(1)} %collective-permute-done.5.refs_1_.refs_2_), channel_id=1, source_target_pairs={{0,32},{64,96},{128,160},{192,224},{256,288},{320,352},{384,416},{... | collective-permute-start | bytes 1179656 | tf_op jit(solution)/shard_map/ppermute | solution.py:321
  73.1 3.1 %collective-permute-done.10.refs_1_ = bf16[768,256]{1,0:T(8,128)(2,1)S(1)} collective-permute-done((bf16[768,256]{1,0:T(8,128)(2,1)S(1)}, bf16[768,256]{1,0:T(8,128)(2,1)S(1)}, u32[]{:S(2)}, u32[]{:S(2)}) %collective-permute-start.10) | collective-permute-done | bytes 393248 | tf_op jit(solution)/shard_map/ppermute | solution.py:321
  78.1 1.9 %collective-permute-done.6.refs_0_ = bf16[768,256]{1,0:T(8,128)(2,1)S(1)} collective-permute-done((bf16[768,256]{1,0:T(8,128)(2,1)S(1)}, bf16[768,256]{1,0:T(8,128)(2,1)S(1)}, u32[]{:S(2)}, u32[]{:S(2)}) %collective-permute-start.6) | collective-permute-done | bytes 393248 | tf_op jit(solution)/shard_map/ppermute | solution.py:321
  80.1 4.1 %collective-permute-start.7 = (bf16[768,256]{1,0:T(8,128)(2,1)S(1)}, bf16[768,256]{1,0:T(8,128)(2,1)S(1)}, u32[]{:S(2)}, u32[]{:S(2)}) collective-permute-start(bf16[768,256]{1,0:T(8,128)(2,1)S(1)} %collective-permute-done.6.refs_0_), channel_id=1, source_target_pairs={{32,64},{96,128},{160,192},{224,256},{288,320},{352,384},{416,448}... | collective-permute-start | bytes 1179656 | tf_op jit(solution)/shard_map/ppermute | solution.py:321
  86.2 3.1 %collective-permute-done.11.refs_0_ = bf16[768,256]{1,0:T(8,128)(2,1)S(1)} collective-permute-done((bf16[768,256]{1,0:T(8,128)(2,1)S(1)}, bf16[768,256]{1,0:T(8,128)(2,1)S(1)}, u32[]{:S(2)}, u32[]{:S(2)}) %collective-permute-start.11) | collective-permute-done | bytes 393248 | tf_op jit(solution)/shard_map/ppermute | solution.py:321
  90.2 6.1 %collective-permute-start.14 = (bf16[768,128]{1,0:T(8,128)(2,1)S(1)}, bf16[768,128]{1,0:T(8,128)(2,1)S(1)}, u32[]{:S(2)}, u32[]{:S(2)}) collective-permute-start(bf16[768,128]{1,0:T(8,128)(2,1)S(1)} %shard_map.63), channel_id=1, source_target_pairs={{0,256},{32,288},{64,320},{96,352},{128,384},{160,416},{192,448},{... | collective-permute-start | bytes 589832 | tf_op jit(solution)/shard_map/ppermute | solution.py:341
  97.0 2.0 %collective-permute-start.8 = (bf16[768,256]{1,0:T(8,128)(2,1)S(1)}, bf16[768,256]{1,0:T(8,128)(2,1)S(1)}, u32[]{:S(2)}, u32[]{:S(2)}) collective-permute-start(bf16[768,256]{1,0:T(8,128)(2,1)S(1)} %collective-permute-done.7.refs_1_), channel_id=1, source_target_pairs={{0,32},{64,96},{128,160},{192,224},{256,288},{320,352},{384,416},{... | collective-permute-start | bytes 1179656 | tf_op jit(solution)/shard_map/ppermute | solution.py:321
  99.9 3.8 %collective-permute-done.8.refs_0_ = bf16[768,256]{1,0:T(8,128)(2,1)S(1)} collective-permute-done((bf16[768,256]{1,0:T(8,128)(2,1)S(1)}, bf16[768,256]{1,0:T(8,128)(2,1)S(1)}, u32[]{:S(2)}, u32[]{:S(2)}) %collective-permute-start.8) | collective-permute-done | bytes 393248 | tf_op jit(solution)/shard_map/ppermute | solution.py:321
  104.7 17.5 %all_to_all.15.rows_ref = bf16[8,96,128]{2,1,0:T(8,128)(2,1)S(1)} all-to-all(bf16[8,96,128]{2,1,0:T(8,128)(2,1)S(1)} %bitcast.5), channel_id=1, replica_groups=mesh['ctx'=16,'head'=8,'batch'=4] {'head'}, dimensions={0} | all-to-all | bytes 393216 | tf_op jit(solution)/shard_map/all_to_all | solution.py:318
  122.7 9.2 %all_to_all.16 = bf16[8,96,128]{2,1,0:T(8,128)(2,1)S(1)} all-to-all(bf16[8,96,128]{2,1,0:T(8,128)(2,1)S(1)} %shard_map.65), channel_id=1, replica_groups=mesh['ctx'=16,'head'=8,'batch'=4] {'head'}, dimensions={0} | all-to-all | bytes 393216 | tf_op jit(solution)/shard_map/all_to_all | solution.py:318
  (39 shorter events, 14.4 us)
Async XLA Ops:
  3.8 11.3 %copy-start.4 = (bf16[128,1024]{1,0:T(8,128)(2,1)S(1)}, bf16[128,1024]{1,0:T(8,128)(2,1)}, u32[]{:S(2)}) copy-start(bf16[128,1024]{1,0:T(8,128)(2,1)} %param.9) | copy-start | bytes 786436
  3.8 39.7 %all-to-all-start = ((bf16[12,128,512]{2,1,0:T(8,128)(2,1)}), bf16[12,128,512]{2,1,0:T(8,128)(2,1)S(1)}, u32[]{:S(2)}, u32[]{:S(2)}) async-start(bf16[12,128,512]{2,1,0:T(8,128)(2,1)} %shard_map.55), calls=%async_computation | async-start | bytes 3145728 | tf_op jit(solution)/shard_map/all_to_all | solution.py:326
  15.0 28.4 %copy-start.2 = (s32[1,4,6]{2,1,0:T(4,128)S(1)}, s32[1,4,6]{2,1,0:T(4,128)}, u32[]{:S(2)}) copy-start(s32[1,4,6]{2,1,0:T(4,128)} %param.6) | copy-start | bytes 292
  15.0 10.1 %collective-permute-start.1 = (bf16[128,1024]{1,0:T(8,128)(2,1)S(1)}, bf16[128,1024]{1,0:T(8,128)(2,1)S(1)}, u32[]{:S(2)}, u32[]{:S(2)}) collective-permute-start(bf16[128,1024]{1,0:T(8,128)(2,1)S(1)} %copy-done.4), channel_id=1, source_target_pairs={{0,24},{4,28},{8,16},{12,20},{16,8},{20,12},{24,0},{28,4},{1,25},{... | collective-permute-start | bytes 786440 | tf_op jit(solution)/shard_map/ppermute | solution.py:307
  19.5 8.5 %collective-permute-start = (bf16[128,1024]{1,0:T(8,128)(2,1)S(1)}, bf16[128,1024]{1,0:T(8,128)(2,1)S(1)}, u32[]{:S(2)}, u32[]{:S(2)}) collective-permute-start(bf16[128,1024]{1,0:T(8,128)(2,1)S(1)} %copy-done.4), channel_id=1, source_target_pairs={{0,8},{4,12},{8,0},{12,4},{16,24},{20,28},{24,16},{28,20},{1,9},{5... | collective-permute-start | bytes 786440 | tf_op jit(solution)/shard_map/ppermute | solution.py:307
  25.1 6.4 %collective-permute-start.2 = (bf16[64,1024]{1,0:T(8,128)(2,1)S(1)}, bf16[64,1024]{1,0:T(8,128)(2,1)S(1)}, u32[]{:S(2)}, u32[]{:S(2)}) collective-permute-start(bf16[64,1024]{1,0:T(8,128)(2,1)S(1)} %slice.8), channel_id=1, source_target_pairs={{0,8},{4,12},{8,0},{12,4},{16,24},{20,28},{24,16},{28,20},{1,9},{5... | collective-permute-start | bytes 393224 | tf_op jit(solution)/shard_map/ppermute | solution.py:308
  28.0 25.8 %copy-start.3 = (s32[1,4]{1,0:T(1,128)S(1)}, s32[1,4]{1,0:T(1,128)}, u32[]{:S(2)}) copy-start(s32[1,4]{1,0:T(1,128)} %hist_ref.15) | copy-start | bytes 52
  28.0 7.2 %collective-permute-start.3 = (bf16[64,1024]{1,0:T(8,128)(2,1)S(1)}, bf16[64,1024]{1,0:T(8,128)(2,1)S(1)}, u32[]{:S(2)}, u32[]{:S(2)}) collective-permute-start(bf16[64,1024]{1,0:T(8,128)(2,1)S(1)} %slice.9), channel_id=1, source_target_pairs={{0,24},{4,28},{8,16},{12,20},{16,8},{20,12},{24,0},{28,4},{1,25},{... | collective-permute-start | bytes 393224 | tf_op jit(solution)/shard_map/ppermute | solution.py:308
  35.3 7.2 %collective-permute-start.4 = (bf16[512,1024]{1,0:T(8,128)(2,1)S(1)}, bf16[512,1024]{1,0:T(8,128)(2,1)S(1)}, u32[]{:S(2)}, u32[]{:S(2)}) collective-permute-start(bf16[512,1024]{1,0:T(8,128)(2,1)S(1)} %constant_dynamic-update-slice_fusion.mine_ref), channel_id=1, source_target_pairs={{0,4},{4,0},{8,12},{12,8},{16,20},{20,16},{24,28},{28,24},{1,5},{5... | collective-permute-start | bytes 3145736 | tf_op jit(solution)/shard_map/ppermute | solution.py:310
  42.5 1.0 copy-start
  44.1 12.6 %collective-permute-start.9 = (bf16[768,256]{1,0:T(8,128)(2,1)S(1)}, bf16[768,256]{1,0:T(8,128)(2,1)S(1)}, u32[]{:S(2)}, u32[]{:S(2)}) collective-permute-start(bf16[768,256]{1,0:T(8,128)(2,1)S(1)} %get-tuple-element.17.refs_0_), channel_id=1, source_target_pairs={{0,32},{64,96},{128,160},{192,224},{256,288},{320,352},{384,416},{... | collective-permute-start | bytes 1179656 | tf_op jit(solution)/shard_map/ppermute | solution.py:321
  47.1 22.3 %collective-permute-start.5 = (bf16[768,256]{1,0:T(8,128)(2,1)S(1)}, bf16[768,256]{1,0:T(8,128)(2,1)S(1)}, u32[]{:S(2)}, u32[]{:S(2)}) collective-permute-start(bf16[768,256]{1,0:T(8,128)(2,1)S(1)} %get-tuple-element.17.refs_0_), channel_id=1, source_target_pairs={{32,64},{96,128},{160,192},{224,256},{288,320},{352,384},{416,448}... | collective-permute-start | bytes 1179656 | tf_op jit(solution)/shard_map/ppermute | solution.py:321
  52.5 18.8 %collective-permute-start.13 = (bf16[768,128]{1,0:T(8,128)(2,1)S(1)}, bf16[768,128]{1,0:T(8,128)(2,1)S(1)}, u32[]{:S(2)}, u32[]{:S(2)}) collective-permute-start(bf16[768,128]{1,0:T(8,128)(2,1)S(1)} %get-tuple-element.16.q_ref), channel_id=1, source_target_pairs={{256,0},{288,32},{320,64},{352,96},{384,128},{416,160},{448,192},{... | collective-permute-start | bytes 589832 | tf_op jit(solution)/shard_map/ppermute | solution.py:334
  56.7 19.4 %collective-permute-start.10 = (bf16[768,256]{1,0:T(8,128)(2,1)S(1)}, bf16[768,256]{1,0:T(8,128)(2,1)S(1)}, u32[]{:S(2)}, u32[]{:S(2)}) collective-permute-start(bf16[768,256]{1,0:T(8,128)(2,1)S(1)} %collective-permute-done.9.refs_0_.refs_1_), channel_id=1, source_target_pairs={{32,64},{96,128},{160,192},{224,256},{288,320},{352,384},{416,448}... | collective-permute-start | bytes 1179656 | tf_op jit(solution)/shard_map/ppermute | solution.py:321
  69.4 10.7 %collective-permute-start.6 = (bf16[768,256]{1,0:T(8,128)(2,1)S(1)}, bf16[768,256]{1,0:T(8,128)(2,1)S(1)}, u32[]{:S(2)}, u32[]{:S(2)}) collective-permute-start(bf16[768,256]{1,0:T(8,128)(2,1)S(1)} %collective-permute-done.5.refs_1_.refs_2_), channel_id=1, source_target_pairs={{0,32},{64,96},{128,160},{192,224},{256,288},{320,352},{384,416},{... | collective-permute-start | bytes 1179656 | tf_op jit(solution)/shard_map/ppermute | solution.py:321
  76.2 13.1 %collective-permute-start.11 = (bf16[768,256]{1,0:T(8,128)(2,1)S(1)}, bf16[768,256]{1,0:T(8,128)(2,1)S(1)}, u32[]{:S(2)}, u32[]{:S(2)}) collective-permute-start(bf16[768,256]{1,0:T(8,128)(2,1)S(1)} %collective-permute-done.10.refs_1_), channel_id=1, source_target_pairs={{0,32},{64,96},{128,160},{192,224},{256,288},{320,352},{384,416},{... | collective-permute-start | bytes 1179656 | tf_op jit(solution)/shard_map/ppermute | solution.py:321
  80.1 9.2 %collective-permute-start.7 = (bf16[768,256]{1,0:T(8,128)(2,1)S(1)}, bf16[768,256]{1,0:T(8,128)(2,1)S(1)}, u32[]{:S(2)}, u32[]{:S(2)}) collective-permute-start(bf16[768,256]{1,0:T(8,128)(2,1)S(1)} %collective-permute-done.6.refs_0_), channel_id=1, source_target_pairs={{32,64},{96,128},{160,192},{224,256},{288,320},{352,384},{416,448}... | collective-permute-start | bytes 1179656 | tf_op jit(solution)/shard_map/ppermute | solution.py:321
  90.2 9.7 %collective-permute-start.14 = (bf16[768,128]{1,0:T(8,128)(2,1)S(1)}, bf16[768,128]{1,0:T(8,128)(2,1)S(1)}, u32[]{:S(2)}, u32[]{:S(2)}) collective-permute-start(bf16[768,128]{1,0:T(8,128)(2,1)S(1)} %shard_map.63), channel_id=1, source_target_pairs={{0,256},{32,288},{64,320},{96,352},{128,384},{160,416},{192,448},{... | collective-permute-start | bytes 589832 | tf_op jit(solution)/shard_map/ppermute | solution.py:341
  96.3 3.6 %collective-permute-start.12 = (bf16[768,256]{1,0:T(8,128)(2,1)S(1)}, bf16[768,256]{1,0:T(8,128)(2,1)S(1)}, u32[]{:S(2)}, u32[]{:S(2)}) collective-permute-start(bf16[768,256]{1,0:T(8,128)(2,1)S(1)} %collective-permute-done.11.refs_0_), channel_id=1, source_target_pairs={{32,64},{96,128},{160,192},{224,256},{288,320},{352,384},{416,448}... | collective-permute-start | bytes 1179656 | tf_op jit(solution)/shard_map/ppermute | solution.py:321
  97.0 6.6 %collective-permute-start.8 = (bf16[768,256]{1,0:T(8,128)(2,1)S(1)}, bf16[768,256]{1,0:T(8,128)(2,1)S(1)}, u32[]{:S(2)}, u32[]{:S(2)}) collective-permute-start(bf16[768,256]{1,0:T(8,128)(2,1)S(1)} %collective-permute-done.7.refs_1_), channel_id=1, source_target_pairs={{0,32},{64,96},{128,160},{192,224},{256,288},{320,352},{384,416},{... | collective-permute-start | bytes 1179656 | tf_op jit(solution)/shard_map/ppermute | solution.py:321
  103.7 18.5 %copy-start.1 = (bf16[512,1024]{1,0:T(8,128)(2,1)S(1)}, bf16[512,1024]{1,0:T(8,128)(2,1)}, u32[]{:S(2)}) copy-start(bf16[512,1024]{1,0:T(8,128)(2,1)} %copy-done) | copy-start | bytes 3145732

commit v7 on v6

--- a/solution.py
+++ b/solution.py
@@ -30,7 +30,8 @@
     return pltpu.CompilerParams(vmem_limit_bytes=mib * 1024 * 1024)
 
 
-def pick_kernel(shard_ref, slot_ref, ingest_ref, out_ref, buf, sems):
+def pick_kernel(shard_ref, slot_ref, ingest_ref, kvq_ref, *refs):
+    update_refs, buf, sems = refs[:GROUPS], refs[-2], refs[-1]
     me = lax.axis_index("batch")
     copies = []
     for g in range(GROUPS):
@@ -49,16 +50,21 @@
             copies.append(copy)
     for at, copy in enumerate(copies):
         copy.wait()
-        out_ref[at] = buf[at].reshape(BLOCK, 4 * HD)
+        kvq_ref[at] = buf[at].reshape(BLOCK, 4 * HD)[:, : 3 * HD]
+    for ahead, update_ref in enumerate(update_refs):
+        g = (me + ahead) % GROUPS
+        for r in range(CAPACITY):
+            update_ref[r] = buf[g * CAPACITY + r].reshape(BLOCK, 4 * HD)[:, 3 * HD :]
 
 
 def pick(shards, slots, ingested):
     count = GROUPS * CAPACITY
+    update = jax.ShapeDtypeStruct((CAPACITY, BLOCK, HD), jnp.bfloat16)
     return pl.pallas_call(
         pick_kernel,
-        out_shape=jax.ShapeDtypeStruct((count, BLOCK, 4 * HD), jnp.bfloat16),
+        out_shape=[jax.ShapeDtypeStruct((count, BLOCK, 3 * HD), jnp.bfloat16)] + [update] * GROUPS,
         in_specs=[SMEM, SMEM, ANY],
-        out_specs=VMEM,
+        out_specs=[VMEM] * (1 + GROUPS),
         scratch_shapes=[
             pltpu.VMEM((count, BLOCK, 4, HD), jnp.bfloat16),
             pltpu.SemaphoreType.DMA((count,)),
@@ -67,32 +73,37 @@
     )(shards, slots, ingested)
 
 
-def block_places(shard_ref):
+def block_sources(shard_ref):
     me = lax.axis_index("batch")
     shards = [shard_ref[me, k] for k in range(PER_OWNER)]
     for k in range(PER_OWNER):
         rank = jnp.int32(0)
         for earlier in range(k):
             rank = rank + (shards[earlier] == shards[k]).astype(jnp.int32)
-        yield slice(k * BLOCK, (k + 1) * BLOCK), shards[k] * CAPACITY + rank
-
-
-def order_kernel(shard_ref, in_ref, unit_ref, query_ref, update_ref):
-    for rows, at in block_places(shard_ref):
+        yield slice(k * BLOCK, (k + 1) * BLOCK), shards[k], rank
+
+
+def order_kernel(shard_ref, in_ref, *refs):
+    unit_ref, query_ref = refs[len(refs) // 2 - 1 : len(refs) // 2 + 1]
+    for rows, shard, rank in block_sources(shard_ref):
+        at = shard * CAPACITY + rank
         query_ref[rows, :] = in_ref[at, :, :HD]
-        unit_ref[rows, :] = in_ref[at, :, HD : 3 * HD]
-        update_ref[rows, :] = in_ref[at, :, 3 * HD :]
-
-
-def in_order(shards, blocks):
-    shape = jax.ShapeDtypeStruct((ROWS, HD), jnp.bfloat16)
+        unit_ref[rows, :] = in_ref[at, :, HD:]
+
+
+def in_order(shards, blocks, later):
     return pl.pallas_call(
         order_kernel,
-        out_shape=[jax.ShapeDtypeStruct((ROWS, 2 * HD), jnp.bfloat16), shape, shape],
-        in_specs=[SMEM, VMEM],
-        out_specs=[VMEM] * 3,
-        compiler_params=params(),
-    )(shards, blocks)
+        out_shape=[
+            jax.ShapeDtypeStruct((ROWS, 2 * HD), jnp.bfloat16),
+            jax.ShapeDtypeStruct((ROWS, HD), jnp.bfloat16),
+        ]
+        + [jax.ShapeDtypeStruct(x.shape, x.dtype) for x in later],
+        in_specs=[SMEM, VMEM] + [ANY] * len(later),
+        out_specs=[VMEM] * 2 + [ANY] * len(later),
+        input_output_aliases={2 + i: 2 + i for i in range(len(later))},
+        compiler_params=params(),
+    )(shards, blocks, *later)
 
 
 def unit_owner(stream, step):
@@ -227,9 +238,9 @@
     )(hist, q, *units, *(() if first else (acc,)))
 
 
-def last_kernel(names, hist_ref, q_ref, *refs):
+def last_kernel(names, hist_ref, shard_ref, q_ref, *refs):
     units = refs[: len(names)]
-    acc_in, lent_ref, update_ref, out_ref, acc_ref = refs[len(names) :]
+    acc_in, lent_ref, *update_refs, out_ref, acc_ref = refs[len(names) :]
     me = lax.axis_index("ctx")
     acc_ref[...] = acc_in[...]
 
@@ -240,22 +251,28 @@
     ends = history_ends(hist_ref)
     owners = [unit_owner(*name) for name in names]
     add_units(ends, me * ROWS, q_ref, list(zip(owners, units)), acc_ref)
-    a = acc_ref[...]
-    mean = jnp.mean(a * a, axis=-1, keepdims=True)
-    normed = a * lax.rsqrt(mean + 1e-6)
-    out_ref[...] = (normed * update_ref[...].astype(jnp.float32)).astype(jnp.bfloat16)
-
-
-def attend_last(hist, q, units, names, acc, lent, update):
+    group = lax.axis_index("batch")
+    for rows, shard, rank in block_sources(shard_ref):
+        a = acc_ref[rows, :]
+        mean = jnp.mean(a * a, axis=-1, keepdims=True)
+        normed = a * lax.rsqrt(mean + 1e-6)
+        behind = (group + GROUPS - shard) % GROUPS
+        update = update_refs[0][rank]
+        for d in range(1, GROUPS):
+            update = jnp.where(behind == d, update_refs[d][rank], update)
+        out_ref[rows, :] = (normed * update.astype(jnp.float32)).astype(jnp.bfloat16)
+
+
+def attend_last(hist, shards, q, units, names, acc, lent, updates):
     return pl.pallas_call(
         functools.partial(last_kernel, names),
         out_shape=jax.ShapeDtypeStruct((ROWS, HD), jnp.bfloat16),
-        in_specs=[SMEM] + [VMEM] * (4 + len(units)),
+        in_specs=[SMEM, SMEM] + [VMEM] * (3 + len(units) + len(updates)),
         out_specs=VMEM,
         scratch_shapes=[pltpu.VMEM((ROWS, HD), jnp.float32)],
         cost_estimate=estimate(len(units)),
         compiler_params=params(),
-    )(hist, q, *units, acc, lent, update)
+    )(hist, shards, q, *units, acc, lent, *updates)
 
 
 def near_heads(head):
@@ -321,12 +338,15 @@
         return [move(last[1 - stream], perm=stream_pairs(stream, step)) for stream in range(2)]
 
     names = [((0, 0),)] + [((0, step), (1, step)) for step in range(1, 5)]
-    blocks = pick(shards, slots, ingested)
+    blocks, *updates = pick(shards, slots, ingested)
     w_late, blocks = lax.optimization_barrier((w_out, blocks))
     arrived = lax.all_to_all(blocks, "batch", split_axis=0, concat_axis=0, tiled=True)
     mine, theirs = gather_w(w_late)
-    mine, theirs, arrived = lax.optimization_barrier((mine, theirs, arrived))
-    own, q, update = in_order(shards, arrived)
+    mine, arrived = lax.optimization_barrier((mine, arrived))
+    own, q, *sent = in_order(shards, arrived, updates[1:])
+    for ahead in range(1, GROUPS):
+        pairs = [(i, (i + ahead) % GROUPS) for i in range(GROUPS)]
+        updates[ahead] = lax.ppermute(sent[ahead - 1], "batch", pairs)
     first = step_on([own, own], 1)
     second = step_on(first, 2)
     third = step_on(second, 3)
@@ -340,7 +360,7 @@
     lent = attend_lent(hist_len, lent_q, third, names[3], lent, final=True)
     lent = move(lent, perm=RETURN)
     acc = attend(hist_len, q, third, names[3], acc)
-    gated = attend_last(hist_len, q, fourth, names[4], acc, lent, update)
+    gated = attend_last(hist_len, shards, q, fourth, names[4], acc, lent, updates)
     rows = to_all(gated.reshape(HEADS, CHUNK, HD))
     mixed = to_all(project(rows, mine, theirs))
     return mixed.reshape(1, ROWS, HD)

time: 134 us -> 142 us (1.060)
  starting transfers between devices: 67 us -> 84.7 us
  blocking collectives: 26.7 us -> 9.24 us
  waiting for transfers between devices: 22.4 us -> 30.2 us
    ppermute x0 -> x3, starting transfers between devices: none -> 17.8 us  [body(): updates[ahead] = lax.ppermute(sent[ahead - 1], 'batch', pairs)]
    all_to_all x2 -> x1, blocking collectives: 26.7 us -> 9.24 us  [to_all(): return lax.all_to_all(x, 'head', 0, 0, tiled=True)]
    all_to_all x0 -> x1, starting transfers between devices: none -> 10.3 us  [to_all(): return lax.all_to_all(x, 'head', 0, 0, tiled=True)]
    ppermute x8, starting transfers between devices: 31.6 us -> 24.9 us  [step_on(): move(last[1 - stream], perm=stream_pairs(stream, step))]
    all_to_all x0 -> x1, waiting for transfers between devices: none -> 5.89 us  [to_all(): return lax.all_to_all(x, 'head', 0, 0, tiled=True)]
    ppermute x1, waiting for transfers between devices: 0.01 us -> 3.89 us  [body(): lent_q = move(q, perm=LEND)]
    ppermute x1, starting transfers between devices: 6.14 us -> 3.56 us  [body(): lent = move(lent, perm=RETURN)]
    ppermute x1, waiting for transfers between devices: 2.26 us -> 0.01 us  [gather_w(): return (mine, cross(mine, perm=CORE))]
  transfers between devices with their start and end apart: 16 -> 20, of which waited for: 8 -> 10; matrix products, arithmetic and copies ran while one was open for 0% -> 0% of each run, Pallas kernels for 6% -> 7%
where the time goes in v7:
time: 142 us; the launch traced here: 141 us
  starting transfers between devices  84.7 us (60%)
  waiting for transfers between devices  30.2 us (21%)
  Pallas kernels  15.7 us (11%)
  blocking collectives  9.24 us (7%)
    ppermute x8, starting transfers between devices, step_on(): move(last[1 - stream], perm=stream_pairs(stream, step))  24.9 us
    ppermute x3, starting transfers between devices, body(): updates[ahead] = lax.ppermute(sent[ahead - 1], 'batch', pairs)  17.8 us
    ppermute x8, waiting for transfers between devices, step_on(): move(last[1 - stream], perm=stream_pairs(stream, step))  11.8 us
    all_to_all x1, starting transfers between devices, body(): lax.all_to_all(blocks, 'batch', split_axis=0, concat_axis=0, tiled=True)  10.7 us
    all_to_all x1, starting transfers between devices, to_all(): return lax.all_to_all(x, 'head', 0, 0, tiled=True)  10.3 us
    all_to_all x1, blocking collectives, to_all(): return lax.all_to_all(x, 'head', 0, 0, tiled=True)  9.24 us
    ppermute x2, starting transfers between devices, gather_w(): even, odd = (cross(w, perm=X_EVEN), cross(w, perm=X_ODD))  6.3 us
    all_to_all x1, waiting for transfers between devices, to_all(): return lax.all_to_all(x, 'head', 0, 0, tiled=True)  5.89 us
  transfers between devices with their start and end apart: 20, of which 10 were waited for; matrix products, arithmetic and copies ran while one was open for 0% of the time, Pallas kernels for 7%

profile of v7, /device:TPU:1, one launch (start us, length us, event | category | flops | bytes accessed | tf_op | source)
XLA Modules:
  0.0 141.1 jit_solution(16981577956408076779)
XLA Ops:
  0.0 4.3 %shard_map.55 = (bf16[12,128,384]{2,1,0:T(8,128)(2,1)}, bf16[3,128,128]{2,1,0:T(8,128)(2,1)}, bf16[3,128,128]{2,1,0:T(8,128)(2,1)}, bf16[3,128,128]{2,1,0:T(8,128)(2,1)}, bf16[3,128,128]{2,1,0:T(8,128)(2,1)}) custom-call(s32[4,6]{1,0:T(4,128)} %bitcast.5, s32[4,6]{1,0:T(4,128)} %bitcast.10, bf16[12,128,4,128]{3,2,1,0:T(4,128)(2,1)} %bitcast.8), custom_call_target="tpu_custom_call" | custom-call | tf_op jit(solution)/shard_map/pallas_call | solution.py:63
  4.3 10.7 %all-to-all-start = ((bf16[12,128,384]{2,1,0:T(8,128)(2,1)}), bf16[12,128,384]{2,1,0:T(8,128)(2,1)S(1)}, u32[]{:S(2)}, u32[]{:S(2)}) async-start(bf16[12,128,384]{2,1,0:T(8,128)(2,1)} %get-tuple-element.21), calls=%async_computation | async-start | bytes 2359296 | tf_op jit(solution)/shard_map/all_to_all | solution.py:343
  15.1 4.4 %collective-permute-start.1 = (bf16[128,1024]{1,0:T(8,128)(2,1)S(1)}, bf16[128,1024]{1,0:T(8,128)(2,1)S(1)}, u32[]{:S(2)}, u32[]{:S(2)}) collective-permute-start(bf16[128,1024]{1,0:T(8,128)(2,1)S(1)} %copy-done.6), channel_id=1, source_target_pairs={{0,24},{4,28},{8,16},{12,20},{16,8},{20,12},{24,0},{28,4},{1,25},{... | collective-permute-start | bytes 786440 | tf_op jit(solution)/shard_map/ppermute | solution.py:324
  21.4 3.6 %collective-permute-done.1 = bf16[128,1024]{1,0:T(8,128)(2,1)S(1)} collective-permute-done((bf16[128,1024]{1,0:T(8,128)(2,1)S(1)}, bf16[128,1024]{1,0:T(8,128)(2,1)S(1)}, u32[]{:S(2)}, u32[]{:S(2)}) %collective-permute-start.1) | collective-permute-done | bytes 262176 | tf_op jit(solution)/shard_map/ppermute | solution.py:324
  27.9 3.5 %collective-permute-start.3 = (bf16[64,1024]{1,0:T(8,128)(2,1)S(1)}, bf16[64,1024]{1,0:T(8,128)(2,1)S(1)}, u32[]{:S(2)}, u32[]{:S(2)}) collective-permute-start(bf16[64,1024]{1,0:T(8,128)(2,1)S(1)} %slice.9), channel_id=1, source_target_pairs={{0,24},{4,28},{8,16},{12,20},{16,8},{20,12},{24,0},{28,4},{1,25},{... | collective-permute-start | bytes 393224 | tf_op jit(solution)/shard_map/ppermute | solution.py:325
  31.5 3.7 %collective-permute-done.3 = bf16[64,1024]{1,0:T(8,128)(2,1)S(1)} collective-permute-done((bf16[64,1024]{1,0:T(8,128)(2,1)S(1)}, bf16[64,1024]{1,0:T(8,128)(2,1)S(1)}, u32[]{:S(2)}, u32[]{:S(2)}) %collective-permute-start.3) | collective-permute-done | bytes 131104 | tf_op jit(solution)/shard_map/ppermute | solution.py:325
  36.3 3.6 %collective-permute-start.8 = (bf16[768,256]{1,0:T(8,128)(2,1)S(1)}, bf16[768,256]{1,0:T(8,128)(2,1)S(1)}, u32[]{:S(2)}, u32[]{:S(2)}) collective-permute-start(bf16[768,256]{1,0:T(8,128)(2,1)S(1)} %get-tuple-element.27.refs_0_), channel_id=1, source_target_pairs={{0,32},{64,96},{128,160},{192,224},{256,288},{320,352},{384,416},{... | collective-permute-start | bytes 1179656 | tf_op jit(solution)/shard_map/ppermute | solution.py:338
  39.9 6.3 %collective-permute-start.4 = (bf16[768,256]{1,0:T(8,128)(2,1)S(1)}, bf16[768,256]{1,0:T(8,128)(2,1)S(1)}, u32[]{:S(2)}, u32[]{:S(2)}) collective-permute-start(bf16[768,256]{1,0:T(8,128)(2,1)S(1)} %get-tuple-element.27.refs_0_), channel_id=1, source_target_pairs={{32,64},{96,128},{160,192},{224,256},{288,320},{352,384},{416,448}... | collective-permute-start | bytes 1179656 | tf_op jit(solution)/shard_map/ppermute | solution.py:338
  46.2 4.5 %collective-permute-start.17 = (bf16[512,1024]{1,0:T(8,128)(2,1)S(1)}, bf16[512,1024]{1,0:T(8,128)(2,1)S(1)}, u32[]{:S(2)}, u32[]{:S(2)}) collective-permute-start(bf16[512,1024]{1,0:T(8,128)(2,1)S(1)} %constant_dynamic-update-slice_fusion.mine_ref), channel_id=1, source_target_pairs={{0,4},{4,0},{8,12},{12,8},{16,20},{20,16},{24,28},{28,24},{1,5},{5... | collective-permute-start | bytes 3145736 | tf_op jit(solution)/shard_map/ppermute | solution.py:327
  50.7 10.7 %collective-permute-start.14 = (bf16[3,128,128]{2,1,0:T(8,128)(2,1)S(1)}, bf16[3,128,128]{2,1,0:T(8,128)(2,1)S(1)}, u32[]{:S(2)}, u32[]{:S(2)}) collective-permute-start(bf16[3,128,128]{2,1,0:T(8,128)(2,1)S(1)} %get-tuple-element.29), channel_id=1, source_target_pairs={{0,1},{1,2},{2,3},{3,0},{4,5},{5,6},{6,7},{7,4},{8,9},{9,10},{10,1... | collective-permute-start | bytes 294920 | tf_op jit(solution)/shard_map/ppermute | solution.py:349
  62.7 2.9 %shard_map.57.refs_2_ = f32[768,128]{1,0:T(8,128)S(1)} custom-call(s32[1,4]{1,0:T(1,128)S(1)} %copy-done.5, bf16[768,128]{1,0:T(8,128)(2,1)S(1)} %get-tuple-element.26.q_ref, bf16[768,256]{1,0:T(8,128)(2,1)S(1)} %get-tuple-element.27.refs_0_), custom_call_target="tpu_custom_call" | custom-call | flops 2415919104 | bytes 1048576 | tf_op jit(solution)/shard_map/pallas_call | solution.py:199
  65.6 3.9 %collective-permute-done.12.q_ref = bf16[768,128]{1,0:T(8,128)(2,1)S(1)} collective-permute-done((bf16[768,128]{1,0:T(8,128)(2,1)S(1)}, bf16[768,128]{1,0:T(8,128)(2,1)S(1)}, u32[]{:S(2)}, u32[]{:S(2)}) %collective-permute-start.12) | collective-permute-done | bytes 196640 | tf_op jit(solution)/shard_map/ppermute | solution.py:354
  69.5 3.7 %collective-permute-start.15 = (bf16[3,128,128]{2,1,0:T(8,128)(2,1)S(1)}, bf16[3,128,128]{2,1,0:T(8,128)(2,1)S(1)}, u32[]{:S(2)}, u32[]{:S(2)}) collective-permute-start(bf16[3,128,128]{2,1,0:T(8,128)(2,1)S(1)} %get-tuple-element.30), channel_id=1, source_target_pairs={{0,2},{1,3},{2,0},{3,1},{4,6},{5,7},{6,4},{7,5},{8,10},{9,11},{10,... | collective-permute-start | bytes 294920 | tf_op jit(solution)/shard_map/ppermute | solution.py:349
  79.6 3.2 %collective-permute-done.9.refs_1_ = bf16[768,256]{1,0:T(8,128)(2,1)S(1)} collective-permute-done((bf16[768,256]{1,0:T(8,128)(2,1)S(1)}, bf16[768,256]{1,0:T(8,128)(2,1)S(1)}, u32[]{:S(2)}, u32[]{:S(2)}) %collective-permute-start.9) | collective-permute-done | bytes 393248 | tf_op jit(solution)/shard_map/ppermute | solution.py:338
  82.8 3.2 %collective-permute-start.10 = (bf16[768,256]{1,0:T(8,128)(2,1)S(1)}, bf16[768,256]{1,0:T(8,128)(2,1)S(1)}, u32[]{:S(2)}, u32[]{:S(2)}) collective-permute-start(bf16[768,256]{1,0:T(8,128)(2,1)S(1)} %collective-permute-done.9.refs_1_), channel_id=1, source_target_pairs={{0,32},{64,96},{128,160},{192,224},{256,288},{320,352},{384,416},{... | collective-permute-start | bytes 1179656 | tf_op jit(solution)/shard_map/ppermute | solution.py:338
  86.7 3.5 %collective-permute-start.6 = (bf16[768,256]{1,0:T(8,128)(2,1)S(1)}, bf16[768,256]{1,0:T(8,128)(2,1)S(1)}, u32[]{:S(2)}, u32[]{:S(2)}) collective-permute-start(bf16[768,256]{1,0:T(8,128)(2,1)S(1)} %collective-permute-done.5.refs_0_), channel_id=1, source_target_pairs={{32,64},{96,128},{160,192},{224,256},{288,320},{352,384},{416,448}... | collective-permute-start | bytes 1179656 | tf_op jit(solution)/shard_map/ppermute | solution.py:338
  92.2 3.7 %collective-permute-done.10.refs_0_ = bf16[768,256]{1,0:T(8,128)(2,1)S(1)} collective-permute-done((bf16[768,256]{1,0:T(8,128)(2,1)S(1)}, bf16[768,256]{1,0:T(8,128)(2,1)S(1)}, u32[]{:S(2)}, u32[]{:S(2)}) %collective-permute-start.10) | collective-permute-done | bytes 393248 | tf_op jit(solution)/shard_map/ppermute | solution.py:338
  95.9 3.4 %collective-permute-start.16 = (bf16[3,128,128]{2,1,0:T(8,128)(2,1)S(1)}, bf16[3,128,128]{2,1,0:T(8,128)(2,1)S(1)}, u32[]{:S(2)}, u32[]{:S(2)}) collective-permute-start(bf16[3,128,128]{2,1,0:T(8,128)(2,1)S(1)} %get-tuple-element.31), channel_id=1, source_target_pairs={{0,3},{1,0},{2,1},{3,2},{4,7},{5,4},{6,5},{7,6},{8,11},{9,8},{10,9... | collective-permute-start | bytes 294920 | tf_op jit(solution)/shard_map/ppermute | solution.py:349
  100.3 3.6 %collective-permute-start.13 = (bf16[768,128]{1,0:T(8,128)(2,1)S(1)}, bf16[768,128]{1,0:T(8,128)(2,1)S(1)}, u32[]{:S(2)}, u32[]{:S(2)}) collective-permute-start(bf16[768,128]{1,0:T(8,128)(2,1)S(1)} %shard_map.63), channel_id=1, source_target_pairs={{0,256},{32,288},{64,320},{96,352},{128,384},{160,416},{192,448},{... | collective-permute-start | bytes 589832 | tf_op jit(solution)/shard_map/ppermute | solution.py:361
  104.6 3.0 %collective-permute-start.7 = (bf16[768,256]{1,0:T(8,128)(2,1)S(1)}, bf16[768,256]{1,0:T(8,128)(2,1)S(1)}, u32[]{:S(2)}, u32[]{:S(2)}) collective-permute-start(bf16[768,256]{1,0:T(8,128)(2,1)S(1)} %collective-permute-done.6.refs_1_), channel_id=1, source_target_pairs={{0,32},{64,96},{128,160},{192,224},{256,288},{320,352},{384,416},{... | collective-permute-start | bytes 1179656 | tf_op jit(solution)/shard_map/ppermute | solution.py:338
  108.5 4.2 %collective-permute-done.7.refs_0_ = bf16[768,256]{1,0:T(8,128)(2,1)S(1)} collective-permute-done((bf16[768,256]{1,0:T(8,128)(2,1)S(1)}, bf16[768,256]{1,0:T(8,128)(2,1)S(1)}, u32[]{:S(2)}, u32[]{:S(2)}) %collective-permute-start.7) | collective-permute-done | bytes 393248 | tf_op jit(solution)/shard_map/ppermute | solution.py:338
  114.5 10.3 %all-to-all-start.1 = ((bf16[8,96,128]{2,1,0:T(8,128)(2,1)}), bf16[8,96,128]{2,1,0:T(8,128)(2,1)S(1)}, u32[]{:S(2)}, u32[]{:S(2)}) async-start(bf16[8,96,128]{2,1,0:T(8,128)(2,1)} %bitcast.3), calls=%async_computation.1 | async-start | bytes 393216 | tf_op jit(solution)/shard_map/all_to_all | solution.py:335
  124.8 5.9 %all-to-all-done.1.rows_ref = bf16[8,96,128]{2,1,0:T(8,128)(2,1)S(1)} async-done(((bf16[8,96,128]{2,1,0:T(8,128)(2,1)}), bf16[8,96,128]{2,1,0:T(8,128)(2,1)S(1)}, u32[]{:S(2)}, u32[]{:S(2)}) %all-to-all-start.1) | async-done | bytes 196640 | tf_op jit(solution)/shard_map/all_to_all | solution.py:335
  131.2 9.2 %all_to_all.15 = bf16[8,96,128]{2,1,0:T(8,128)(2,1)S(1)} all-to-all(bf16[8,96,128]{2,1,0:T(8,128)(2,1)S(1)} %shard_map.65), channel_id=1, replica_groups=mesh['ctx'=16,'head'=8,'batch'=4] {'head'}, dimensions={0} | all-to-all | bytes 393216 | tf_op jit(solution)/shard_map/all_to_all | solution.py:335
  (50 shorter events, 21.7 us)
Async XLA Ops:
  4.3 31.3 %all-to-all-start = ((bf16[12,128,384]{2,1,0:T(8,128)(2,1)}), bf16[12,128,384]{2,1,0:T(8,128)(2,1)S(1)}, u32[]{:S(2)}, u32[]{:S(2)}) async-start(bf16[12,128,384]{2,1,0:T(8,128)(2,1)} %get-tuple-element.21), calls=%async_computation | async-start | bytes 2359296 | tf_op jit(solution)/shard_map/all_to_all | solution.py:343
  15.1 9.9 %collective-permute-start.1 = (bf16[128,1024]{1,0:T(8,128)(2,1)S(1)}, bf16[128,1024]{1,0:T(8,128)(2,1)S(1)}, u32[]{:S(2)}, u32[]{:S(2)}) collective-permute-start(bf16[128,1024]{1,0:T(8,128)(2,1)S(1)} %copy-done.6), channel_id=1, source_target_pairs={{0,24},{4,28},{8,16},{12,20},{16,8},{20,12},{24,0},{28,4},{1,25},{... | collective-permute-start | bytes 786440 | tf_op jit(solution)/shard_map/ppermute | solution.py:324
  19.4 8.5 %collective-permute-start = (bf16[128,1024]{1,0:T(8,128)(2,1)S(1)}, bf16[128,1024]{1,0:T(8,128)(2,1)S(1)}, u32[]{:S(2)}, u32[]{:S(2)}) collective-permute-start(bf16[128,1024]{1,0:T(8,128)(2,1)S(1)} %copy-done.6), channel_id=1, source_target_pairs={{0,8},{4,12},{8,0},{12,4},{16,24},{20,28},{24,16},{28,20},{1,9},{5... | collective-permute-start | bytes 786440 | tf_op jit(solution)/shard_map/ppermute | solution.py:324
  21.4 14.2 %copy-start = (bf16[3,128,128]{2,1,0:T(8,128)(2,1)S(1)}, bf16[3,128,128]{2,1,0:T(8,128)(2,1)}, u32[]{:S(2)}) copy-start(bf16[3,128,128]{2,1,0:T(8,128)(2,1)} %get-tuple-element.23.refs_0_) | copy-start | bytes 294916
  21.4 14.2 %copy-start.1 = (bf16[3,128,128]{2,1,0:T(8,128)(2,1)S(1)}, bf16[3,128,128]{2,1,0:T(8,128)(2,1)}, u32[]{:S(2)}) copy-start(bf16[3,128,128]{2,1,0:T(8,128)(2,1)} %get-tuple-element.24.refs_1_) | copy-start | bytes 294916
  21.4 14.2 %copy-start.2 = (bf16[3,128,128]{2,1,0:T(8,128)(2,1)S(1)}, bf16[3,128,128]{2,1,0:T(8,128)(2,1)}, u32[]{:S(2)}) copy-start(bf16[3,128,128]{2,1,0:T(8,128)(2,1)} %get-tuple-element.25.refs_2_) | copy-start | bytes 294916
  25.0 6.4 %collective-permute-start.2 = (bf16[64,1024]{1,0:T(8,128)(2,1)S(1)}, bf16[64,1024]{1,0:T(8,128)(2,1)S(1)}, u32[]{:S(2)}, u32[]{:S(2)}) collective-permute-start(bf16[64,1024]{1,0:T(8,128)(2,1)S(1)} %slice.8), channel_id=1, source_target_pairs={{0,8},{4,12},{8,0},{12,4},{16,24},{20,28},{24,16},{28,20},{1,9},{5... | collective-permute-start | bytes 393224 | tf_op jit(solution)/shard_map/ppermute | solution.py:325
  27.9 7.2 %collective-permute-start.3 = (bf16[64,1024]{1,0:T(8,128)(2,1)S(1)}, bf16[64,1024]{1,0:T(8,128)(2,1)S(1)}, u32[]{:S(2)}, u32[]{:S(2)}) collective-permute-start(bf16[64,1024]{1,0:T(8,128)(2,1)S(1)} %slice.9), channel_id=1, source_target_pairs={{0,24},{4,28},{8,16},{12,20},{16,8},{20,12},{24,0},{28,4},{1,25},{... | collective-permute-start | bytes 393224 | tf_op jit(solution)/shard_map/ppermute | solution.py:325
  31.4 31.3 %copy-start.5 = (s32[1,4]{1,0:T(1,128)S(1)}, s32[1,4]{1,0:T(1,128)}, u32[]{:S(2)}) copy-start(s32[1,4]{1,0:T(1,128)} %hist_ref.15) | copy-start | bytes 52
  36.3 36.9 %collective-permute-start.8 = (bf16[768,256]{1,0:T(8,128)(2,1)S(1)}, bf16[768,256]{1,0:T(8,128)(2,1)S(1)}, u32[]{:S(2)}, u32[]{:S(2)}) collective-permute-start(bf16[768,256]{1,0:T(8,128)(2,1)S(1)} %get-tuple-element.27.refs_0_), channel_id=1, source_target_pairs={{0,32},{64,96},{128,160},{192,224},{256,288},{320,352},{384,416},{... | collective-permute-start | bytes 1179656 | tf_op jit(solution)/shard_map/ppermute | solution.py:338
  39.9 36.0 %collective-permute-start.4 = (bf16[768,256]{1,0:T(8,128)(2,1)S(1)}, bf16[768,256]{1,0:T(8,128)(2,1)S(1)}, u32[]{:S(2)}, u32[]{:S(2)}) collective-permute-start(bf16[768,256]{1,0:T(8,128)(2,1)S(1)} %get-tuple-element.27.refs_0_), channel_id=1, source_target_pairs={{32,64},{96,128},{160,192},{224,256},{288,320},{352,384},{416,448}... | collective-permute-start | bytes 1179656 | tf_op jit(solution)/shard_map/ppermute | solution.py:338
  46.2 78.6 %collective-permute-start.17 = (bf16[512,1024]{1,0:T(8,128)(2,1)S(1)}, bf16[512,1024]{1,0:T(8,128)(2,1)S(1)}, u32[]{:S(2)}, u32[]{:S(2)}) collective-permute-start(bf16[512,1024]{1,0:T(8,128)(2,1)S(1)} %constant_dynamic-update-slice_fusion.mine_ref), channel_id=1, source_target_pairs={{0,4},{4,0},{8,12},{12,8},{16,20},{20,16},{24,28},{28,24},{1,5},{5... | collective-permute-start | bytes 3145736 | tf_op jit(solution)/shard_map/ppermute | solution.py:327
  50.7 53.1 %collective-permute-start.14 = (bf16[3,128,128]{2,1,0:T(8,128)(2,1)S(1)}, bf16[3,128,128]{2,1,0:T(8,128)(2,1)S(1)}, u32[]{:S(2)}, u32[]{:S(2)}) collective-permute-start(bf16[3,128,128]{2,1,0:T(8,128)(2,1)S(1)} %get-tuple-element.29), channel_id=1, source_target_pairs={{0,1},{1,2},{2,3},{3,0},{4,5},{5,6},{6,7},{7,4},{8,9},{9,10},{10,1... | collective-permute-start | bytes 294920 | tf_op jit(solution)/shard_map/ppermute | solution.py:349
  61.4 8.1 %collective-permute-start.12 = (bf16[768,128]{1,0:T(8,128)(2,1)S(1)}, bf16[768,128]{1,0:T(8,128)(2,1)S(1)}, u32[]{:S(2)}, u32[]{:S(2)}) collective-permute-start(bf16[768,128]{1,0:T(8,128)(2,1)S(1)} %get-tuple-element.26.q_ref), channel_id=1, source_target_pairs={{256,0},{288,32},{320,64},{352,96},{384,128},{416,160},{448,192},{... | collective-permute-start | bytes 589832 | tf_op jit(solution)/shard_map/ppermute | solution.py:354
  69.5 35.1 %collective-permute-start.15 = (bf16[3,128,128]{2,1,0:T(8,128)(2,1)S(1)}, bf16[3,128,128]{2,1,0:T(8,128)(2,1)S(1)}, u32[]{:S(2)}, u32[]{:S(2)}) collective-permute-start(bf16[3,128,128]{2,1,0:T(8,128)(2,1)S(1)} %get-tuple-element.30), channel_id=1, source_target_pairs={{0,2},{1,3},{2,0},{3,1},{4,6},{5,7},{6,4},{7,5},{8,10},{9,11},{10,... | collective-permute-start | bytes 294920 | tf_op jit(solution)/shard_map/ppermute | solution.py:349
  73.2 9.6 %collective-permute-start.9 = (bf16[768,256]{1,0:T(8,128)(2,1)S(1)}, bf16[768,256]{1,0:T(8,128)(2,1)S(1)}, u32[]{:S(2)}, u32[]{:S(2)}) collective-permute-start(bf16[768,256]{1,0:T(8,128)(2,1)S(1)} %collective-permute-done.8.refs_0_.refs_1_), channel_id=1, source_target_pairs={{32,64},{96,128},{160,192},{224,256},{288,320},{352,384},{416,448}... | collective-permute-start | bytes 1179656 | tf_op jit(solution)/shard_map/ppermute | solution.py:338
  75.9 10.8 %collective-permute-start.5 = (bf16[768,256]{1,0:T(8,128)(2,1)S(1)}, bf16[768,256]{1,0:T(8,128)(2,1)S(1)}, u32[]{:S(2)}, u32[]{:S(2)}) collective-permute-start(bf16[768,256]{1,0:T(8,128)(2,1)S(1)} %collective-permute-done.4.refs_1_.refs_2_), channel_id=1, source_target_pairs={{0,32},{64,96},{128,160},{192,224},{256,288},{320,352},{384,416},{... | collective-permute-start | bytes 1179656 | tf_op jit(solution)/shard_map/ppermute | solution.py:338
  82.8 13.1 %collective-permute-start.10 = (bf16[768,256]{1,0:T(8,128)(2,1)S(1)}, bf16[768,256]{1,0:T(8,128)(2,1)S(1)}, u32[]{:S(2)}, u32[]{:S(2)}) collective-permute-start(bf16[768,256]{1,0:T(8,128)(2,1)S(1)} %collective-permute-done.9.refs_1_), channel_id=1, source_target_pairs={{0,32},{64,96},{128,160},{192,224},{256,288},{320,352},{384,416},{... | collective-permute-start | bytes 1179656 | tf_op jit(solution)/shard_map/ppermute | solution.py:338
  86.7 12.7 %collective-permute-start.6 = (bf16[768,256]{1,0:T(8,128)(2,1)S(1)}, bf16[768,256]{1,0:T(8,128)(2,1)S(1)}, u32[]{:S(2)}, u32[]{:S(2)}) collective-permute-start(bf16[768,256]{1,0:T(8,128)(2,1)S(1)} %collective-permute-done.5.refs_0_), channel_id=1, source_target_pairs={{32,64},{96,128},{160,192},{224,256},{288,320},{352,384},{416,448}... | collective-permute-start | bytes 1179656 | tf_op jit(solution)/shard_map/ppermute | solution.py:338
  95.9 12.5 %collective-permute-start.16 = (bf16[3,128,128]{2,1,0:T(8,128)(2,1)S(1)}, bf16[3,128,128]{2,1,0:T(8,128)(2,1)S(1)}, u32[]{:S(2)}, u32[]{:S(2)}) collective-permute-start(bf16[3,128,128]{2,1,0:T(8,128)(2,1)S(1)} %get-tuple-element.31), channel_id=1, source_target_pairs={{0,3},{1,0},{2,1},{3,2},{4,7},{5,4},{6,5},{7,6},{8,11},{9,8},{10,9... | collective-permute-start | bytes 294920 | tf_op jit(solution)/shard_map/ppermute | solution.py:349
  100.3 8.2 %collective-permute-start.13 = (bf16[768,128]{1,0:T(8,128)(2,1)S(1)}, bf16[768,128]{1,0:T(8,128)(2,1)S(1)}, u32[]{:S(2)}, u32[]{:S(2)}) collective-permute-start(bf16[768,128]{1,0:T(8,128)(2,1)S(1)} %shard_map.63), channel_id=1, source_target_pairs={{0,256},{32,288},{64,320},{96,352},{128,384},{160,416},{192,448},{... | collective-permute-start | bytes 589832 | tf_op jit(solution)/shard_map/ppermute | solution.py:361
  103.9 4.6 %collective-permute-start.11 = (bf16[768,256]{1,0:T(8,128)(2,1)S(1)}, bf16[768,256]{1,0:T(8,128)(2,1)S(1)}, u32[]{:S(2)}, u32[]{:S(2)}) collective-permute-start(bf16[768,256]{1,0:T(8,128)(2,1)S(1)} %collective-permute-done.10.refs_0_), channel_id=1, source_target_pairs={{32,64},{96,128},{160,192},{224,256},{288,320},{352,384},{416,448}... | collective-permute-start | bytes 1179656 | tf_op jit(solution)/shard_map/ppermute | solution.py:338
  104.6 8.2 %collective-permute-start.7 = (bf16[768,256]{1,0:T(8,128)(2,1)S(1)}, bf16[768,256]{1,0:T(8,128)(2,1)S(1)}, u32[]{:S(2)}, u32[]{:S(2)}) collective-permute-start(bf16[768,256]{1,0:T(8,128)(2,1)S(1)} %collective-permute-done.6.refs_1_), channel_id=1, source_target_pairs={{0,32},{64,96},{128,160},{192,224},{256,288},{320,352},{384,416},{... | collective-permute-start | bytes 1179656 | tf_op jit(solution)/shard_map/ppermute | solution.py:338
  114.5 16.2 %all-to-all-start.1 = ((bf16[8,96,128]{2,1,0:T(8,128)(2,1)}), bf16[8,96,128]{2,1,0:T(8,128)(2,1)S(1)}, u32[]{:S(2)}, u32[]{:S(2)}) async-start(bf16[8,96,128]{2,1,0:T(8,128)(2,1)} %bitcast.3), calls=%async_computation.1 | async-start | bytes 393216 | tf_op jit(solution)/shard_map/all_to_all | solution.py:335
  (3 other events, 37.4 us)

commit v8 on v6

--- a/solution.py
+++ b/solution.py
@@ -97,9 +97,9 @@
 
 def unit_owner(stream, step):
     me = lax.axis_index("ctx")
-    plane, row = me // PLANE, me % PLANE
-    wrapped = plane * PLANE + (row + step) % PLANE if step < 4 else -1
-    return jnp.where((row + stream) % 2 == 1, me - step, wrapped)
+    if stream == "up":
+        return me - step
+    return me // PLANE * PLANE + (me % PLANE + step) % PLANE
 
 
 def history_ends(hist_ref):
@@ -295,12 +295,6 @@
 RETURN = [(i, i + PLANE) for i in range(PLANE)]
 
 
-def stream_pairs(stream, step):
-    ups = [(i, j) for i, j in UP if i % 2 == stream]
-    downs = [(i, j) for i, j in DOWN if i % 2 != stream]
-    return ups + (downs if step < 4 else [])
-
-
 def gather_w(w):
     cross = functools.partial(lax.ppermute, axis_name="head")
     half = HD // 2
@@ -317,30 +311,28 @@
     def to_all(x):
         return lax.all_to_all(x, "head", 0, 0, tiled=True)
 
-    def step_on(last, step):
-        return [move(last[1 - stream], perm=stream_pairs(stream, step)) for stream in range(2)]
-
-    names = [((0, 0),)] + [((0, step), (1, step)) for step in range(1, 5)]
     blocks = pick(shards, slots, ingested)
     w_late, blocks = lax.optimization_barrier((w_out, blocks))
     arrived = lax.all_to_all(blocks, "batch", split_axis=0, concat_axis=0, tiled=True)
     mine, theirs = gather_w(w_late)
     mine, theirs, arrived = lax.optimization_barrier((mine, theirs, arrived))
     own, q, update = in_order(shards, arrived)
-    first = step_on([own, own], 1)
-    second = step_on(first, 2)
-    third = step_on(second, 3)
-    fourth = step_on(third, 4)
+    up, down = [own], [own]
+    for step in range(4):
+        up.append(move(up[-1], perm=UP))
+        if step < 3:
+            down.append(move(down[-1], perm=DOWN))
     lent_q = move(q, perm=LEND)
-    acc = attend(hist_len, q, (own,), names[0])
-    acc = attend(hist_len, q, first, names[1], acc)
-    lent = attend_lent(hist_len, lent_q, (own, *first), names[0] + names[1])
-    acc = attend(hist_len, q, second, names[2], acc)
-    lent = attend_lent(hist_len, lent_q, second, names[2], lent)
-    lent = attend_lent(hist_len, lent_q, third, names[3], lent, final=True)
+    acc = attend(hist_len, q, (own,), (("up", 0),))
+    acc = attend(hist_len, q, (up[1], down[1]), (("up", 1), ("down", 1)), acc)
+    lent = attend_lent(hist_len, lent_q, (own, down[1]), (("down", 0), ("down", 1)))
+    acc = attend(hist_len, q, (up[2], down[2]), (("up", 2), ("down", 2)), acc)
+    lent = attend_lent(
+        hist_len, lent_q, (down[2], down[3]), (("down", 2), ("down", 3)), lent, final=True
+    )
     lent = move(lent, perm=RETURN)
-    acc = attend(hist_len, q, third, names[3], acc)
-    gated = attend_last(hist_len, q, fourth, names[4], acc, lent, update)
+    acc = attend(hist_len, q, (up[3], down[3]), (("up", 3), ("down", 3)), acc)
+    gated = attend_last(hist_len, q, (up[4],), (("up", 4),), acc, lent, update)
     rows = to_all(gated.reshape(HEADS, CHUNK, HD))
     mixed = to_all(project(rows, mine, theirs))
     return mixed.reshape(1, ROWS, HD)

time: 134 us -> 131 us (0.978)
  the two profiles are of different devices: /device:TPU:1 before, /device:TPU:64 now
where the time goes in v8:
time: 131 us
  starting transfers between devices  53.1 us (41%)
  waiting for transfers between devices  42.7 us (33%)
  blocking collectives  20.2 us (15%)
  Pallas kernels  12.6 us (10%)
  local copies, waits for them, and re-layouts  1.77 us (1%)
    all_to_all x2, blocking collectives, to_all(): return lax.all_to_all(x, 'head', 0, 0, tiled=True)  20.2 us
    ppermute x3, starting transfers between devices, body(): down.append(move(down[-1], perm=DOWN))  16.9 us
    ppermute x4, waiting for transfers between devices, body(): up.append(move(up[-1], perm=UP))  12.3 us
    all_to_all x1, waiting for transfers between devices, body(): lax.all_to_all(blocks, 'batch', split_axis=0, concat_axis=0, tiled=True)  11.2 us
    all_to_all x1, starting transfers between devices, body(): lax.all_to_all(blocks, 'batch', split_axis=0, concat_axis=0, tiled=True)  10.2 us
    ppermute x4, starting transfers between devices, body(): up.append(move(up[-1], perm=UP))  7.84 us
    ppermute x2, starting transfers between devices, gather_w(): even, odd = (cross(w, perm=X_EVEN), cross(w, perm=X_ODD))  6.92 us
    ppermute x2, starting transfers between devices, gather_w(): far = [cross(odd[:half], perm=X_EVEN), cross(even[half:], perm=X_ODD)]  5.63 us
  transfers between devices with their start and end apart: 15, of which 12 were waited for; matrix products, arithmetic and copies ran while one was open for 0% of the time, Pallas kernels for 5%

profile of v8, /device:TPU:64, one launch (start us, length us, event | category | flops | bytes accessed | tf_op | source)
XLA Modules:
  0.0 130.7 jit_solution(18296422986064863278)
XLA Ops:
  0.0 3.8 %shard_map.55 = bf16[12,128,512]{2,1,0:T(8,128)(2,1)} custom-call(s32[4,6]{1,0:T(4,128)} %bitcast.6, s32[4,6]{1,0:T(4,128)} %bitcast.10, bf16[12,128,4,128]{3,2,1,0:T(4,128)(2,1)} %bitcast.8), custom_call_target="tpu_custom_call" | custom-call | tf_op jit(solution)/shard_map/pallas_call | solution.py:57
  3.8 10.2 %all-to-all-start = ((bf16[12,128,512]{2,1,0:T(8,128)(2,1)}), bf16[12,128,512]{2,1,0:T(8,128)(2,1)S(1)}, u32[]{:S(2)}, u32[]{:S(2)}) async-start(bf16[12,128,512]{2,1,0:T(8,128)(2,1)} %shard_map.55), calls=%async_computation | async-start | bytes 3145728 | tf_op jit(solution)/shard_map/all_to_all | solution.py:316
  14.0 4.8 %collective-permute-start.1 = (bf16[128,1024]{1,0:T(8,128)(2,1)S(1)}, bf16[128,1024]{1,0:T(8,128)(2,1)S(1)}, u32[]{:S(2)}, u32[]{:S(2)}) collective-permute-start(bf16[128,1024]{1,0:T(8,128)(2,1)S(1)} %copy-done.4), channel_id=1, source_target_pairs={{0,24},{4,28},{8,16},{12,20},{16,8},{20,12},{24,0},{28,4},{1,25},{... | collective-permute-start | bytes 786440 | tf_op jit(solution)/shard_map/ppermute | solution.py:301
  18.8 2.1 %collective-permute-start = (bf16[128,1024]{1,0:T(8,128)(2,1)S(1)}, bf16[128,1024]{1,0:T(8,128)(2,1)S(1)}, u32[]{:S(2)}, u32[]{:S(2)}) collective-permute-start(bf16[128,1024]{1,0:T(8,128)(2,1)S(1)} %copy-done.4), channel_id=1, source_target_pairs={{0,8},{4,12},{8,0},{12,4},{16,24},{20,28},{24,16},{28,20},{1,9},{5... | collective-permute-start | bytes 786440 | tf_op jit(solution)/shard_map/ppermute | solution.py:301
  20.9 4.0 %collective-permute-done.1 = bf16[128,1024]{1,0:T(8,128)(2,1)S(1)} collective-permute-done((bf16[128,1024]{1,0:T(8,128)(2,1)S(1)}, bf16[128,1024]{1,0:T(8,128)(2,1)S(1)}, u32[]{:S(2)}, u32[]{:S(2)}) %collective-permute-start.1) | collective-permute-done | bytes 262176 | tf_op jit(solution)/shard_map/ppermute | solution.py:301
  25.0 2.2 %collective-permute-start.2 = (bf16[64,1024]{1,0:T(8,128)(2,1)S(1)}, bf16[64,1024]{1,0:T(8,128)(2,1)S(1)}, u32[]{:S(2)}, u32[]{:S(2)}) collective-permute-start(bf16[64,1024]{1,0:T(8,128)(2,1)S(1)} %slice.8), channel_id=1, source_target_pairs={{0,8},{4,12},{8,0},{12,4},{16,24},{20,28},{24,16},{28,20},{1,9},{5... | collective-permute-start | bytes 393224 | tf_op jit(solution)/shard_map/ppermute | solution.py:302
  28.2 3.4 %collective-permute-start.3 = (bf16[64,1024]{1,0:T(8,128)(2,1)S(1)}, bf16[64,1024]{1,0:T(8,128)(2,1)S(1)}, u32[]{:S(2)}, u32[]{:S(2)}) collective-permute-start(bf16[64,1024]{1,0:T(8,128)(2,1)S(1)} %slice.9), channel_id=1, source_target_pairs={{0,24},{4,28},{8,16},{12,20},{16,8},{20,12},{24,0},{28,4},{1,25},{... | collective-permute-start | bytes 393224 | tf_op jit(solution)/shard_map/ppermute | solution.py:302
  31.9 4.4 %collective-permute-done.3 = bf16[64,1024]{1,0:T(8,128)(2,1)S(1)} collective-permute-done((bf16[64,1024]{1,0:T(8,128)(2,1)S(1)}, bf16[64,1024]{1,0:T(8,128)(2,1)S(1)}, u32[]{:S(2)}, u32[]{:S(2)}) %collective-permute-start.3) | collective-permute-done | bytes 131104 | tf_op jit(solution)/shard_map/ppermute | solution.py:302
  36.3 1.9 %collective-permute-start.4 = (bf16[512,1024]{1,0:T(8,128)(2,1)S(1)}, bf16[512,1024]{1,0:T(8,128)(2,1)S(1)}, u32[]{:S(2)}, u32[]{:S(2)}) collective-permute-start(bf16[512,1024]{1,0:T(8,128)(2,1)S(1)} %constant_dynamic-update-slice_fusion.mine_ref), channel_id=1, source_target_pairs={{0,4},{4,0},{8,12},{12,8},{16,20},{20,16},{24,28},{28,24},{1,5},{5... | collective-permute-start | bytes 3145736 | tf_op jit(solution)/shard_map/ppermute | solution.py:304
  38.2 2.6 %collective-permute-done.4.theirs_ref = bf16[512,1024]{1,0:T(8,128)(2,1)S(1)} collective-permute-done((bf16[512,1024]{1,0:T(8,128)(2,1)S(1)}, bf16[512,1024]{1,0:T(8,128)(2,1)S(1)}, u32[]{:S(2)}, u32[]{:S(2)}) %collective-permute-start.4) | collective-permute-done | bytes 1048608 | tf_op jit(solution)/shard_map/ppermute | solution.py:304
  41.8 11.2 %all-to-all-done.in_ref = bf16[12,128,512]{2,1,0:T(8,128)(2,1)S(1)} async-done(((bf16[12,128,512]{2,1,0:T(8,128)(2,1)}), bf16[12,128,512]{2,1,0:T(8,128)(2,1)S(1)}, u32[]{:S(2)}, u32[]{:S(2)}) %all-to-all-start) | async-done | bytes 1572896 | tf_op jit(solution)/shard_map/all_to_all | solution.py:316
  53.7 5.2 %collective-permute-start.9 = (bf16[768,256]{1,0:T(8,128)(2,1)S(1)}, bf16[768,256]{1,0:T(8,128)(2,1)S(1)}, u32[]{:S(2)}, u32[]{:S(2)}) collective-permute-start(bf16[768,256]{1,0:T(8,128)(2,1)S(1)} %get-tuple-element.17.refs_0_), channel_id=1, source_target_pairs={{0,224},{32,0},{64,32},{96,64},{128,96},{160,128},{192,160},{224,1... | collective-permute-start | bytes 1179656 | tf_op jit(solution)/shard_map/ppermute | solution.py:324
  58.9 1.9 %collective-permute-start.5 = (bf16[768,256]{1,0:T(8,128)(2,1)S(1)}, bf16[768,256]{1,0:T(8,128)(2,1)S(1)}, u32[]{:S(2)}, u32[]{:S(2)}) collective-permute-start(bf16[768,256]{1,0:T(8,128)(2,1)S(1)} %get-tuple-element.17.refs_0_), channel_id=1, source_target_pairs={{0,32},{32,64},{64,96},{96,128},{128,160},{160,192},{192,224},{224... | collective-permute-start | bytes 1179656 | tf_op jit(solution)/shard_map/ppermute | solution.py:322
  60.8 2.4 %collective-permute-start.12 = (bf16[768,128]{1,0:T(8,128)(2,1)S(1)}, bf16[768,128]{1,0:T(8,128)(2,1)S(1)}, u32[]{:S(2)}, u32[]{:S(2)}) collective-permute-start(bf16[768,128]{1,0:T(8,128)(2,1)S(1)} %get-tuple-element.16.q_ref), channel_id=1, source_target_pairs={{256,0},{288,32},{320,64},{352,96},{384,128},{416,160},{448,192},{... | collective-permute-start | bytes 589832 | tf_op jit(solution)/shard_map/ppermute | solution.py:325
  63.2 2.9 %shard_map.57.refs_2_ = f32[768,128]{1,0:T(8,128)S(1)} custom-call(s32[1,4]{1,0:T(1,128)S(1)} %copy-done.3, bf16[768,128]{1,0:T(8,128)(2,1)S(1)} %get-tuple-element.16.q_ref, bf16[768,256]{1,0:T(8,128)(2,1)S(1)} %get-tuple-element.17.refs_0_), custom_call_target="tpu_custom_call" | custom-call | flops 2415919104 | bytes 1048576 | tf_op jit(solution)/shard_map/pallas_call | solution.py:188
  66.1 6.1 %collective-permute-start.10 = (bf16[768,256]{1,0:T(8,128)(2,1)S(1)}, bf16[768,256]{1,0:T(8,128)(2,1)S(1)}, u32[]{:S(2)}, u32[]{:S(2)}) collective-permute-start(bf16[768,256]{1,0:T(8,128)(2,1)S(1)} %collective-permute-done.9.refs_1_), channel_id=1, source_target_pairs={{0,224},{32,0},{64,32},{96,64},{128,96},{160,128},{192,160},{224,1... | collective-permute-start | bytes 1179656 | tf_op jit(solution)/shard_map/ppermute | solution.py:324
  75.7 2.0 %collective-permute-done.10.refs_1_.refs_0_ = bf16[768,256]{1,0:T(8,128)(2,1)S(1)} collective-permute-done((bf16[768,256]{1,0:T(8,128)(2,1)S(1)}, bf16[768,256]{1,0:T(8,128)(2,1)S(1)}, u32[]{:S(2)}, u32[]{:S(2)}) %collective-permute-start.10) | collective-permute-done | bytes 393248 | tf_op jit(solution)/shard_map/ppermute | solution.py:324
  77.7 5.6 %collective-permute-start.11 = (bf16[768,256]{1,0:T(8,128)(2,1)S(1)}, bf16[768,256]{1,0:T(8,128)(2,1)S(1)}, u32[]{:S(2)}, u32[]{:S(2)}) collective-permute-start(bf16[768,256]{1,0:T(8,128)(2,1)S(1)} %collective-permute-done.10.refs_1_.refs_0_), channel_id=1, source_target_pairs={{0,224},{32,0},{64,32},{96,64},{128,96},{160,128},{192,160},{224,1... | collective-permute-start | bytes 1179656 | tf_op jit(solution)/shard_map/ppermute | solution.py:324
  90.4 6.1 %collective-permute-done.7.refs_0_ = bf16[768,256]{1,0:T(8,128)(2,1)S(1)} collective-permute-done((bf16[768,256]{1,0:T(8,128)(2,1)S(1)}, bf16[768,256]{1,0:T(8,128)(2,1)S(1)}, u32[]{:S(2)}, u32[]{:S(2)}) %collective-permute-start.7) | collective-permute-done | bytes 393248 | tf_op jit(solution)/shard_map/ppermute | solution.py:322
  96.5 2.1 %collective-permute-start.8 = (bf16[768,256]{1,0:T(8,128)(2,1)S(1)}, bf16[768,256]{1,0:T(8,128)(2,1)S(1)}, u32[]{:S(2)}, u32[]{:S(2)}) collective-permute-start(bf16[768,256]{1,0:T(8,128)(2,1)S(1)} %collective-permute-done.7.refs_0_), channel_id=1, source_target_pairs={{0,32},{32,64},{64,96},{96,128},{128,160},{160,192},{192,224},{224... | collective-permute-start | bytes 1179656 | tf_op jit(solution)/shard_map/ppermute | solution.py:322
  99.5 4.0 %collective-permute-done.13.refs_2_ = bf16[768,128]{1,0:T(8,128)(2,1)S(1)} collective-permute-done((bf16[768,128]{1,0:T(8,128)(2,1)S(1)}, bf16[768,128]{1,0:T(8,128)(2,1)S(1)}, u32[]{:S(2)}, u32[]{:S(2)}) %collective-permute-start.13) | collective-permute-done | bytes 196640 | tf_op jit(solution)/shard_map/ppermute | solution.py:333
  103.5 4.8 %collective-permute-done.8.refs_0_ = bf16[768,256]{1,0:T(8,128)(2,1)S(1)} collective-permute-done((bf16[768,256]{1,0:T(8,128)(2,1)S(1)}, bf16[768,256]{1,0:T(8,128)(2,1)S(1)}, u32[]{:S(2)}, u32[]{:S(2)}) %collective-permute-start.8) | collective-permute-done | bytes 393248 | tf_op jit(solution)/shard_map/ppermute | solution.py:322
  109.4 10.9 %all_to_all.15.rows_ref = bf16[8,96,128]{2,1,0:T(8,128)(2,1)S(1)} all-to-all(bf16[8,96,128]{2,1,0:T(8,128)(2,1)S(1)} %bitcast.5), channel_id=1, replica_groups=mesh['ctx'=16,'head'=8,'batch'=4] {'head'}, dimensions={0} | all-to-all | bytes 393216 | tf_op jit(solution)/shard_map/all_to_all | solution.py:312
  120.8 9.2 %all_to_all.16 = bf16[8,96,128]{2,1,0:T(8,128)(2,1)S(1)} all-to-all(bf16[8,96,128]{2,1,0:T(8,128)(2,1)S(1)} %shard_map.64), channel_id=1, replica_groups=mesh['ctx'=16,'head'=8,'batch'=4] {'head'}, dimensions={0} | all-to-all | bytes 393216 | tf_op jit(solution)/shard_map/all_to_all | solution.py:312
  (36 shorter events, 16.5 us)
Async XLA Ops:
  3.8 10.2 %copy-start.4 = (bf16[128,1024]{1,0:T(8,128)(2,1)S(1)}, bf16[128,1024]{1,0:T(8,128)(2,1)}, u32[]{:S(2)}) copy-start(bf16[128,1024]{1,0:T(8,128)(2,1)} %param.9) | copy-start | bytes 786436
  3.8 49.2 %all-to-all-start = ((bf16[12,128,512]{2,1,0:T(8,128)(2,1)}), bf16[12,128,512]{2,1,0:T(8,128)(2,1)S(1)}, u32[]{:S(2)}, u32[]{:S(2)}) async-start(bf16[12,128,512]{2,1,0:T(8,128)(2,1)} %shard_map.55), calls=%async_computation | async-start | bytes 3145728 | tf_op jit(solution)/shard_map/all_to_all | solution.py:316
  14.0 39.0 %copy-start.2 = (s32[1,4,6]{2,1,0:T(4,128)S(1)}, s32[1,4,6]{2,1,0:T(4,128)}, u32[]{:S(2)}) copy-start(s32[1,4,6]{2,1,0:T(4,128)} %param.6) | copy-start | bytes 292
  14.0 11.0 %collective-permute-start.1 = (bf16[128,1024]{1,0:T(8,128)(2,1)S(1)}, bf16[128,1024]{1,0:T(8,128)(2,1)S(1)}, u32[]{:S(2)}, u32[]{:S(2)}) collective-permute-start(bf16[128,1024]{1,0:T(8,128)(2,1)S(1)} %copy-done.4), channel_id=1, source_target_pairs={{0,24},{4,28},{8,16},{12,20},{16,8},{20,12},{24,0},{28,4},{1,25},{... | collective-permute-start | bytes 786440 | tf_op jit(solution)/shard_map/ppermute | solution.py:301
  18.8 9.4 %collective-permute-start = (bf16[128,1024]{1,0:T(8,128)(2,1)S(1)}, bf16[128,1024]{1,0:T(8,128)(2,1)S(1)}, u32[]{:S(2)}, u32[]{:S(2)}) collective-permute-start(bf16[128,1024]{1,0:T(8,128)(2,1)S(1)} %copy-done.4), channel_id=1, source_target_pairs={{0,8},{4,12},{8,0},{12,4},{16,24},{20,28},{24,16},{28,20},{1,9},{5... | collective-permute-start | bytes 786440 | tf_op jit(solution)/shard_map/ppermute | solution.py:301
  25.0 6.9 %collective-permute-start.2 = (bf16[64,1024]{1,0:T(8,128)(2,1)S(1)}, bf16[64,1024]{1,0:T(8,128)(2,1)S(1)}, u32[]{:S(2)}, u32[]{:S(2)}) collective-permute-start(bf16[64,1024]{1,0:T(8,128)(2,1)S(1)} %slice.8), channel_id=1, source_target_pairs={{0,8},{4,12},{8,0},{12,4},{16,24},{20,28},{24,16},{28,20},{1,9},{5... | collective-permute-start | bytes 393224 | tf_op jit(solution)/shard_map/ppermute | solution.py:302
  28.2 35.0 %copy-start.3 = (s32[1,4]{1,0:T(1,128)S(1)}, s32[1,4]{1,0:T(1,128)}, u32[]{:S(2)}) copy-start(s32[1,4]{1,0:T(1,128)} %hist_ref.13) | copy-start | bytes 52
  28.2 8.1 %collective-permute-start.3 = (bf16[64,1024]{1,0:T(8,128)(2,1)S(1)}, bf16[64,1024]{1,0:T(8,128)(2,1)S(1)}, u32[]{:S(2)}, u32[]{:S(2)}) collective-permute-start(bf16[64,1024]{1,0:T(8,128)(2,1)S(1)} %slice.9), channel_id=1, source_target_pairs={{0,24},{4,28},{8,16},{12,20},{16,8},{20,12},{24,0},{28,4},{1,25},{... | collective-permute-start | bytes 393224 | tf_op jit(solution)/shard_map/ppermute | solution.py:302
  36.3 4.6 %collective-permute-start.4 = (bf16[512,1024]{1,0:T(8,128)(2,1)S(1)}, bf16[512,1024]{1,0:T(8,128)(2,1)S(1)}, u32[]{:S(2)}, u32[]{:S(2)}) collective-permute-start(bf16[512,1024]{1,0:T(8,128)(2,1)S(1)} %constant_dynamic-update-slice_fusion.mine_ref), channel_id=1, source_target_pairs={{0,4},{4,0},{8,12},{12,8},{16,20},{20,16},{24,28},{28,24},{1,5},{5... | collective-permute-start | bytes 3145736 | tf_op jit(solution)/shard_map/ppermute | solution.py:304
  40.8 1.0 copy-start
  53.7 12.4 %collective-permute-start.9 = (bf16[768,256]{1,0:T(8,128)(2,1)S(1)}, bf16[768,256]{1,0:T(8,128)(2,1)S(1)}, u32[]{:S(2)}, u32[]{:S(2)}) collective-permute-start(bf16[768,256]{1,0:T(8,128)(2,1)S(1)} %get-tuple-element.17.refs_0_), channel_id=1, source_target_pairs={{0,224},{32,0},{64,32},{96,64},{128,96},{160,128},{192,160},{224,1... | collective-permute-start | bytes 1179656 | tf_op jit(solution)/shard_map/ppermute | solution.py:324
  58.9 14.0 %collective-permute-start.5 = (bf16[768,256]{1,0:T(8,128)(2,1)S(1)}, bf16[768,256]{1,0:T(8,128)(2,1)S(1)}, u32[]{:S(2)}, u32[]{:S(2)}) collective-permute-start(bf16[768,256]{1,0:T(8,128)(2,1)S(1)} %get-tuple-element.17.refs_0_), channel_id=1, source_target_pairs={{0,32},{32,64},{64,96},{96,128},{128,160},{160,192},{192,224},{224... | collective-permute-start | bytes 1179656 | tf_op jit(solution)/shard_map/ppermute | solution.py:322
  60.8 11.4 %collective-permute-start.12 = (bf16[768,128]{1,0:T(8,128)(2,1)S(1)}, bf16[768,128]{1,0:T(8,128)(2,1)S(1)}, u32[]{:S(2)}, u32[]{:S(2)}) collective-permute-start(bf16[768,128]{1,0:T(8,128)(2,1)S(1)} %get-tuple-element.16.q_ref), channel_id=1, source_target_pairs={{256,0},{288,32},{320,64},{352,96},{384,128},{416,160},{448,192},{... | collective-permute-start | bytes 589832 | tf_op jit(solution)/shard_map/ppermute | solution.py:325
  66.1 11.5 %collective-permute-start.10 = (bf16[768,256]{1,0:T(8,128)(2,1)S(1)}, bf16[768,256]{1,0:T(8,128)(2,1)S(1)}, u32[]{:S(2)}, u32[]{:S(2)}) collective-permute-start(bf16[768,256]{1,0:T(8,128)(2,1)S(1)} %collective-permute-done.9.refs_1_), channel_id=1, source_target_pairs={{0,224},{32,0},{64,32},{96,64},{128,96},{160,128},{192,160},{224,1... | collective-permute-start | bytes 1179656 | tf_op jit(solution)/shard_map/ppermute | solution.py:324
  72.9 11.8 %collective-permute-start.6 = (bf16[768,256]{1,0:T(8,128)(2,1)S(1)}, bf16[768,256]{1,0:T(8,128)(2,1)S(1)}, u32[]{:S(2)}, u32[]{:S(2)}) collective-permute-start(bf16[768,256]{1,0:T(8,128)(2,1)S(1)} %collective-permute-done.5.refs_0_), channel_id=1, source_target_pairs={{0,32},{32,64},{64,96},{96,128},{128,160},{160,192},{192,224},{224... | collective-permute-start | bytes 1179656 | tf_op jit(solution)/shard_map/ppermute | solution.py:322
  77.7 10.9 %collective-permute-start.11 = (bf16[768,256]{1,0:T(8,128)(2,1)S(1)}, bf16[768,256]{1,0:T(8,128)(2,1)S(1)}, u32[]{:S(2)}, u32[]{:S(2)}) collective-permute-start(bf16[768,256]{1,0:T(8,128)(2,1)S(1)} %collective-permute-done.10.refs_1_.refs_0_), channel_id=1, source_target_pairs={{0,224},{32,0},{64,32},{96,64},{128,96},{160,128},{192,160},{224,1... | collective-permute-start | bytes 1179656 | tf_op jit(solution)/shard_map/ppermute | solution.py:324
  84.7 11.9 %collective-permute-start.7 = (bf16[768,256]{1,0:T(8,128)(2,1)S(1)}, bf16[768,256]{1,0:T(8,128)(2,1)S(1)}, u32[]{:S(2)}, u32[]{:S(2)}) collective-permute-start(bf16[768,256]{1,0:T(8,128)(2,1)S(1)} %collective-permute-done.6.refs_0_), channel_id=1, source_target_pairs={{0,32},{32,64},{64,96},{96,128},{128,160},{160,192},{192,224},{224... | collective-permute-start | bytes 1179656 | tf_op jit(solution)/shard_map/ppermute | solution.py:322
  89.1 14.4 %collective-permute-start.13 = (bf16[768,128]{1,0:T(8,128)(2,1)S(1)}, bf16[768,128]{1,0:T(8,128)(2,1)S(1)}, u32[]{:S(2)}, u32[]{:S(2)}) collective-permute-start(bf16[768,128]{1,0:T(8,128)(2,1)S(1)} %shard_map.62), channel_id=1, source_target_pairs={{0,256},{32,288},{64,320},{96,352},{128,384},{160,416},{192,448},{... | collective-permute-start | bytes 589832 | tf_op jit(solution)/shard_map/ppermute | solution.py:333
  96.5 11.8 %collective-permute-start.8 = (bf16[768,256]{1,0:T(8,128)(2,1)S(1)}, bf16[768,256]{1,0:T(8,128)(2,1)S(1)}, u32[]{:S(2)}, u32[]{:S(2)}) collective-permute-start(bf16[768,256]{1,0:T(8,128)(2,1)S(1)} %collective-permute-done.7.refs_0_), channel_id=1, source_target_pairs={{0,32},{32,64},{64,96},{96,128},{128,160},{160,192},{192,224},{224... | collective-permute-start | bytes 1179656 | tf_op jit(solution)/shard_map/ppermute | solution.py:322
  108.3 12.0 %copy-start.1 = (bf16[512,1024]{1,0:T(8,128)(2,1)S(1)}, bf16[512,1024]{1,0:T(8,128)(2,1)}, u32[]{:S(2)}) copy-start(bf16[512,1024]{1,0:T(8,128)(2,1)} %copy-done) | copy-start | bytes 3145732

commit v9 on v8

--- a/solution.py
+++ b/solution.py
@@ -97,9 +97,10 @@
 
 def unit_owner(stream, step):
     me = lax.axis_index("ctx")
-    if stream == "up":
+    if step == 4:
         return me - step
-    return me // PLANE * PLANE + (me % PLANE + step) % PLANE
+    ahead = step if stream == "down" else PLANE - step
+    return me // PLANE * PLANE + (me % PLANE + ahead) % PLANE
 
 
 def history_ends(hist_ref):
@@ -289,8 +290,9 @@
 CORE = [(h, h ^ 1) for h in range(HEADS)]
 X_EVEN = [(h, near_heads(h)[1]) for h in range(HEADS)]
 X_ODD = [(h, near_heads(h)[2]) for h in range(HEADS)]
-UP = [(i, i + 1) for i in range(CTXS - 1)]
-DOWN = [(i, i // PLANE * PLANE + (i - 1) % PLANE) for i in range(CTXS)]
+UP = [(i, i // PLANE * PLANE + (i + 1) % PLANE) for i in range(CTXS)]
+DOWN = [(j, i) for i, j in UP]
+LAST_UP = [(i % PLANE if j % PLANE < 4 else i, j) for i, j in UP if j >= 4]
 LEND = [(i + PLANE, i) for i in range(PLANE)]
 RETURN = [(i, i + PLANE) for i in range(PLANE)]
 
@@ -318,20 +320,21 @@
     mine, theirs, arrived = lax.optimization_barrier((mine, theirs, arrived))
     own, q, update = in_order(shards, arrived)
     up, down = [own], [own]
-    for step in range(4):
+    for step in range(3):
         up.append(move(up[-1], perm=UP))
-        if step < 3:
-            down.append(move(down[-1], perm=DOWN))
+        down.append(move(down[-1], perm=DOWN))
+    up.append(move(up[-1], perm=LAST_UP))
+    names = [(("up", step), ("down", step)) for step in range(4)]
+    units = list(zip(up, down))
     lent_q = move(q, perm=LEND)
     acc = attend(hist_len, q, (own,), (("up", 0),))
-    acc = attend(hist_len, q, (up[1], down[1]), (("up", 1), ("down", 1)), acc)
-    lent = attend_lent(hist_len, lent_q, (own, down[1]), (("down", 0), ("down", 1)))
-    acc = attend(hist_len, q, (up[2], down[2]), (("up", 2), ("down", 2)), acc)
-    lent = attend_lent(
-        hist_len, lent_q, (down[2], down[3]), (("down", 2), ("down", 3)), lent, final=True
-    )
+    acc = attend(hist_len, q, units[1], names[1], acc)
+    lent = attend_lent(hist_len, lent_q, (own, *units[1]), (("up", 0), *names[1]))
+    acc = attend(hist_len, q, units[2], names[2], acc)
+    lent = attend_lent(hist_len, lent_q, units[2], names[2], lent)
+    lent = attend_lent(hist_len, lent_q, units[3], names[3], lent, final=True)
     lent = move(lent, perm=RETURN)
-    acc = attend(hist_len, q, (up[3], down[3]), (("up", 3), ("down", 3)), acc)
+    acc = attend(hist_len, q, units[3], names[3], acc)
     gated = attend_last(hist_len, q, (up[4],), (("up", 4),), acc, lent, update)
     rows = to_all(gated.reshape(HEADS, CHUNK, HD))
     mixed = to_all(project(rows, mine, theirs))

time: 131 us -> 134 us (1.023)
  the two profiles are of different devices: /device:TPU:64 before, /device:TPU:1 now
where the time goes in v9:
time: 134 us; the launch traced here: 133 us
  starting transfers between devices  61.7 us (46%)
  blocking collectives  28 us (21%)
  waiting for transfers between devices  26.9 us (20%)
  Pallas kernels  14.3 us (11%)
  local copies, waits for them, and re-layouts  1.77 us (1%)
    all_to_all x2, blocking collectives, to_all(): return lax.all_to_all(x, 'head', 0, 0, tiled=True)  28 us
    ppermute x3, starting transfers between devices, body(): down.append(move(down[-1], perm=DOWN))  15.3 us
    all_to_all x1, starting transfers between devices, body(): lax.all_to_all(blocks, 'batch', split_axis=0, concat_axis=0, tiled=True)  11.6 us
    ppermute x1, starting transfers between devices, body(): lent = move(lent, perm=RETURN)  9.79 us
    ppermute x2, starting transfers between devices, gather_w(): even, odd = (cross(w, perm=X_EVEN), cross(w, perm=X_ODD))  6.43 us
    ppermute x3, starting transfers between devices, body(): up.append(move(up[-1], perm=UP))  5.76 us
    pallas_call x4, Pallas kernels, attend(): pl.pallas_call(functools.partial(attend_kernel, names, first), out_shape=...  5.54 us
    ppermute x2, starting transfers between devices, gather_w(): far = [cross(odd[:half], perm=X_EVEN), cross(even[half:], perm=X_ODD)]  5.38 us
  transfers between devices with their start and end apart: 15, of which 11 were waited for; matrix products, arithmetic and copies ran while one was open for 0% of the time, Pallas kernels for 6%

profile of v9, /device:TPU:1, one launch (start us, length us, event | category | flops | bytes accessed | tf_op | source)
XLA Modules:
  0.0 133.0 jit_solution(10770145482946907605)
XLA Ops:
  0.0 3.8 %shard_map.55 = bf16[12,128,512]{2,1,0:T(8,128)(2,1)} custom-call(s32[4,6]{1,0:T(4,128)} %bitcast.6, s32[4,6]{1,0:T(4,128)} %bitcast.10, bf16[12,128,4,128]{3,2,1,0:T(4,128)(2,1)} %bitcast.8), custom_call_target="tpu_custom_call" | custom-call | tf_op jit(solution)/shard_map/pallas_call | solution.py:57
  3.8 11.6 %all-to-all-start = ((bf16[12,128,512]{2,1,0:T(8,128)(2,1)}), bf16[12,128,512]{2,1,0:T(8,128)(2,1)S(1)}, u32[]{:S(2)}, u32[]{:S(2)}) async-start(bf16[12,128,512]{2,1,0:T(8,128)(2,1)} %shard_map.55), calls=%async_computation | async-start | bytes 3145728 | tf_op jit(solution)/shard_map/all_to_all | solution.py:318
  15.4 4.5 %collective-permute-start.1 = (bf16[128,1024]{1,0:T(8,128)(2,1)S(1)}, bf16[128,1024]{1,0:T(8,128)(2,1)S(1)}, u32[]{:S(2)}, u32[]{:S(2)}) collective-permute-start(bf16[128,1024]{1,0:T(8,128)(2,1)S(1)} %copy-done.4), channel_id=1, source_target_pairs={{0,24},{4,28},{8,16},{12,20},{16,8},{20,12},{24,0},{28,4},{1,25},{... | collective-permute-start | bytes 786440 | tf_op jit(solution)/shard_map/ppermute | solution.py:303
  19.9 1.9 %collective-permute-start = (bf16[128,1024]{1,0:T(8,128)(2,1)S(1)}, bf16[128,1024]{1,0:T(8,128)(2,1)S(1)}, u32[]{:S(2)}, u32[]{:S(2)}) collective-permute-start(bf16[128,1024]{1,0:T(8,128)(2,1)S(1)} %copy-done.4), channel_id=1, source_target_pairs={{0,8},{4,12},{8,0},{12,4},{16,24},{20,28},{24,16},{28,20},{1,9},{5... | collective-permute-start | bytes 786440 | tf_op jit(solution)/shard_map/ppermute | solution.py:303
  21.9 3.6 %collective-permute-done.1 = bf16[128,1024]{1,0:T(8,128)(2,1)S(1)} collective-permute-done((bf16[128,1024]{1,0:T(8,128)(2,1)S(1)}, bf16[128,1024]{1,0:T(8,128)(2,1)S(1)}, u32[]{:S(2)}, u32[]{:S(2)}) %collective-permute-start.1) | collective-permute-done | bytes 262176 | tf_op jit(solution)/shard_map/ppermute | solution.py:303
  25.5 1.9 %collective-permute-start.2 = (bf16[64,1024]{1,0:T(8,128)(2,1)S(1)}, bf16[64,1024]{1,0:T(8,128)(2,1)S(1)}, u32[]{:S(2)}, u32[]{:S(2)}) collective-permute-start(bf16[64,1024]{1,0:T(8,128)(2,1)S(1)} %slice.8), channel_id=1, source_target_pairs={{0,8},{4,12},{8,0},{12,4},{16,24},{20,28},{24,16},{28,20},{1,9},{5... | collective-permute-start | bytes 393224 | tf_op jit(solution)/shard_map/ppermute | solution.py:304
  28.4 3.5 %collective-permute-start.3 = (bf16[64,1024]{1,0:T(8,128)(2,1)S(1)}, bf16[64,1024]{1,0:T(8,128)(2,1)S(1)}, u32[]{:S(2)}, u32[]{:S(2)}) collective-permute-start(bf16[64,1024]{1,0:T(8,128)(2,1)S(1)} %slice.9), channel_id=1, source_target_pairs={{0,24},{4,28},{8,16},{12,20},{16,8},{20,12},{24,0},{28,4},{1,25},{... | collective-permute-start | bytes 393224 | tf_op jit(solution)/shard_map/ppermute | solution.py:304
  31.9 3.7 %collective-permute-done.3 = bf16[64,1024]{1,0:T(8,128)(2,1)S(1)} collective-permute-done((bf16[64,1024]{1,0:T(8,128)(2,1)S(1)}, bf16[64,1024]{1,0:T(8,128)(2,1)S(1)}, u32[]{:S(2)}, u32[]{:S(2)}) %collective-permute-start.3) | collective-permute-done | bytes 131104 | tf_op jit(solution)/shard_map/ppermute | solution.py:304
  35.6 4.9 %collective-permute-start.4 = (bf16[512,1024]{1,0:T(8,128)(2,1)S(1)}, bf16[512,1024]{1,0:T(8,128)(2,1)S(1)}, u32[]{:S(2)}, u32[]{:S(2)}) collective-permute-start(bf16[512,1024]{1,0:T(8,128)(2,1)S(1)} %constant_dynamic-update-slice_fusion.mine_ref), channel_id=1, source_target_pairs={{0,4},{4,0},{8,12},{12,8},{16,20},{20,16},{24,28},{28,24},{1,5},{5... | collective-permute-start | bytes 3145736 | tf_op jit(solution)/shard_map/ppermute | solution.py:306
  40.5 2.3 %collective-permute-done.4.theirs_ref = bf16[512,1024]{1,0:T(8,128)(2,1)S(1)} collective-permute-done((bf16[512,1024]{1,0:T(8,128)(2,1)S(1)}, bf16[512,1024]{1,0:T(8,128)(2,1)S(1)}, u32[]{:S(2)}, u32[]{:S(2)}) %collective-permute-start.4) | collective-permute-done | bytes 1048608 | tf_op jit(solution)/shard_map/ppermute | solution.py:306
  44.5 4.6 %collective-permute-start.9 = (bf16[768,256]{1,0:T(8,128)(2,1)S(1)}, bf16[768,256]{1,0:T(8,128)(2,1)S(1)}, u32[]{:S(2)}, u32[]{:S(2)}) collective-permute-start(bf16[768,256]{1,0:T(8,128)(2,1)S(1)} %get-tuple-element.17.refs_0_), channel_id=1, source_target_pairs={{32,0},{64,32},{96,64},{128,96},{160,128},{192,160},{224,192},{0,2... | collective-permute-start | bytes 1179656 | tf_op jit(solution)/shard_map/ppermute | solution.py:325
  49.1 1.9 %collective-permute-start.5 = (bf16[768,256]{1,0:T(8,128)(2,1)S(1)}, bf16[768,256]{1,0:T(8,128)(2,1)S(1)}, u32[]{:S(2)}, u32[]{:S(2)}) collective-permute-start(bf16[768,256]{1,0:T(8,128)(2,1)S(1)} %get-tuple-element.17.refs_0_), channel_id=1, source_target_pairs={{0,32},{32,64},{64,96},{96,128},{128,160},{160,192},{192,224},{224... | collective-permute-start | bytes 1179656 | tf_op jit(solution)/shard_map/ppermute | solution.py:324
  52.3 2.9 %shard_map.57.refs_2_ = f32[768,128]{1,0:T(8,128)S(1)} custom-call(s32[1,4]{1,0:T(1,128)S(1)} %copy-done.3, bf16[768,128]{1,0:T(8,128)(2,1)S(1)} %get-tuple-element.16.q_ref, bf16[768,256]{1,0:T(8,128)(2,1)S(1)} %get-tuple-element.17.refs_0_), custom_call_target="tpu_custom_call" | custom-call | flops 2415919104 | bytes 1048576 | tf_op jit(solution)/shard_map/pallas_call | solution.py:189
  55.2 2.0 %collective-permute-done.9.refs_1_.refs_2_ = bf16[768,256]{1,0:T(8,128)(2,1)S(1)} collective-permute-done((bf16[768,256]{1,0:T(8,128)(2,1)S(1)}, bf16[768,256]{1,0:T(8,128)(2,1)S(1)}, u32[]{:S(2)}, u32[]{:S(2)}) %collective-permute-start.9) | collective-permute-done | bytes 393248 | tf_op jit(solution)/shard_map/ppermute | solution.py:325
  57.2 5.3 %collective-permute-start.10 = (bf16[768,256]{1,0:T(8,128)(2,1)S(1)}, bf16[768,256]{1,0:T(8,128)(2,1)S(1)}, u32[]{:S(2)}, u32[]{:S(2)}) collective-permute-start(bf16[768,256]{1,0:T(8,128)(2,1)S(1)} %collective-permute-done.9.refs_1_.refs_2_), channel_id=1, source_target_pairs={{32,0},{64,32},{96,64},{128,96},{160,128},{192,160},{224,192},{0,2... | collective-permute-start | bytes 1179656 | tf_op jit(solution)/shard_map/ppermute | solution.py:325
  64.5 2.7 %collective-permute-done.12.q_ref = bf16[768,128]{1,0:T(8,128)(2,1)S(1)} collective-permute-done((bf16[768,128]{1,0:T(8,128)(2,1)S(1)}, bf16[768,128]{1,0:T(8,128)(2,1)S(1)}, u32[]{:S(2)}, u32[]{:S(2)}) %collective-permute-start.12) | collective-permute-done | bytes 196640 | tf_op jit(solution)/shard_map/ppermute | solution.py:329
  69.7 5.3 %collective-permute-start.11 = (bf16[768,256]{1,0:T(8,128)(2,1)S(1)}, bf16[768,256]{1,0:T(8,128)(2,1)S(1)}, u32[]{:S(2)}, u32[]{:S(2)}) collective-permute-start(bf16[768,256]{1,0:T(8,128)(2,1)S(1)} %collective-permute-done.10.refs_1_), channel_id=1, source_target_pairs={{32,0},{64,32},{96,64},{128,96},{160,128},{192,160},{224,192},{0,2... | collective-permute-start | bytes 1179656 | tf_op jit(solution)/shard_map/ppermute | solution.py:325
  75.0 1.9 %collective-permute-start.7 = (bf16[768,256]{1,0:T(8,128)(2,1)S(1)}, bf16[768,256]{1,0:T(8,128)(2,1)S(1)}, u32[]{:S(2)}, u32[]{:S(2)}) collective-permute-start(bf16[768,256]{1,0:T(8,128)(2,1)S(1)} %collective-permute-done.6.refs_0_), channel_id=1, source_target_pairs={{0,32},{32,64},{64,96},{96,128},{128,160},{160,192},{192,224},{224... | collective-permute-start | bytes 1179656 | tf_op jit(solution)/shard_map/ppermute | solution.py:324
  78.9 2.1 %collective-permute-done.11.refs_1_ = bf16[768,256]{1,0:T(8,128)(2,1)S(1)} collective-permute-done((bf16[768,256]{1,0:T(8,128)(2,1)S(1)}, bf16[768,256]{1,0:T(8,128)(2,1)S(1)}, u32[]{:S(2)}, u32[]{:S(2)}) %collective-permute-start.11) | collective-permute-done | bytes 393248 | tf_op jit(solution)/shard_map/ppermute | solution.py:325
  81.0 5.1 %collective-permute-done.7.refs_0_ = bf16[768,256]{1,0:T(8,128)(2,1)S(1)} collective-permute-done((bf16[768,256]{1,0:T(8,128)(2,1)S(1)}, bf16[768,256]{1,0:T(8,128)(2,1)S(1)}, u32[]{:S(2)}, u32[]{:S(2)}) %collective-permute-start.7) | collective-permute-done | bytes 393248 | tf_op jit(solution)/shard_map/ppermute | solution.py:324
  87.0 9.8 %collective-permute-start.13 = (bf16[768,128]{1,0:T(8,128)(2,1)S(1)}, bf16[768,128]{1,0:T(8,128)(2,1)S(1)}, u32[]{:S(2)}, u32[]{:S(2)}) collective-permute-start(bf16[768,128]{1,0:T(8,128)(2,1)S(1)} %shard_map.63), channel_id=1, source_target_pairs={{0,256},{32,288},{64,320},{96,352},{128,384},{160,416},{192,448},{... | collective-permute-start | bytes 589832 | tf_op jit(solution)/shard_map/ppermute | solution.py:336
  99.4 3.5 %collective-permute-done.8.refs_0_ = bf16[768,256]{1,0:T(8,128)(2,1)S(1)} collective-permute-done((bf16[768,256]{1,0:T(8,128)(2,1)S(1)}, bf16[768,256]{1,0:T(8,128)(2,1)S(1)}, u32[]{:S(2)}, u32[]{:S(2)}) %collective-permute-start.8) | collective-permute-done | bytes 393248 | tf_op jit(solution)/shard_map/ppermute | solution.py:326
  103.9 18.8 %all_to_all.15.rows_ref = bf16[8,96,128]{2,1,0:T(8,128)(2,1)S(1)} all-to-all(bf16[8,96,128]{2,1,0:T(8,128)(2,1)S(1)} %bitcast.5), channel_id=1, replica_groups=mesh['ctx'=16,'head'=8,'batch'=4] {'head'}, dimensions={0} | all-to-all | bytes 393216 | tf_op jit(solution)/shard_map/all_to_all | solution.py:314
  123.1 9.2 %all_to_all.16 = bf16[8,96,128]{2,1,0:T(8,128)(2,1)S(1)} all-to-all(bf16[8,96,128]{2,1,0:T(8,128)(2,1)S(1)} %shard_map.65), channel_id=1, replica_groups=mesh['ctx'=16,'head'=8,'batch'=4] {'head'}, dimensions={0} | all-to-all | bytes 393216 | tf_op jit(solution)/shard_map/all_to_all | solution.py:314
  (37 shorter events, 16.0 us)
Async XLA Ops:
  3.8 11.6 %copy-start.4 = (bf16[128,1024]{1,0:T(8,128)(2,1)S(1)}, bf16[128,1024]{1,0:T(8,128)(2,1)}, u32[]{:S(2)}) copy-start(bf16[128,1024]{1,0:T(8,128)(2,1)} %param.9) | copy-start | bytes 786436
  3.8 40.0 %all-to-all-start = ((bf16[12,128,512]{2,1,0:T(8,128)(2,1)}), bf16[12,128,512]{2,1,0:T(8,128)(2,1)S(1)}, u32[]{:S(2)}, u32[]{:S(2)}) async-start(bf16[12,128,512]{2,1,0:T(8,128)(2,1)} %shard_map.55), calls=%async_computation | async-start | bytes 3145728 | tf_op jit(solution)/shard_map/all_to_all | solution.py:318
  15.4 28.4 %copy-start.2 = (s32[1,4,6]{2,1,0:T(4,128)S(1)}, s32[1,4,6]{2,1,0:T(4,128)}, u32[]{:S(2)}) copy-start(s32[1,4,6]{2,1,0:T(4,128)} %param.6) | copy-start | bytes 292
  15.4 10.1 %collective-permute-start.1 = (bf16[128,1024]{1,0:T(8,128)(2,1)S(1)}, bf16[128,1024]{1,0:T(8,128)(2,1)S(1)}, u32[]{:S(2)}, u32[]{:S(2)}) collective-permute-start(bf16[128,1024]{1,0:T(8,128)(2,1)S(1)} %copy-done.4), channel_id=1, source_target_pairs={{0,24},{4,28},{8,16},{12,20},{16,8},{20,12},{24,0},{28,4},{1,25},{... | collective-permute-start | bytes 786440 | tf_op jit(solution)/shard_map/ppermute | solution.py:303
  19.9 8.5 %collective-permute-start = (bf16[128,1024]{1,0:T(8,128)(2,1)S(1)}, bf16[128,1024]{1,0:T(8,128)(2,1)S(1)}, u32[]{:S(2)}, u32[]{:S(2)}) collective-permute-start(bf16[128,1024]{1,0:T(8,128)(2,1)S(1)} %copy-done.4), channel_id=1, source_target_pairs={{0,8},{4,12},{8,0},{12,4},{16,24},{20,28},{24,16},{28,20},{1,9},{5... | collective-permute-start | bytes 786440 | tf_op jit(solution)/shard_map/ppermute | solution.py:303
  25.5 6.4 %collective-permute-start.2 = (bf16[64,1024]{1,0:T(8,128)(2,1)S(1)}, bf16[64,1024]{1,0:T(8,128)(2,1)S(1)}, u32[]{:S(2)}, u32[]{:S(2)}) collective-permute-start(bf16[64,1024]{1,0:T(8,128)(2,1)S(1)} %slice.8), channel_id=1, source_target_pairs={{0,8},{4,12},{8,0},{12,4},{16,24},{20,28},{24,16},{28,20},{1,9},{5... | collective-permute-start | bytes 393224 | tf_op jit(solution)/shard_map/ppermute | solution.py:304
  28.4 24.0 %copy-start.3 = (s32[1,4]{1,0:T(1,128)S(1)}, s32[1,4]{1,0:T(1,128)}, u32[]{:S(2)}) copy-start(s32[1,4]{1,0:T(1,128)} %hist_ref.15) | copy-start | bytes 52
  28.4 7.2 %collective-permute-start.3 = (bf16[64,1024]{1,0:T(8,128)(2,1)S(1)}, bf16[64,1024]{1,0:T(8,128)(2,1)S(1)}, u32[]{:S(2)}, u32[]{:S(2)}) collective-permute-start(bf16[64,1024]{1,0:T(8,128)(2,1)S(1)} %slice.9), channel_id=1, source_target_pairs={{0,24},{4,28},{8,16},{12,20},{16,8},{20,12},{24,0},{28,4},{1,25},{... | collective-permute-start | bytes 393224 | tf_op jit(solution)/shard_map/ppermute | solution.py:304
  35.6 7.2 %collective-permute-start.4 = (bf16[512,1024]{1,0:T(8,128)(2,1)S(1)}, bf16[512,1024]{1,0:T(8,128)(2,1)S(1)}, u32[]{:S(2)}, u32[]{:S(2)}) collective-permute-start(bf16[512,1024]{1,0:T(8,128)(2,1)S(1)} %constant_dynamic-update-slice_fusion.mine_ref), channel_id=1, source_target_pairs={{0,4},{4,0},{8,12},{12,8},{16,20},{20,16},{24,28},{28,24},{1,5},{5... | collective-permute-start | bytes 3145736 | tf_op jit(solution)/shard_map/ppermute | solution.py:306
  42.8 1.0 copy-start
  44.5 12.8 %collective-permute-start.9 = (bf16[768,256]{1,0:T(8,128)(2,1)S(1)}, bf16[768,256]{1,0:T(8,128)(2,1)S(1)}, u32[]{:S(2)}, u32[]{:S(2)}) collective-permute-start(bf16[768,256]{1,0:T(8,128)(2,1)S(1)} %get-tuple-element.17.refs_0_), channel_id=1, source_target_pairs={{32,0},{64,32},{96,64},{128,96},{160,128},{192,160},{224,192},{0,2... | collective-permute-start | bytes 1179656 | tf_op jit(solution)/shard_map/ppermute | solution.py:325
  49.1 13.4 %collective-permute-start.5 = (bf16[768,256]{1,0:T(8,128)(2,1)S(1)}, bf16[768,256]{1,0:T(8,128)(2,1)S(1)}, u32[]{:S(2)}, u32[]{:S(2)}) collective-permute-start(bf16[768,256]{1,0:T(8,128)(2,1)S(1)} %get-tuple-element.17.refs_0_), channel_id=1, source_target_pairs={{0,32},{32,64},{64,96},{96,128},{128,160},{160,192},{192,224},{224... | collective-permute-start | bytes 1179656 | tf_op jit(solution)/shard_map/ppermute | solution.py:324
  51.0 16.2 %collective-permute-start.12 = (bf16[768,128]{1,0:T(8,128)(2,1)S(1)}, bf16[768,128]{1,0:T(8,128)(2,1)S(1)}, u32[]{:S(2)}, u32[]{:S(2)}) collective-permute-start(bf16[768,128]{1,0:T(8,128)(2,1)S(1)} %get-tuple-element.16.q_ref), channel_id=1, source_target_pairs={{256,0},{288,32},{320,64},{352,96},{384,128},{416,160},{448,192},{... | collective-permute-start | bytes 589832 | tf_op jit(solution)/shard_map/ppermute | solution.py:329
  57.2 12.5 %collective-permute-start.10 = (bf16[768,256]{1,0:T(8,128)(2,1)S(1)}, bf16[768,256]{1,0:T(8,128)(2,1)S(1)}, u32[]{:S(2)}, u32[]{:S(2)}) collective-permute-start(bf16[768,256]{1,0:T(8,128)(2,1)S(1)} %collective-permute-done.9.refs_1_.refs_2_), channel_id=1, source_target_pairs={{32,0},{64,32},{96,64},{128,96},{160,128},{192,160},{224,192},{0,2... | collective-permute-start | bytes 1179656 | tf_op jit(solution)/shard_map/ppermute | solution.py:325
  62.5 12.5 %collective-permute-start.6 = (bf16[768,256]{1,0:T(8,128)(2,1)S(1)}, bf16[768,256]{1,0:T(8,128)(2,1)S(1)}, u32[]{:S(2)}, u32[]{:S(2)}) collective-permute-start(bf16[768,256]{1,0:T(8,128)(2,1)S(1)} %collective-permute-done.5.refs_0_.refs_1_), channel_id=1, source_target_pairs={{0,32},{32,64},{64,96},{96,128},{128,160},{160,192},{192,224},{224... | collective-permute-start | bytes 1179656 | tf_op jit(solution)/shard_map/ppermute | solution.py:324
  69.7 11.3 %collective-permute-start.11 = (bf16[768,256]{1,0:T(8,128)(2,1)S(1)}, bf16[768,256]{1,0:T(8,128)(2,1)S(1)}, u32[]{:S(2)}, u32[]{:S(2)}) collective-permute-start(bf16[768,256]{1,0:T(8,128)(2,1)S(1)} %collective-permute-done.10.refs_1_), channel_id=1, source_target_pairs={{32,0},{64,32},{96,64},{128,96},{160,128},{192,160},{224,192},{0,2... | collective-permute-start | bytes 1179656 | tf_op jit(solution)/shard_map/ppermute | solution.py:325
  75.0 11.0 %collective-permute-start.7 = (bf16[768,256]{1,0:T(8,128)(2,1)S(1)}, bf16[768,256]{1,0:T(8,128)(2,1)S(1)}, u32[]{:S(2)}, u32[]{:S(2)}) collective-permute-start(bf16[768,256]{1,0:T(8,128)(2,1)S(1)} %collective-permute-done.6.refs_0_), channel_id=1, source_target_pairs={{0,32},{32,64},{64,96},{96,128},{128,160},{160,192},{192,224},{224... | collective-permute-start | bytes 1179656 | tf_op jit(solution)/shard_map/ppermute | solution.py:324
  87.0 12.4 %collective-permute-start.13 = (bf16[768,128]{1,0:T(8,128)(2,1)S(1)}, bf16[768,128]{1,0:T(8,128)(2,1)S(1)}, u32[]{:S(2)}, u32[]{:S(2)}) collective-permute-start(bf16[768,128]{1,0:T(8,128)(2,1)S(1)} %shard_map.63), channel_id=1, source_target_pairs={{0,256},{32,288},{64,320},{96,352},{128,384},{160,416},{192,448},{... | collective-permute-start | bytes 589832 | tf_op jit(solution)/shard_map/ppermute | solution.py:336
  96.8 6.0 %collective-permute-start.8 = (bf16[768,256]{1,0:T(8,128)(2,1)S(1)}, bf16[768,256]{1,0:T(8,128)(2,1)S(1)}, u32[]{:S(2)}, u32[]{:S(2)}) collective-permute-start(bf16[768,256]{1,0:T(8,128)(2,1)S(1)} %collective-permute-done.7.refs_0_), channel_id=1, source_target_pairs={{96,128},{128,160},{160,192},{192,224},{0,288},{32,320},{64,352},{... | collective-permute-start | bytes 1179656 | tf_op jit(solution)/shard_map/ppermute | solution.py:326
  102.8 19.8 %copy-start.1 = (bf16[512,1024]{1,0:T(8,128)(2,1)S(1)}, bf16[512,1024]{1,0:T(8,128)(2,1)}, u32[]{:S(2)}) copy-start(bf16[512,1024]{1,0:T(8,128)(2,1)} %copy-done) | copy-start | bytes 3145732

commit v10 on v8

--- a/solution.py
+++ b/solution.py
@@ -30,7 +30,7 @@
     return pltpu.CompilerParams(vmem_limit_bytes=mib * 1024 * 1024)
 
 
-def pick_kernel(shard_ref, slot_ref, ingest_ref, out_ref, buf, sems):
+def pick_kernel(shard_ref, slot_ref, ingest_ref, unit_ref, row_ref, buf, sems):
     me = lax.axis_index("batch")
     copies = []
     for g in range(GROUPS):
@@ -49,16 +49,19 @@
             copies.append(copy)
     for at, copy in enumerate(copies):
         copy.wait()
-        out_ref[at] = buf[at].reshape(BLOCK, 4 * HD)
+        flat = buf[at].reshape(BLOCK, 4 * HD)
+        unit_ref[at] = flat[:, HD : 3 * HD]
+        row_ref[at, :, :HD] = flat[:, :HD]
+        row_ref[at, :, HD:] = flat[:, 3 * HD :]
 
 
 def pick(shards, slots, ingested):
     count = GROUPS * CAPACITY
     return pl.pallas_call(
         pick_kernel,
-        out_shape=jax.ShapeDtypeStruct((count, BLOCK, 4 * HD), jnp.bfloat16),
+        out_shape=[jax.ShapeDtypeStruct((count, BLOCK, 2 * HD), jnp.bfloat16)] * 2,
         in_specs=[SMEM, SMEM, ANY],
-        out_specs=VMEM,
+        out_specs=[VMEM] * 2,
         scratch_shapes=[
             pltpu.VMEM((count, BLOCK, 4, HD), jnp.bfloat16),
             pltpu.SemaphoreType.DMA((count,)),
@@ -77,22 +80,36 @@
         yield slice(k * BLOCK, (k + 1) * BLOCK), shards[k] * CAPACITY + rank
 
 
-def order_kernel(shard_ref, in_ref, unit_ref, query_ref, update_ref):
+def order_unit_kernel(shard_ref, in_ref, unit_ref):
+    for rows, at in block_places(shard_ref):
+        unit_ref[rows, :] = in_ref[at]
+
+
+def order_unit(shards, blocks):
+    return pl.pallas_call(
+        order_unit_kernel,
+        out_shape=jax.ShapeDtypeStruct((ROWS, 2 * HD), jnp.bfloat16),
+        in_specs=[SMEM, VMEM],
+        out_specs=VMEM,
+        compiler_params=params(),
+    )(shards, blocks)
+
+
+def order_rows_kernel(shard_ref, in_ref, *refs):
+    query_ref, update_ref = refs[-2:]
     for rows, at in block_places(shard_ref):
         query_ref[rows, :] = in_ref[at, :, :HD]
-        unit_ref[rows, :] = in_ref[at, :, HD : 3 * HD]
-        update_ref[rows, :] = in_ref[at, :, 3 * HD :]
-
-
-def in_order(shards, blocks):
-    shape = jax.ShapeDtypeStruct((ROWS, HD), jnp.bfloat16)
-    return pl.pallas_call(
-        order_kernel,
-        out_shape=[jax.ShapeDtypeStruct((ROWS, 2 * HD), jnp.bfloat16), shape, shape],
-        in_specs=[SMEM, VMEM],
-        out_specs=[VMEM] * 3,
-        compiler_params=params(),
-    )(shards, blocks)
+        update_ref[rows, :] = in_ref[at, :, HD:]
+
+
+def order_rows(shards, blocks, earlier):
+    return pl.pallas_call(
+        order_rows_kernel,
+        out_shape=[jax.ShapeDtypeStruct((ROWS, HD), jnp.bfloat16)] * 2,
+        in_specs=[SMEM, VMEM] + [ANY] * len(earlier),
+        out_specs=[VMEM] * 2,
+        compiler_params=params(),
+    )(shards, blocks, *earlier)
 
 
 def unit_owner(stream, step):
@@ -175,22 +192,22 @@
     add_units(ends, me * ROWS, q_ref, list(zip(owners, units)), acc_ref)
 
 
-def estimate(units):
+def estimate(units, weight=WEIGHT):
     return pl.CostEstimate(
-        flops=WEIGHT * 4 * ROWS * ROWS * HD * units,
+        flops=weight * 4 * ROWS * ROWS * HD * units,
         bytes_accessed=1 << 20,
         transcendentals=ROWS * ROWS * units,
     )
 
 
-def attend(hist, q, units, names, acc=None):
+def attend(hist, q, units, names, acc=None, weight=WEIGHT):
     first = acc is None
     return pl.pallas_call(
         functools.partial(attend_kernel, names, first),
         out_shape=jax.ShapeDtypeStruct((ROWS, HD), jnp.float32),
         in_specs=[SMEM] + [VMEM] * (1 + len(units) + (0 if first else 1)),
         out_specs=VMEM,
-        cost_estimate=estimate(len(units)),
+        cost_estimate=estimate(len(units), weight),
         compiler_params=params(),
     )(hist, q, *units, *(() if first else (acc,)))
 
@@ -288,6 +305,7 @@
 
 CORE = [(h, h ^ 1) for h in range(HEADS)]
 X_EVEN = [(h, near_heads(h)[1]) for h in range(HEADS)]
+X_FAR = [(h, near_heads(h)[3]) for h in range(HEADS)]
 X_ODD = [(h, near_heads(h)[2]) for h in range(HEADS)]
 UP = [(i, i + 1) for i in range(CTXS - 1)]
 DOWN = [(i, i // PLANE * PLANE + (i - 1) % PLANE) for i in range(CTXS)]
@@ -295,13 +313,8 @@
 RETURN = [(i, i + PLANE) for i in range(PLANE)]
 
 
-def gather_w(w):
-    cross = functools.partial(lax.ppermute, axis_name="head")
-    half = HD // 2
-    even, odd = cross(w, perm=X_EVEN), cross(w, perm=X_ODD)
-    far = [cross(odd[:half], perm=X_EVEN), cross(even[half:], perm=X_ODD)]
-    mine = jnp.concatenate([w, even, odd, *far])
-    return mine, cross(mine, perm=CORE)
+def gather_near(w):
+    return [lax.ppermute(w, "head", perm) for perm in (X_EVEN, X_ODD, X_FAR)]
 
 
 def body(ingest, src_shard, src_slot, hist_len, w_out):
@@ -311,22 +324,28 @@
     def to_all(x):
         return lax.all_to_all(x, "head", 0, 0, tiled=True)
 
-    blocks = pick(shards, slots, ingested)
-    w_late, blocks = lax.optimization_barrier((w_out, blocks))
-    arrived = lax.all_to_all(blocks, "batch", split_axis=0, concat_axis=0, tiled=True)
-    mine, theirs = gather_w(w_late)
-    mine, theirs, arrived = lax.optimization_barrier((mine, theirs, arrived))
-    own, q, update = in_order(shards, arrived)
+    def to_owners(x):
+        return lax.all_to_all(x, "batch", split_axis=0, concat_axis=0, tiled=True)
+
+    unit_blocks, row_blocks = pick(shards, slots, ingested)
+    w_late, unit_blocks = lax.optimization_barrier((w_out, unit_blocks))
+    *near, row_blocks = lax.optimization_barrier((*gather_near(w_late), row_blocks))
+    own = order_unit(shards, to_owners(unit_blocks))
+    mine = jnp.concatenate([w_late, *near])
+    theirs = lax.ppermute(mine, "head", CORE)
+    row_blocks = to_owners(row_blocks)
     up, down = [own], [own]
     for step in range(4):
         up.append(move(up[-1], perm=UP))
         if step < 3:
             down.append(move(down[-1], perm=DOWN))
+    q, update = order_rows(shards, row_blocks, (up[2], down[2]))
     lent_q = move(q, perm=LEND)
-    acc = attend(hist_len, q, (own,), (("up", 0),))
-    acc = attend(hist_len, q, (up[1], down[1]), (("up", 1), ("down", 1)), acc)
+    acc = attend(
+        hist_len, q, (own, up[1], down[1]), (("up", 0), ("up", 1), ("down", 1)), None, 1
+    )
     lent = attend_lent(hist_len, lent_q, (own, down[1]), (("down", 0), ("down", 1)))
-    acc = attend(hist_len, q, (up[2], down[2]), (("up", 2), ("down", 2)), acc)
+    acc = attend(hist_len, q, (up[2], down[2]), (("up", 2), ("down", 2)), acc, 2)
     lent = attend_lent(
         hist_len, lent_q, (down[2], down[3]), (("down", 2), ("down", 3)), lent, final=True
     )

time: 131 us -> 134 us (1.023)
  the two profiles are of different devices: /device:TPU:64 before, /device:TPU:56 now
where the time goes in v10:
time: 134 us; the launch traced here: 133 us
  starting transfers between devices  65.9 us (49%)
  waiting for transfers between devices  31.6 us (24%)
  Pallas kernels  25.7 us (19%)
  blocking collectives  9.23 us (7%)
    ppermute x4, starting transfers between devices, body(): up.append(move(up[-1], perm=UP))  20.9 us
    all_to_all x2, starting transfers between devices, to_owners(): return lax.all_to_all(x, 'batch', split_axis=0, concat_axis=0, tiled=True)  17.8 us
    ppermute x4, waiting for transfers between devices, body(): up.append(move(up[-1], perm=UP))  14.4 us
    pallas_call x3, Pallas kernels, attend(): pl.pallas_call(functools.partial(attend_kernel, names, first), out_shape=...  13.9 us
    ppermute x3, starting transfers between devices, gather_near(): return [lax.ppermute(w, 'head', perm) for perm in (X_EVEN, X_ODD, X_FAR)]  9.89 us
    all_to_all x1, blocking collectives, to_all(): return lax.all_to_all(x, 'head', 0, 0, tiled=True)  9.23 us
    ppermute x3, starting transfers between devices, body(): down.append(move(down[-1], perm=DOWN))  8.44 us
    ppermute x3, waiting for transfers between devices, gather_near(): return [lax.ppermute(w, 'head', perm) for perm in (X_EVEN, X_ODD, X_FAR)]  7.17 us
  transfers between devices with their start and end apart: 16, of which 8 were waited for; matrix products, arithmetic and copies ran while one was open for 0% of the time, Pallas kernels for 16%

profile of v10, /device:TPU:56, one launch (start us, length us, event | category | flops | bytes accessed | tf_op | source)
XLA Modules:
  0.0 133.5 jit_solution(3202040732196300242)
XLA Ops:
  0.0 4.3 %shard_map.55 = (bf16[12,128,256]{2,1,0:T(8,128)(2,1)}, bf16[12,128,256]{2,1,0:T(8,128)(2,1)}) custom-call(s32[4,6]{1,0:T(4,128)} %bitcast.5, s32[4,6]{1,0:T(4,128)} %bitcast.10, bf16[12,128,4,128]{3,2,1,0:T(4,128)(2,1)} %bitcast.8), custom_call_target="tpu_custom_call" | custom-call | tf_op jit(solution)/shard_map/pallas_call | solution.py:60
  4.4 10.0 %all-to-all-start.1 = ((bf16[12,128,256]{2,1,0:T(8,128)(2,1)}), bf16[12,128,256]{2,1,0:T(8,128)(2,1)S(1)}, u32[]{:S(2)}, u32[]{:S(2)}) async-start(bf16[12,128,256]{2,1,0:T(8,128)(2,1)} %get-tuple-element.19), calls=%async_computation.1 | async-start | bytes 1572864 | tf_op jit(solution)/shard_map/all_to_all | solution.py:328
  14.3 4.9 %collective-permute-start.2 = (bf16[128,1024]{1,0:T(8,128)(2,1)S(1)}, bf16[128,1024]{1,0:T(8,128)(2,1)S(1)}, u32[]{:S(2)}, u32[]{:S(2)}) collective-permute-start(bf16[128,1024]{1,0:T(8,128)(2,1)S(1)} %copy-done.2), channel_id=1, source_target_pairs={{0,16},{4,20},{8,24},{12,28},{16,0},{20,4},{24,8},{28,12},{1,17},{... | collective-permute-start | bytes 786440 | tf_op jit(solution)/shard_map/ppermute | solution.py:317
  19.3 3.0 %collective-permute-start.1 = (bf16[128,1024]{1,0:T(8,128)(2,1)S(1)}, bf16[128,1024]{1,0:T(8,128)(2,1)S(1)}, u32[]{:S(2)}, u32[]{:S(2)}) collective-permute-start(bf16[128,1024]{1,0:T(8,128)(2,1)S(1)} %copy-done.2), channel_id=1, source_target_pairs={{0,24},{4,28},{8,16},{12,20},{16,8},{20,12},{24,0},{28,4},{1,25},{... | collective-permute-start | bytes 786440 | tf_op jit(solution)/shard_map/ppermute | solution.py:317
  22.3 1.9 %collective-permute-start = (bf16[128,1024]{1,0:T(8,128)(2,1)S(1)}, bf16[128,1024]{1,0:T(8,128)(2,1)S(1)}, u32[]{:S(2)}, u32[]{:S(2)}) collective-permute-start(bf16[128,1024]{1,0:T(8,128)(2,1)S(1)} %copy-done.2), channel_id=1, source_target_pairs={{0,8},{4,12},{8,0},{12,4},{16,24},{20,28},{24,16},{28,20},{1,9},{5... | collective-permute-start | bytes 786440 | tf_op jit(solution)/shard_map/ppermute | solution.py:317
  25.6 5.5 %collective-permute-done.1 = bf16[128,1024]{1,0:T(8,128)(2,1)S(1)} collective-permute-done((bf16[128,1024]{1,0:T(8,128)(2,1)S(1)}, bf16[128,1024]{1,0:T(8,128)(2,1)S(1)}, u32[]{:S(2)}, u32[]{:S(2)}) %collective-permute-start.1) | collective-permute-done | bytes 262176 | tf_op jit(solution)/shard_map/ppermute | solution.py:317
  31.4 7.8 %all-to-all-start = ((bf16[12,128,256]{2,1,0:T(8,128)(2,1)}), bf16[12,128,256]{2,1,0:T(8,128)(2,1)S(1)}, u32[]{:S(2)}, u32[]{:S(2)}) async-start(bf16[12,128,256]{2,1,0:T(8,128)(2,1)} %get-tuple-element.18), calls=%async_computation | async-start | bytes 1572864 | tf_op jit(solution)/shard_map/all_to_all | solution.py:328
  39.9 3.9 %collective-permute-start.5 = (bf16[768,256]{1,0:T(8,128)(2,1)S(1)}, bf16[768,256]{1,0:T(8,128)(2,1)}, u32[]{:S(2)}, u32[]{:S(2)}) collective-permute-start(bf16[768,256]{1,0:T(8,128)(2,1)S(1)} %shard_map.56.refs_0_), channel_id=1, source_target_pairs={{0,224},{32,0},{64,32},{96,64},{128,96},{160,128},{192,160},{224,1... | collective-permute-start | bytes 1179656 | tf_op jit(solution)/shard_map/ppermute | solution.py:341
  43.7 4.9 %collective-permute-start.3 = (bf16[768,256]{1,0:T(8,128)(2,1)S(1)}, bf16[768,256]{1,0:T(8,128)(2,1)}, u32[]{:S(2)}, u32[]{:S(2)}) collective-permute-start(bf16[768,256]{1,0:T(8,128)(2,1)S(1)} %shard_map.56.refs_0_), channel_id=1, source_target_pairs={{0,32},{32,64},{64,96},{96,128},{128,160},{160,192},{192,224},{224... | collective-permute-start | bytes 1179656 | tf_op jit(solution)/shard_map/ppermute | solution.py:339
  48.7 3.2 %collective-permute-done.5.refs_2_.refs_1_ = bf16[768,256]{1,0:T(8,128)(2,1)} collective-permute-done((bf16[768,256]{1,0:T(8,128)(2,1)S(1)}, bf16[768,256]{1,0:T(8,128)(2,1)}, u32[]{:S(2)}, u32[]{:S(2)}) %collective-permute-start.5) | collective-permute-done | bytes 393248 | tf_op jit(solution)/shard_map/ppermute | solution.py:341
  51.9 2.7 %collective-permute-start.6 = (bf16[768,256]{1,0:T(8,128)(2,1)}, bf16[768,256]{1,0:T(8,128)(2,1)}, u32[]{:S(2)}, u32[]{:S(2)}) collective-permute-start(bf16[768,256]{1,0:T(8,128)(2,1)} %collective-permute-done.5.refs_2_.refs_1_), channel_id=1, source_target_pairs={{0,224},{32,0},{64,32},{96,64},{128,96},{160,128},{192,160},{224,1... | collective-permute-start | bytes 1179656 | tf_op jit(solution)/shard_map/ppermute | solution.py:341
  54.6 6.1 %collective-permute-done.3.refs_1_ = bf16[768,256]{1,0:T(8,128)(2,1)} collective-permute-done((bf16[768,256]{1,0:T(8,128)(2,1)S(1)}, bf16[768,256]{1,0:T(8,128)(2,1)}, u32[]{:S(2)}, u32[]{:S(2)}) %collective-permute-start.3) | collective-permute-done | bytes 393248 | tf_op jit(solution)/shard_map/ppermute | solution.py:339
  60.7 6.6 %collective-permute-start.4 = (bf16[768,256]{1,0:T(8,128)(2,1)}, bf16[768,256]{1,0:T(8,128)(2,1)}, u32[]{:S(2)}, u32[]{:S(2)}) collective-permute-start(bf16[768,256]{1,0:T(8,128)(2,1)} %collective-permute-done.3.refs_1_), channel_id=1, source_target_pairs={{0,32},{32,64},{64,96},{96,128},{128,160},{160,192},{192,224},{224... | collective-permute-start | bytes 1179656 | tf_op jit(solution)/shard_map/ppermute | solution.py:339
  69.4 4.2 %collective-permute-done.4.refs_0_ = bf16[768,256]{1,0:T(8,128)(2,1)} collective-permute-done((bf16[768,256]{1,0:T(8,128)(2,1)}, bf16[768,256]{1,0:T(8,128)(2,1)}, u32[]{:S(2)}, u32[]{:S(2)}) %collective-permute-start.4) | collective-permute-done | bytes 393248 | tf_op jit(solution)/shard_map/ppermute | solution.py:339
  77.6 7.2 %collective-permute-start.7 = (bf16[768,256]{1,0:T(8,128)(2,1)}, bf16[768,256]{1,0:T(8,128)(2,1)S(1)}, u32[]{:S(2)}, u32[]{:S(2)}) collective-permute-start(bf16[768,256]{1,0:T(8,128)(2,1)} %collective-permute-done.4.refs_0_), channel_id=1, source_target_pairs={{0,32},{32,64},{64,96},{96,128},{128,160},{160,192},{192,224},{224... | collective-permute-start | bytes 1179656 | tf_op jit(solution)/shard_map/ppermute | solution.py:339
  84.8 6.2 %shard_map.58.refs_2_ = f32[768,128]{1,0:T(8,128)S(1)} custom-call(s32[1,4]{1,0:T(1,128)S(1)} %copy-done.1, bf16[768,128]{1,0:T(8,128)(2,1)S(1)} %get-tuple-element.20.q_ref, bf16[768,256]{1,0:T(8,128)(2,1)S(1)} %shard_map.56.refs_0_, bf16[768,256]{1,0:T(8,128)(2,1)} %collective-permute-done.3.refs_1_, bf16[768,256]{1,0:T(8,128)(2,1)} %collective-permute-done.5.refs_2_.refs_1_), custom_call_target="tpu_custom_call" | custom-call | flops 905969664 | bytes 1048576 | tf_op jit(solution)/shard_map/pallas_call | solution.py:205
  91.0 4.1 %shard_map.59.refs_2_ = f32[768,128]{1,0:T(8,128)S(1)} custom-call(s32[1,4]{1,0:T(1,128)S(1)} %copy-done.1, bf16[768,128]{1,0:T(8,128)(2,1)S(1)} %get-tuple-element.20.q_ref, bf16[768,256]{1,0:T(8,128)(2,1)} %collective-permute-done.4.refs_0_, bf16[768,256]{1,0:T(8,128)(2,1)} %collective-permute-done.6.refs_1_.refs_0_, f32[768,128]{1,0:T(8,128)S(1)} %shard_map.58.refs_2_), custom_call_target="tpu_custom_call" | custom-call | flops 1207959552 | bytes 1048576 | tf_op jit(solution)/shard_map/pallas_call | solution.py:205
  99.2 2.1 %collective-permute-start.8 = (bf16[768,256]{1,0:T(8,128)(2,1)S(1)}, bf16[768,256]{1,0:T(8,128)(2,1)S(1)}, u32[]{:S(2)}, u32[]{:S(2)}) collective-permute-start(bf16[768,256]{1,0:T(8,128)(2,1)S(1)} %collective-permute-done.7.refs_0_), channel_id=1, source_target_pairs={{0,32},{32,64},{64,96},{96,128},{128,160},{160,192},{192,224},{224... | collective-permute-start | bytes 1179656 | tf_op jit(solution)/shard_map/ppermute | solution.py:339
  101.3 3.6 %shard_map.60.refs_1_ = f32[768,128]{1,0:T(8,128)S(1)} custom-call(s32[1,4]{1,0:T(1,128)S(1)} %copy-done.1, bf16[768,128]{1,0:T(8,128)(2,1)S(1)} %get-tuple-element.20.q_ref, bf16[768,256]{1,0:T(8,128)(2,1)S(1)} %collective-permute-done.7.refs_0_, bf16[768,256]{1,0:T(8,128)(2,1)S(1)} %collective-permute-done.9.refs_1_, f32[768,128]{1,0:T(8,128)S(1)} %shard_map.59.refs_2_), custom_call_target="tpu_custom_call" | custom-call | flops 4831838208 | bytes 1048576 | tf_op jit(solution)/shard_map/pallas_call | solution.py:205
  104.9 4.0 %collective-permute-done.8.refs_0_ = bf16[768,256]{1,0:T(8,128)(2,1)S(1)} collective-permute-done((bf16[768,256]{1,0:T(8,128)(2,1)S(1)}, bf16[768,256]{1,0:T(8,128)(2,1)S(1)}, u32[]{:S(2)}, u32[]{:S(2)}) %collective-permute-start.8) | collective-permute-done | bytes 393248 | tf_op jit(solution)/shard_map/ppermute | solution.py:339
  108.9 3.1 %shard_map.63 = bf16[768,128]{1,0:T(8,128)(2,1)} custom-call(s32[1,4]{1,0:T(1,128)S(1)} %copy-done.1, bf16[768,128]{1,0:T(8,128)(2,1)S(1)} %get-tuple-element.20.q_ref, bf16[768,256]{1,0:T(8,128)(2,1)S(1)} %collective-permute-done.8.refs_0_, f32[768,128]{1,0:T(8,128)S(1)} %shard_map.60.refs_1_, bf16[768,128]{1,0:T(8,128)(2,1)S(1)} %collective-permute-done.11.refs_2_, ...), custom_call_target="tpu_custom_call" | custom-call | flops 2415919104 | bytes 1048576 | tf_op jit(solution)/shard_map/pallas_call | solution.py:267
  112.0 4.3 %all-to-all-start.2 = ((bf16[8,96,128]{2,1,0:T(8,128)(2,1)}), bf16[8,96,128]{2,1,0:T(8,128)(2,1)S(1)}, u32[]{:S(2)}, u32[]{:S(2)}) async-start(bf16[8,96,128]{2,1,0:T(8,128)(2,1)} %bitcast.3), calls=%async_computation.2 | async-start | bytes 393216 | tf_op jit(solution)/shard_map/all_to_all | solution.py:325
  116.3 6.8 %all-to-all-done.2.rows_ref = bf16[8,96,128]{2,1,0:T(8,128)(2,1)S(1)} async-done(((bf16[8,96,128]{2,1,0:T(8,128)(2,1)}), bf16[8,96,128]{2,1,0:T(8,128)(2,1)S(1)}, u32[]{:S(2)}, u32[]{:S(2)}) %all-to-all-start.2) | async-done | bytes 196640 | tf_op jit(solution)/shard_map/all_to_all | solution.py:325
  123.6 9.2 %all_to_all.20 = bf16[8,96,128]{2,1,0:T(8,128)(2,1)S(1)} all-to-all(bf16[8,96,128]{2,1,0:T(8,128)(2,1)S(1)} %shard_map.64), channel_id=1, replica_groups=mesh['ctx'=16,'head'=8,'batch'=4] {'head'}, dimensions={0} | all-to-all | bytes 393216 | tf_op jit(solution)/shard_map/all_to_all | solution.py:325
  (30 shorter events, 13.3 us)
Async XLA Ops:
  0.0 14.3 %copy-start.2 = (bf16[128,1024]{1,0:T(8,128)(2,1)S(1)}, bf16[128,1024]{1,0:T(8,128)(2,1)}, u32[]{:S(2)}) copy-start(bf16[128,1024]{1,0:T(8,128)(2,1)} %param.9) | copy-start | bytes 786436
  4.3 34.9 %copy-start = (s32[1,4,6]{2,1,0:T(4,128)S(1)}, s32[1,4,6]{2,1,0:T(4,128)}, u32[]{:S(2)}) copy-start(s32[1,4,6]{2,1,0:T(4,128)} %param.6) | copy-start | bytes 292
  4.4 27.1 %all-to-all-start.1 = ((bf16[12,128,256]{2,1,0:T(8,128)(2,1)}), bf16[12,128,256]{2,1,0:T(8,128)(2,1)S(1)}, u32[]{:S(2)}, u32[]{:S(2)}) async-start(bf16[12,128,256]{2,1,0:T(8,128)(2,1)} %get-tuple-element.19), calls=%async_computation.1 | async-start | bytes 1572864 | tf_op jit(solution)/shard_map/all_to_all | solution.py:328
  14.3 11.3 %collective-permute-start.2 = (bf16[128,1024]{1,0:T(8,128)(2,1)S(1)}, bf16[128,1024]{1,0:T(8,128)(2,1)S(1)}, u32[]{:S(2)}, u32[]{:S(2)}) collective-permute-start(bf16[128,1024]{1,0:T(8,128)(2,1)S(1)} %copy-done.2), channel_id=1, source_target_pairs={{0,16},{4,20},{8,24},{12,28},{16,0},{20,4},{24,8},{28,12},{1,17},{... | collective-permute-start | bytes 786440 | tf_op jit(solution)/shard_map/ppermute | solution.py:317
  19.3 11.8 %collective-permute-start.1 = (bf16[128,1024]{1,0:T(8,128)(2,1)S(1)}, bf16[128,1024]{1,0:T(8,128)(2,1)S(1)}, u32[]{:S(2)}, u32[]{:S(2)}) collective-permute-start(bf16[128,1024]{1,0:T(8,128)(2,1)S(1)} %copy-done.2), channel_id=1, source_target_pairs={{0,24},{4,28},{8,16},{12,20},{16,8},{20,12},{24,0},{28,4},{1,25},{... | collective-permute-start | bytes 786440 | tf_op jit(solution)/shard_map/ppermute | solution.py:317
  22.3 9.1 %collective-permute-start = (bf16[128,1024]{1,0:T(8,128)(2,1)S(1)}, bf16[128,1024]{1,0:T(8,128)(2,1)S(1)}, u32[]{:S(2)}, u32[]{:S(2)}) collective-permute-start(bf16[128,1024]{1,0:T(8,128)(2,1)S(1)} %copy-done.2), channel_id=1, source_target_pairs={{0,8},{4,12},{8,0},{12,4},{16,24},{20,28},{24,16},{28,20},{1,9},{5... | collective-permute-start | bytes 786440 | tf_op jit(solution)/shard_map/ppermute | solution.py:317
  31.4 38.0 %all-to-all-start = ((bf16[12,128,256]{2,1,0:T(8,128)(2,1)}), bf16[12,128,256]{2,1,0:T(8,128)(2,1)S(1)}, u32[]{:S(2)}, u32[]{:S(2)}) async-start(bf16[12,128,256]{2,1,0:T(8,128)(2,1)} %get-tuple-element.18), calls=%async_computation | async-start | bytes 1572864 | tf_op jit(solution)/shard_map/all_to_all | solution.py:328
  39.9 12.0 %collective-permute-start.5 = (bf16[768,256]{1,0:T(8,128)(2,1)S(1)}, bf16[768,256]{1,0:T(8,128)(2,1)}, u32[]{:S(2)}, u32[]{:S(2)}) collective-permute-start(bf16[768,256]{1,0:T(8,128)(2,1)S(1)} %shard_map.56.refs_0_), channel_id=1, source_target_pairs={{0,224},{32,0},{64,32},{96,64},{128,96},{160,128},{192,160},{224,1... | collective-permute-start | bytes 1179656 | tf_op jit(solution)/shard_map/ppermute | solution.py:341
  43.7 17.0 %collective-permute-start.3 = (bf16[768,256]{1,0:T(8,128)(2,1)S(1)}, bf16[768,256]{1,0:T(8,128)(2,1)}, u32[]{:S(2)}, u32[]{:S(2)}) collective-permute-start(bf16[768,256]{1,0:T(8,128)(2,1)S(1)} %shard_map.56.refs_0_), channel_id=1, source_target_pairs={{0,32},{32,64},{64,96},{96,128},{128,160},{160,192},{192,224},{224... | collective-permute-start | bytes 1179656 | tf_op jit(solution)/shard_map/ppermute | solution.py:339
  51.9 17.5 %collective-permute-start.6 = (bf16[768,256]{1,0:T(8,128)(2,1)}, bf16[768,256]{1,0:T(8,128)(2,1)}, u32[]{:S(2)}, u32[]{:S(2)}) collective-permute-start(bf16[768,256]{1,0:T(8,128)(2,1)} %collective-permute-done.5.refs_2_.refs_1_), channel_id=1, source_target_pairs={{0,224},{32,0},{64,32},{96,64},{128,96},{160,128},{192,160},{224,1... | collective-permute-start | bytes 1179656 | tf_op jit(solution)/shard_map/ppermute | solution.py:341
  60.7 13.0 %collective-permute-start.4 = (bf16[768,256]{1,0:T(8,128)(2,1)}, bf16[768,256]{1,0:T(8,128)(2,1)}, u32[]{:S(2)}, u32[]{:S(2)}) collective-permute-start(bf16[768,256]{1,0:T(8,128)(2,1)} %collective-permute-done.3.refs_1_), channel_id=1, source_target_pairs={{0,32},{32,64},{64,96},{96,128},{128,160},{160,192},{192,224},{224... | collective-permute-start | bytes 1179656 | tf_op jit(solution)/shard_map/ppermute | solution.py:339
  67.4 17.4 %copy-start.1 = (s32[1,4]{1,0:T(1,128)S(1)}, s32[1,4]{1,0:T(1,128)}, u32[]{:S(2)}) copy-start(s32[1,4]{1,0:T(1,128)} %hist_ref.11) | copy-start | bytes 52
  67.5 48.8 %collective-permute-start.12 = (bf16[512,1024]{1,0:T(8,128)(2,1)S(1)}, bf16[512,1024]{1,0:T(8,128)(2,1)S(1)}, u32[]{:S(2)}, u32[]{:S(2)}) collective-permute-start(bf16[512,1024]{1,0:T(8,128)(2,1)S(1)} %constant_dynamic-update-slice_fusion.mine_ref), channel_id=1, source_target_pairs={{0,4},{4,0},{8,12},{12,8},{16,20},{20,16},{24,28},{28,24},{1,5},{5... | collective-permute-start | bytes 3145736 | tf_op jit(solution)/shard_map/ppermute | solution.py:335
  74.3 20.8 %collective-permute-start.10 = (bf16[768,128]{1,0:T(8,128)(2,1)S(1)}, bf16[768,128]{1,0:T(8,128)(2,1)S(1)}, u32[]{:S(2)}, u32[]{:S(2)}) collective-permute-start(bf16[768,128]{1,0:T(8,128)(2,1)S(1)} %get-tuple-element.20.q_ref), channel_id=1, source_target_pairs={{256,0},{288,32},{320,64},{352,96},{384,128},{416,160},{448,192},{... | collective-permute-start | bytes 589832 | tf_op jit(solution)/shard_map/ppermute | solution.py:343
  75.6 20.9 %collective-permute-start.9 = (bf16[768,256]{1,0:T(8,128)(2,1)}, bf16[768,256]{1,0:T(8,128)(2,1)S(1)}, u32[]{:S(2)}, u32[]{:S(2)}) collective-permute-start(bf16[768,256]{1,0:T(8,128)(2,1)} %collective-permute-done.6.refs_1_.refs_0_), channel_id=1, source_target_pairs={{0,224},{32,0},{64,32},{96,64},{128,96},{160,128},{192,160},{224,1... | collective-permute-start | bytes 1179656 | tf_op jit(solution)/shard_map/ppermute | solution.py:341
  77.6 21.6 %collective-permute-start.7 = (bf16[768,256]{1,0:T(8,128)(2,1)}, bf16[768,256]{1,0:T(8,128)(2,1)S(1)}, u32[]{:S(2)}, u32[]{:S(2)}) collective-permute-start(bf16[768,256]{1,0:T(8,128)(2,1)} %collective-permute-done.4.refs_0_), channel_id=1, source_target_pairs={{0,32},{32,64},{64,96},{96,128},{128,160},{160,192},{192,224},{224... | collective-permute-start | bytes 1179656 | tf_op jit(solution)/shard_map/ppermute | solution.py:339
  97.9 7.0 %collective-permute-start.11 = (bf16[768,128]{1,0:T(8,128)(2,1)S(1)}, bf16[768,128]{1,0:T(8,128)(2,1)S(1)}, u32[]{:S(2)}, u32[]{:S(2)}) collective-permute-start(bf16[768,128]{1,0:T(8,128)(2,1)S(1)} %shard_map.62), channel_id=1, source_target_pairs={{0,256},{32,288},{64,320},{96,352},{128,384},{160,416},{192,448},{... | collective-permute-start | bytes 589832 | tf_op jit(solution)/shard_map/ppermute | solution.py:352
  99.2 9.7 %collective-permute-start.8 = (bf16[768,256]{1,0:T(8,128)(2,1)S(1)}, bf16[768,256]{1,0:T(8,128)(2,1)S(1)}, u32[]{:S(2)}, u32[]{:S(2)}) collective-permute-start(bf16[768,256]{1,0:T(8,128)(2,1)S(1)} %collective-permute-done.7.refs_0_), channel_id=1, source_target_pairs={{0,32},{32,64},{64,96},{96,128},{128,160},{160,192},{192,224},{224... | collective-permute-start | bytes 1179656 | tf_op jit(solution)/shard_map/ppermute | solution.py:339
  112.0 11.2 %all-to-all-start.2 = ((bf16[8,96,128]{2,1,0:T(8,128)(2,1)}), bf16[8,96,128]{2,1,0:T(8,128)(2,1)S(1)}, u32[]{:S(2)}, u32[]{:S(2)}) async-start(bf16[8,96,128]{2,1,0:T(8,128)(2,1)} %bitcast.3), calls=%async_computation.2 | async-start | bytes 393216 | tf_op jit(solution)/shard_map/all_to_all | solution.py:325

commit v11 on v10

--- a/solution.py
+++ b/solution.py
@@ -114,9 +114,10 @@
 
 def unit_owner(stream, step):
     me = lax.axis_index("ctx")
-    if stream == "up":
+    if step == 4:
         return me - step
-    return me // PLANE * PLANE + (me % PLANE + step) % PLANE
+    ahead = step if stream == "down" else PLANE - step
+    return me // PLANE * PLANE + (me % PLANE + ahead) % PLANE
 
 
 def history_ends(hist_ref):
@@ -307,8 +308,9 @@
 X_EVEN = [(h, near_heads(h)[1]) for h in range(HEADS)]
 X_FAR = [(h, near_heads(h)[3]) for h in range(HEADS)]
 X_ODD = [(h, near_heads(h)[2]) for h in range(HEADS)]
-UP = [(i, i + 1) for i in range(CTXS - 1)]
-DOWN = [(i, i // PLANE * PLANE + (i - 1) % PLANE) for i in range(CTXS)]
+UP = [(i, i // PLANE * PLANE + (i + 1) % PLANE) for i in range(CTXS)]
+DOWN = [(j, i) for i, j in UP]
+LAST_UP = [(i % PLANE if j % PLANE < 4 else i, j) for i, j in UP if j >= 4]
 LEND = [(i + PLANE, i) for i in range(PLANE)]
 RETURN = [(i, i + PLANE) for i in range(PLANE)]
 
@@ -335,22 +337,22 @@
     theirs = lax.ppermute(mine, "head", CORE)
     row_blocks = to_owners(row_blocks)
     up, down = [own], [own]
-    for step in range(4):
+    for step in range(3):
         up.append(move(up[-1], perm=UP))
-        if step < 3:
-            down.append(move(down[-1], perm=DOWN))
-    q, update = order_rows(shards, row_blocks, (up[2], down[2]))
+        down.append(move(down[-1], perm=DOWN))
+    up.append(move(up[-1], perm=LAST_UP))
+    names = [(("up", step), ("down", step)) for step in range(4)]
+    units = list(zip(up, down))
+    q, update = order_rows(shards, row_blocks, units[2])
     lent_q = move(q, perm=LEND)
-    acc = attend(
-        hist_len, q, (own, up[1], down[1]), (("up", 0), ("up", 1), ("down", 1)), None, 1
-    )
-    lent = attend_lent(hist_len, lent_q, (own, down[1]), (("down", 0), ("down", 1)))
-    acc = attend(hist_len, q, (up[2], down[2]), (("up", 2), ("down", 2)), acc, 2)
-    lent = attend_lent(
-        hist_len, lent_q, (down[2], down[3]), (("down", 2), ("down", 3)), lent, final=True
-    )
+    early, early_names = (own, *units[1]), (("up", 0), *names[1])
+    acc = attend(hist_len, q, early, early_names, None, 1)
+    lent = attend_lent(hist_len, lent_q, early, early_names)
+    acc = attend(hist_len, q, units[2], names[2], acc, 2)
+    lent = attend_lent(hist_len, lent_q, units[2], names[2], lent)
+    lent = attend_lent(hist_len, lent_q, units[3], names[3], lent, final=True)
     lent = move(lent, perm=RETURN)
-    acc = attend(hist_len, q, (up[3], down[3]), (("up", 3), ("down", 3)), acc)
+    acc = attend(hist_len, q, units[3], names[3], acc)
     gated = attend_last(hist_len, q, (up[4],), (("up", 4),), acc, lent, update)
     rows = to_all(gated.reshape(HEADS, CHUNK, HD))
     mixed = to_all(project(rows, mine, theirs))

time: 134 us -> 128 us (0.955)
  the two profiles are of different devices: /device:TPU:56 before, /device:TPU:1 now
where the time goes in v11:
time: 128 us; the launch traced here: 127 us
  starting transfers between devices  75.6 us (59%)
  waiting for transfers between devices  23.1 us (18%)
  Pallas kernels  17.9 us (14%)
  blocking collectives  9.24 us (7%)
    all_to_all x2, starting transfers between devices, to_owners(): return lax.all_to_all(x, 'batch', split_axis=0, concat_axis=0, tiled=True)  16.9 us
    ppermute x3, starting transfers between devices, body(): down.append(move(down[-1], perm=DOWN))  13.5 us
    all_to_all x1, starting transfers between devices, to_all(): return lax.all_to_all(x, 'head', 0, 0, tiled=True)  13.2 us
    ppermute x3, starting transfers between devices, gather_near(): return [lax.ppermute(w, 'head', perm) for perm in (X_EVEN, X_ODD, X_FAR)]  9.33 us
    all_to_all x1, blocking collectives, to_all(): return lax.all_to_all(x, 'head', 0, 0, tiled=True)  9.24 us
    ppermute x3, waiting for transfers between devices, gather_near(): return [lax.ppermute(w, 'head', perm) for perm in (X_EVEN, X_ODD, X_FAR)]  7.47 us
    ppermute x1, starting transfers between devices, body(): lent = move(lent, perm=RETURN)  6.91 us
    ppermute x3, starting transfers between devices, body(): up.append(move(up[-1], perm=UP))  6.42 us
  transfers between devices with their start and end apart: 16, of which 6 were waited for; matrix products, arithmetic and copies ran while one was open for 0% of the time, Pallas kernels for 10%

profile of v11, /device:TPU:1, one launch (start us, length us, event | category | flops | bytes accessed | tf_op | source)
XLA Modules:
  0.0 127.0 jit_solution(11770975895928140252)
XLA Ops:
  0.0 4.5 %shard_map.55 = (bf16[12,128,256]{2,1,0:T(8,128)(2,1)}, bf16[12,128,256]{2,1,0:T(8,128)(2,1)}) custom-call(s32[4,6]{1,0:T(4,128)} %bitcast.5, s32[4,6]{1,0:T(4,128)} %bitcast.10, bf16[12,128,4,128]{3,2,1,0:T(4,128)(2,1)} %bitcast.8), custom_call_target="tpu_custom_call" | custom-call | tf_op jit(solution)/shard_map/pallas_call | solution.py:60
  4.5 10.5 %all-to-all-start.1 = ((bf16[12,128,256]{2,1,0:T(8,128)(2,1)}), bf16[12,128,256]{2,1,0:T(8,128)(2,1)S(1)}, u32[]{:S(2)}, u32[]{:S(2)}) async-start(bf16[12,128,256]{2,1,0:T(8,128)(2,1)} %get-tuple-element.19), calls=%async_computation.1 | async-start | bytes 1572864 | tf_op jit(solution)/shard_map/all_to_all | solution.py:330
  15.0 4.6 %collective-permute-start.2 = (bf16[128,1024]{1,0:T(8,128)(2,1)S(1)}, bf16[128,1024]{1,0:T(8,128)(2,1)S(1)}, u32[]{:S(2)}, u32[]{:S(2)}) collective-permute-start(bf16[128,1024]{1,0:T(8,128)(2,1)S(1)} %copy-done.2), channel_id=1, source_target_pairs={{0,16},{4,20},{8,24},{12,28},{16,0},{20,4},{24,8},{28,12},{1,17},{... | collective-permute-start | bytes 786440 | tf_op jit(solution)/shard_map/ppermute | solution.py:319
  19.7 2.8 %collective-permute-start.1 = (bf16[128,1024]{1,0:T(8,128)(2,1)S(1)}, bf16[128,1024]{1,0:T(8,128)(2,1)S(1)}, u32[]{:S(2)}, u32[]{:S(2)}) collective-permute-start(bf16[128,1024]{1,0:T(8,128)(2,1)S(1)} %copy-done.2), channel_id=1, source_target_pairs={{0,24},{4,28},{8,16},{12,20},{16,8},{20,12},{24,0},{28,4},{1,25},{... | collective-permute-start | bytes 786440 | tf_op jit(solution)/shard_map/ppermute | solution.py:319
  22.4 1.9 %collective-permute-start = (bf16[128,1024]{1,0:T(8,128)(2,1)S(1)}, bf16[128,1024]{1,0:T(8,128)(2,1)S(1)}, u32[]{:S(2)}, u32[]{:S(2)}) collective-permute-start(bf16[128,1024]{1,0:T(8,128)(2,1)S(1)} %copy-done.2), channel_id=1, source_target_pairs={{0,8},{4,12},{8,0},{12,4},{16,24},{20,28},{24,16},{28,20},{1,9},{5... | collective-permute-start | bytes 786440 | tf_op jit(solution)/shard_map/ppermute | solution.py:319
  25.3 6.6 %collective-permute-done.1 = bf16[128,1024]{1,0:T(8,128)(2,1)S(1)} collective-permute-done((bf16[128,1024]{1,0:T(8,128)(2,1)S(1)}, bf16[128,1024]{1,0:T(8,128)(2,1)S(1)}, u32[]{:S(2)}, u32[]{:S(2)}) %collective-permute-start.1) | collective-permute-done | bytes 262176 | tf_op jit(solution)/shard_map/ppermute | solution.py:319
  31.8 6.4 %all-to-all-start = ((bf16[12,128,256]{2,1,0:T(8,128)(2,1)}), bf16[12,128,256]{2,1,0:T(8,128)(2,1)S(1)}, u32[]{:S(2)}, u32[]{:S(2)}) async-start(bf16[12,128,256]{2,1,0:T(8,128)(2,1)} %get-tuple-element.18), calls=%async_computation | async-start | bytes 1572864 | tf_op jit(solution)/shard_map/all_to_all | solution.py:330
  38.8 5.3 %collective-permute-start.5 = (bf16[768,256]{1,0:T(8,128)(2,1)S(1)}, bf16[768,256]{1,0:T(8,128)(2,1)}, u32[]{:S(2)}, u32[]{:S(2)}) collective-permute-start(bf16[768,256]{1,0:T(8,128)(2,1)S(1)} %shard_map.56.refs_0_), channel_id=1, source_target_pairs={{32,0},{64,32},{96,64},{128,96},{160,128},{192,160},{224,192},{0,2... | collective-permute-start | bytes 1179656 | tf_op jit(solution)/shard_map/ppermute | solution.py:342
  44.2 1.9 %collective-permute-start.3 = (bf16[768,256]{1,0:T(8,128)(2,1)S(1)}, bf16[768,256]{1,0:T(8,128)(2,1)}, u32[]{:S(2)}, u32[]{:S(2)}) collective-permute-start(bf16[768,256]{1,0:T(8,128)(2,1)S(1)} %shard_map.56.refs_0_), channel_id=1, source_target_pairs={{0,32},{32,64},{64,96},{96,128},{128,160},{160,192},{192,224},{224... | collective-permute-start | bytes 1179656 | tf_op jit(solution)/shard_map/ppermute | solution.py:341
  46.1 3.8 %collective-permute-done.5.refs_2_ = bf16[768,256]{1,0:T(8,128)(2,1)} collective-permute-done((bf16[768,256]{1,0:T(8,128)(2,1)S(1)}, bf16[768,256]{1,0:T(8,128)(2,1)}, u32[]{:S(2)}, u32[]{:S(2)}) %collective-permute-start.5) | collective-permute-done | bytes 393248 | tf_op jit(solution)/shard_map/ppermute | solution.py:342
  49.9 5.4 %collective-permute-start.6 = (bf16[768,256]{1,0:T(8,128)(2,1)}, bf16[768,256]{1,0:T(8,128)(2,1)}, u32[]{:S(2)}, u32[]{:S(2)}) collective-permute-start(bf16[768,256]{1,0:T(8,128)(2,1)} %collective-permute-done.5.refs_2_), channel_id=1, source_target_pairs={{32,0},{64,32},{96,64},{128,96},{160,128},{192,160},{224,192},{0,2... | collective-permute-start | bytes 1179656 | tf_op jit(solution)/shard_map/ppermute | solution.py:342
  55.3 1.9 %collective-permute-start.4 = (bf16[768,256]{1,0:T(8,128)(2,1)}, bf16[768,256]{1,0:T(8,128)(2,1)}, u32[]{:S(2)}, u32[]{:S(2)}) collective-permute-start(bf16[768,256]{1,0:T(8,128)(2,1)} %collective-permute-done.3.refs_1_), channel_id=1, source_target_pairs={{0,32},{32,64},{64,96},{96,128},{128,160},{160,192},{192,224},{224... | collective-permute-start | bytes 1179656 | tf_op jit(solution)/shard_map/ppermute | solution.py:341
  57.3 5.8 %collective-permute-start.12 = (bf16[512,1024]{1,0:T(8,128)(2,1)S(1)}, bf16[512,1024]{1,0:T(8,128)(2,1)S(1)}, u32[]{:S(2)}, u32[]{:S(2)}) collective-permute-start(bf16[512,1024]{1,0:T(8,128)(2,1)S(1)} %constant_dynamic-update-slice_fusion.mine_ref), channel_id=1, source_target_pairs={{0,4},{4,0},{8,12},{12,8},{16,20},{20,16},{24,28},{28,24},{1,5},{5... | collective-permute-start | bytes 3145736 | tf_op jit(solution)/shard_map/ppermute | solution.py:337
  63.2 2.2 %collective-permute-done.4.refs_0_ = bf16[768,256]{1,0:T(8,128)(2,1)} collective-permute-done((bf16[768,256]{1,0:T(8,128)(2,1)}, bf16[768,256]{1,0:T(8,128)(2,1)}, u32[]{:S(2)}, u32[]{:S(2)}) %collective-permute-start.4) | collective-permute-done | bytes 393248 | tf_op jit(solution)/shard_map/ppermute | solution.py:341
  67.3 2.7 %collective-permute-start.9 = (bf16[768,256]{1,0:T(8,128)(2,1)}, bf16[768,256]{1,0:T(8,128)(2,1)S(1)}, u32[]{:S(2)}, u32[]{:S(2)}) collective-permute-start(bf16[768,256]{1,0:T(8,128)(2,1)} %collective-permute-done.6.refs_1_), channel_id=1, source_target_pairs={{32,0},{64,32},{96,64},{128,96},{160,128},{192,160},{224,192},{0,2... | collective-permute-start | bytes 1179656 | tf_op jit(solution)/shard_map/ppermute | solution.py:342
  70.0 2.6 %collective-permute-start.7 = (bf16[768,256]{1,0:T(8,128)(2,1)}, bf16[768,256]{1,0:T(8,128)(2,1)S(1)}, u32[]{:S(2)}, u32[]{:S(2)}) collective-permute-start(bf16[768,256]{1,0:T(8,128)(2,1)} %collective-permute-done.4.refs_0_), channel_id=1, source_target_pairs={{0,32},{32,64},{64,96},{96,128},{128,160},{160,192},{192,224},{224... | collective-permute-start | bytes 1179656 | tf_op jit(solution)/shard_map/ppermute | solution.py:341
  72.6 3.6 %shard_map.58.refs_2_ = f32[768,128]{1,0:T(8,128)S(1)} custom-call(s32[1,4]{1,0:T(1,128)S(1)} %copy-done.1, bf16[768,128]{1,0:T(8,128)(2,1)S(1)} %get-tuple-element.20.q_ref, bf16[768,256]{1,0:T(8,128)(2,1)S(1)} %shard_map.56.refs_0_, bf16[768,256]{1,0:T(8,128)(2,1)} %collective-permute-done.3.refs_1_, bf16[768,256]{1,0:T(8,128)(2,1)} %collective-permute-done.5.refs_2_), custom_call_target="tpu_custom_call" | custom-call | flops 905969664 | bytes 1048576 | tf_op jit(solution)/shard_map/pallas_call | solution.py:206
  81.8 6.9 %collective-permute-start.11 = (bf16[768,128]{1,0:T(8,128)(2,1)S(1)}, bf16[768,128]{1,0:T(8,128)(2,1)S(1)}, u32[]{:S(2)}, u32[]{:S(2)}) collective-permute-start(bf16[768,128]{1,0:T(8,128)(2,1)S(1)} %shard_map.63), channel_id=1, source_target_pairs={{0,256},{32,288},{64,320},{96,352},{128,384},{160,416},{192,448},{... | collective-permute-start | bytes 589832 | tf_op jit(solution)/shard_map/ppermute | solution.py:354
  88.7 2.3 %collective-permute-start.8 = (bf16[768,256]{1,0:T(8,128)(2,1)S(1)}, bf16[768,256]{1,0:T(8,128)(2,1)S(1)}, u32[]{:S(2)}, u32[]{:S(2)}) collective-permute-start(bf16[768,256]{1,0:T(8,128)(2,1)S(1)} %collective-permute-done.7.refs_0_), channel_id=1, source_target_pairs={{96,128},{128,160},{160,192},{192,224},{0,288},{32,320},{64,352},{... | collective-permute-start | bytes 1179656 | tf_op jit(solution)/shard_map/ppermute | solution.py:343
  92.0 3.8 %collective-permute-done.8.refs_0_ = bf16[768,256]{1,0:T(8,128)(2,1)S(1)} collective-permute-done((bf16[768,256]{1,0:T(8,128)(2,1)S(1)}, bf16[768,256]{1,0:T(8,128)(2,1)S(1)}, u32[]{:S(2)}, u32[]{:S(2)}) %collective-permute-start.8) | collective-permute-done | bytes 393248 | tf_op jit(solution)/shard_map/ppermute | solution.py:343
  95.8 1.7 %shard_map.64 = bf16[768,128]{1,0:T(8,128)(2,1)} custom-call(s32[1,4]{1,0:T(1,128)S(1)} %copy-done.1, bf16[768,128]{1,0:T(8,128)(2,1)S(1)} %get-tuple-element.20.q_ref, bf16[768,256]{1,0:T(8,128)(2,1)S(1)} %collective-permute-done.8.refs_0_, f32[768,128]{1,0:T(8,128)S(1)} %shard_map.60.refs_1_, bf16[768,128]{1,0:T(8,128)(2,1)S(1)} %collective-permute-done.11.refs_2_, ...), custom_call_target="tpu_custom_call" | custom-call | flops 2415919104 | bytes 1048576 | tf_op jit(solution)/shard_map/pallas_call | solution.py:268
  97.5 13.2 %all-to-all-start.2 = ((bf16[8,96,128]{2,1,0:T(8,128)(2,1)}), bf16[8,96,128]{2,1,0:T(8,128)(2,1)S(1)}, u32[]{:S(2)}, u32[]{:S(2)}) async-start(bf16[8,96,128]{2,1,0:T(8,128)(2,1)} %bitcast.3), calls=%async_computation.2 | async-start | bytes 393216 | tf_op jit(solution)/shard_map/all_to_all | solution.py:327
  110.7 5.9 %all-to-all-done.2.rows_ref = bf16[8,96,128]{2,1,0:T(8,128)(2,1)S(1)} async-done(((bf16[8,96,128]{2,1,0:T(8,128)(2,1)}), bf16[8,96,128]{2,1,0:T(8,128)(2,1)S(1)}, u32[]{:S(2)}, u32[]{:S(2)}) %all-to-all-start.2) | async-done | bytes 196640 | tf_op jit(solution)/shard_map/all_to_all | solution.py:327
  117.0 9.2 %all_to_all.20 = bf16[8,96,128]{2,1,0:T(8,128)(2,1)S(1)} all-to-all(bf16[8,96,128]{2,1,0:T(8,128)(2,1)S(1)} %shard_map.65), channel_id=1, replica_groups=mesh['ctx'=16,'head'=8,'batch'=4] {'head'}, dimensions={0} | all-to-all | bytes 393216 | tf_op jit(solution)/shard_map/all_to_all | solution.py:327
  (31 shorter events, 11.1 us)
Async XLA Ops:
  0.0 15.0 %copy-start.2 = (bf16[128,1024]{1,0:T(8,128)(2,1)S(1)}, bf16[128,1024]{1,0:T(8,128)(2,1)}, u32[]{:S(2)}) copy-start(bf16[128,1024]{1,0:T(8,128)(2,1)} %param.9) | copy-start | bytes 786436
  4.5 33.7 %copy-start = (s32[1,4,6]{2,1,0:T(4,128)S(1)}, s32[1,4,6]{2,1,0:T(4,128)}, u32[]{:S(2)}) copy-start(s32[1,4,6]{2,1,0:T(4,128)} %param.6) | copy-start | bytes 292
  4.5 27.3 %all-to-all-start.1 = ((bf16[12,128,256]{2,1,0:T(8,128)(2,1)}), bf16[12,128,256]{2,1,0:T(8,128)(2,1)S(1)}, u32[]{:S(2)}, u32[]{:S(2)}) async-start(bf16[12,128,256]{2,1,0:T(8,128)(2,1)} %get-tuple-element.19), calls=%async_computation.1 | async-start | bytes 1572864 | tf_op jit(solution)/shard_map/all_to_all | solution.py:330
  15.0 10.2 %collective-permute-start.2 = (bf16[128,1024]{1,0:T(8,128)(2,1)S(1)}, bf16[128,1024]{1,0:T(8,128)(2,1)S(1)}, u32[]{:S(2)}, u32[]{:S(2)}) collective-permute-start(bf16[128,1024]{1,0:T(8,128)(2,1)S(1)} %copy-done.2), channel_id=1, source_target_pairs={{0,16},{4,20},{8,24},{12,28},{16,0},{20,4},{24,8},{28,12},{1,17},{... | collective-permute-start | bytes 786440 | tf_op jit(solution)/shard_map/ppermute | solution.py:319
  19.7 12.2 %collective-permute-start.1 = (bf16[128,1024]{1,0:T(8,128)(2,1)S(1)}, bf16[128,1024]{1,0:T(8,128)(2,1)S(1)}, u32[]{:S(2)}, u32[]{:S(2)}) collective-permute-start(bf16[128,1024]{1,0:T(8,128)(2,1)S(1)} %copy-done.2), channel_id=1, source_target_pairs={{0,24},{4,28},{8,16},{12,20},{16,8},{20,12},{24,0},{28,4},{1,25},{... | collective-permute-start | bytes 786440 | tf_op jit(solution)/shard_map/ppermute | solution.py:319
  22.4 9.4 %collective-permute-start = (bf16[128,1024]{1,0:T(8,128)(2,1)S(1)}, bf16[128,1024]{1,0:T(8,128)(2,1)S(1)}, u32[]{:S(2)}, u32[]{:S(2)}) collective-permute-start(bf16[128,1024]{1,0:T(8,128)(2,1)S(1)} %copy-done.2), channel_id=1, source_target_pairs={{0,8},{4,12},{8,0},{12,4},{16,24},{20,28},{24,16},{28,20},{1,9},{5... | collective-permute-start | bytes 786440 | tf_op jit(solution)/shard_map/ppermute | solution.py:319
  31.8 31.3 %all-to-all-start = ((bf16[12,128,256]{2,1,0:T(8,128)(2,1)}), bf16[12,128,256]{2,1,0:T(8,128)(2,1)S(1)}, u32[]{:S(2)}, u32[]{:S(2)}) async-start(bf16[12,128,256]{2,1,0:T(8,128)(2,1)} %get-tuple-element.18), calls=%async_computation | async-start | bytes 1572864 | tf_op jit(solution)/shard_map/all_to_all | solution.py:330
  38.8 11.0 %collective-permute-start.5 = (bf16[768,256]{1,0:T(8,128)(2,1)S(1)}, bf16[768,256]{1,0:T(8,128)(2,1)}, u32[]{:S(2)}, u32[]{:S(2)}) collective-permute-start(bf16[768,256]{1,0:T(8,128)(2,1)S(1)} %shard_map.56.refs_0_), channel_id=1, source_target_pairs={{32,0},{64,32},{96,64},{128,96},{160,128},{192,160},{224,192},{0,2... | collective-permute-start | bytes 1179656 | tf_op jit(solution)/shard_map/ppermute | solution.py:342
  44.2 11.1 %collective-permute-start.3 = (bf16[768,256]{1,0:T(8,128)(2,1)S(1)}, bf16[768,256]{1,0:T(8,128)(2,1)}, u32[]{:S(2)}, u32[]{:S(2)}) collective-permute-start(bf16[768,256]{1,0:T(8,128)(2,1)S(1)} %shard_map.56.refs_0_), channel_id=1, source_target_pairs={{0,32},{32,64},{64,96},{96,128},{128,160},{160,192},{192,224},{224... | collective-permute-start | bytes 1179656 | tf_op jit(solution)/shard_map/ppermute | solution.py:341
  49.9 13.3 %collective-permute-start.6 = (bf16[768,256]{1,0:T(8,128)(2,1)}, bf16[768,256]{1,0:T(8,128)(2,1)}, u32[]{:S(2)}, u32[]{:S(2)}) collective-permute-start(bf16[768,256]{1,0:T(8,128)(2,1)} %collective-permute-done.5.refs_2_), channel_id=1, source_target_pairs={{32,0},{64,32},{96,64},{128,96},{160,128},{192,160},{224,192},{0,2... | collective-permute-start | bytes 1179656 | tf_op jit(solution)/shard_map/ppermute | solution.py:342
  55.3 10.0 %collective-permute-start.4 = (bf16[768,256]{1,0:T(8,128)(2,1)}, bf16[768,256]{1,0:T(8,128)(2,1)}, u32[]{:S(2)}, u32[]{:S(2)}) collective-permute-start(bf16[768,256]{1,0:T(8,128)(2,1)} %collective-permute-done.3.refs_1_), channel_id=1, source_target_pairs={{0,32},{32,64},{64,96},{96,128},{128,160},{160,192},{192,224},{224... | collective-permute-start | bytes 1179656 | tf_op jit(solution)/shard_map/ppermute | solution.py:341
  57.2 15.4 %copy-start.1 = (s32[1,4]{1,0:T(1,128)S(1)}, s32[1,4]{1,0:T(1,128)}, u32[]{:S(2)}) copy-start(s32[1,4]{1,0:T(1,128)} %hist_ref.13) | copy-start | bytes 52
  57.3 53.3 %collective-permute-start.12 = (bf16[512,1024]{1,0:T(8,128)(2,1)S(1)}, bf16[512,1024]{1,0:T(8,128)(2,1)S(1)}, u32[]{:S(2)}, u32[]{:S(2)}) collective-permute-start(bf16[512,1024]{1,0:T(8,128)(2,1)S(1)} %constant_dynamic-update-slice_fusion.mine_ref), channel_id=1, source_target_pairs={{0,4},{4,0},{8,12},{12,8},{16,20},{20,16},{24,28},{28,24},{1,5},{5... | collective-permute-start | bytes 3145736 | tf_op jit(solution)/shard_map/ppermute | solution.py:337
  66.0 11.7 %collective-permute-start.10 = (bf16[768,128]{1,0:T(8,128)(2,1)S(1)}, bf16[768,128]{1,0:T(8,128)(2,1)S(1)}, u32[]{:S(2)}, u32[]{:S(2)}) collective-permute-start(bf16[768,128]{1,0:T(8,128)(2,1)S(1)} %get-tuple-element.20.q_ref), channel_id=1, source_target_pairs={{256,0},{288,32},{320,64},{352,96},{384,128},{416,160},{448,192},{... | collective-permute-start | bytes 589832 | tf_op jit(solution)/shard_map/ppermute | solution.py:347
  67.3 13.5 %collective-permute-start.9 = (bf16[768,256]{1,0:T(8,128)(2,1)}, bf16[768,256]{1,0:T(8,128)(2,1)S(1)}, u32[]{:S(2)}, u32[]{:S(2)}) collective-permute-start(bf16[768,256]{1,0:T(8,128)(2,1)} %collective-permute-done.6.refs_1_), channel_id=1, source_target_pairs={{32,0},{64,32},{96,64},{128,96},{160,128},{192,160},{224,192},{0,2... | collective-permute-start | bytes 1179656 | tf_op jit(solution)/shard_map/ppermute | solution.py:342
  70.0 10.8 %collective-permute-start.7 = (bf16[768,256]{1,0:T(8,128)(2,1)}, bf16[768,256]{1,0:T(8,128)(2,1)S(1)}, u32[]{:S(2)}, u32[]{:S(2)}) collective-permute-start(bf16[768,256]{1,0:T(8,128)(2,1)} %collective-permute-done.4.refs_0_), channel_id=1, source_target_pairs={{0,32},{32,64},{64,96},{96,128},{128,160},{160,192},{192,224},{224... | collective-permute-start | bytes 1179656 | tf_op jit(solution)/shard_map/ppermute | solution.py:341
  81.8 10.2 %collective-permute-start.11 = (bf16[768,128]{1,0:T(8,128)(2,1)S(1)}, bf16[768,128]{1,0:T(8,128)(2,1)S(1)}, u32[]{:S(2)}, u32[]{:S(2)}) collective-permute-start(bf16[768,128]{1,0:T(8,128)(2,1)S(1)} %shard_map.63), channel_id=1, source_target_pairs={{0,256},{32,288},{64,320},{96,352},{128,384},{160,416},{192,448},{... | collective-permute-start | bytes 589832 | tf_op jit(solution)/shard_map/ppermute | solution.py:354
  88.7 7.1 %collective-permute-start.8 = (bf16[768,256]{1,0:T(8,128)(2,1)S(1)}, bf16[768,256]{1,0:T(8,128)(2,1)S(1)}, u32[]{:S(2)}, u32[]{:S(2)}) collective-permute-start(bf16[768,256]{1,0:T(8,128)(2,1)S(1)} %collective-permute-done.7.refs_0_), channel_id=1, source_target_pairs={{96,128},{128,160},{160,192},{192,224},{0,288},{32,320},{64,352},{... | collective-permute-start | bytes 1179656 | tf_op jit(solution)/shard_map/ppermute | solution.py:343
  97.5 19.1 %all-to-all-start.2 = ((bf16[8,96,128]{2,1,0:T(8,128)(2,1)}), bf16[8,96,128]{2,1,0:T(8,128)(2,1)S(1)}, u32[]{:S(2)}, u32[]{:S(2)}) async-start(bf16[8,96,128]{2,1,0:T(8,128)(2,1)} %bitcast.3), calls=%async_computation.2 | async-start | bytes 393216 | tf_op jit(solution)/shard_map/all_to_all | solution.py:327

commit v12 on v8

--- a/solution.py
+++ b/solution.py
@@ -19,7 +19,7 @@
 ROWS = BLOCK * PER_OWNER
 CHUNK = ROWS // HEADS
 TILE = 256
-WEIGHT = 8
+WEIGHT = 2
 HALF_SCALE = 0.5 / math.sqrt(HD)
 VMEM = pl.BlockSpec(memory_space=pltpu.VMEM)
 SMEM = pl.BlockSpec(memory_space=pltpu.SMEM)

time: 131 us -> 134 us (1.023)
  the two profiles are of different devices: /device:TPU:64 before, /device:TPU:1 now
where the time goes in v12:
time: 134 us; the launch traced here: 133 us
  starting transfers between devices  69.3 us (52%)
  waiting for transfers between devices  28.1 us (21%)
  blocking collectives  20.2 us (15%)
  Pallas kernels  13.3 us (10%)
  local copies, waits for them, and re-layouts  1.77 us (1%)
    ppermute x3, starting transfers between devices, body(): down.append(move(down[-1], perm=DOWN))  28.6 us
    all_to_all x2, blocking collectives, to_all(): return lax.all_to_all(x, 'head', 0, 0, tiled=True)  20.2 us
    all_to_all x1, starting transfers between devices, body(): lax.all_to_all(blocks, 'batch', split_axis=0, concat_axis=0, tiled=True)  11.4 us
    ppermute x1, waiting for transfers between devices, body(): lent = move(lent, perm=RETURN)  9.29 us
    ppermute x3, waiting for transfers between devices, body(): down.append(move(down[-1], perm=DOWN))  8.31 us
    ppermute x4, starting transfers between devices, body(): up.append(move(up[-1], perm=UP))  7.1 us
    ppermute x2, starting transfers between devices, gather_w(): even, odd = (cross(w, perm=X_EVEN), cross(w, perm=X_ODD))  6.43 us
    pallas_call x4, Pallas kernels, attend(): pl.pallas_call(functools.partial(attend_kernel, names, first), out_shape=...  5.52 us
  transfers between devices with their start and end apart: 15, of which 7 were waited for; matrix products, arithmetic and copies ran while one was open for 0% of the time, Pallas kernels for 5%

profile of v12, /device:TPU:1, one launch (start us, length us, event | category | flops | bytes accessed | tf_op | source)
XLA Modules:
  0.0 133.0 jit_solution(12430682893704646152)
XLA Ops:
  0.0 3.8 %shard_map.55 = bf16[12,128,512]{2,1,0:T(8,128)(2,1)} custom-call(s32[4,6]{1,0:T(4,128)} %bitcast.6, s32[4,6]{1,0:T(4,128)} %bitcast.10, bf16[12,128,4,128]{3,2,1,0:T(4,128)(2,1)} %bitcast.8), custom_call_target="tpu_custom_call" | custom-call | tf_op jit(solution)/shard_map/pallas_call | solution.py:57
  3.9 11.4 %all-to-all-start = ((bf16[12,128,512]{2,1,0:T(8,128)(2,1)}), bf16[12,128,512]{2,1,0:T(8,128)(2,1)S(1)}, u32[]{:S(2)}, u32[]{:S(2)}) async-start(bf16[12,128,512]{2,1,0:T(8,128)(2,1)} %shard_map.55), calls=%async_computation | async-start | bytes 3145728 | tf_op jit(solution)/shard_map/all_to_all | solution.py:316
  15.3 4.5 %collective-permute-start.1 = (bf16[128,1024]{1,0:T(8,128)(2,1)S(1)}, bf16[128,1024]{1,0:T(8,128)(2,1)S(1)}, u32[]{:S(2)}, u32[]{:S(2)}) collective-permute-start(bf16[128,1024]{1,0:T(8,128)(2,1)S(1)} %copy-done.4), channel_id=1, source_target_pairs={{0,24},{4,28},{8,16},{12,20},{16,8},{20,12},{24,0},{28,4},{1,25},{... | collective-permute-start | bytes 786440 | tf_op jit(solution)/shard_map/ppermute | solution.py:301
  19.8 1.9 %collective-permute-start = (bf16[128,1024]{1,0:T(8,128)(2,1)S(1)}, bf16[128,1024]{1,0:T(8,128)(2,1)S(1)}, u32[]{:S(2)}, u32[]{:S(2)}) collective-permute-start(bf16[128,1024]{1,0:T(8,128)(2,1)S(1)} %copy-done.4), channel_id=1, source_target_pairs={{0,8},{4,12},{8,0},{12,4},{16,24},{20,28},{24,16},{28,20},{1,9},{5... | collective-permute-start | bytes 786440 | tf_op jit(solution)/shard_map/ppermute | solution.py:301
  21.7 3.6 %collective-permute-done.1 = bf16[128,1024]{1,0:T(8,128)(2,1)S(1)} collective-permute-done((bf16[128,1024]{1,0:T(8,128)(2,1)S(1)}, bf16[128,1024]{1,0:T(8,128)(2,1)S(1)}, u32[]{:S(2)}, u32[]{:S(2)}) %collective-permute-start.1) | collective-permute-done | bytes 262176 | tf_op jit(solution)/shard_map/ppermute | solution.py:301
  25.4 1.9 %collective-permute-start.2 = (bf16[64,1024]{1,0:T(8,128)(2,1)S(1)}, bf16[64,1024]{1,0:T(8,128)(2,1)S(1)}, u32[]{:S(2)}, u32[]{:S(2)}) collective-permute-start(bf16[64,1024]{1,0:T(8,128)(2,1)S(1)} %slice.8), channel_id=1, source_target_pairs={{0,8},{4,12},{8,0},{12,4},{16,24},{20,28},{24,16},{28,20},{1,9},{5... | collective-permute-start | bytes 393224 | tf_op jit(solution)/shard_map/ppermute | solution.py:302
  28.3 3.5 %collective-permute-start.3 = (bf16[64,1024]{1,0:T(8,128)(2,1)S(1)}, bf16[64,1024]{1,0:T(8,128)(2,1)S(1)}, u32[]{:S(2)}, u32[]{:S(2)}) collective-permute-start(bf16[64,1024]{1,0:T(8,128)(2,1)S(1)} %slice.9), channel_id=1, source_target_pairs={{0,24},{4,28},{8,16},{12,20},{16,8},{20,12},{24,0},{28,4},{1,25},{... | collective-permute-start | bytes 393224 | tf_op jit(solution)/shard_map/ppermute | solution.py:302
  31.8 3.7 %collective-permute-done.3 = bf16[64,1024]{1,0:T(8,128)(2,1)S(1)} collective-permute-done((bf16[64,1024]{1,0:T(8,128)(2,1)S(1)}, bf16[64,1024]{1,0:T(8,128)(2,1)S(1)}, u32[]{:S(2)}, u32[]{:S(2)}) %collective-permute-start.3) | collective-permute-done | bytes 131104 | tf_op jit(solution)/shard_map/ppermute | solution.py:302
  35.5 4.9 %collective-permute-start.4 = (bf16[512,1024]{1,0:T(8,128)(2,1)S(1)}, bf16[512,1024]{1,0:T(8,128)(2,1)S(1)}, u32[]{:S(2)}, u32[]{:S(2)}) collective-permute-start(bf16[512,1024]{1,0:T(8,128)(2,1)S(1)} %constant_dynamic-update-slice_fusion.mine_ref), channel_id=1, source_target_pairs={{0,4},{4,0},{8,12},{12,8},{16,20},{20,16},{24,28},{28,24},{1,5},{5... | collective-permute-start | bytes 3145736 | tf_op jit(solution)/shard_map/ppermute | solution.py:304
  40.4 2.3 %collective-permute-done.4.theirs_ref = bf16[512,1024]{1,0:T(8,128)(2,1)S(1)} collective-permute-done((bf16[512,1024]{1,0:T(8,128)(2,1)S(1)}, bf16[512,1024]{1,0:T(8,128)(2,1)S(1)}, u32[]{:S(2)}, u32[]{:S(2)}) %collective-permute-start.4) | collective-permute-done | bytes 1048608 | tf_op jit(solution)/shard_map/ppermute | solution.py:304
  44.4 3.2 %collective-permute-start.5 = (bf16[768,256]{1,0:T(8,128)(2,1)S(1)}, bf16[768,256]{1,0:T(8,128)(2,1)S(1)}, u32[]{:S(2)}, u32[]{:S(2)}) collective-permute-start(bf16[768,256]{1,0:T(8,128)(2,1)S(1)} %get-tuple-element.17.refs_0_), channel_id=1, source_target_pairs={{0,32},{32,64},{64,96},{96,128},{128,160},{160,192},{192,224},{224... | collective-permute-start | bytes 1179656 | tf_op jit(solution)/shard_map/ppermute | solution.py:322
  47.5 14.3 %collective-permute-start.9 = (bf16[768,256]{1,0:T(8,128)(2,1)S(1)}, bf16[768,256]{1,0:T(8,128)(2,1)S(1)}, u32[]{:S(2)}, u32[]{:S(2)}) collective-permute-start(bf16[768,256]{1,0:T(8,128)(2,1)S(1)} %get-tuple-element.17.refs_0_), channel_id=1, source_target_pairs={{0,224},{32,0},{64,32},{96,64},{128,96},{160,128},{192,160},{224,1... | collective-permute-start | bytes 1179656 | tf_op jit(solution)/shard_map/ppermute | solution.py:324
  61.9 1.3 collective-permute-start.6
  63.2 5.3 %collective-permute-done.9.refs_1_ = bf16[768,256]{1,0:T(8,128)(2,1)S(1)} collective-permute-done((bf16[768,256]{1,0:T(8,128)(2,1)S(1)}, bf16[768,256]{1,0:T(8,128)(2,1)S(1)}, u32[]{:S(2)}, u32[]{:S(2)}) %collective-permute-start.9) | collective-permute-done | bytes 393248 | tf_op jit(solution)/shard_map/ppermute | solution.py:324
  68.5 6.5 %collective-permute-start.10 = (bf16[768,256]{1,0:T(8,128)(2,1)S(1)}, bf16[768,256]{1,0:T(8,128)(2,1)S(1)}, u32[]{:S(2)}, u32[]{:S(2)}) collective-permute-start(bf16[768,256]{1,0:T(8,128)(2,1)S(1)} %collective-permute-done.9.refs_1_), channel_id=1, source_target_pairs={{0,224},{32,0},{64,32},{96,64},{128,96},{160,128},{192,160},{224,1... | collective-permute-start | bytes 1179656 | tf_op jit(solution)/shard_map/ppermute | solution.py:324
  75.0 1.3 collective-permute-start.7
  77.6 3.0 %collective-permute-done.10.refs_1_.refs_0_ = bf16[768,256]{1,0:T(8,128)(2,1)S(1)} collective-permute-done((bf16[768,256]{1,0:T(8,128)(2,1)S(1)}, bf16[768,256]{1,0:T(8,128)(2,1)S(1)}, u32[]{:S(2)}, u32[]{:S(2)}) %collective-permute-start.10) | collective-permute-done | bytes 393248 | tf_op jit(solution)/shard_map/ppermute | solution.py:324
  80.7 7.8 %collective-permute-start.11 = (bf16[768,256]{1,0:T(8,128)(2,1)S(1)}, bf16[768,256]{1,0:T(8,128)(2,1)S(1)}, u32[]{:S(2)}, u32[]{:S(2)}) collective-permute-start(bf16[768,256]{1,0:T(8,128)(2,1)S(1)} %collective-permute-done.10.refs_1_.refs_0_), channel_id=1, source_target_pairs={{0,224},{32,0},{64,32},{96,64},{128,96},{160,128},{192,160},{224,1... | collective-permute-start | bytes 1179656 | tf_op jit(solution)/shard_map/ppermute | solution.py:324
  88.5 2.9 %shard_map.57.refs_2_ = f32[768,128]{1,0:T(8,128)S(1)} custom-call(s32[1,4]{1,0:T(1,128)S(1)} %copy-done.3, bf16[768,128]{1,0:T(8,128)(2,1)S(1)} %get-tuple-element.16.q_ref, bf16[768,256]{1,0:T(8,128)(2,1)S(1)} %get-tuple-element.17.refs_0_), custom_call_target="tpu_custom_call" | custom-call | flops 603979776 | bytes 1048576 | tf_op jit(solution)/shard_map/pallas_call | solution.py:188
  92.3 1.3 collective-permute-start.8
  95.4 4.2 %collective-permute-start.13 = (bf16[768,128]{1,0:T(8,128)(2,1)S(1)}, bf16[768,128]{1,0:T(8,128)(2,1)S(1)}, u32[]{:S(2)}, u32[]{:S(2)}) collective-permute-start(bf16[768,128]{1,0:T(8,128)(2,1)S(1)} %shard_map.62), channel_id=1, source_target_pairs={{0,256},{32,288},{64,320},{96,352},{128,384},{160,416},{192,448},{... | collective-permute-start | bytes 589832 | tf_op jit(solution)/shard_map/ppermute | solution.py:333
  101.3 9.3 %collective-permute-done.13.refs_2_ = bf16[768,128]{1,0:T(8,128)(2,1)S(1)} collective-permute-done((bf16[768,128]{1,0:T(8,128)(2,1)S(1)}, bf16[768,128]{1,0:T(8,128)(2,1)S(1)}, u32[]{:S(2)}, u32[]{:S(2)}) %collective-permute-start.13) | collective-permute-done | bytes 196640 | tf_op jit(solution)/shard_map/ppermute | solution.py:333
  111.7 10.9 %all_to_all.15.rows_ref = bf16[8,96,128]{2,1,0:T(8,128)(2,1)S(1)} all-to-all(bf16[8,96,128]{2,1,0:T(8,128)(2,1)S(1)} %bitcast.5), channel_id=1, replica_groups=mesh['ctx'=16,'head'=8,'batch'=4] {'head'}, dimensions={0} | all-to-all | bytes 393216 | tf_op jit(solution)/shard_map/all_to_all | solution.py:312
  123.1 9.2 %all_to_all.16 = bf16[8,96,128]{2,1,0:T(8,128)(2,1)S(1)} all-to-all(bf16[8,96,128]{2,1,0:T(8,128)(2,1)S(1)} %shard_map.64), channel_id=1, replica_groups=mesh['ctx'=16,'head'=8,'batch'=4] {'head'}, dimensions={0} | all-to-all | bytes 393216 | tf_op jit(solution)/shard_map/all_to_all | solution.py:312
  (36 shorter events, 10.6 us)
Async XLA Ops:
  3.8 11.4 %copy-start.4 = (bf16[128,1024]{1,0:T(8,128)(2,1)S(1)}, bf16[128,1024]{1,0:T(8,128)(2,1)}, u32[]{:S(2)}) copy-start(bf16[128,1024]{1,0:T(8,128)(2,1)} %param.9) | copy-start | bytes 786436
  3.9 39.8 %all-to-all-start = ((bf16[12,128,512]{2,1,0:T(8,128)(2,1)}), bf16[12,128,512]{2,1,0:T(8,128)(2,1)S(1)}, u32[]{:S(2)}, u32[]{:S(2)}) async-start(bf16[12,128,512]{2,1,0:T(8,128)(2,1)} %shard_map.55), calls=%async_computation | async-start | bytes 3145728 | tf_op jit(solution)/shard_map/all_to_all | solution.py:316
  15.3 28.4 %copy-start.2 = (s32[1,4,6]{2,1,0:T(4,128)S(1)}, s32[1,4,6]{2,1,0:T(4,128)}, u32[]{:S(2)}) copy-start(s32[1,4,6]{2,1,0:T(4,128)} %param.6) | copy-start | bytes 292
  15.3 10.1 %collective-permute-start.1 = (bf16[128,1024]{1,0:T(8,128)(2,1)S(1)}, bf16[128,1024]{1,0:T(8,128)(2,1)S(1)}, u32[]{:S(2)}, u32[]{:S(2)}) collective-permute-start(bf16[128,1024]{1,0:T(8,128)(2,1)S(1)} %copy-done.4), channel_id=1, source_target_pairs={{0,24},{4,28},{8,16},{12,20},{16,8},{20,12},{24,0},{28,4},{1,25},{... | collective-permute-start | bytes 786440 | tf_op jit(solution)/shard_map/ppermute | solution.py:301
  19.8 8.5 %collective-permute-start = (bf16[128,1024]{1,0:T(8,128)(2,1)S(1)}, bf16[128,1024]{1,0:T(8,128)(2,1)S(1)}, u32[]{:S(2)}, u32[]{:S(2)}) collective-permute-start(bf16[128,1024]{1,0:T(8,128)(2,1)S(1)} %copy-done.4), channel_id=1, source_target_pairs={{0,8},{4,12},{8,0},{12,4},{16,24},{20,28},{24,16},{28,20},{1,9},{5... | collective-permute-start | bytes 786440 | tf_op jit(solution)/shard_map/ppermute | solution.py:301
  25.4 6.4 %collective-permute-start.2 = (bf16[64,1024]{1,0:T(8,128)(2,1)S(1)}, bf16[64,1024]{1,0:T(8,128)(2,1)S(1)}, u32[]{:S(2)}, u32[]{:S(2)}) collective-permute-start(bf16[64,1024]{1,0:T(8,128)(2,1)S(1)} %slice.8), channel_id=1, source_target_pairs={{0,8},{4,12},{8,0},{12,4},{16,24},{20,28},{24,16},{28,20},{1,9},{5... | collective-permute-start | bytes 393224 | tf_op jit(solution)/shard_map/ppermute | solution.py:302
  28.3 60.2 %copy-start.3 = (s32[1,4]{1,0:T(1,128)S(1)}, s32[1,4]{1,0:T(1,128)}, u32[]{:S(2)}) copy-start(s32[1,4]{1,0:T(1,128)} %hist_ref.13) | copy-start | bytes 52
  28.3 7.2 %collective-permute-start.3 = (bf16[64,1024]{1,0:T(8,128)(2,1)S(1)}, bf16[64,1024]{1,0:T(8,128)(2,1)S(1)}, u32[]{:S(2)}, u32[]{:S(2)}) collective-permute-start(bf16[64,1024]{1,0:T(8,128)(2,1)S(1)} %slice.9), channel_id=1, source_target_pairs={{0,24},{4,28},{8,16},{12,20},{16,8},{20,12},{24,0},{28,4},{1,25},{... | collective-permute-start | bytes 393224 | tf_op jit(solution)/shard_map/ppermute | solution.py:302
  35.5 7.2 %collective-permute-start.4 = (bf16[512,1024]{1,0:T(8,128)(2,1)S(1)}, bf16[512,1024]{1,0:T(8,128)(2,1)S(1)}, u32[]{:S(2)}, u32[]{:S(2)}) collective-permute-start(bf16[512,1024]{1,0:T(8,128)(2,1)S(1)} %constant_dynamic-update-slice_fusion.mine_ref), channel_id=1, source_target_pairs={{0,4},{4,0},{8,12},{12,8},{16,20},{20,16},{24,28},{28,24},{1,5},{5... | collective-permute-start | bytes 3145736 | tf_op jit(solution)/shard_map/ppermute | solution.py:304
  42.7 1.0 copy-start
  44.4 17.5 %collective-permute-start.5 = (bf16[768,256]{1,0:T(8,128)(2,1)S(1)}, bf16[768,256]{1,0:T(8,128)(2,1)S(1)}, u32[]{:S(2)}, u32[]{:S(2)}) collective-permute-start(bf16[768,256]{1,0:T(8,128)(2,1)S(1)} %get-tuple-element.17.refs_0_), channel_id=1, source_target_pairs={{0,32},{32,64},{64,96},{96,128},{128,160},{160,192},{192,224},{224... | collective-permute-start | bytes 1179656 | tf_op jit(solution)/shard_map/ppermute | solution.py:322
  47.5 20.9 %collective-permute-start.9 = (bf16[768,256]{1,0:T(8,128)(2,1)S(1)}, bf16[768,256]{1,0:T(8,128)(2,1)S(1)}, u32[]{:S(2)}, u32[]{:S(2)}) collective-permute-start(bf16[768,256]{1,0:T(8,128)(2,1)S(1)} %get-tuple-element.17.refs_0_), channel_id=1, source_target_pairs={{0,224},{32,0},{64,32},{96,64},{128,96},{160,128},{192,160},{224,1... | collective-permute-start | bytes 1179656 | tf_op jit(solution)/shard_map/ppermute | solution.py:324
  61.9 13.1 %collective-permute-start.6 = (bf16[768,256]{1,0:T(8,128)(2,1)S(1)}, bf16[768,256]{1,0:T(8,128)(2,1)S(1)}, u32[]{:S(2)}, u32[]{:S(2)}) collective-permute-start(bf16[768,256]{1,0:T(8,128)(2,1)S(1)} %collective-permute-done.5.refs_0_), channel_id=1, source_target_pairs={{0,32},{32,64},{64,96},{96,128},{128,160},{160,192},{192,224},{224... | collective-permute-start | bytes 1179656 | tf_op jit(solution)/shard_map/ppermute | solution.py:322
  68.5 12.2 %collective-permute-start.10 = (bf16[768,256]{1,0:T(8,128)(2,1)S(1)}, bf16[768,256]{1,0:T(8,128)(2,1)S(1)}, u32[]{:S(2)}, u32[]{:S(2)}) collective-permute-start(bf16[768,256]{1,0:T(8,128)(2,1)S(1)} %collective-permute-done.9.refs_1_), channel_id=1, source_target_pairs={{0,224},{32,0},{64,32},{96,64},{128,96},{160,128},{192,160},{224,1... | collective-permute-start | bytes 1179656 | tf_op jit(solution)/shard_map/ppermute | solution.py:324
  75.0 17.3 %collective-permute-start.7 = (bf16[768,256]{1,0:T(8,128)(2,1)S(1)}, bf16[768,256]{1,0:T(8,128)(2,1)S(1)}, u32[]{:S(2)}, u32[]{:S(2)}) collective-permute-start(bf16[768,256]{1,0:T(8,128)(2,1)S(1)} %collective-permute-done.6.refs_0_), channel_id=1, source_target_pairs={{0,32},{32,64},{64,96},{96,128},{128,160},{160,192},{192,224},{224... | collective-permute-start | bytes 1179656 | tf_op jit(solution)/shard_map/ppermute | solution.py:322
  76.3 15.1 %collective-permute-start.12 = (bf16[768,128]{1,0:T(8,128)(2,1)S(1)}, bf16[768,128]{1,0:T(8,128)(2,1)S(1)}, u32[]{:S(2)}, u32[]{:S(2)}) collective-permute-start(bf16[768,128]{1,0:T(8,128)(2,1)S(1)} %get-tuple-element.16.q_ref), channel_id=1, source_target_pairs={{256,0},{288,32},{320,64},{352,96},{384,128},{416,160},{448,192},{... | collective-permute-start | bytes 589832 | tf_op jit(solution)/shard_map/ppermute | solution.py:325
  80.7 13.8 %collective-permute-start.11 = (bf16[768,256]{1,0:T(8,128)(2,1)S(1)}, bf16[768,256]{1,0:T(8,128)(2,1)S(1)}, u32[]{:S(2)}, u32[]{:S(2)}) collective-permute-start(bf16[768,256]{1,0:T(8,128)(2,1)S(1)} %collective-permute-done.10.refs_1_.refs_0_), channel_id=1, source_target_pairs={{0,224},{32,0},{64,32},{96,64},{128,96},{160,128},{192,160},{224,1... | collective-permute-start | bytes 1179656 | tf_op jit(solution)/shard_map/ppermute | solution.py:324
  92.3 18.4 %collective-permute-start.8 = (bf16[768,256]{1,0:T(8,128)(2,1)S(1)}, bf16[768,256]{1,0:T(8,128)(2,1)S(1)}, u32[]{:S(2)}, u32[]{:S(2)}) collective-permute-start(bf16[768,256]{1,0:T(8,128)(2,1)S(1)} %collective-permute-done.7.refs_0_), channel_id=1, source_target_pairs={{0,32},{32,64},{64,96},{96,128},{128,160},{160,192},{192,224},{224... | collective-permute-start | bytes 1179656 | tf_op jit(solution)/shard_map/ppermute | solution.py:322
  95.4 15.2 %collective-permute-start.13 = (bf16[768,128]{1,0:T(8,128)(2,1)S(1)}, bf16[768,128]{1,0:T(8,128)(2,1)S(1)}, u32[]{:S(2)}, u32[]{:S(2)}) collective-permute-start(bf16[768,128]{1,0:T(8,128)(2,1)S(1)} %shard_map.62), channel_id=1, source_target_pairs={{0,256},{32,288},{64,320},{96,352},{128,384},{160,416},{192,448},{... | collective-permute-start | bytes 589832 | tf_op jit(solution)/shard_map/ppermute | solution.py:333
  101.3 21.3 %copy-start.1 = (bf16[512,1024]{1,0:T(8,128)(2,1)S(1)}, bf16[512,1024]{1,0:T(8,128)(2,1)}, u32[]{:S(2)}) copy-start(bf16[512,1024]{1,0:T(8,128)(2,1)} %copy-done) | copy-start | bytes 3145732
